TPU v7x, 32 devices: a whole 2x2x4 slice. The times are simulated.
32 devices in a mesh: dp: 2 (over core), code: 16 (over z, y, x).
Axes of the slice: x: 2, y: 2, z: 4, core: 2. Of those that a mesh axis runs over, the one named last changes fastest.
Arguments:
- tokens: bfloat16 [1024, 256], P('dp'), may hold values from -0.59765625 to 0.59765625
- codebook: bfloat16 [131072, 256], P('code'), may hold values from -3 to 3
- gumbel_perturbation: bfloat16 [1024, 131072], P('dp', 'code'), may hold values from -1 to 120
- grad_out: bfloat16 [1024, 256], P('dp'), may hold values from -1.5 to 1.5
Outputs:
- quantized: float32 [1024, 256], P('dp')
- token_gradient: float32 [1024, 256], P('dp')
- grad_codebook: float32 [16, 8192, 256], P('code', 'dp')
All inputs are finite; a program needn't handle non-finite values.
Results may differ from a plain program's by a relative error of at most 0.017.
Values may be sent and summed in bfloat16 or wider, within the bound.
No kernel may reach another device: no remote copies, remote signals or barrier semaphores. Data moves between devices by JAX's collectives and lax.ppermute only.
A program may use at most 128 MiB of HBM per device.

v0:
```python
import jax
import jax.numpy as jnp
from jax import lax
from jax.sharding import PartitionSpec as P

SOFTMAX_HEAT = 0.5


def token_code_scores(left, codebook):
    return lax.dot_general(
        left, codebook, (((1,), (1,)), ((), ())), preferred_element_type=jnp.float32
    )


def over_tokens(left, right):
    return lax.dot_general(
        left, right, (((0,), (0,)), ((), ())), preferred_element_type=jnp.float32
    )


def local(tokens, codebook, gumbel_perturbation, grad_out):
    code_scores = (
        token_code_scores(tokens, codebook) + gumbel_perturbation.astype(jnp.float32)
    ) / SOFTMAX_HEAT
    row_max = lax.pmax(jnp.max(code_scores, axis=1), "code")
    weights = jnp.exp(code_scores - row_max[:, None])
    row_total = lax.psum(jnp.sum(weights, axis=1), "code")
    relaxed_codes = (weights / row_total[:, None]).astype(jnp.bfloat16)
    local_mix = jnp.dot(relaxed_codes, codebook, preferred_element_type=jnp.float32)
    relaxed_gradient = token_code_scores(grad_out, codebook)
    product = relaxed_codes * relaxed_gradient
    local_inner = jnp.sum(product, axis=1)
    weighted = product.astype(jnp.bfloat16)
    local_pulled = jnp.dot(weighted, codebook, preferred_element_type=jnp.float32)
    quantized = lax.psum(local_mix.astype(jnp.bfloat16), "code").astype(jnp.float32)
    gathered_codes, weighted_inner_total = lax.psum((local_pulled, local_inner), "code")
    token_gradient = (gathered_codes - weighted_inner_total[:, None] * quantized) / SOFTMAX_HEAT
    score_gradient = (
        relaxed_codes * (relaxed_gradient - weighted_inner_total[:, None]) / SOFTMAX_HEAT
    ).astype(jnp.bfloat16)
    own_rows = lax.psum_scatter(
        (over_tokens(relaxed_codes, grad_out) + over_tokens(score_gradient, tokens)).astype(
            jnp.bfloat16
        ),
        "dp",
        scatter_dimension=0,
        tiled=True,
    ).astype(jnp.float32)
    return (quantized, token_gradient, own_rows[None])


def solution(mesh):
    in_specs = (P("dp", None), P("code", None), P("dp", "code"), P("dp", None))
    out_specs = (P("dp", None), P("dp", None), P("code", "dp", None))
    return jax.shard_map(local, mesh=mesh, in_specs=in_specs, out_specs=out_specs, check_vma=False)
```

profile of v0, /device:TPU:0, one launch (start us, length us, event | category | flops | bytes accessed | tf_op | source)
XLA Modules:
  0.0 364.0 jit_solution(12480782700765281892)
XLA Ops:
  8.0 0.0 copy-start
  8.0 0.0 all-reduce.3.cloned.1.call-start
  8.1 13.0 %fusion.12 = (f32[512]{0:T(512)S(1)}, f32[512,8192]{1,0:T(8,128)}) fusion(bf16[512,8192]{1,0:T(8,128)(2,1)} %param.6, bf16[512,256]{1,0:T(8,128)(2,1)} %param.4, bf16[8192,256]{1,0:T(8,128)(2,1)} %param.5), kind=kOutput, calls=%fused_computation.19 | convolution fusion | flops 2164260352 | bytes 29624320 | tf_op jit(solution)/shard_map/dot_general | solution.py:10
  21.0 43.5 %pmax.7 = f32[512]{0:T(512)S(1)} all-reduce(f32[512]{0:T(512)S(1)} %get-tuple-element.7), channel_id=1, replica_groups=mesh['dp'=2,'code'=16] {'code'}, use_global_device_ids=true, to_apply=%region_1.0 | all-reduce | flops 512 | bytes 4096 | tf_op jit(solution)/shard_map/pmax | solution.py:25
  64.5 8.1 %fusion.2 = f32[512]{0:T(512)S(1)} fusion(f32[512,8192]{1,0:T(8,128)} %get-tuple-element.8, f32[512]{0:T(512)S(1)} %pmax.7), kind=kLoop, calls=%fused_computation.7 | loop fusion | flops 8388096 | bytes 16781312 | tf_op jit(solution)/shard_map/reduce_sum | solution.py:27
  72.6 36.6 %psum.28 = f32[512]{0:T(512)S(1)} all-reduce(f32[512]{0:T(512)S(1)} %fusion.2), channel_id=1, replica_groups=mesh['dp'=2,'code'=16] {'code'}, use_global_device_ids=true, to_apply=%region_3.0 | all-reduce | flops 512 | bytes 4096 | tf_op jit(solution)/shard_map/psum | solution.py:27
  109.2 0.0 copy-done
  109.2 15.1 %fusion.3 = (f32[512]{0:T(512)S(1)}, bf16[512,8192]{1,0:T(8,128)(2,1)}, f32[512,8192]{1,0:T(8,128)}) fusion(f32[512]{0:T(512)S(1)} %psum.28, f32[512,8192]{1,0:T(8,128)} %get-tuple-element.8, f32[512]{0:T(512)S(1)} %pmax.7, bf16[512,256]{1,0:T(8,128)(2,1)S(1)} %copy-done, bf16[8192,256]{1,0:T(8,128)(2,1)} %param.5), kind=kOutput, calls=%fused_computation.8 | convolution fusion | flops 2172648960 | bytes 46405632 | tf_op jit(solution)/shard_map/dot_general | solution.py:10
  124.3 7.6 %convolution_convert_fusion = bf16[512,256]{1,0:T(8,128)(2,1)} fusion(bf16[512,8192]{1,0:T(8,128)(2,1)} %get-tuple-element.6, bf16[8192,256]{1,0:T(8,128)(2,1)} %param.5), kind=kOutput, calls=%fused_computation.16 | convolution fusion | flops 2147614720 | bytes 12845056 | tf_op jit(solution)/shard_map/dot_general | solution.py:29
  131.9 0.0 all-reduce.3.cloned.1.call-update
  131.9 0.2 all-reduce.5.cloned.1.call-start
  132.2 12.6 %fusion.6 = f32[512,256]{1,0:T(8,128)} fusion(bf16[8192,256]{1,0:T(8,128)(2,1)} %param.5, f32[512,8192]{1,0:T(8,128)} %get-tuple-element.9, bf16[512,8192]{1,0:T(8,128)(2,1)} %get-tuple-element.6), kind=kOutput, calls=%fused_computation.12 | convolution fusion | flops 2160066560 | bytes 29884416 | tf_op jit(solution)/shard_map/dot_general | solution.py:34
  144.7 0.0 all-reduce.5.cloned.1.call-update
  144.8 0.0 copy-start.1
  144.8 0.0 reduce-scatter.2.cloned.1.call-start
  144.8 9.0 %fusion.13 = f32[8192,256]{1,0:T(8,128)} fusion(bf16[512,8192]{1,0:T(8,128)(2,1)} %get-tuple-element.6, bf16[512,256]{1,0:T(8,128)(2,1)S(1)} %copy-done), kind=kOutput, calls=%fused_computation.20 | convolution fusion | flops 2147483648 | bytes 17039360 | tf_op jit(solution)/shard_map/dot_general | solution.py:16
  153.9 38.6 %psum.31 = f32[512]{0:T(512)S(1)} all-reduce(f32[512]{0:T(512)S(1)} %get-tuple-element.5), channel_id=1, replica_groups=mesh['dp'=2,'code'=16] {'code'}, use_global_device_ids=true, to_apply=%region_7.0 | all-reduce | flops 512 | bytes 4096 | tf_op jit(solution)/shard_map/psum | solution.py:36
  192.5 0.0 copy-done.1
  192.5 17.7 %fusion.5 = bf16[8192,256]{1,0:T(8,128)(2,1)} fusion(f32[8192,256]{1,0:T(8,128)} %fusion.13, bf16[512,256]{1,0:T(8,128)(2,1)S(1)} %copy-done.1, bf16[512,8192]{1,0:T(8,128)(2,1)} %get-tuple-element.6, f32[512,8192]{1,0:T(8,128)} %get-tuple-element.9, f32[512]{0:T(512)S(1)} %psum.31), kind=kOutput, calls=%fused_computation.11 | convolution fusion | flops 2172649472 | bytes 38012928 | tf_op jit(solution)/shard_map/dot_general | solution.py:16
  210.2 0.0 reduce-scatter.2.cloned.1.call-update
  210.2 26.4 %all-reduce.3.cloned.1.call-done = bf16[512,256]{1,0:T(8,128)(2,1)} async-done(((bf16[512,256]{1,0:T(8,128)(2,1)}), bf16[512,256]{1,0:T(8,128)(2,1)}) %all-reduce.3.cloned.1.call-update) | async-done | bytes 262160 | tf_op jit(solution)/shard_map/psum | solution.py:35
  236.6 113.9 %all-reduce.5.cloned.1.call-done = f32[512,256]{1,0:T(8,128)} async-done(((f32[512,256]{1,0:T(8,128)}), f32[512,256]{1,0:T(8,128)}) %all-reduce.5.cloned.1.call-update) | async-done | bytes 524304 | tf_op jit(solution)/shard_map/psum | solution.py:36
  350.5 2.1 subtract_multiply_fusion
  352.6 0.0 reduce-scatter.2.cloned.1.call-done
  352.6 3.9 %bitcast_convert_fusion = f32[1,4096,256]{2,1,0:T(8,128)} fusion(bf16[4096,256]{1,0:T(8,128)(2,1)} %reduce-scatter.2.cloned.1.call-done), kind=kLoop, calls=%fused_computation.15 | loop fusion | flops 1048576 | bytes 6291456 | tf_op jit(solution)/shard_map/broadcast_in_dim | solution.py:49
Async XLA Ops:
  8.0 101.2 %copy-start = (bf16[512,256]{1,0:T(8,128)(2,1)S(1)}, bf16[512,256]{1,0:T(8,128)(2,1)}, u32[]{:S(2)}) copy-start(bf16[512,256]{1,0:T(8,128)(2,1)} %param.7) | copy-start | bytes 786436
  8.0 228.6 %all-reduce.3.cloned.1.call-start = ((), (), s32[]{:S(2)}) async-start(), calls=%async_computation.1 | async-start | bytes 524288 | tf_op jit(solution)/shard_map/psum | solution.py:35
  131.9 218.5 %all-reduce.5.cloned.1.call-start = ((), (), s32[]{:S(2)}) async-start(), calls=%async_computation.2 | async-start | bytes 1048576 | tf_op jit(solution)/shard_map/psum | solution.py:36
  144.8 47.7 %copy-start.1 = (bf16[512,256]{1,0:T(8,128)(2,1)S(1)}, bf16[512,256]{1,0:T(8,128)(2,1)}, u32[]{:S(2)}) copy-start(bf16[512,256]{1,0:T(8,128)(2,1)} %param.4) | copy-start | bytes 786436
  144.8 207.8 %reduce-scatter.2.cloned.1.call-start = ((), (), s32[]{:S(2)}) async-start(), calls=%async_computation.3 | async-start | bytes 6291456 | tf_op jit(solution)/shard_map/reduce_scatter | solution.py:41
Sparse Core Ops, SparseCore 0:
  132.1 104.5 all-reduce.2
  243.1 107.2 all-reduce.4
Sparse Core Ops, SparseCore 1:
  210.3 7.8 reduce-scatter.1
where the time goes:
time: 364 us
  waiting for transfers between devices  140 us (38%)
  blocking collectives  119 us (33%)
  matrix products  75 us (21%)
  between operations  15.5 us (4%)
  other arithmetic  14.2 us (4%)
    psum x1, waiting for transfers between devices, local(): lax.psum((local_pulled, local_inner), 'code')  114 us
    pmax x1, blocking collectives, local(): row_max = lax.pmax(jnp.max(code_scores, axis=1), 'code')  43.5 us
    psum x1, blocking collectives, local(): lax.psum((local_pulled, local_inner), 'code')  38.6 us
    psum x1, blocking collectives, local(): row_total = lax.psum(jnp.sum(weights, axis=1), 'code')  36.6 us
    dot_general x2, matrix products, token_code_scores(): lax.dot_general(left, codebook, (((1,), (1,)), ((), ())), preferred_eleme...  28.1 us
    dot_general x2, matrix products, over_tokens(): lax.dot_general(left, right, (((0,), (0,)), ((), ())), preferred_element_...  26.7 us
    psum x1, waiting for transfers between devices, local(): lax.psum(local_mix.astype(jnp.bfloat16), 'code').astype(jnp.float32)  26.4 us
    dot_general x1, matrix products, local(): jnp.dot(weighted, codebook, preferred_element_type=jnp.float32)  12.6 us
  transfers between devices with their start and end apart: 3, of which 2 were waited for; matrix products, arithmetic and copies ran while one was open for 11% of the time, Pallas kernels for 0%

commit v1 on v0

v1 whole, which is shorter than its diff:
```python
import jax
import jax.numpy as jnp
from jax import lax
from jax.sharding import PartitionSpec as P

SOFTMAX_HEAT = 0.5
BF16 = jnp.bfloat16
F32 = jnp.float32


def token_code_scores(left, codebook):
    return lax.dot_general(left, codebook, (((1,), (1,)), ((), ())), preferred_element_type=F32)


def over_tokens(left, right):
    return lax.dot_general(left, right, (((0,), (0,)), ((), ())), preferred_element_type=F32)


def swap(value, axis, size, mask):
    return lax.ppermute(value, axis, [(i, i ^ mask) for i in range(size)])


def halving_sum(value, axis, size):
    at = lax.axis_index(axis)
    rows = value.shape[0]
    mask = 1
    while mask < size:
        rows //= 2
        upper = (at // mask) % 2
        keep = lax.dynamic_slice_in_dim(value, upper * rows, rows, 0)
        give = lax.dynamic_slice_in_dim(value, (1 - upper) * rows, rows, 0)
        got = swap(give, axis, size, mask)
        value = (keep.astype(F32) + got.astype(F32)).astype(BF16)
        mask *= 2
    mask = size // 2
    while mask:
        upper = (at // mask) % 2
        got = swap(value, axis, size, mask)
        low = jnp.where(upper == 0, value, got)
        high = jnp.where(upper == 0, got, value)
        value = jnp.concatenate([low, high], axis=0)
        mask //= 2
    return value


def local(n_dp, n_code, tokens, codebook, gumbel_perturbation, grad_out):
    scores = (
        token_code_scores(tokens, codebook) + gumbel_perturbation.astype(F32)
    ) / SOFTMAX_HEAT
    own_max = jnp.max(scores, axis=1)
    weights = jnp.exp(scores - own_max[:, None])
    own_total = jnp.sum(weights, axis=1)
    codes = weights.astype(BF16)
    gradient = token_code_scores(grad_out, codebook)
    product = codes.astype(F32) * gradient
    own_inner = jnp.sum(product, axis=1)

    own = jnp.stack([own_max, own_total, own_inner])
    stats = [own] + [swap(own, "code", n_code, d) for d in range(1, n_code)]
    stats = jnp.stack(stats)
    row_max = jnp.max(stats[:, 0], axis=0)
    shift = jnp.exp(stats[:, 0] - row_max)
    total = jnp.sum(stats[:, 1] * shift, axis=0)
    inner = jnp.sum(stats[:, 2] * shift, axis=0) / total
    scale = (shift[0] / total)[:, None]

    mix = jnp.dot(codes, codebook, preferred_element_type=F32)
    pulled = jnp.dot(product.astype(BF16), codebook, preferred_element_type=F32)
    part = jnp.concatenate(
        [scale * mix, (pulled - inner[:, None] * mix) * (scale / SOFTMAX_HEAT)], axis=1
    ).astype(BF16)
    summed = halving_sum(part, "code", n_code).astype(F32)
    width = tokens.shape[1]
    quantized, token_gradient = summed[:, :width], summed[:, width:]

    score_gradient = (codes.astype(F32) * (gradient - inner[:, None])).astype(BF16)
    group = (
        over_tokens(codes, (scale * grad_out.astype(F32)).astype(BF16))
        + over_tokens(score_gradient, (scale / SOFTMAX_HEAT * tokens.astype(F32)).astype(BF16))
    ).astype(BF16)
    at = lax.axis_index("dp")
    rows = group.shape[0] // n_dp
    own_rows = lax.dynamic_slice_in_dim(group, at * rows, rows, 0).astype(F32)
    for d in range(1, n_dp):
        give = lax.dynamic_slice_in_dim(group, (at ^ d) * rows, rows, 0)
        own_rows = own_rows + swap(give, "dp", n_dp, d).astype(F32)
    return (quantized, token_gradient, own_rows[None])


def solution(mesh):
    n_dp, n_code = mesh.shape["dp"], mesh.shape["code"]

    def call(*args):
        return local(n_dp, n_code, *args)

    in_specs = (P("dp", None), P("code", None), P("dp", "code"), P("dp", None))
    out_specs = (P("dp", None), P("dp", None), P("code", "dp", None))
    return jax.shard_map(call, mesh=mesh, in_specs=in_specs, out_specs=out_specs, check_vma=False)
```

time: 364 us -> 154 us (0.42)
  blocking collectives: 119 us -> 0 us
  waiting for transfers between devices: 140 us -> 35.2 us
  starting transfers between devices: 0.3 us -> 33.8 us
  between operations: 15.5 us -> 1.05 us
  other arithmetic: 14.2 us -> 5.91 us
  local copies, waits for them, and re-layouts: 0.02 us -> 4.59 us
    psum x2 -> x0, waiting for transfers between devices: 140 us -> none  [the longest x1 114 us: local(): lax.psum((local_pulled, local_inner), 'code')]
    psum x2 -> x0, blocking collectives: 75.1 us -> none  [the longest x1 38.6 us: local(): lax.psum((local_pulled, local_inner), 'code')]
    pmax x1 -> x0, blocking collectives: 43.5 us -> none  [local(): row_max = lax.pmax(jnp.max(code_scores, axis=1), 'code')]
    ppermute x0 -> x24, waiting for transfers between devices: none -> 35.2 us  [swap(): return lax.ppermute(value, axis, [(i, i ^ mask) for i in range(size)])]
    ppermute x0 -> x24, starting transfers between devices: none -> 33.8 us  [swap(): return lax.ppermute(value, axis, [(i, i ^ mask) for i in range(size)])]
    reduce_sum x1, other arithmetic: 8.11 us -> 0.03 us  [local(): inner = jnp.sum(stats[:, 2] * shift, axis=0) / total]
  transfers between devices with their start and end apart: 3 -> 24, of which waited for: 2 -> 9; matrix products, arithmetic and copies ran while one was open for 11% -> 20% of each run, Pallas kernels for 0% -> 0%
where the time goes in v1:
time: 154 us
  matrix products  73.2 us (48%)
  waiting for transfers between devices  35.2 us (23%)
  starting transfers between devices  33.8 us (22%)
  other arithmetic  5.91 us (4%)
  local copies, waits for them, and re-layouts  4.59 us (3%)
    ppermute x24, waiting for transfers between devices, swap(): return lax.ppermute(value, axis, [(i, i ^ mask) for i in range(size)])  35.2 us
    ppermute x24, starting transfers between devices, swap(): return lax.ppermute(value, axis, [(i, i ^ mask) for i in range(size)])  33.8 us
    dot_general x2, matrix products, token_code_scores(): lax.dot_general(left, codebook, (((1,), (1,)), ((), ())), preferred_eleme...  28.1 us
    dot_general x2, matrix products, over_tokens(): lax.dot_general(left, right, (((0,), (0,)), ((), ())), preferred_element_...  26.3 us
    dot_general x1, matrix products, local(): pulled = jnp.dot(product.astype(BF16), codebook, preferred_element_type=F32)  11.8 us
    dot_general x1, matrix products, local(): mix = jnp.dot(codes, codebook, preferred_element_type=F32)  6.95 us
    broadcast_in_dim x1, other arithmetic, local(): return (quantized, token_gradient, own_rows[None])  4.7 us
  transfers between devices with their start and end apart: 24, of which 9 were waited for; matrix products, arithmetic and copies ran while one was open for 20% of the time, Pallas kernels for 0%

profile of v1, /device:TPU:0, one launch (start us, length us, event | category | flops | bytes accessed | tf_op | source)
XLA Modules:
  0.0 153.7 jit_solution(9923073794038617588)
XLA Ops:
  0.6 13.0 %fusion.33 = (f32[512]{0:T(512)S(1)}, f32[512,8192]{1,0:T(8,128)}) fusion(bf16[512,8192]{1,0:T(8,128)(2,1)} %param.6, bf16[512,256]{1,0:T(8,128)(2,1)} %param.4, bf16[8192,256]{1,0:T(8,128)(2,1)} %param.5), kind=kOutput, calls=%fused_computation.62 | convolution fusion | flops 2164260352 | bytes 29624320 | tf_op jit(solution)/shard_map/dot_general | solution.py:12
  13.7 15.1 %fusion.4 = (f32[512]{0:T(512)S(1)}, bf16[512,8192]{1,0:T(8,128)(2,1)}, f32[512]{0:T(512)S(1)}, f32[512,8192]{1,0:T(8,128)}) fusion(f32[512,8192]{1,0:T(8,128)} %get-tuple-element.31, f32[512]{0:T(512)S(1)} %get-tuple-element.30, bf16[512,256]{1,0:T(8,128)(2,1)S(1)} %copy-done, bf16[8192,256]{1,0:T(8,128)(2,1)} %param.5), kind=kOutput, calls=%fused_computation.8 | convolution fusion | flops 2172648448 | bytes 46405632 | tf_op jit(solution)/shard_map/dot_general | solution.py:12
  28.8 3.0 %collective-permute-start = (f32[3,512]{1,0:T(4,128)S(1)}, f32[3,512]{1,0:T(4,128)S(1)}, u32[]{:S(2)}, u32[]{:S(2)}) collective-permute-start(f32[3,512]{1,0:T(4,128)S(1)} %get-tuple-element.27), channel_id=1, source_target_pairs={{0,1},{1,0},{2,3},{3,2},{4,5},{5,4},{6,7},{7,6},{8,9},{9,8},{10,11... | collective-permute-start | bytes 18440 | tf_op jit(solution)/shard_map/ppermute | solution.py:20
  31.8 1.5 collective-permute-start.1
  33.3 2.0 %collective-permute-start.3 = (f32[3,512]{1,0:T(4,128)S(1)}, f32[3,512]{1,0:T(4,128)S(1)}, u32[]{:S(2)}, u32[]{:S(2)}) collective-permute-start(f32[3,512]{1,0:T(4,128)S(1)} %get-tuple-element.27), channel_id=1, source_target_pairs={{0,4},{1,5},{2,6},{3,7},{4,0},{5,1},{6,2},{7,3},{8,12},{9,13},{10,... | collective-permute-start | bytes 18440 | tf_op jit(solution)/shard_map/ppermute | solution.py:20
  35.3 1.4 collective-permute-start.4
  36.7 2.5 %collective-permute-start.5 = (f32[3,512]{1,0:T(4,128)S(1)}, f32[3,512]{1,0:T(4,128)S(1)}, u32[]{:S(2)}, u32[]{:S(2)}) collective-permute-start(f32[3,512]{1,0:T(4,128)S(1)} %get-tuple-element.27), channel_id=1, source_target_pairs={{0,6},{1,7},{2,4},{3,5},{4,2},{5,3},{6,0},{7,1},{8,14},{9,15},{10,... | collective-permute-start | bytes 18440 | tf_op jit(solution)/shard_map/ppermute | solution.py:20
  39.3 2.9 %collective-permute-start.7 = (f32[3,512]{1,0:T(4,128)S(1)}, f32[3,512]{1,0:T(4,128)S(1)}, u32[]{:S(2)}, u32[]{:S(2)}) collective-permute-start(f32[3,512]{1,0:T(4,128)S(1)} %get-tuple-element.27), channel_id=1, source_target_pairs={{0,8},{1,9},{2,10},{3,11},{4,12},{5,13},{6,14},{7,15},{8,0},{9,1},... | collective-permute-start | bytes 18440 | tf_op jit(solution)/shard_map/ppermute | solution.py:20
  42.2 1.3 collective-permute-start.8
  43.5 3.5 %collective-permute-start.9 = (f32[3,512]{1,0:T(4,128)S(1)}, f32[3,512]{1,0:T(4,128)S(1)}, u32[]{:S(2)}, u32[]{:S(2)}) collective-permute-start(f32[3,512]{1,0:T(4,128)S(1)} %get-tuple-element.27), channel_id=1, source_target_pairs={{0,10},{1,11},{2,8},{3,9},{4,14},{5,15},{6,12},{7,13},{8,2},{9,3},... | collective-permute-start | bytes 18440 | tf_op jit(solution)/shard_map/ppermute | solution.py:20
  47.1 3.8 %collective-permute-start.11 = (f32[3,512]{1,0:T(4,128)S(1)}, f32[3,512]{1,0:T(4,128)S(1)}, u32[]{:S(2)}, u32[]{:S(2)}) collective-permute-start(f32[3,512]{1,0:T(4,128)S(1)} %get-tuple-element.27), channel_id=1, source_target_pairs={{0,12},{1,13},{2,14},{3,15},{4,8},{5,9},{6,10},{7,11},{8,4},{9,5},... | collective-permute-start | bytes 18440 | tf_op jit(solution)/shard_map/ppermute | solution.py:20
  50.9 1.2 collective-permute-start.12
  52.1 4.6 %collective-permute-start.13 = (f32[3,512]{1,0:T(4,128)S(1)}, f32[3,512]{1,0:T(4,128)S(1)}, u32[]{:S(2)}, u32[]{:S(2)}) collective-permute-start(f32[3,512]{1,0:T(4,128)S(1)} %get-tuple-element.27), channel_id=1, source_target_pairs={{0,14},{1,15},{2,12},{3,13},{4,10},{5,11},{6,8},{7,9},{8,6},{9,7},... | collective-permute-start | bytes 18440 | tf_op jit(solution)/shard_map/ppermute | solution.py:20
  57.3 1.2 collective-permute-done.13
  58.4 5.4 %collective-permute-done.14 = f32[3,512]{1,0:T(4,128)S(1)} collective-permute-done((f32[3,512]{1,0:T(4,128)S(1)}, f32[3,512]{1,0:T(4,128)S(1)}, u32[]{:S(2)}, u32[]{:S(2)}) %collective-permute-start.14) | collective-permute-done | bytes 6176 | tf_op jit(solution)/shard_map/ppermute | solution.py:20
  64.1 7.0 %multiply_convert_fusion.2 = (bf16[512,256]{0,1:T(8,128)(2,1)S(1)}, f32[512,256]{0,1:T(8,128)S(1)}) fusion(f32[512]{0:T(512)S(1)} %get-tuple-element.12, bf16[512,8192]{1,0:T(8,128)(2,1)} %get-tuple-element.15, bf16[8192,256]{1,0:T(8,128)(2,1)} %param.5), kind=kOutput, calls=%fused_computation.25 | convolution fusion | flops 2147745792 | bytes 13371392 | tf_op jit(solution)/shard_map/dot_general | solution.py:67
  71.1 11.8 %fusion.16 = bf16[512,256]{0,1:T(8,128)(2,1)S(1)} fusion(bf16[8192,256]{1,0:T(8,128)(2,1)} %param.5, f32[512,8192]{1,0:T(8,128)} %get-tuple-element.32, bf16[512,8192]{1,0:T(8,128)(2,1)} %get-tuple-element.15, f32[512,256]{0,1:T(8,128)S(1)} %get-tuple-element.34, f32[512]{0:T(512)S(1)} %get-tuple-element.11, f32[512]{0:T(512)S(1)} %get-tuple-element.29), kind=kOutput, calls=%fused_computation.16 | convolution fusion | flops 2160590848 | bytes 30150656 | tf_op jit(solution)/shard_map/dot_general | solution.py:68
  83.5 5.8 %collective-permute-done.15 = bf16[256,512]{0,1:T(8,128)(2,1)S(1)} collective-permute-done((bf16[256,512]{0,1:T(8,128)(2,1)S(1)}, bf16[256,512]{0,1:T(8,128)(2,1)S(1)}, u32[]{:S(2)}, u32[]{:S(2)}) %collective-permute-start.15) | collective-permute-done | bytes 262176 | tf_op jit(solution)/shard_map/ppermute | solution.py:20
  90.4 4.1 %collective-permute-done.16 = bf16[128,512]{0,1:T(8,128)(2,1)S(1)} collective-permute-done((bf16[128,512]{0,1:T(8,128)(2,1)S(1)}, bf16[128,512]{0,1:T(8,128)(2,1)S(1)}, u32[]{:S(2)}, u32[]{:S(2)}) %collective-permute-start.16) | collective-permute-done | bytes 131104 | tf_op jit(solution)/shard_map/ppermute | solution.py:20
  94.7 9.0 %fusion.19 = f32[8192,256]{1,0:T(8,128)} fusion(bf16[512,8192]{1,0:T(8,128)(2,1)} %get-tuple-element.15, bf16[512,256]{0,1:T(8,128)(2,1)S(1)} %copy.28, f32[512]{0:T(512)S(1)} %get-tuple-element.12), kind=kOutput, calls=%fused_computation.26 | convolution fusion | flops 2147876864 | bytes 17041408 | tf_op jit(solution)/shard_map/dot_general | solution.py:16
  104.0 0.8 collective-permute-start.18
  104.8 17.3 %fusion.5 = bf16[8192,256]{1,0:T(8,128)(2,1)} fusion(f32[8192,256]{1,0:T(8,128)} %fusion.19, bf16[512,8192]{1,0:T(8,128)(2,1)} %get-tuple-element.15, f32[512,8192]{1,0:T(8,128)} %get-tuple-element.32, f32[512]{0:T(512)S(1)} %get-tuple-element.29, bf16[512,256]{0,1:T(8,128)(2,1)S(1)} %copy.29, f32[512]{0:T(512)S(1)} %get-tuple-element.11), kind=kOutput, calls=%fused_computation.10 | convolution fusion | flops 2168848384 | bytes 38014976 | tf_op jit(solution)/shard_map/dot_general | solution.py:16
  122.2 2.2 %collective-permute-start.19 = (bf16[32,512]{0,1:T(8,128)(2,1)S(1)}, bf16[32,512]{0,1:T(8,128)(2,1)S(1)}, u32[]{:S(2)}, u32[]{:S(2)}) collective-permute-start(bf16[32,512]{0,1:T(8,128)(2,1)S(1)} %add_convert_fusion.1), channel_id=1, source_target_pairs={{0,8},{1,9},{2,10},{3,11},{4,12},{5,13},{6,14},{7,15},{8,0},{9,1},... | collective-permute-start | bytes 98312 | tf_op jit(solution)/shard_map/ppermute | solution.py:20
  124.4 1.7 %constant_dynamic-slice_fusion = bf16[4096,256]{1,0:T(8,128)(2,1)S(1)} fusion(bf16[8192,256]{1,0:T(8,128)(2,1)} %fusion.5, s32[]{:T(128)S(6)} %select_n.148), kind=kLoop, calls=%fused_computation.55 | loop fusion | bytes 4194308 | tf_op jit(solution)/shard_map/dynamic_slice | solution.py:85
  126.3 3.3 %collective-permute-done.19 = bf16[32,512]{0,1:T(8,128)(2,1)S(1)} collective-permute-done((bf16[32,512]{0,1:T(8,128)(2,1)S(1)}, bf16[32,512]{0,1:T(8,128)(2,1)S(1)}, u32[]{:S(2)}, u32[]{:S(2)}) %collective-permute-start.19) | collective-permute-done | bytes 32800 | tf_op jit(solution)/shard_map/ppermute | solution.py:20
  130.1 4.7 %collective-permute-done.20 = bf16[64,512]{0,1:T(8,128)(2,1)S(1)} collective-permute-done((bf16[64,512]{0,1:T(8,128)(2,1)S(1)}, bf16[64,512]{0,1:T(8,128)(2,1)S(1)}, u32[]{:S(2)}, u32[]{:S(2)}) %collective-permute-start.20) | collective-permute-done | bytes 65568 | tf_op jit(solution)/shard_map/ppermute | solution.py:20
  135.6 4.4 %collective-permute-done.21 = bf16[128,512]{0,1:T(8,128)(2,1)S(1)} collective-permute-done((bf16[128,512]{0,1:T(8,128)(2,1)S(1)}, bf16[128,512]{0,1:T(8,128)(2,1)S(1)}, u32[]{:S(2)}, u32[]{:S(2)}) %collective-permute-start.21) | collective-permute-done | bytes 131104 | tf_op jit(solution)/shard_map/ppermute | solution.py:20
  140.2 0.6 collective-permute-start.22
  140.8 5.8 %collective-permute-done.22 = bf16[256,512]{0,1:T(8,128)(2,1)S(1)} collective-permute-done((bf16[256,512]{0,1:T(8,128)(2,1)S(1)}, bf16[256,512]{0,1:T(8,128)(2,1)S(1)}, u32[]{:S(2)}, u32[]{:S(2)}) %collective-permute-start.22) | collective-permute-done | bytes 262176 | tf_op jit(solution)/shard_map/ppermute | solution.py:20
  147.0 1.0 copy.30
  148.0 1.0 copy.31
  149.0 4.7 %add_bitcast_fusion = f32[1,4096,256]{2,1,0:T(8,128)} fusion(bf16[4096,256]{1,0:T(8,128)(2,1)} %collective-permute-done.23, bf16[8192,256]{1,0:T(8,128)(2,1)} %fusion.5, s32[]{:T(128)S(6)} %select_n.147), kind=kLoop, calls=%fused_computation.13 | loop fusion | flops 3145728 | bytes 8388612 | tf_op jit(solution)/shard_map/broadcast_in_dim | solution.py:87
  (71 shorter events, 4.9 us)
Async XLA Ops:
  0.6 13.0 %copy-start = (bf16[512,256]{1,0:T(8,128)(2,1)S(1)}, bf16[512,256]{1,0:T(8,128)(2,1)}, u32[]{:S(2)}) copy-start(bf16[512,256]{1,0:T(8,128)(2,1)} %param.7) | copy-start | bytes 786436
  28.8 8.0 %collective-permute-start = (f32[3,512]{1,0:T(4,128)S(1)}, f32[3,512]{1,0:T(4,128)S(1)}, u32[]{:S(2)}, u32[]{:S(2)}) collective-permute-start(f32[3,512]{1,0:T(4,128)S(1)} %get-tuple-element.27), channel_id=1, source_target_pairs={{0,1},{1,0},{2,3},{3,2},{4,5},{5,4},{6,7},{7,6},{8,9},{9,8},{10,11... | collective-permute-start | bytes 18440 | tf_op jit(solution)/shard_map/ppermute | solution.py:20
  31.8 7.5 %collective-permute-start.1 = (f32[3,512]{1,0:T(4,128)S(1)}, f32[3,512]{1,0:T(4,128)S(1)}, u32[]{:S(2)}, u32[]{:S(2)}) collective-permute-start(f32[3,512]{1,0:T(4,128)S(1)} %get-tuple-element.27), channel_id=1, source_target_pairs={{0,2},{1,3},{2,0},{3,1},{4,6},{5,7},{6,4},{7,5},{8,10},{9,11},{10,... | collective-permute-start | bytes 18440 | tf_op jit(solution)/shard_map/ppermute | solution.py:20
  33.3 6.0 %collective-permute-start.2 = (f32[3,512]{1,0:T(4,128)S(1)}, f32[3,512]{1,0:T(4,128)S(1)}, u32[]{:S(2)}, u32[]{:S(2)}) collective-permute-start(f32[3,512]{1,0:T(4,128)S(1)} %get-tuple-element.27), channel_id=1, source_target_pairs={{0,3},{1,2},{2,1},{3,0},{4,7},{5,6},{6,5},{7,4},{8,11},{9,10},{10,... | collective-permute-start | bytes 18440 | tf_op jit(solution)/shard_map/ppermute | solution.py:20
  33.3 8.9 %collective-permute-start.3 = (f32[3,512]{1,0:T(4,128)S(1)}, f32[3,512]{1,0:T(4,128)S(1)}, u32[]{:S(2)}, u32[]{:S(2)}) collective-permute-start(f32[3,512]{1,0:T(4,128)S(1)} %get-tuple-element.27), channel_id=1, source_target_pairs={{0,4},{1,5},{2,6},{3,7},{4,0},{5,1},{6,2},{7,3},{8,12},{9,13},{10,... | collective-permute-start | bytes 18440 | tf_op jit(solution)/shard_map/ppermute | solution.py:20
  35.3 8.2 %collective-permute-start.4 = (f32[3,512]{1,0:T(4,128)S(1)}, f32[3,512]{1,0:T(4,128)S(1)}, u32[]{:S(2)}, u32[]{:S(2)}) collective-permute-start(f32[3,512]{1,0:T(4,128)S(1)} %get-tuple-element.27), channel_id=1, source_target_pairs={{0,5},{1,4},{2,7},{3,6},{4,1},{5,0},{6,3},{7,2},{8,13},{9,12},{10,... | collective-permute-start | bytes 18440 | tf_op jit(solution)/shard_map/ppermute | solution.py:20
  36.7 10.3 %collective-permute-start.5 = (f32[3,512]{1,0:T(4,128)S(1)}, f32[3,512]{1,0:T(4,128)S(1)}, u32[]{:S(2)}, u32[]{:S(2)}) collective-permute-start(f32[3,512]{1,0:T(4,128)S(1)} %get-tuple-element.27), channel_id=1, source_target_pairs={{0,6},{1,7},{2,4},{3,5},{4,2},{5,3},{6,0},{7,1},{8,14},{9,15},{10,... | collective-permute-start | bytes 18440 | tf_op jit(solution)/shard_map/ppermute | solution.py:20
  39.3 7.8 %collective-permute-start.6 = (f32[3,512]{1,0:T(4,128)S(1)}, f32[3,512]{1,0:T(4,128)S(1)}, u32[]{:S(2)}, u32[]{:S(2)}) collective-permute-start(f32[3,512]{1,0:T(4,128)S(1)} %get-tuple-element.27), channel_id=1, source_target_pairs={{0,7},{1,6},{2,5},{3,4},{4,3},{5,2},{6,1},{7,0},{8,15},{9,14},{10,... | collective-permute-start | bytes 18440 | tf_op jit(solution)/shard_map/ppermute | solution.py:20
  39.3 11.6 %collective-permute-start.7 = (f32[3,512]{1,0:T(4,128)S(1)}, f32[3,512]{1,0:T(4,128)S(1)}, u32[]{:S(2)}, u32[]{:S(2)}) collective-permute-start(f32[3,512]{1,0:T(4,128)S(1)} %get-tuple-element.27), channel_id=1, source_target_pairs={{0,8},{1,9},{2,10},{3,11},{4,12},{5,13},{6,14},{7,15},{8,0},{9,1},... | collective-permute-start | bytes 18440 | tf_op jit(solution)/shard_map/ppermute | solution.py:20
  42.2 9.8 %collective-permute-start.8 = (f32[3,512]{1,0:T(4,128)S(1)}, f32[3,512]{1,0:T(4,128)S(1)}, u32[]{:S(2)}, u32[]{:S(2)}) collective-permute-start(f32[3,512]{1,0:T(4,128)S(1)} %get-tuple-element.27), channel_id=1, source_target_pairs={{0,9},{1,8},{2,11},{3,10},{4,13},{5,12},{6,15},{7,14},{8,1},{9,0},... | collective-permute-start | bytes 18440 | tf_op jit(solution)/shard_map/ppermute | solution.py:20
  43.5 13.1 %collective-permute-start.9 = (f32[3,512]{1,0:T(4,128)S(1)}, f32[3,512]{1,0:T(4,128)S(1)}, u32[]{:S(2)}, u32[]{:S(2)}) collective-permute-start(f32[3,512]{1,0:T(4,128)S(1)} %get-tuple-element.27), channel_id=1, source_target_pairs={{0,10},{1,11},{2,8},{3,9},{4,14},{5,15},{6,12},{7,13},{8,2},{9,3},... | collective-permute-start | bytes 18440 | tf_op jit(solution)/shard_map/ppermute | solution.py:20
  47.0 9.8 %collective-permute-start.10 = (f32[3,512]{1,0:T(4,128)S(1)}, f32[3,512]{1,0:T(4,128)S(1)}, u32[]{:S(2)}, u32[]{:S(2)}) collective-permute-start(f32[3,512]{1,0:T(4,128)S(1)} %get-tuple-element.27), channel_id=1, source_target_pairs={{0,11},{1,10},{2,9},{3,8},{4,15},{5,14},{6,13},{7,12},{8,3},{9,2},... | collective-permute-start | bytes 18440 | tf_op jit(solution)/shard_map/ppermute | solution.py:20
  47.1 9.8 %collective-permute-start.11 = (f32[3,512]{1,0:T(4,128)S(1)}, f32[3,512]{1,0:T(4,128)S(1)}, u32[]{:S(2)}, u32[]{:S(2)}) collective-permute-start(f32[3,512]{1,0:T(4,128)S(1)} %get-tuple-element.27), channel_id=1, source_target_pairs={{0,12},{1,13},{2,14},{3,15},{4,8},{5,9},{6,10},{7,11},{8,4},{9,5},... | collective-permute-start | bytes 18440 | tf_op jit(solution)/shard_map/ppermute | solution.py:20
  50.9 6.3 %collective-permute-start.12 = (f32[3,512]{1,0:T(4,128)S(1)}, f32[3,512]{1,0:T(4,128)S(1)}, u32[]{:S(2)}, u32[]{:S(2)}) collective-permute-start(f32[3,512]{1,0:T(4,128)S(1)} %get-tuple-element.27), channel_id=1, source_target_pairs={{0,13},{1,12},{2,15},{3,14},{4,9},{5,8},{6,11},{7,10},{8,5},{9,4},... | collective-permute-start | bytes 18440 | tf_op jit(solution)/shard_map/ppermute | solution.py:20
  52.1 6.4 %collective-permute-start.13 = (f32[3,512]{1,0:T(4,128)S(1)}, f32[3,512]{1,0:T(4,128)S(1)}, u32[]{:S(2)}, u32[]{:S(2)}) collective-permute-start(f32[3,512]{1,0:T(4,128)S(1)} %get-tuple-element.27), channel_id=1, source_target_pairs={{0,14},{1,15},{2,12},{3,13},{4,10},{5,11},{6,8},{7,9},{8,6},{9,7},... | collective-permute-start | bytes 18440 | tf_op jit(solution)/shard_map/ppermute | solution.py:20
  56.6 7.2 %collective-permute-start.14 = (f32[3,512]{1,0:T(4,128)S(1)}, f32[3,512]{1,0:T(4,128)S(1)}, u32[]{:S(2)}, u32[]{:S(2)}) collective-permute-start(f32[3,512]{1,0:T(4,128)S(1)} %get-tuple-element.27), channel_id=1, source_target_pairs={{0,15},{1,14},{2,13},{3,12},{4,11},{5,10},{6,9},{7,8},{8,7},{9,6},... | collective-permute-start | bytes 18440 | tf_op jit(solution)/shard_map/ppermute | solution.py:20
  71.1 19.1 %copy-start.1 = (bf16[512,256]{1,0:T(8,128)(2,1)S(1)}, bf16[512,256]{1,0:T(8,128)(2,1)}, u32[]{:S(2)}) copy-start(bf16[512,256]{1,0:T(8,128)(2,1)} %param.4) | copy-start | bytes 786436
  82.9 6.4 %collective-permute-start.15 = (bf16[256,512]{0,1:T(8,128)(2,1)S(1)}, bf16[256,512]{0,1:T(8,128)(2,1)S(1)}, u32[]{:S(2)}, u32[]{:S(2)}) collective-permute-start(bf16[256,512]{0,1:T(8,128)(2,1)S(1)} %fusion.20), channel_id=1, source_target_pairs={{0,1},{1,0},{2,3},{3,2},{4,5},{5,4},{6,7},{7,6},{8,9},{9,8},{10,11... | collective-permute-start | bytes 786440 | tf_op jit(solution)/shard_map/ppermute | solution.py:20
  89.5 5.0 %collective-permute-start.16 = (bf16[128,512]{0,1:T(8,128)(2,1)S(1)}, bf16[128,512]{0,1:T(8,128)(2,1)S(1)}, u32[]{:S(2)}, u32[]{:S(2)}) collective-permute-start(bf16[128,512]{0,1:T(8,128)(2,1)S(1)} %constant_dynamic-slice_fusion.3), channel_id=1, source_target_pairs={{0,2},{1,3},{2,0},{3,1},{4,6},{5,7},{6,4},{7,5},{8,10},{9,11},{10,... | collective-permute-start | bytes 393224 | tf_op jit(solution)/shard_map/ppermute | solution.py:20
  94.6 9.1 %collective-permute-start.17 = (bf16[64,512]{0,1:T(8,128)(2,1)S(1)}, bf16[64,512]{0,1:T(8,128)(2,1)S(1)}, u32[]{:S(2)}, u32[]{:S(2)}) collective-permute-start(bf16[64,512]{0,1:T(8,128)(2,1)S(1)} %constant_dynamic-slice_fusion.2), channel_id=1, source_target_pairs={{0,4},{1,5},{2,6},{3,7},{4,0},{5,1},{6,2},{7,3},{8,12},{9,13},{10,... | collective-permute-start | bytes 196616 | tf_op jit(solution)/shard_map/ppermute | solution.py:20
  104.0 18.1 %collective-permute-start.18 = (bf16[32,512]{0,1:T(8,128)(2,1)S(1)}, bf16[32,512]{0,1:T(8,128)(2,1)S(1)}, u32[]{:S(2)}, u32[]{:S(2)}) collective-permute-start(bf16[32,512]{0,1:T(8,128)(2,1)S(1)} %constant_dynamic-slice_fusion.1), channel_id=1, source_target_pairs={{0,8},{1,9},{2,10},{3,11},{4,12},{5,13},{6,14},{7,15},{8,0},{9,1},... | collective-permute-start | bytes 98312 | tf_op jit(solution)/shard_map/ppermute | solution.py:20
  122.2 7.3 %collective-permute-start.19 = (bf16[32,512]{0,1:T(8,128)(2,1)S(1)}, bf16[32,512]{0,1:T(8,128)(2,1)S(1)}, u32[]{:S(2)}, u32[]{:S(2)}) collective-permute-start(bf16[32,512]{0,1:T(8,128)(2,1)S(1)} %add_convert_fusion.1), channel_id=1, source_target_pairs={{0,8},{1,9},{2,10},{3,11},{4,12},{5,13},{6,14},{7,15},{8,0},{9,1},... | collective-permute-start | bytes 98312 | tf_op jit(solution)/shard_map/ppermute | solution.py:20
  126.2 22.8 %collective-permute-start.23 = (bf16[4096,256]{1,0:T(8,128)(2,1)S(1)}, bf16[4096,256]{1,0:T(8,128)(2,1)}, u32[]{:S(2)}, u32[]{:S(2)}) collective-permute-start(bf16[4096,256]{1,0:T(8,128)(2,1)S(1)} %constant_dynamic-slice_fusion), channel_id=1, source_target_pairs={{0,16},{16,0},{1,17},{17,1},{2,18},{18,2},{3,19},{19,3},{4,20},{20... | collective-permute-start | bytes 6291464 | tf_op jit(solution)/shard_map/ppermute | solution.py:20
  129.7 5.0 %collective-permute-start.20 = (bf16[64,512]{0,1:T(8,128)(2,1)S(1)}, bf16[64,512]{0,1:T(8,128)(2,1)S(1)}, u32[]{:S(2)}, u32[]{:S(2)}) collective-permute-start(bf16[64,512]{0,1:T(8,128)(2,1)S(1)} %pad_maximum_fusion.1), channel_id=1, source_target_pairs={{0,4},{1,5},{2,6},{3,7},{4,0},{5,1},{6,2},{7,3},{8,12},{9,13},{10,... | collective-permute-start | bytes 196616 | tf_op jit(solution)/shard_map/ppermute | solution.py:20
  135.0 5.0 %collective-permute-start.21 = (bf16[128,512]{0,1:T(8,128)(2,1)S(1)}, bf16[128,512]{0,1:T(8,128)(2,1)S(1)}, u32[]{:S(2)}, u32[]{:S(2)}) collective-permute-start(bf16[128,512]{0,1:T(8,128)(2,1)S(1)} %pad_maximum_fusion.2), channel_id=1, source_target_pairs={{0,2},{1,3},{2,0},{3,1},{4,6},{5,7},{6,4},{7,5},{8,10},{9,11},{10,... | collective-permute-start | bytes 393224 | tf_op jit(solution)/shard_map/ppermute | solution.py:20
  140.2 6.4 %collective-permute-start.22 = (bf16[256,512]{0,1:T(8,128)(2,1)S(1)}, bf16[256,512]{0,1:T(8,128)(2,1)S(1)}, u32[]{:S(2)}, u32[]{:S(2)}) collective-permute-start(bf16[256,512]{0,1:T(8,128)(2,1)S(1)} %pad_maximum_fusion), channel_id=1, source_target_pairs={{0,1},{1,0},{2,3},{3,2},{4,5},{5,4},{6,7},{7,6},{8,9},{9,8},{10,11... | collective-permute-start | bytes 786440 | tf_op jit(solution)/shard_map/ppermute | solution.py:20

commit v2 on v1

--- a/solution.py
+++ b/solution.py
@@ -20,27 +20,18 @@
     return lax.ppermute(value, axis, [(i, i ^ mask) for i in range(size)])
 
 
-def halving_sum(value, axis, size):
-    at = lax.axis_index(axis)
-    rows = value.shape[0]
-    mask = 1
-    while mask < size:
-        rows //= 2
-        upper = (at // mask) % 2
-        keep = lax.dynamic_slice_in_dim(value, upper * rows, rows, 0)
-        give = lax.dynamic_slice_in_dim(value, (1 - upper) * rows, rows, 0)
-        got = swap(give, axis, size, mask)
-        value = (keep.astype(F32) + got.astype(F32)).astype(BF16)
-        mask *= 2
-    mask = size // 2
-    while mask:
-        upper = (at // mask) % 2
-        got = swap(value, axis, size, mask)
-        low = jnp.where(upper == 0, value, got)
-        high = jnp.where(upper == 0, got, value)
-        value = jnp.concatenate([low, high], axis=0)
-        mask //= 2
-    return value
+def spread(value, axis, size):
+    whole = jnp.broadcast_to(value[None], (size,) + value.shape)
+    return lax.all_to_all(whole, axis, 0, 0, tiled=True)
+
+
+def sum_over(value, axis, size):
+    rows = value.shape[0] // size
+    pieces = lax.all_to_all(
+        value.reshape(size, rows, value.shape[1]), axis, 0, 0, tiled=True
+    )
+    own = jnp.sum(pieces.astype(F32), axis=0).astype(BF16)
+    return spread(own, axis, size).reshape(value.shape)
 
 
 def local(n_dp, n_code, tokens, codebook, gumbel_perturbation, grad_out):
@@ -56,20 +47,19 @@
     own_inner = jnp.sum(product, axis=1)
 
     own = jnp.stack([own_max, own_total, own_inner])
-    stats = [own] + [swap(own, "code", n_code, d) for d in range(1, n_code)]
-    stats = jnp.stack(stats)
+    stats = spread(own, "code", n_code)
     row_max = jnp.max(stats[:, 0], axis=0)
     shift = jnp.exp(stats[:, 0] - row_max)
     total = jnp.sum(stats[:, 1] * shift, axis=0)
     inner = jnp.sum(stats[:, 2] * shift, axis=0) / total
-    scale = (shift[0] / total)[:, None]
+    scale = (jnp.exp(own_max - row_max) / total)[:, None]
 
     mix = jnp.dot(codes, codebook, preferred_element_type=F32)
     pulled = jnp.dot(product.astype(BF16), codebook, preferred_element_type=F32)
     part = jnp.concatenate(
         [scale * mix, (pulled - inner[:, None] * mix) * (scale / SOFTMAX_HEAT)], axis=1
     ).astype(BF16)
-    summed = halving_sum(part, "code", n_code).astype(F32)
+    summed = sum_over(part, "code", n_code).astype(F32)
     width = tokens.shape[1]
     quantized, token_gradient = summed[:, :width], summed[:, width:]
 

time: 154 us -> 129 us (0.84)
  starting transfers between devices: 33.8 us -> 15.8 us
  matrix products: 73.2 us -> 68.3 us
    ppermute x24 -> x1, waiting for transfers between devices: 35.2 us -> 0.01 us  [swap(): return lax.ppermute(value, axis, [(i, i ^ mask) for i in range(size)])]
    all_to_all x0 -> x3, waiting for transfers between devices: none -> 33.9 us  [the longest x2 21.7 us: spread(): return lax.all_to_all(whole, axis, 0, 0, tiled=True)]
    ppermute x24 -> x1, starting transfers between devices: 33.8 us -> 0.07 us  [swap(): return lax.ppermute(value, axis, [(i, i ^ mask) for i in range(size)])]
    all_to_all x0 -> x3, starting transfers between devices: none -> 15.7 us  [the longest x2 12.1 us: spread(): return lax.all_to_all(whole, axis, 0, 0, tiled=True)]
    dot_general x1, matrix products: 6.95 us -> 2.33 us  [local(): mix = jnp.dot(codes, codebook, preferred_element_type=F32)]
    unnamed x8 -> x10, local copies, waits for them, and re-layouts: 2.28 us -> 0.03 us
  transfers between devices with their start and end apart: 24 -> 4, of which waited for: 9 -> 3; matrix products, arithmetic and copies ran while one was open for 20% -> 3% of each run, Pallas kernels for 0% -> 0%
where the time goes in v2:
time: 129 us
  matrix products  68.3 us (53%)
  waiting for transfers between devices  33.9 us (26%)
  starting transfers between devices  15.8 us (12%)
  other arithmetic  5.92 us (5%)
  local copies, waits for them, and re-layouts  4.33 us (3%)
    dot_general x2, matrix products, token_code_scores(): lax.dot_general(left, codebook, (((1,), (1,)), ((), ())), preferred_eleme...  28 us
    dot_general x2, matrix products, over_tokens(): lax.dot_general(left, right, (((0,), (0,)), ((), ())), preferred_element_...  26.3 us
    all_to_all x2, waiting for transfers between devices, spread(): return lax.all_to_all(whole, axis, 0, 0, tiled=True)  21.7 us
    all_to_all x1, waiting for transfers between devices, sum_over(): lax.all_to_all(value.reshape(size, rows, value.shape[1]), axis, 0, 0, til...  12.2 us
    all_to_all x2, starting transfers between devices, spread(): return lax.all_to_all(whole, axis, 0, 0, tiled=True)  12.1 us
    dot_general x1, matrix products, local(): pulled = jnp.dot(product.astype(BF16), codebook, preferred_element_type=F32)  11.7 us
    broadcast_in_dim x1, other arithmetic, local(): return (quantized, token_gradient, own_rows[None])  4.7 us
    all_to_all x1, starting transfers between devices, sum_over(): lax.all_to_all(value.reshape(size, rows, value.shape[1]), axis, 0, 0, til...  3.57 us
  transfers between devices with their start and end apart: 4, of which 3 were waited for; matrix products, arithmetic and copies ran while one was open for 3% of the time, Pallas kernels for 0%

profile of v2, /device:TPU:0, one launch (start us, length us, event | category | flops | bytes accessed | tf_op | source)
XLA Modules:
  0.0 129.0 jit_solution(3106134603885982730)
XLA Ops:
  0.6 0.0 copy-start.1
  0.6 13.0 %fusion.30 = (f32[512]{0:T(512)S(1)}, f32[512,8192]{1,0:T(8,128)}) fusion(bf16[512,8192]{1,0:T(8,128)(2,1)} %param.6, bf16[512,256]{1,0:T(8,128)(2,1)} %param.4, bf16[8192,256]{1,0:T(8,128)(2,1)} %param.5), kind=kOutput, calls=%fused_computation.40 | convolution fusion | flops 2164260352 | bytes 29624320 | tf_op jit(solution)/shard_map/dot_general | solution.py:12
  13.6 0.0 copy-done.1
  13.6 15.1 %fusion.4 = (f32[512]{0:T(512)S(1)}, bf16[512,8192]{1,0:T(8,128)(2,1)}, f32[512]{0:T(512)S(1)}, f32[512,8192]{1,0:T(8,128)}) fusion(f32[512,8192]{1,0:T(8,128)} %get-tuple-element.18, f32[512]{0:T(512)S(1)} %get-tuple-element.17, bf16[512,256]{1,0:T(8,128)(2,1)S(1)} %copy-done.1, bf16[8192,256]{1,0:T(8,128)(2,1)} %param.5), kind=kOutput, calls=%fused_computation.8 | convolution fusion | flops 2172648448 | bytes 46405632 | tf_op jit(solution)/shard_map/dot_general | solution.py:12
  28.7 0.7 broadcast_in_dim.6
  29.4 8.3 %all-to-all-start = ((f32[16,3,512]{2,1,0:T(4,128)}), f32[16,3,512]{2,1,0:T(4,128)S(1)}, u32[]{:S(2)}, u32[]{:S(2)}) async-start(f32[16,3,512]{2,1,0:T(4,128)} %broadcast_in_dim.6), calls=%async_computation | async-start | bytes 262144 | tf_op jit(solution)/shard_map/all_to_all | solution.py:25
  37.7 7.8 %all-to-all-done = f32[16,3,512]{2,1,0:T(4,128)S(1)} async-done(((f32[16,3,512]{2,1,0:T(4,128)}), f32[16,3,512]{2,1,0:T(4,128)S(1)}, u32[]{:S(2)}, u32[]{:S(2)}) %all-to-all-start) | async-done | bytes 98336 | tf_op jit(solution)/shard_map/all_to_all | solution.py:25
  45.5 0.1 fusion.29
  45.6 0.0 slice-start.1
  45.6 0.0 copy-start
  45.7 9.2 %fusion.19 = f32[8192,256]{1,0:T(8,128)} fusion(bf16[512,8192]{1,0:T(8,128)(2,1)} %get-tuple-element.8, bf16[512,256]{1,0:T(8,128)(2,1)S(1)} %copy-done.1, f32[512]{0:T(512)S(1)} %get-tuple-element.6), kind=kOutput, calls=%fused_computation.22 | convolution fusion | flops 2147876864 | bytes 17041408 | tf_op jit(solution)/shard_map/dot_general | solution.py:16
  54.9 0.0 slice-done
  54.9 0.0 slice-done.1
  54.9 0.0 copy-done
  54.9 0.0 copy-start.2
  54.9 2.3 %multiply_convert_fusion.2 = (bf16[512,256]{1,0:T(8,128)(2,1)S(1)}, f32[512,256]{1,0:T(8,128)S(1)}) fusion(f32[512]{0:T(512)S(1)} %get-tuple-element.6, bf16[512,8192]{1,0:T(8,128)(2,1)S(1)} %bitcast.39, bf16[8192,256]{1,0:T(8,128)(2,1)S(1)} %copy-done), kind=kOutput, calls=%fused_computation.21 | convolution fusion | flops 2147745792 | bytes 13371392 | tf_op jit(solution)/shard_map/dot_general | solution.py:57
  57.3 0.0 copy-done.2
  57.3 17.0 %fusion.5 = bf16[8192,256]{1,0:T(8,128)(2,1)} fusion(f32[8192,256]{1,0:T(8,128)} %fusion.19, bf16[512,8192]{1,0:T(8,128)(2,1)} %get-tuple-element.8, f32[512,8192]{1,0:T(8,128)} %get-tuple-element.19, f32[512]{0:T(512)S(1)} %get-tuple-element.16, bf16[512,256]{1,0:T(8,128)(2,1)S(1)} %copy-done.2, f32[512]{0:T(512)S(1)} %get-tuple-element.5), kind=kOutput, calls=%fused_computation.10 | convolution fusion | flops 2168848384 | bytes 38014976 | tf_op jit(solution)/shard_map/dot_general | solution.py:16
  74.3 11.7 %fusion.16 = bf16[512,256]{1,0:T(8,128)(2,1)S(1)} fusion(bf16[8192,256]{1,0:T(8,128)(2,1)} %param.5, f32[512,8192]{1,0:T(8,128)} %get-tuple-element.19, bf16[512,8192]{1,0:T(8,128)(2,1)} %get-tuple-element.8, f32[512,256]{1,0:T(8,128)S(1)} %get-tuple-element.21, f32[512]{0:T(512)S(1)} %get-tuple-element.5, f32[512]{0:T(512)S(1)} %get-tuple-element.16), kind=kOutput, calls=%fused_computation.16 | convolution fusion | flops 2160590848 | bytes 30150656 | tf_op jit(solution)/shard_map/dot_general | solution.py:58
  86.0 0.8 pad_maximum_fusion
  86.8 3.6 %all-to-all-start.1 = ((bf16[16,32,512]{2,1,0:T(8,128)(2,1)}), bf16[16,32,512]{2,1,0:T(8,128)(2,1)S(1)}, u32[]{:S(2)}, u32[]{:S(2)}) async-start(bf16[16,32,512]{2,1,0:T(8,128)(2,1)} %pad_maximum_fusion), calls=%async_computation.1 | async-start | bytes 1048576 | tf_op jit(solution)/shard_map/all_to_all | solution.py:30
  90.4 1.7 %constant_dynamic-slice_fusion = bf16[4096,256]{1,0:T(8,128)(2,1)S(1)} fusion(bf16[8192,256]{1,0:T(8,128)(2,1)} %fusion.5, s32[]{:T(128)S(6)} %select_n.7), kind=kLoop, calls=%fused_computation.36 | loop fusion | bytes 4194308 | tf_op jit(solution)/shard_map/dynamic_slice | solution.py:75
  92.2 0.1 collective-permute-start
  92.2 12.2 %all-to-all-done.1 = bf16[16,32,512]{2,1,0:T(8,128)(2,1)S(1)} async-done(((bf16[16,32,512]{2,1,0:T(8,128)(2,1)}), bf16[16,32,512]{2,1,0:T(8,128)(2,1)S(1)}, u32[]{:S(2)}, u32[]{:S(2)}) %all-to-all-start.1) | async-done | bytes 524320 | tf_op jit(solution)/shard_map/all_to_all | solution.py:30
  104.4 0.1 reduce_sum.52
  104.5 0.8 broadcast_in_dim.7
  105.3 3.8 %all-to-all-start.2 = ((bf16[16,32,512]{2,1,0:T(8,128)(2,1)}), bf16[16,32,512]{2,1,0:T(8,128)(2,1)S(1)}, u32[]{:S(2)}, u32[]{:S(2)}) async-start(bf16[16,32,512]{2,1,0:T(8,128)(2,1)} %broadcast_in_dim.7), calls=%async_computation.2 | async-start | bytes 1048576 | tf_op jit(solution)/shard_map/all_to_all | solution.py:25
  109.1 13.9 %all-to-all-done.2 = bf16[16,32,512]{2,1,0:T(8,128)(2,1)S(1)} async-done(((bf16[16,32,512]{2,1,0:T(8,128)(2,1)}), bf16[16,32,512]{2,1,0:T(8,128)(2,1)S(1)}, u32[]{:S(2)}, u32[]{:S(2)}) %all-to-all-start.2) | async-done | bytes 524320 | tf_op jit(solution)/shard_map/all_to_all | solution.py:25
  123.1 0.2 bitcast_convert_fusion
  123.2 1.1 fusion.28
  124.3 0.0 collective-permute-done
  124.3 4.7 %add_bitcast_fusion = f32[1,4096,256]{2,1,0:T(8,128)} fusion(bf16[4096,256]{1,0:T(8,128)(2,1)} %collective-permute-done, bf16[8192,256]{1,0:T(8,128)(2,1)} %fusion.5, s32[]{:T(128)S(6)} %select_n.6), kind=kLoop, calls=%fused_computation.13 | loop fusion | flops 3145728 | bytes 8388612 | tf_op jit(solution)/shard_map/broadcast_in_dim | solution.py:77
  (5 shorter events, 0.1 us)
Async XLA Ops:
  0.6 13.0 %copy-start.1 = (bf16[512,256]{1,0:T(8,128)(2,1)S(1)}, bf16[512,256]{1,0:T(8,128)(2,1)}, u32[]{:S(2)}) copy-start(bf16[512,256]{1,0:T(8,128)(2,1)} %param.7) | copy-start | bytes 786436
  29.4 16.1 %all-to-all-start = ((f32[16,3,512]{2,1,0:T(4,128)}), f32[16,3,512]{2,1,0:T(4,128)S(1)}, u32[]{:S(2)}, u32[]{:S(2)}) async-start(f32[16,3,512]{2,1,0:T(4,128)} %broadcast_in_dim.6), calls=%async_computation | async-start | bytes 262144 | tf_op jit(solution)/shard_map/all_to_all | solution.py:25
  45.5 9.4 %slice-start = ((s8[8388608]{0:T(1024)(128)(4,1)}), s8[4194304]{0:T(1024)(128)(4,1)S(1)}, s32[]{:S(2)}) async-start(s8[8388608]{0:T(1024)(128)(4,1)} %bitcast.38), calls=%async_computation.3 | async-start | bytes 8388608
  45.6 9.3 %slice-start.1 = ((s8[8388608]{0:T(1024)(128)(4,1)}), s8[4194304]{0:T(1024)(128)(4,1)S(1)}, s32[]{:S(2)}) async-start(s8[8388608]{0:T(1024)(128)(4,1)} %bitcast.38), calls=%async_computation.4 | async-start | bytes 8388608
  45.6 9.3 %copy-start = (bf16[8192,256]{1,0:T(8,128)(2,1)S(1)}, bf16[8192,256]{1,0:T(8,128)(2,1)}, u32[]{:S(2)}) copy-start(bf16[8192,256]{1,0:T(8,128)(2,1)} %param.5) | copy-start | bytes 12582916
  54.9 2.4 %copy-start.2 = (bf16[512,256]{1,0:T(8,128)(2,1)S(1)}, bf16[512,256]{1,0:T(8,128)(2,1)}, u32[]{:S(2)}) copy-start(bf16[512,256]{1,0:T(8,128)(2,1)} %param.4) | copy-start | bytes 786436
  86.8 17.6 %all-to-all-start.1 = ((bf16[16,32,512]{2,1,0:T(8,128)(2,1)}), bf16[16,32,512]{2,1,0:T(8,128)(2,1)S(1)}, u32[]{:S(2)}, u32[]{:S(2)}) async-start(bf16[16,32,512]{2,1,0:T(8,128)(2,1)} %pad_maximum_fusion), calls=%async_computation.1 | async-start | bytes 1048576 | tf_op jit(solution)/shard_map/all_to_all | solution.py:30
  92.2 32.1 %collective-permute-start = (bf16[4096,256]{1,0:T(8,128)(2,1)S(1)}, bf16[4096,256]{1,0:T(8,128)(2,1)}, u32[]{:S(2)}, u32[]{:S(2)}) collective-permute-start(bf16[4096,256]{1,0:T(8,128)(2,1)S(1)} %constant_dynamic-slice_fusion), channel_id=1, source_target_pairs={{0,16},{16,0},{1,17},{17,1},{2,18},{18,2},{3,19},{19,3},{4,20},{20... | collective-permute-start | bytes 6291464 | tf_op jit(solution)/shard_map/ppermute | solution.py:20
  105.3 17.8 %all-to-all-start.2 = ((bf16[16,32,512]{2,1,0:T(8,128)(2,1)}), bf16[16,32,512]{2,1,0:T(8,128)(2,1)S(1)}, u32[]{:S(2)}, u32[]{:S(2)}) async-start(bf16[16,32,512]{2,1,0:T(8,128)(2,1)} %broadcast_in_dim.7), calls=%async_computation.2 | async-start | bytes 1048576 | tf_op jit(solution)/shard_map/all_to_all | solution.py:25

commit v3 on v0

v3 whole, which is shorter than its diff:
```python
import functools
import math

import jax
import jax.numpy as jnp
from jax import lax
from jax.experimental import pallas as pl
from jax.experimental.pallas import tpu as pltpu
from jax.sharding import PartitionSpec as P

SOFTMAX_HEAT = 0.5
TO_LOG2 = math.log2(math.e) / SOFTMAX_HEAT
BF16 = jnp.bfloat16
F32 = jnp.float32
MIB = 1 << 20
VMEM = pl.BlockSpec(memory_space=pltpu.VMEM)
SMEM = pl.BlockSpec(memory_space=pltpu.SMEM)
ANY = pl.BlockSpec(memory_space=pl.ANY)


def dot(left, right, left_dim=1, right_dim=0):
    return lax.dot_general(
        left, right, (((left_dim,), (right_dim,)), ((), ())), preferred_element_type=F32
    )


def lane_groups(value):
    return [value[:, j : j + 128] for j in range(0, value.shape[1], 128)]


def stat_lanes(n_code):
    return max(8 * n_code, 128)


def high_low(value):
    high = value.astype(BF16).astype(F32)
    return high, (value - high).astype(BF16).astype(F32)


def forward_kernel(
    n_code, tokens, grad_out, codebook, noise, codes, sent,
    book, noise_in, scores, top, total, mix, pulled, book_sem, noise_sem,
):
    tiles, n_tokens, width = codes.shape
    dim = tokens.shape[1]

    def fetch(t):
        at = pl.multiple_of(t * width, width)
        return (
            pltpu.make_async_copy(codebook.at[pl.ds(at, width)], book.at[t], book_sem.at[t]),
            pltpu.make_async_copy(noise.at[:, pl.ds(at, width)], noise_in.at[t], noise_sem.at[t]),
        )

    for t in range(tiles):
        for copy in fetch(t):
            copy.start()
    top[...] = jnp.full(top.shape, -jnp.inf, F32)

    def score(t, carry):
        for copy in fetch(t):
            copy.wait()
        value = (dot(tokens[...], book[t], 1, 1) + noise_in[t].astype(F32)) * TO_LOG2
        scores[t] = value
        top[...] = functools.reduce(jnp.maximum, lane_groups(value), top[...])
        return carry

    lax.fori_loop(0, tiles, score, 0)
    shift = jnp.max(top[...], axis=1, keepdims=True).astype(BF16).astype(F32)
    top[...] = jnp.broadcast_to(shift, top.shape)
    total[...] = jnp.zeros(total.shape, F32)
    mix[...] = jnp.zeros(mix.shape, F32)
    pulled[...] = jnp.zeros(pulled.shape, F32)

    def soften(t, carry):
        shifts = jnp.concatenate([top[...]] * (width // 128), axis=1)
        weight = jnp.exp2(scores[t] - shifts)
        code = weight.astype(BF16)
        codes[t] = code
        total[...] += sum(lane_groups(weight))
        gradient = dot(grad_out[...], book[t], 1, 1)
        weighted = (weight * gradient).astype(BF16)
        mix[...] += dot(code, book[t])
        pulled[...] += dot(weighted, book[t])
        return carry

    lax.fori_loop(0, tiles, soften, 0)
    own_total = jnp.sum(total[...], axis=1, keepdims=True)
    own_inner = jnp.sum(grad_out[...].astype(F32) * mix[...], axis=1, keepdims=True)
    mean = own_inner / own_total
    rows = n_tokens // n_code
    lanes = stat_lanes(n_code)
    half = lanes // 2
    lane = lax.broadcasted_iota(jnp.int32, (rows, lanes), 1)
    stats = jnp.zeros((rows, lanes), F32)
    columns = high_low(own_total) + high_low(own_inner)
    for g in range(n_code):
        part = slice(g * rows, (g + 1) * rows)
        for i, column in enumerate(columns):
            stats = jnp.where(lane == 4 * g + i, column[part], stats)
        stats = jnp.where((lane - half) // 4 == g, shift[part], stats)
    stats = stats.astype(BF16)
    for g in range(n_code):
        part = slice(g * rows, (g + 1) * rows)
        sent[g, :, :dim] = mix[part].astype(BF16)
        sent[g, :, dim : 2 * dim] = (pulled[part] - mean[part] * mix[part]).astype(BF16)
        sent[g, :, 2 * dim :] = stats


def roll_left(value, by):
    return pltpu.roll(value, value.shape[1] - by, 1)


def merged_stats(received):
    n_code = received.shape[0]
    lanes = stat_lanes(n_code)
    stats = [received[p, :, received.shape[2] - lanes :].astype(F32) for p in range(n_code)]
    top = functools.reduce(jnp.maximum, stats)
    scales = [roll_left(jnp.exp2(s - top), lanes // 2) for s in stats]
    pairs = [s + roll_left(s, 1) for s in stats]
    inners = [roll_left(s, 2) for s in pairs]
    total = sum(a * s for a, s in zip(scales, pairs))
    inner = sum(a * s for a, s in zip(scales, inners)) / total
    means = [i / s for i, s in zip(inners, pairs)]
    return [a / total for a in scales], means, inner


def merge_kernel(me, received, spread):
    n_code, rows, _ = received.shape
    dim = spread.shape[2] // 2
    scales, means, inner = merged_stats(received)
    lane = lax.broadcasted_iota(jnp.int32, inner.shape, 1)
    mine = lane == 4 * me[0]

    def column(value):
        return jnp.sum(jnp.where(mine, value, 0.0), axis=1, keepdims=True)

    quantized = jnp.zeros((rows, dim), F32)
    gradient = jnp.zeros((rows, dim), F32)
    for p in range(n_code):
        scale = column(scales[p])
        offset = column(scales[p] * (means[p] - inner))
        mix = received[p, :, :dim].astype(F32)
        quantized += scale * mix
        gradient += scale * received[p, :, dim : 2 * dim].astype(F32) + offset * mix
    quantized = quantized.astype(BF16)
    gradient = (gradient / SOFTMAX_HEAT).astype(BF16)
    for p in range(n_code):
        spread[p, :, :dim] = quantized
        spread[p, :, dim:] = gradient


def backward_kernel(
    add, where, tokens, grad_out, codebook, codes, received, *rest
):
    if add:
        other, out, book, result, upper, lower, inner_in, book_sem, out_sem = rest
    else:
        out, book, result, upper, lower, inner_in, book_sem = rest
    tiles = book.shape[0]
    n_code, rows, _ = received.shape
    n_tokens, dim = tokens.shape
    width = book.shape[1]
    first = where[1] * tiles

    def fetch(t):
        at = pl.multiple_of((first + t) * width, width)
        return pltpu.make_async_copy(codebook.at[pl.ds(at, width)], book.at[t], book_sem.at[t])

    for t in range(tiles):
        fetch(t).start()

    scales, _, inner = merged_stats(received)
    scale = jnp.zeros(inner.shape, F32)
    for p in range(n_code):
        scale = jnp.where(where[0] == p, scales[p], scale)
    for g in range(n_code):
        part = slice(g * rows, (g + 1) * rows)
        column = scale[:, 4 * g : 4 * g + 1]
        upper[part] = column * grad_out[part].astype(F32)
        lower[part] = column * (tokens[part].astype(F32) / SOFTMAX_HEAT)
        inner_in[part] = jnp.broadcast_to(inner[:, 4 * g : 4 * g + 1], (rows, 128))
    left = upper[...].T.astype(BF16)
    right = lower[...].T.astype(BF16)

    def send(t):
        return pltpu.make_async_copy(
            result.at[t % 2], out.at[pl.ds(pl.multiple_of(t * width, width), width)],
            out_sem.at[t % 2],
        )

    def block(t, carry):
        fetch(t).wait()
        gradient = dot(grad_out[...], book[t], 1, 1)
        code = codes[first + t]
        inners = jnp.concatenate([inner_in[...]] * (width // 128), axis=1)
        score_gradient = (code.astype(F32) * (gradient - inners)).astype(BF16)
        value = dot(left, code) + dot(right, score_gradient)
        value = value.astype(BF16).T
        at = pl.ds(pl.multiple_of(t * width, width), width)
        if add:
            @pl.when(t >= 2)
            def _():
                send(t - 2).wait()
            result[t % 2] = value.astype(F32) + other[at].astype(F32)
            send(t).start()
        else:
            out[at] = value
        return carry

    lax.fori_loop(0, tiles, block, 0)
    if add:
        for t in range(max(tiles - 2, 0), tiles):
            send(t).wait()


def swap(value, axis, size, mask):
    return lax.ppermute(value, axis, [(i, i ^ mask) for i in range(size)])


def local(n_dp, n_code, tokens, codebook, noise, grad_out):
    n_tokens, dim = tokens.shape
    n_codes = codebook.shape[0]
    rows = n_tokens // n_code
    block = n_codes // n_dp
    width = min(1024, block)
    tiles = n_codes // width
    lanes = stat_lanes(n_code)
    products = 2 * n_tokens * n_codes * dim

    codes, sent = pl.pallas_call(
        functools.partial(forward_kernel, n_code),
        out_shape=(
            pltpu.VMEM((tiles, n_tokens, width), BF16),
            jax.ShapeDtypeStruct((n_code, rows, 2 * dim + lanes), BF16),
        ),
        in_specs=[VMEM, VMEM, ANY, ANY],
        out_specs=(VMEM, VMEM),
        scratch_shapes=[
            pltpu.VMEM((tiles, width, dim), BF16),
            pltpu.VMEM((tiles, n_tokens, width), BF16),
            pltpu.VMEM((tiles, n_tokens, width), F32),
            pltpu.VMEM((n_tokens, 128), F32),
            pltpu.VMEM((n_tokens, 128), F32),
            pltpu.VMEM((n_tokens, dim), F32),
            pltpu.VMEM((n_tokens, dim), F32),
            pltpu.SemaphoreType.DMA((tiles,)),
            pltpu.SemaphoreType.DMA((tiles,)),
        ],
        compiler_params=pltpu.CompilerParams(vmem_limit_bytes=46 * MIB),
        cost_estimate=pl.CostEstimate(
            flops=4 * products, bytes_accessed=16 * MIB, transcendentals=n_tokens * n_codes
        ),
        name="forward",
    )(tokens, grad_out, codebook, noise)

    received = lax.all_to_all(sent, "code", 0, 0, tiled=True)
    code_at = lax.axis_index("code")
    spread = pl.pallas_call(
        merge_kernel,
        out_shape=jax.ShapeDtypeStruct((n_code, rows, 2 * dim), BF16),
        in_specs=[SMEM, VMEM],
        out_specs=VMEM,
        name="merge",
    )(code_at[None], received)
    gathered = lax.all_to_all(spread, "code", 0, 0, tiled=True)
    gathered = gathered.reshape(n_tokens, 2 * dim).astype(F32)
    quantized, token_gradient = gathered[:, :dim], gathered[:, dim:]

    def backward(at, other=None):
        add = other is not None
        scratch = [
            pltpu.VMEM((block // width, width, dim), BF16),
            pltpu.VMEM((2, width, dim), F32),
            pltpu.VMEM((n_tokens, dim), F32),
            pltpu.VMEM((n_tokens, dim), F32),
            pltpu.VMEM((n_tokens, 128), F32),
            pltpu.SemaphoreType.DMA((block // width,)),
        ]
        extra = (other,) if add else ()
        return pl.pallas_call(
            functools.partial(backward_kernel, add),
            out_shape=jax.ShapeDtypeStruct((block, dim), F32 if add else BF16),
            in_specs=[SMEM, VMEM, VMEM, ANY, VMEM, VMEM] + [VMEM] * add,
            out_specs=ANY if add else VMEM,
            scratch_shapes=scratch + [pltpu.SemaphoreType.DMA((2,))] * add,
            compiler_params=pltpu.CompilerParams(vmem_limit_bytes=36 * MIB),
            cost_estimate=pl.CostEstimate(
                flops=3 * products // n_dp, bytes_accessed=16 * MIB // n_dp, transcendentals=0
            ),
            name="backward",
        )(jnp.stack([code_at, at]), tokens, grad_out, codebook, codes, received, *extra)

    dp_at = lax.axis_index("dp")
    other = None
    for d in range(1, n_dp):
        got = swap(backward(dp_at ^ d), "dp", n_dp, d)
        other = got if other is None else other.astype(F32) + got.astype(F32)
    return quantized, token_gradient, backward(dp_at, other)[None]


def solution(mesh):
    n_dp, n_code = mesh.shape["dp"], mesh.shape["code"]
    in_specs = (P("dp", None), P("code", None), P("dp", "code"), P("dp", None))
    out_specs = (P("dp", None), P("dp", None), P("code", "dp", None))
    return jax.shard_map(
        functools.partial(local, n_dp, n_code),
        mesh=mesh, in_specs=in_specs, out_specs=out_specs, check_vma=False,
    )
```

time: 364 us -> 97.7 us (0.27)
  blocking collectives: 119 us -> 0 us
  waiting for transfers between devices: 140 us -> 32.8 us
  matrix products: 75 us -> 0 us
  Pallas kernels: 0 us -> 33.8 us
  local copies, waits for them, and re-layouts: 0.02 us -> 15.6 us
  between operations: 15.5 us -> 0.74 us
  other arithmetic: 14.2 us -> 1.32 us
  starting transfers between devices: 0.3 us -> 12.9 us
    psum x2 -> x0, waiting for transfers between devices: 140 us -> none  [the longest x1 114 us: local(): lax.psum((local_pulled, local_inner), 'code')]
    psum x2 -> x0, blocking collectives: 75.1 us -> none  [the longest x1 38.6 us: local(): lax.psum((local_pulled, local_inner), 'code')]
    dot_general x6 -> x0, matrix products: 75 us -> none  [the longest x2 28.1 us: token_code_scores(): lax.dot_general(left, codebook, (((1,), (1,)), ((), ())), preferred_eleme...]
    pmax x1 -> x0, blocking collectives: 43.5 us -> none  [local(): row_max = lax.pmax(jnp.max(code_scores, axis=1), 'code')]
    pallas_call x0 -> x4, Pallas kernels: none -> 33.8 us  [the longest x1 17.1 us: local(): pl.pallas_call(functools.partial(forward_kernel, n_code), out_shape=(pltp...]
    all_to_all x0 -> x2, waiting for transfers between devices: none -> 32.8 us  [the longest x1 17.3 us: local(): received = lax.all_to_all(sent, 'code', 0, 0, tiled=True)]
    unnamed x4 -> x18, local copies, waits for them, and re-layouts: 0.02 us -> 14.6 us
    all_to_all x0 -> x2, starting transfers between devices: none -> 12.8 us  [the longest x1 8.31 us: local(): received = lax.all_to_all(sent, 'code', 0, 0, tiled=True)]
  transfers between devices with their start and end apart: 3 -> 3, of which waited for: 2 -> 2; matrix products, arithmetic and copies ran while one was open for 11% -> 2% of each run, Pallas kernels for 0% -> 3%
where the time goes in v3:
time: 97.7 us; the launch traced here: 97.2 us
  Pallas kernels  33.8 us (35%)
  waiting for transfers between devices  32.8 us (34%)
  local copies, waits for them, and re-layouts  15.6 us (16%)
  starting transfers between devices  12.9 us (13%)
  other arithmetic  1.32 us (1%)
    all_to_all x1, waiting for transfers between devices, local(): received = lax.all_to_all(sent, 'code', 0, 0, tiled=True)  17.3 us
    pallas_call x1, Pallas kernels, local(): pl.pallas_call(functools.partial(forward_kernel, n_code), out_shape=(pltp...  17.1 us
    all_to_all x1, waiting for transfers between devices, local(): gathered = lax.all_to_all(spread, 'code', 0, 0, tiled=True)  15.4 us
    unnamed x18, local copies, waits for them, and re-layouts  14.6 us
    pallas_call x2, Pallas kernels, backward(): pl.pallas_call(functools.partial(backward_kernel, add), out_shape=jax.Sha...  14.3 us
    all_to_all x1, starting transfers between devices, local(): received = lax.all_to_all(sent, 'code', 0, 0, tiled=True)  8.31 us
    all_to_all x1, starting transfers between devices, local(): gathered = lax.all_to_all(spread, 'code', 0, 0, tiled=True)  4.47 us
    pallas_call x1, Pallas kernels, local(): pl.pallas_call(merge_kernel, out_shape=jax.ShapeDtypeStruct((n_code, rows...  2.52 us
  transfers between devices with their start and end apart: 3, of which 2 were waited for; matrix products, arithmetic and copies ran while one was open for 2% of the time, Pallas kernels for 3%

profile of v3, /device:TPU:0, one launch (start us, length us, event | category | flops | bytes accessed | tf_op | source)
XLA Modules:
  0.0 97.2 jit_solution(13837201287234650953)
XLA Ops:
  0.6 0.0 copy-start.7
  0.6 0.0 copy-start.8
  0.7 17.1 %forward.1 = (bf16[8,512,1024]{2,1,0:T(8,128)(2,1)S(1)}, bf16[16,32,640]{2,1,0:T(8,128)(2,1)}) custom-call(bf16[512,256]{1,0:T(8,128)(2,1)} %tokens.5, bf16[512,256]{1,0:T(8,128)(2,1)} %grad_out.5, bf16[8192,256]{1,0:T(8,128)(2,1)} %codebook.5, bf16[512,8192]{1,0:T(8,128)(2,1)} %noise.1), custom_call_target="tpu_custom_call" | custom-call | flops 8589934592 | bytes 16777216 | tf_op jit(solution)/shard_map/forward/pallas_call | solution.py:230
  17.7 0.0 copy-start
  17.7 3.2 %copy-done = bf16[8,512,1024]{2,1,0:T(8,128)(2,1)} copy-done((bf16[8,512,1024]{2,1,0:T(8,128)(2,1)}, bf16[8,512,1024]{2,1,0:T(8,128)(2,1)S(1)}, u32[]{:S(2)}) %copy-start) | copy-done | bytes 8388632
  20.9 8.3 %all-to-all-start = ((bf16[16,32,640]{2,1,0:T(8,128)(2,1)}), bf16[16,32,640]{2,1,0:T(8,128)(2,1)S(1)}, u32[]{:S(2)}, u32[]{:S(2)}) async-start(bf16[16,32,640]{2,1,0:T(8,128)(2,1)} %get-tuple-element.5), calls=%async_computation | async-start | bytes 1310720 | tf_op jit(solution)/shard_map/all_to_all | solution.py:256
  29.3 0.1 pad_add_fusion.1.where
  29.3 17.3 %all-to-all-done.received = bf16[16,32,640]{2,1,0:T(8,128)(2,1)S(1)} async-done(((bf16[16,32,640]{2,1,0:T(8,128)(2,1)}), bf16[16,32,640]{2,1,0:T(8,128)(2,1)S(1)}, u32[]{:S(2)}, u32[]{:S(2)}) %all-to-all-start) | async-done | bytes 655392 | tf_op jit(solution)/shard_map/all_to_all | solution.py:256
  46.7 0.0 copy-start.5
  46.7 0.0 copy-done.7
  46.7 0.0 copy-done.8
  46.7 0.0 copy-start.1
  46.7 3.6 %copy-done.1 = bf16[8,512,1024]{2,1,0:T(8,128)(2,1)S(1)} copy-done((bf16[8,512,1024]{2,1,0:T(8,128)(2,1)S(1)}, bf16[8,512,1024]{2,1,0:T(8,128)(2,1)}, u32[]{:S(2)}) %copy-start.1) | copy-done | bytes 8388632
  50.3 0.0 copy-start.3
  50.3 2.2 %copy-done.3 = bf16[8192,256]{1,0:T(8,128)(2,1)S(1)} copy-done((bf16[8192,256]{1,0:T(8,128)(2,1)S(1)}, bf16[8192,256]{1,0:T(8,128)(2,1)}, u32[]{:S(2)}) %copy-start.3) | copy-done | bytes 4194328
  52.5 7.1 %backward.2 = bf16[4096,256]{1,0:T(8,128)(2,1)} custom-call(s32[2]{0:T(128)S(1)} %pad_add_fusion.1.where, bf16[512,256]{1,0:T(8,128)(2,1)S(1)} %copy-done.7, bf16[512,256]{1,0:T(8,128)(2,1)S(1)} %copy-done.8, bf16[8192,256]{1,0:T(8,128)(2,1)S(1)} %copy-done.3, bf16[8,512,1024]{2,1,0:T(8,128)(2,1)S(1)} %copy-done.1, ...), custom_call_target="tpu_custom_call" | custom-call | flops 3221225472 | bytes 8388608 | tf_op jit(solution)/shard_map/backward/pallas_call | solution.py:280
  59.6 0.0 copy-done.5
  59.6 0.1 collective-permute-start
  59.7 0.0 copy-start.6
  59.7 2.5 %merge.1 = bf16[16,32,512]{2,1,0:T(8,128)(2,1)} custom-call(s32[1]{0:T(128)} %bitcast.me, bf16[16,32,640]{2,1,0:T(8,128)(2,1)} %copy-done.5), custom_call_target="tpu_custom_call" | custom-call | tf_op jit(solution)/shard_map/merge/pallas_call | solution.py:258
  62.2 4.5 %all-to-all-start.1 = ((bf16[16,32,512]{2,1,0:T(8,128)(2,1)}), bf16[16,32,512]{2,1,0:T(8,128)(2,1)}, u32[]{:S(2)}, u32[]{:S(2)}) async-start(bf16[16,32,512]{2,1,0:T(8,128)(2,1)} %merge.1), calls=%async_computation.1 | async-start | bytes 1048576 | tf_op jit(solution)/shard_map/all_to_all | solution.py:265
  66.7 0.1 pad_add_fusion.where
  66.7 15.4 %all-to-all-done.1 = bf16[16,32,512]{2,1,0:T(8,128)(2,1)} async-done(((bf16[16,32,512]{2,1,0:T(8,128)(2,1)}), bf16[16,32,512]{2,1,0:T(8,128)(2,1)}, u32[]{:S(2)}, u32[]{:S(2)}) %all-to-all-start.1) | async-done | bytes 524320 | tf_op jit(solution)/shard_map/all_to_all | solution.py:265
  82.2 1.2 %bitcast_convert_fusion = f32[512,512]{1,0:T(8,128)S(1)} fusion(bf16[16,32,512]{2,1,0:T(8,128)(2,1)} %all-to-all-done.1), kind=kLoop, calls=%fused_computation | loop fusion | flops 262144 | bytes 1572864 | tf_op jit(solution)/shard_map/convert_element_type | solution.py:266
  83.3 1.1 %fusion = (f32[512,256]{1,0:T(8,128)}, f32[512,256]{1,0:T(8,128)}) fusion(f32[512,512]{1,0:T(8,128)S(1)} %bitcast_convert_fusion), kind=kLoop, calls=%fused_computation.3 | loop fusion | bytes 2097152 | tf_op jit(solution)/shard_map/slice | solution.py:267
  84.4 0.0 collective-permute-done.rest_0_
  84.4 0.0 copy-done.6
  84.4 0.0 copy-start.2
  84.4 3.4 %copy-done.2 = bf16[8,512,1024]{2,1,0:T(8,128)(2,1)S(1)} copy-done((bf16[8,512,1024]{2,1,0:T(8,128)(2,1)S(1)}, bf16[8,512,1024]{2,1,0:T(8,128)(2,1)}, u32[]{:S(2)}) %copy-start.2) | copy-done | bytes 8388632
  87.8 0.0 copy-start.4
  87.8 2.2 %copy-done.4 = bf16[8192,256]{1,0:T(8,128)(2,1)S(1)} copy-done((bf16[8192,256]{1,0:T(8,128)(2,1)S(1)}, bf16[8192,256]{1,0:T(8,128)(2,1)}, u32[]{:S(2)}) %copy-start.4) | copy-done | bytes 4194328
  90.0 7.2 %backward.3 = f32[4096,256]{1,0:T(8,128)} custom-call(s32[2]{0:T(128)S(1)} %pad_add_fusion.where, bf16[512,256]{1,0:T(8,128)(2,1)S(1)} %copy-done.7, bf16[512,256]{1,0:T(8,128)(2,1)S(1)} %copy-done.8, bf16[8192,256]{1,0:T(8,128)(2,1)S(1)} %copy-done.4, bf16[8,512,1024]{2,1,0:T(8,128)(2,1)S(1)} %copy-done.2, bf16[16,32,640]{2,1,0:T(8,128)(2,1)S(1)} %copy-done.6, ...), custom_call_target="tpu_custom_call" | custom-call | flops 3221225472 | bytes 8388608 | tf_op jit(solution)/shard_map/backward/pallas_call | solution.py:280
Async XLA Ops:
  0.6 46.0 %copy-start.7 = (bf16[512,256]{1,0:T(8,128)(2,1)S(1)}, bf16[512,256]{1,0:T(8,128)(2,1)}, u32[]{:S(2)}) copy-start(bf16[512,256]{1,0:T(8,128)(2,1)} %tokens.5) | copy-start | bytes 786436
  0.6 46.0 %copy-start.8 = (bf16[512,256]{1,0:T(8,128)(2,1)S(1)}, bf16[512,256]{1,0:T(8,128)(2,1)}, u32[]{:S(2)}) copy-start(bf16[512,256]{1,0:T(8,128)(2,1)} %grad_out.5) | copy-start | bytes 786436
  17.7 3.2 %copy-start = (bf16[8,512,1024]{2,1,0:T(8,128)(2,1)}, bf16[8,512,1024]{2,1,0:T(8,128)(2,1)S(1)}, u32[]{:S(2)}) copy-start(bf16[8,512,1024]{2,1,0:T(8,128)(2,1)S(1)} %get-tuple-element.6.codes) | copy-start | bytes 25165828
  20.9 25.7 %all-to-all-start = ((bf16[16,32,640]{2,1,0:T(8,128)(2,1)}), bf16[16,32,640]{2,1,0:T(8,128)(2,1)S(1)}, u32[]{:S(2)}, u32[]{:S(2)}) async-start(bf16[16,32,640]{2,1,0:T(8,128)(2,1)} %get-tuple-element.5), calls=%async_computation | async-start | bytes 1310720 | tf_op jit(solution)/shard_map/all_to_all | solution.py:256
  46.7 12.9 %copy-start.5 = (bf16[16,32,640]{2,1,0:T(8,128)(2,1)}, bf16[16,32,640]{2,1,0:T(8,128)(2,1)S(1)}, u32[]{:S(2)}) copy-start(bf16[16,32,640]{2,1,0:T(8,128)(2,1)S(1)} %all-to-all-done.received) | copy-start | bytes 1966084
  46.7 3.6 %copy-start.1 = (bf16[8,512,1024]{2,1,0:T(8,128)(2,1)S(1)}, bf16[8,512,1024]{2,1,0:T(8,128)(2,1)}, u32[]{:S(2)}) copy-start(bf16[8,512,1024]{2,1,0:T(8,128)(2,1)} %copy-done) | copy-start | bytes 25165828
  50.3 2.2 %copy-start.3 = (bf16[8192,256]{1,0:T(8,128)(2,1)S(1)}, bf16[8192,256]{1,0:T(8,128)(2,1)}, u32[]{:S(2)}) copy-start(bf16[8192,256]{1,0:T(8,128)(2,1)} %codebook.5) | copy-start | bytes 12582916
  59.6 24.8 %collective-permute-start = (bf16[4096,256]{1,0:T(8,128)(2,1)}, bf16[4096,256]{1,0:T(8,128)(2,1)S(1)}, u32[]{:S(2)}, u32[]{:S(2)}) collective-permute-start(bf16[4096,256]{1,0:T(8,128)(2,1)} %backward.2), channel_id=1, source_target_pairs={{0,16},{16,0},{1,17},{17,1},{2,18},{18,2},{3,19},{19,3},{4,20},{20... | collective-permute-start | bytes 6291464 | tf_op jit(solution)/shard_map/ppermute | solution.py:217
  59.7 24.7 %copy-start.6 = (bf16[16,32,640]{2,1,0:T(8,128)(2,1)S(1)}, bf16[16,32,640]{2,1,0:T(8,128)(2,1)}, u32[]{:S(2)}) copy-start(bf16[16,32,640]{2,1,0:T(8,128)(2,1)} %copy-done.5) | copy-start | bytes 1966084
  62.2 20.0 %all-to-all-start.1 = ((bf16[16,32,512]{2,1,0:T(8,128)(2,1)}), bf16[16,32,512]{2,1,0:T(8,128)(2,1)}, u32[]{:S(2)}, u32[]{:S(2)}) async-start(bf16[16,32,512]{2,1,0:T(8,128)(2,1)} %merge.1), calls=%async_computation.1 | async-start | bytes 1048576 | tf_op jit(solution)/shard_map/all_to_all | solution.py:265
  84.4 3.4 %copy-start.2 = (bf16[8,512,1024]{2,1,0:T(8,128)(2,1)S(1)}, bf16[8,512,1024]{2,1,0:T(8,128)(2,1)}, u32[]{:S(2)}) copy-start(bf16[8,512,1024]{2,1,0:T(8,128)(2,1)} %copy-done) | copy-start | bytes 25165828
  87.8 2.2 %copy-start.4 = (bf16[8192,256]{1,0:T(8,128)(2,1)S(1)}, bf16[8192,256]{1,0:T(8,128)(2,1)}, u32[]{:S(2)}) copy-start(bf16[8192,256]{1,0:T(8,128)(2,1)} %codebook.5) | copy-start | bytes 12582916

commit v4 on v3

--- a/solution.py
+++ b/solution.py
@@ -13,6 +13,8 @@
 BF16 = jnp.bfloat16
 F32 = jnp.float32
 MIB = 1 << 20
+CHUNK = 256
+AHEAD = 3
 VMEM = pl.BlockSpec(memory_space=pltpu.VMEM)
 SMEM = pl.BlockSpec(memory_space=pltpu.SMEM)
 ANY = pl.BlockSpec(memory_space=pl.ANY)
@@ -39,10 +41,12 @@
 
 def forward_kernel(
     n_code, tokens, grad_out, codebook, noise, codes, sent,
-    book, noise_in, scores, top, total, mix, pulled, book_sem, noise_sem,
+    book, noise_in, scores, gradients, code_slots, weighted_slots, top, total, mix, pulled,
+    book_sem, noise_sem,
 ):
     tiles, n_tokens, width = codes.shape
     dim = tokens.shape[1]
+    columns = [slice(c, c + CHUNK) for c in range(0, width, CHUNK)]
 
     def fetch(t):
         at = pl.multiple_of(t * width, width)
@@ -51,39 +55,72 @@
             pltpu.make_async_copy(noise.at[:, pl.ds(at, width)], noise_in.at[t], noise_sem.at[t]),
         )
 
-    for t in range(tiles):
+    def start(t):
         for copy in fetch(t):
             copy.start()
+
+    for t in range(min(AHEAD, tiles)):
+        start(t)
     top[...] = jnp.full(top.shape, -jnp.inf, F32)
 
-    def score(t, carry):
+    def score(t):
         for copy in fetch(t):
             copy.wait()
-        value = (dot(tokens[...], book[t], 1, 1) + noise_in[t].astype(F32)) * TO_LOG2
-        scores[t] = value
-        top[...] = functools.reduce(jnp.maximum, lane_groups(value), top[...])
+
+        @pl.when(t + AHEAD < tiles)
+        def _():
+            start(t + AHEAD)
+
+        for c in columns:
+            keys = book[t, c]
+            value = (dot(tokens[...], keys, 1, 1) + noise_in[t, :, c].astype(F32)) * TO_LOG2
+            scores[t, :, c] = value
+            top[...] = functools.reduce(jnp.maximum, lane_groups(value), top[...])
+            gradients[t, :, c] = dot(grad_out[...], keys, 1, 1)
+
+    def score_pair(i, carry):
+        score(2 * i)
+        score(2 * i + 1)
         return carry
 
-    lax.fori_loop(0, tiles, score, 0)
+    lax.fori_loop(0, tiles // 2, score_pair, 0)
     shift = jnp.max(top[...], axis=1, keepdims=True).astype(BF16).astype(F32)
     top[...] = jnp.broadcast_to(shift, top.shape)
     total[...] = jnp.zeros(total.shape, F32)
     mix[...] = jnp.zeros(mix.shape, F32)
     pulled[...] = jnp.zeros(pulled.shape, F32)
 
-    def soften(t, carry):
-        shifts = jnp.concatenate([top[...]] * (width // 128), axis=1)
-        weight = jnp.exp2(scores[t] - shifts)
-        code = weight.astype(BF16)
-        codes[t] = code
-        total[...] += sum(lane_groups(weight))
-        gradient = dot(grad_out[...], book[t], 1, 1)
-        weighted = (weight * gradient).astype(BF16)
-        mix[...] += dot(code, book[t])
-        pulled[...] += dot(weighted, book[t])
+    def store(t):
+        return pltpu.make_async_copy(noise_in.at[t], codes.at[t], noise_sem.at[t])
+
+    def soften(t, slot):
+        for c in columns:
+            shifts = jnp.concatenate([top[...]] * (CHUNK // 128), axis=1)
+            weight = jnp.exp2(scores[t, :, c] - shifts)
+            total[...] += sum(lane_groups(weight))
+            code = weight.astype(BF16)
+            code_slots[slot, :, c] = code
+            noise_in[t, :, c] = code
+            weighted_slots[slot, :, c] = (weight * gradients[t, :, c]).astype(BF16)
+        store(t).start()
+
+    def accumulate(t, slot):
+        mix[...] += dot(code_slots[slot], book[t])
+        pulled[...] += dot(weighted_slots[slot], book[t])
+
+    def soften_pair(i, carry):
+        soften(2 * i + 1, 1)
+        accumulate(2 * i, 0)
+        soften(2 * i + 2, 0)
+        accumulate(2 * i + 1, 1)
         return carry
 
-    lax.fori_loop(0, tiles, soften, 0)
+    soften(0, 0)
+    lax.fori_loop(0, tiles // 2 - 1, soften_pair, 0)
+    soften(tiles - 1, 1)
+    accumulate(tiles - 2, 0)
+    accumulate(tiles - 1, 1)
+
     own_total = jnp.sum(total[...], axis=1, keepdims=True)
     own_inner = jnp.sum(grad_out[...].astype(F32) * mix[...], axis=1, keepdims=True)
     mean = own_inner / own_total
@@ -92,18 +129,20 @@
     half = lanes // 2
     lane = lax.broadcasted_iota(jnp.int32, (rows, lanes), 1)
     stats = jnp.zeros((rows, lanes), F32)
-    columns = high_low(own_total) + high_low(own_inner)
+    parts = high_low(own_total) + high_low(own_inner)
     for g in range(n_code):
-        part = slice(g * rows, (g + 1) * rows)
-        for i, column in enumerate(columns):
-            stats = jnp.where(lane == 4 * g + i, column[part], stats)
-        stats = jnp.where((lane - half) // 4 == g, shift[part], stats)
+        at = slice(g * rows, (g + 1) * rows)
+        for i, part in enumerate(parts):
+            stats = jnp.where(lane == 4 * g + i, part[at], stats)
+        stats = jnp.where((lane - half) // 4 == g, shift[at], stats)
     stats = stats.astype(BF16)
     for g in range(n_code):
-        part = slice(g * rows, (g + 1) * rows)
-        sent[g, :, :dim] = mix[part].astype(BF16)
-        sent[g, :, dim : 2 * dim] = (pulled[part] - mean[part] * mix[part]).astype(BF16)
+        at = slice(g * rows, (g + 1) * rows)
+        sent[g, :, :dim] = mix[at].astype(BF16)
+        sent[g, :, dim : 2 * dim] = (pulled[at] - mean[at] * mix[at]).astype(BF16)
         sent[g, :, 2 * dim :] = stats
+    for t in range(tiles):
+        store(t).wait()
 
 
 def roll_left(value, by):
@@ -149,25 +188,25 @@
         spread[p, :, dim:] = gradient
 
 
-def backward_kernel(
-    add, where, tokens, grad_out, codebook, codes, received, *rest
-):
+def backward_kernel(add, where, tokens, grad_out, codebook, codes, received, *rest):
     if add:
-        other, out, book, result, upper, lower, inner_in, book_sem, out_sem = rest
+        other, out, book, code_in, upper, lower, inner_in, book_sem, code_sem, result, out_sem = rest
     else:
-        out, book, result, upper, lower, inner_in, book_sem = rest
-    tiles = book.shape[0]
+        out, book, code_in, upper, lower, inner_in, book_sem, code_sem = rest
+    tiles, width, dim = book.shape
     n_code, rows, _ = received.shape
-    n_tokens, dim = tokens.shape
-    width = book.shape[1]
     first = where[1] * tiles
 
     def fetch(t):
         at = pl.multiple_of((first + t) * width, width)
-        return pltpu.make_async_copy(codebook.at[pl.ds(at, width)], book.at[t], book_sem.at[t])
+        return (
+            pltpu.make_async_copy(codebook.at[pl.ds(at, width)], book.at[t], book_sem.at[t]),
+            pltpu.make_async_copy(codes.at[first + t], code_in.at[t], code_sem.at[t]),
+        )
 
     for t in range(tiles):
-        fetch(t).start()
+        for copy in fetch(t):
+            copy.start()
 
     scales, _, inner = merged_stats(received)
     scale = jnp.zeros(inner.shape, F32)
@@ -184,33 +223,40 @@
 
     def send(t):
         return pltpu.make_async_copy(
-            result.at[t % 2], out.at[pl.ds(pl.multiple_of(t * width, width), width)],
-            out_sem.at[t % 2],
+            result.at[t], out.at[pl.ds(pl.multiple_of(t * width, width), width)], out_sem.at[t]
         )
 
     def block(t, carry):
-        fetch(t).wait()
-        gradient = dot(grad_out[...], book[t], 1, 1)
-        code = codes[first + t]
-        inners = jnp.concatenate([inner_in[...]] * (width // 128), axis=1)
-        score_gradient = (code.astype(F32) * (gradient - inners)).astype(BF16)
-        value = dot(left, code) + dot(right, score_gradient)
-        value = value.astype(BF16).T
-        at = pl.ds(pl.multiple_of(t * width, width), width)
+        for copy in fetch(t):
+            copy.wait()
+        for c in range(0, width, CHUNK):
+            gradient = dot(grad_out[...], book[t, c : c + CHUNK], 1, 1)
+            code = code_in[t, :, c : c + CHUNK]
+            inners = jnp.concatenate([inner_in[...]] * (CHUNK // 128), axis=1)
+            score_gradient = (code.astype(F32) * (gradient - inners)).astype(BF16)
+            value = (dot(left, code) + dot(right, score_gradient)).astype(BF16).T
+            at = pl.ds(pl.multiple_of(t * width + c, CHUNK), CHUNK)
+            if add:
+                result[t, c : c + CHUNK] = value.astype(F32) + other[at].astype(F32)
+            else:
+                out[at] = value
         if add:
-            @pl.when(t >= 2)
-            def _():
-                send(t - 2).wait()
-            result[t % 2] = value.astype(F32) + other[at].astype(F32)
             send(t).start()
-        else:
-            out[at] = value
         return carry
 
     lax.fori_loop(0, tiles, block, 0)
     if add:
-        for t in range(max(tiles - 2, 0), tiles):
+        for t in range(tiles):
             send(t).wait()
+
+
+def unpack_kernel(gathered, quantized, gradient):
+    n_code, rows, both = gathered.shape
+    dim = both // 2
+    for g in range(n_code):
+        at = slice(g * rows, (g + 1) * rows)
+        quantized[at] = gathered[g, :, :dim].astype(F32)
+        gradient[at] = gathered[g, :, dim:].astype(F32)
 
 
 def swap(value, axis, size, mask):
@@ -230,15 +276,18 @@
     codes, sent = pl.pallas_call(
         functools.partial(forward_kernel, n_code),
         out_shape=(
-            pltpu.VMEM((tiles, n_tokens, width), BF16),
+            pltpu.HBM((tiles, n_tokens, width), BF16),
             jax.ShapeDtypeStruct((n_code, rows, 2 * dim + lanes), BF16),
         ),
         in_specs=[VMEM, VMEM, ANY, ANY],
-        out_specs=(VMEM, VMEM),
+        out_specs=(ANY, VMEM),
         scratch_shapes=[
             pltpu.VMEM((tiles, width, dim), BF16),
             pltpu.VMEM((tiles, n_tokens, width), BF16),
             pltpu.VMEM((tiles, n_tokens, width), F32),
+            pltpu.VMEM((tiles, n_tokens, width), F32),
+            pltpu.VMEM((2, n_tokens, width), BF16),
+            pltpu.VMEM((2, n_tokens, width), BF16),
             pltpu.VMEM((n_tokens, 128), F32),
             pltpu.VMEM((n_tokens, 128), F32),
             pltpu.VMEM((n_tokens, dim), F32),
@@ -246,9 +295,9 @@
             pltpu.SemaphoreType.DMA((tiles,)),
             pltpu.SemaphoreType.DMA((tiles,)),
         ],
-        compiler_params=pltpu.CompilerParams(vmem_limit_bytes=46 * MIB),
+        compiler_params=pltpu.CompilerParams(vmem_limit_bytes=60 * MIB),
         cost_estimate=pl.CostEstimate(
-            flops=4 * products, bytes_accessed=16 * MIB, transcendentals=n_tokens * n_codes
+            flops=4 * products, bytes_accessed=24 * MIB, transcendentals=n_tokens * n_codes
         ),
         name="forward",
     )(tokens, grad_out, codebook, noise)
@@ -262,28 +311,40 @@
         out_specs=VMEM,
         name="merge",
     )(code_at[None], received)
+    received, spread = lax.optimization_barrier((received, spread))
     gathered = lax.all_to_all(spread, "code", 0, 0, tiled=True)
-    gathered = gathered.reshape(n_tokens, 2 * dim).astype(F32)
-    quantized, token_gradient = gathered[:, :dim], gathered[:, dim:]
+    quantized, token_gradient = pl.pallas_call(
+        unpack_kernel,
+        out_shape=(jax.ShapeDtypeStruct((n_tokens, dim), F32),) * 2,
+        in_specs=[VMEM],
+        out_specs=(VMEM, VMEM),
+        name="unpack",
+    )(gathered)
 
     def backward(at, other=None):
         add = other is not None
         scratch = [
             pltpu.VMEM((block // width, width, dim), BF16),
-            pltpu.VMEM((2, width, dim), F32),
+            pltpu.VMEM((block // width, n_tokens, width), BF16),
             pltpu.VMEM((n_tokens, dim), F32),
             pltpu.VMEM((n_tokens, dim), F32),
             pltpu.VMEM((n_tokens, 128), F32),
             pltpu.SemaphoreType.DMA((block // width,)),
+            pltpu.SemaphoreType.DMA((block // width,)),
         ]
+        if add:
+            scratch += [
+                pltpu.VMEM((block // width, width, dim), F32),
+                pltpu.SemaphoreType.DMA((block // width,)),
+            ]
         extra = (other,) if add else ()
         return pl.pallas_call(
             functools.partial(backward_kernel, add),
             out_shape=jax.ShapeDtypeStruct((block, dim), F32 if add else BF16),
-            in_specs=[SMEM, VMEM, VMEM, ANY, VMEM, VMEM] + [VMEM] * add,
+            in_specs=[SMEM, VMEM, VMEM, ANY, ANY, VMEM] + [VMEM] * add,
             out_specs=ANY if add else VMEM,
-            scratch_shapes=scratch + [pltpu.SemaphoreType.DMA((2,))] * add,
-            compiler_params=pltpu.CompilerParams(vmem_limit_bytes=36 * MIB),
+            scratch_shapes=scratch,
+            compiler_params=pltpu.CompilerParams(vmem_limit_bytes=60 * MIB),
             cost_estimate=pl.CostEstimate(
                 flops=3 * products // n_dp, bytes_accessed=16 * MIB // n_dp, transcendentals=0
             ),

time: 97.7 us -> 91.6 us (0.938)
  local copies, waits for them, and re-layouts: 15.6 us -> 3.04 us
  Pallas kernels: 33.8 us -> 41.6 us
  waiting for transfers between devices: 32.8 us -> 31.6 us
    unnamed x18 -> x6, local copies, waits for them, and re-layouts: 14.6 us -> 3.04 us
    pallas_call x2, Pallas kernels: 14.3 us -> 20.3 us  [backward(): pl.pallas_call(functools.partial(backward_kernel, add), out_shape=jax.Sha...]
    pallas_call x0 -> x1, Pallas kernels: none -> 2.07 us  [local(): pl.pallas_call(unpack_kernel, out_shape=(jax.ShapeDtypeStruct((n_tokens,...]
    convert_element_type x1 -> x0, other arithmetic: 1.16 us -> none  [local(): gathered = gathered.reshape(n_tokens, 2 * dim).astype(F32)]
    another operation x2, other arithmetic: 0.15 us -> 1.24 us  [backward(): jnp.stack([code_at, at])]
    slice x1 -> x0, local copies, waits for them, and re-layouts: 1.05 us -> none  [local(): quantized, token_gradient = (gathered[:, :dim], gathered[:, dim:])]
  transfers between devices with their start and end apart: 3 -> 3, of which waited for: 2 -> 2; matrix products, arithmetic and copies ran while one was open for 2% -> 1% of each run, Pallas kernels for 3% -> 2%
where the time goes in v4:
time: 91.6 us; the launch traced here: 91.1 us
  Pallas kernels  41.6 us (45%)
  waiting for transfers between devices  31.6 us (34%)
  starting transfers between devices  12.8 us (14%)
  local copies, waits for them, and re-layouts  3.04 us (3%)
  other arithmetic  1.24 us (1%)
    pallas_call x2, Pallas kernels, backward(): pl.pallas_call(functools.partial(backward_kernel, add), out_shape=jax.Sha...  20.3 us
    pallas_call x1, Pallas kernels, local(): pl.pallas_call(functools.partial(forward_kernel, n_code), out_shape=(pltp...  16.8 us
    all_to_all x1, waiting for transfers between devices, local(): received = lax.all_to_all(sent, 'code', 0, 0, tiled=True)  16.8 us
    all_to_all x1, waiting for transfers between devices, local(): gathered = lax.all_to_all(spread, 'code', 0, 0, tiled=True)  14.9 us
    all_to_all x1, starting transfers between devices, local(): received = lax.all_to_all(sent, 'code', 0, 0, tiled=True)  8.32 us
    all_to_all x1, starting transfers between devices, local(): gathered = lax.all_to_all(spread, 'code', 0, 0, tiled=True)  4.43 us
    unnamed x6, local copies, waits for them, and re-layouts  3.04 us
    pallas_call x1, Pallas kernels, local(): pl.pallas_call(merge_kernel, out_shape=jax.ShapeDtypeStruct((n_code, rows...  2.45 us
  transfers between devices with their start and end apart: 3, of which 2 were waited for; matrix products, arithmetic and copies ran while one was open for 1% of the time, Pallas kernels for 2%

profile of v4, /device:TPU:0, one launch (start us, length us, event | category | flops | bytes accessed | tf_op | source)
XLA Modules:
  0.0 91.1 jit_solution(12625860736419757656)
XLA Ops:
  0.6 16.8 %forward.1 = (bf16[8,512,1024]{2,1,0:T(8,128)(2,1)}, bf16[16,32,640]{2,1,0:T(8,128)(2,1)}) custom-call(bf16[512,256]{1,0:T(8,128)(2,1)} %tokens.5, bf16[512,256]{1,0:T(8,128)(2,1)} %grad_out.5, bf16[8192,256]{1,0:T(8,128)(2,1)} %codebook.5, bf16[512,8192]{1,0:T(8,128)(2,1)} %noise.1), custom_call_target="tpu_custom_call" | custom-call | flops 8589934592 | bytes 25165824 | tf_op jit(solution)/shard_map/forward/pallas_call | solution.py:276
  17.4 8.3 %all-to-all-start = ((bf16[16,32,640]{2,1,0:T(8,128)(2,1)}), bf16[16,32,640]{2,1,0:T(8,128)(2,1)S(1)}, u32[]{:S(2)}, u32[]{:S(2)}) async-start(bf16[16,32,640]{2,1,0:T(8,128)(2,1)} %get-tuple-element.9), calls=%async_computation | async-start | bytes 1310720 | tf_op jit(solution)/shard_map/all_to_all | solution.py:305
  25.8 0.6 pad_add_fusion.1.where
  26.4 16.8 %all-to-all-done.received = bf16[16,32,640]{2,1,0:T(8,128)(2,1)S(1)} async-done(((bf16[16,32,640]{2,1,0:T(8,128)(2,1)}), bf16[16,32,640]{2,1,0:T(8,128)(2,1)S(1)}, u32[]{:S(2)}, u32[]{:S(2)}) %all-to-all-start) | async-done | bytes 655392 | tf_op jit(solution)/shard_map/all_to_all | solution.py:305
  43.2 0.0 copy-start
  43.2 0.8 copy-done
  44.0 2.4 %merge.1 = bf16[16,32,512]{2,1,0:T(8,128)(2,1)} custom-call(s32[1]{0:T(128)} %bitcast.me, bf16[16,32,640]{2,1,0:T(8,128)(2,1)} %copy-done), custom_call_target="tpu_custom_call" | custom-call | tf_op jit(solution)/shard_map/merge/pallas_call | solution.py:307
  46.5 9.9 %backward.2 = bf16[4096,256]{1,0:T(8,128)(2,1)} custom-call(s32[2]{0:T(128)} %pad_add_fusion.1.where, bf16[512,256]{1,0:T(8,128)(2,1)} %tokens.5, bf16[512,256]{1,0:T(8,128)(2,1)} %grad_out.5, bf16[8192,256]{1,0:T(8,128)(2,1)} %codebook.5, bf16[8,512,1024]{2,1,0:T(8,128)(2,1)} %get-tuple-element.13.codes, bf16[16,32,640]{2,1,0:T(8,128)(2,1)} %copy-done), custom_call_target="tpu_custom_call" | custom-call | flops 3221225472 | bytes 8388608 | tf_op jit(solution)/shard_map/backward/pallas_call | solution.py:341
  56.4 0.1 collective-permute-start
  56.5 4.4 %all-to-all-start.1 = ((bf16[16,32,512]{2,1,0:T(8,128)(2,1)}), bf16[16,32,512]{2,1,0:T(8,128)(2,1)S(1)}, u32[]{:S(2)}, u32[]{:S(2)}) async-start(bf16[16,32,512]{2,1,0:T(8,128)(2,1)} %merge.1), calls=%async_computation.1 | async-start | bytes 1048576 | tf_op jit(solution)/shard_map/all_to_all | solution.py:315
  60.9 0.6 pad_add_fusion.where
  61.5 14.9 %all-to-all-done.1.gathered = bf16[16,32,512]{2,1,0:T(8,128)(2,1)S(1)} async-done(((bf16[16,32,512]{2,1,0:T(8,128)(2,1)}), bf16[16,32,512]{2,1,0:T(8,128)(2,1)S(1)}, u32[]{:S(2)}, u32[]{:S(2)}) %all-to-all-start.1) | async-done | bytes 524320 | tf_op jit(solution)/shard_map/all_to_all | solution.py:315
  76.4 0.0 copy-start.2
  76.4 0.8 copy-done.2
  77.3 2.1 %unpack.1 = (f32[512,256]{1,0:T(8,128)}, f32[512,256]{1,0:T(8,128)}) custom-call(bf16[16,32,512]{2,1,0:T(8,128)(2,1)} %copy-done.2), custom_call_target="tpu_custom_call" | custom-call | tf_op jit(solution)/shard_map/unpack/pallas_call | solution.py:316
  79.3 0.0 collective-permute-done.rest_0_
  79.3 0.0 copy-start.1
  79.3 1.4 %copy-done.1 = bf16[4096,256]{1,0:T(8,128)(2,1)} copy-done((bf16[4096,256]{1,0:T(8,128)(2,1)}, bf16[4096,256]{1,0:T(8,128)(2,1)S(1)}, u32[]{:S(2)}) %copy-start.1) | copy-done | bytes 2097176
  80.7 10.4 %backward.3 = f32[4096,256]{1,0:T(8,128)} custom-call(s32[2]{0:T(128)} %pad_add_fusion.where, bf16[512,256]{1,0:T(8,128)(2,1)} %tokens.5, bf16[512,256]{1,0:T(8,128)(2,1)} %grad_out.5, bf16[8192,256]{1,0:T(8,128)(2,1)} %codebook.5, bf16[8,512,1024]{2,1,0:T(8,128)(2,1)} %get-tuple-element.13.codes, bf16[16,32,640]{2,1,0:T(8,128)(2,1)} %copy-done, ...), custom_call_target="tpu_custom_call" | custom-call | flops 3221225472 | bytes 8388608 | tf_op jit(solution)/shard_map/backward/pallas_call | solution.py:341
Async XLA Ops:
  17.4 25.8 %all-to-all-start = ((bf16[16,32,640]{2,1,0:T(8,128)(2,1)}), bf16[16,32,640]{2,1,0:T(8,128)(2,1)S(1)}, u32[]{:S(2)}, u32[]{:S(2)}) async-start(bf16[16,32,640]{2,1,0:T(8,128)(2,1)} %get-tuple-element.9), calls=%async_computation | async-start | bytes 1310720 | tf_op jit(solution)/shard_map/all_to_all | solution.py:305
  43.2 0.8 copy-start
  56.4 22.9 %collective-permute-start = (bf16[4096,256]{1,0:T(8,128)(2,1)}, bf16[4096,256]{1,0:T(8,128)(2,1)S(1)}, u32[]{:S(2)}, u32[]{:S(2)}) collective-permute-start(bf16[4096,256]{1,0:T(8,128)(2,1)} %backward.2), channel_id=1, source_target_pairs={{0,16},{16,0},{1,17},{17,1},{2,18},{18,2},{3,19},{19,3},{4,20},{20... | collective-permute-start | bytes 6291464 | tf_op jit(solution)/shard_map/ppermute | solution.py:263
  56.5 19.9 %all-to-all-start.1 = ((bf16[16,32,512]{2,1,0:T(8,128)(2,1)}), bf16[16,32,512]{2,1,0:T(8,128)(2,1)S(1)}, u32[]{:S(2)}, u32[]{:S(2)}) async-start(bf16[16,32,512]{2,1,0:T(8,128)(2,1)} %merge.1), calls=%async_computation.1 | async-start | bytes 1048576 | tf_op jit(solution)/shard_map/all_to_all | solution.py:315
  76.4 0.8 copy-start.2
  79.3 1.4 %copy-start.1 = (bf16[4096,256]{1,0:T(8,128)(2,1)}, bf16[4096,256]{1,0:T(8,128)(2,1)S(1)}, u32[]{:S(2)}) copy-start(bf16[4096,256]{1,0:T(8,128)(2,1)S(1)} %collective-permute-done.rest_0_) | copy-start | bytes 6291460

commit v5 on v4

v5 whole, which is shorter than its diff:
```python
import functools
import math

import jax
import jax.numpy as jnp
from jax import lax
from jax.experimental import pallas as pl
from jax.experimental.pallas import tpu as pltpu
from jax.sharding import PartitionSpec as P

SOFTMAX_HEAT = 0.5
TO_LOG2 = math.log2(math.e) / SOFTMAX_HEAT
BF16 = jnp.bfloat16
F32 = jnp.float32
MIB = 1 << 20
CHUNK = 256
AHEAD = 3
ROWS = 64
LARGEST = 2.0**60
VMEM = pl.BlockSpec(memory_space=pltpu.VMEM)
SMEM = pl.BlockSpec(memory_space=pltpu.SMEM)
ANY = pl.BlockSpec(memory_space=pl.ANY)


def dot(left, right, left_dim=1, right_dim=0):
    return lax.dot_general(
        left, right, (((left_dim,), (right_dim,)), ((), ())), preferred_element_type=F32
    )


def lane_groups(value):
    return [value[:, j : j + 128] for j in range(0, value.shape[1], 128)]


def stat_lanes(n_code):
    return max(8 * n_code, 128)


def high_low(value):
    high = value.astype(BF16).astype(F32)
    return high, (value - high).astype(BF16).astype(F32)


def forward_kernel(
    n_code, tokens, grad_out, codebook, noise, codes, sent,
    pair, book, noise_in, slot_a, slot_b, shifts, total, sums, book_sem, noise_sem, code_sem,
):
    tiles, n_tokens, width = codes.shape
    dim = tokens.shape[1]
    columns = [slice(c, c + CHUNK) for c in range(0, width, CHUNK)]
    slots = (slot_a, slot_b)

    def fetch(t):
        at = pl.multiple_of(t * width, width)
        return (
            pltpu.make_async_copy(codebook.at[pl.ds(at, width)], book.at[t], book_sem.at[t]),
            pltpu.make_async_copy(noise.at[:, pl.ds(at, width)], noise_in.at[t], noise_sem.at[t]),
        )

    def start(t):
        for copy in fetch(t):
            copy.start()

    def arrive(t):
        for copy in fetch(t):
            copy.wait()

    for t in range(min(AHEAD + 1, tiles)):
        start(t)
    for r in range(0, n_tokens, ROWS):
        pair[2 * r : 2 * r + ROWS] = tokens[r : r + ROWS]
        pair[2 * r + ROWS : 2 * r + 2 * ROWS] = grad_out[r : r + ROWS]

    def raise_shift(t, some):
        for c in some:
            value = (dot(tokens[...], book[t, c], 1, 1) + noise_in[t, :, c].astype(F32)) * TO_LOG2
            shifts[...] = functools.reduce(jnp.maximum, lane_groups(value), shifts[...])

    def store(t, s):
        return pltpu.make_async_copy(
            slots[s].at[pl.ds(0, n_tokens)], codes.at[t], code_sem.at[s]
        )

    def soften(t, s, fresh):
        if fresh is not None:
            @pl.when(fresh)
            def _():
                arrive(t)

                @pl.when(t + AHEAD < tiles)
                def _():
                    start(t + AHEAD)

        slot = slots[s]
        for c in columns:
            both = dot(pair[...], book[t, c], 1, 1)
            for r in range(0, n_tokens, ROWS):
                at = slice(r, r + ROWS)
                score = both[2 * r : 2 * r + ROWS] + noise_in[t, at, c].astype(F32)
                shift = jnp.concatenate([shifts[at]] * (CHUNK // 128), axis=1)
                weight = jnp.exp2(score * TO_LOG2 - shift)
                total[at] += sum(lane_groups(weight))
                slot[at, c] = weight.astype(BF16)
                gradient = both[2 * r + ROWS : 2 * r + 2 * ROWS]
                slot[n_tokens + r : n_tokens + r + ROWS, c] = (weight * gradient).astype(BF16)
        store(t, s).start()

    def accumulate(t, s):
        sums[...] += dot(slots[s][...], book[t])

    def attempt(state):
        again, _ = state
        fresh = again == 0
        shifts[...] = jnp.full(shifts.shape, -jnp.inf, F32)

        @pl.when(fresh)
        def _():
            raise_shift(0, columns[:2])

        @pl.when(jnp.logical_not(fresh))
        def _():
            def over(t, carry):
                raise_shift(t, columns)
                return carry

            lax.fori_loop(0, tiles, over, 0)

        shift = jnp.max(shifts[...], axis=1, keepdims=True).astype(BF16).astype(F32)
        shifts[...] = jnp.broadcast_to(shift, shifts.shape)
        total[...] = jnp.zeros(total.shape, F32)
        sums[...] = jnp.zeros(sums.shape, F32)
        soften(0, 0, None)

        def soften_pair(i, carry):
            @pl.when(i > 0)
            def _():
                store(2 * i - 1, 1).wait()

            soften(2 * i + 1, 1, fresh)
            accumulate(2 * i, 0)
            store(2 * i, 0).wait()
            soften(2 * i + 2, 0, fresh)
            accumulate(2 * i + 1, 1)
            return carry

        lax.fori_loop(0, tiles // 2 - 1, soften_pair, 0)
        if tiles > 2:
            store(tiles - 3, 1).wait()
        soften(tiles - 1, 1, fresh)
        accumulate(tiles - 2, 0)
        accumulate(tiles - 1, 1)
        store(tiles - 2, 0).wait()
        store(tiles - 1, 1).wait()
        fits = jnp.max(total[...]) < LARGEST
        return again + 1, jnp.logical_and(fresh, jnp.logical_not(fits))

    arrive(0)
    lax.while_loop(lambda state: state[1], attempt, (jnp.int32(0), jnp.bool_(True)))

    shift = shifts[:, :1]
    mix = sums[:n_tokens]
    pulled = sums[n_tokens:]
    own_total = jnp.sum(total[...], axis=1, keepdims=True)
    own_inner = jnp.sum(grad_out[...].astype(F32) * mix, axis=1, keepdims=True)
    mean = own_inner / own_total
    rows = n_tokens // n_code
    lanes = stat_lanes(n_code)
    half = lanes // 2
    lane = lax.broadcasted_iota(jnp.int32, (rows, lanes), 1)
    stats = jnp.zeros((rows, lanes), F32)
    parts = high_low(own_total) + high_low(own_inner)
    for g in range(n_code):
        at = slice(g * rows, (g + 1) * rows)
        for i, part in enumerate(parts):
            stats = jnp.where(lane == 4 * g + i, part[at], stats)
        stats = jnp.where((lane - half) // 4 == g, shift[at], stats)
    stats = stats.astype(BF16)
    for g in range(n_code):
        at = slice(g * rows, (g + 1) * rows)
        sent[g, :, :dim] = mix[at].astype(BF16)
        sent[g, :, dim : 2 * dim] = (pulled[at] - mean[at] * mix[at]).astype(BF16)
        sent[g, :, 2 * dim :] = stats


def roll_left(value, by):
    return pltpu.roll(value, value.shape[1] - by, 1)


def merged_stats(received):
    n_code = received.shape[0]
    lanes = stat_lanes(n_code)
    stats = [received[p, :, received.shape[2] - lanes :].astype(F32) for p in range(n_code)]
    top = functools.reduce(jnp.maximum, stats)
    scales = [roll_left(jnp.exp2(s - top), lanes // 2) for s in stats]
    pairs = [s + roll_left(s, 1) for s in stats]
    inners = [roll_left(s, 2) for s in pairs]
    total = sum(a * s for a, s in zip(scales, pairs))
    inner = sum(a * s for a, s in zip(scales, inners)) / total
    means = [i / s for i, s in zip(inners, pairs)]
    return [a / total for a in scales], means, inner


def merge_kernel(me, received, spread):
    n_code, rows, _ = received.shape
    dim = spread.shape[2] // 2
    scales, means, inner = merged_stats(received)
    lane = lax.broadcasted_iota(jnp.int32, inner.shape, 1)
    mine = lane == 4 * me[0]

    def column(value):
        return jnp.sum(jnp.where(mine, value, 0.0), axis=1, keepdims=True)

    quantized = jnp.zeros((rows, dim), F32)
    gradient = jnp.zeros((rows, dim), F32)
    for p in range(n_code):
        scale = column(scales[p])
        offset = column(scales[p] * (means[p] - inner))
        mix = received[p, :, :dim].astype(F32)
        quantized += scale * mix
        gradient += scale * received[p, :, dim : 2 * dim].astype(F32) + offset * mix
    quantized = quantized.astype(BF16)
    gradient = (gradient / SOFTMAX_HEAT).astype(BF16)
    for p in range(n_code):
        spread[p, :, :dim] = quantized
        spread[p, :, dim:] = gradient


def backward_kernel(prepared, where, *rest):
    if prepared:
        grad_out, codebook, codes, operands, inners, out, *rest = rest
    else:
        tokens, grad_out, codebook, codes, received, out, operands, inners, upper, lower, *rest = rest
    book, code_in, result, book_sem, code_sem, out_sem = rest
    tiles, width, dim = book.shape
    n_tokens = grad_out.shape[0]
    first = where[1] * tiles

    def fetch(t):
        at = pl.multiple_of((first + t) * width, width)
        return (
            pltpu.make_async_copy(codebook.at[pl.ds(at, width)], book.at[t], book_sem.at[t]),
            pltpu.make_async_copy(codes.at[first + t], code_in.at[t], code_sem.at[t]),
        )

    def start(t):
        for copy in fetch(t):
            copy.start()

    for t in range(min(AHEAD, tiles)):
        start(t)

    if not prepared:
        n_code, rows, _ = received.shape
        scales, _, inner = merged_stats(received)
        scale = jnp.zeros(inner.shape, F32)
        for p in range(n_code):
            scale = jnp.where(where[0] == p, scales[p], scale)
        for g in range(n_code):
            part = slice(g * rows, (g + 1) * rows)
            column = scale[:, 4 * g : 4 * g + 1]
            upper[part] = column * grad_out[part].astype(F32)
            lower[part] = column * (tokens[part].astype(F32) / SOFTMAX_HEAT)
            inners[part] = jnp.broadcast_to(inner[:, 4 * g : 4 * g + 1], (rows, 128))
        operands[0] = upper[...].T.astype(BF16)
        operands[1] = lower[...].T.astype(BF16)

    def send(t):
        return pltpu.make_async_copy(
            result.at[t], out.at[pl.ds(pl.multiple_of(t * width, width), width)], out_sem.at[t]
        )

    def block(t, carry):
        for copy in fetch(t):
            copy.wait()

        @pl.when(t + AHEAD < tiles)
        def _():
            start(t + AHEAD)

        for c in range(0, width, CHUNK):
            gradient = dot(grad_out[...], book[t, c : c + CHUNK], 1, 1)
            code = code_in[t, :, c : c + CHUNK]
            inner = jnp.concatenate([inners[...]] * (CHUNK // 128), axis=1)
            score_gradient = (code.astype(F32) * (gradient - inner)).astype(BF16)
            value = dot(operands[0], code) + dot(operands[1], score_gradient)
            result[t, c : c + CHUNK] = value.astype(BF16).T
        send(t).start()
        return carry

    lax.fori_loop(0, tiles, block, 0)
    for t in range(tiles):
        send(t).wait()


def add_kernel(*refs):
    out = refs[-1]
    out[...] = sum(ref[...].astype(F32) for ref in refs[:-1])


def unpack_kernel(gathered, quantized, gradient):
    n_code, rows, both = gathered.shape
    dim = both // 2
    for g in range(n_code):
        at = slice(g * rows, (g + 1) * rows)
        quantized[at] = gathered[g, :, :dim].astype(F32)
        gradient[at] = gathered[g, :, dim:].astype(F32)


def swap(value, axis, size, mask):
    return lax.ppermute(value, axis, [(i, i ^ mask) for i in range(size)])


def local(n_dp, n_code, tokens, codebook, noise, grad_out):
    n_tokens, dim = tokens.shape
    n_codes = codebook.shape[0]
    rows = n_tokens // n_code
    block = n_codes // n_dp
    width = min(1024, block)
    tiles = n_codes // width
    lanes = stat_lanes(n_code)
    products = 2 * n_tokens * n_codes * dim

    codes, sent = pl.pallas_call(
        functools.partial(forward_kernel, n_code),
        out_shape=(
            pltpu.HBM((tiles, n_tokens, width), BF16),
            jax.ShapeDtypeStruct((n_code, rows, 2 * dim + lanes), BF16),
        ),
        in_specs=[VMEM, VMEM, ANY, ANY],
        out_specs=(ANY, VMEM),
        scratch_shapes=[
            pltpu.VMEM((2 * n_tokens, dim), BF16),
            pltpu.VMEM((tiles, width, dim), BF16),
            pltpu.VMEM((tiles, n_tokens, width), BF16),
            pltpu.VMEM((2 * n_tokens, width), BF16),
            pltpu.VMEM((2 * n_tokens, width), BF16),
            pltpu.VMEM((n_tokens, 128), F32),
            pltpu.VMEM((n_tokens, 128), F32),
            pltpu.VMEM((2 * n_tokens, dim), F32),
            pltpu.SemaphoreType.DMA((tiles,)),
            pltpu.SemaphoreType.DMA((tiles,)),
            pltpu.SemaphoreType.DMA((2,)),
        ],
        compiler_params=pltpu.CompilerParams(vmem_limit_bytes=60 * MIB),
        cost_estimate=pl.CostEstimate(
            flops=4 * products, bytes_accessed=24 * MIB, transcendentals=n_tokens * n_codes
        ),
        name="forward",
    )(tokens, grad_out, codebook, noise)

    received = lax.all_to_all(sent, "code", 0, 0, tiled=True)
    code_at = lax.axis_index("code")
    spread = pl.pallas_call(
        merge_kernel,
        out_shape=jax.ShapeDtypeStruct((n_code, rows, 2 * dim), BF16),
        in_specs=[SMEM, VMEM],
        out_specs=VMEM,
        name="merge",
    )(code_at[None], received)
    received, spread = lax.optimization_barrier((received, spread))
    gathered = lax.all_to_all(spread, "code", 0, 0, tiled=True)
    quantized, token_gradient = pl.pallas_call(
        unpack_kernel,
        out_shape=(jax.ShapeDtypeStruct((n_tokens, dim), F32),) * 2,
        in_specs=[VMEM],
        out_specs=(VMEM, VMEM),
        cost_estimate=pl.CostEstimate(flops=0, bytes_accessed=64 * MIB, transcendentals=0),
        name="unpack",
    )(gathered)

    block_tiles = block // width
    streams = [
        pltpu.VMEM((block_tiles, width, dim), BF16),
        pltpu.VMEM((block_tiles, n_tokens, width), BF16),
        pltpu.VMEM((block_tiles, width, dim), BF16),
        pltpu.SemaphoreType.DMA((block_tiles,)),
        pltpu.SemaphoreType.DMA((block_tiles,)),
        pltpu.SemaphoreType.DMA((block_tiles,)),
    ]
    block_shape = jax.ShapeDtypeStruct((block, dim), BF16)
    common = dict(
        compiler_params=pltpu.CompilerParams(vmem_limit_bytes=60 * MIB),
        cost_estimate=pl.CostEstimate(
            flops=3 * products // n_dp, bytes_accessed=16 * MIB // n_dp, transcendentals=0
        ),
    )
    dp_at = lax.axis_index("dp")
    first, operands, inners = pl.pallas_call(
        functools.partial(backward_kernel, False),
        out_shape=(
            block_shape,
            jax.ShapeDtypeStruct((2, dim, n_tokens), BF16),
            jax.ShapeDtypeStruct((n_tokens, 128), F32),
        ),
        in_specs=[SMEM, VMEM, VMEM, ANY, ANY, VMEM],
        out_specs=(ANY, VMEM, VMEM),
        scratch_shapes=[
            pltpu.VMEM((n_tokens, dim), F32), pltpu.VMEM((n_tokens, dim), F32),
        ] + streams,
        name="backward_first",
        **common,
    )(jnp.stack([code_at, dp_at ^ (n_dp - 1)]), tokens, grad_out, codebook, codes, received)

    def backward(at):
        return pl.pallas_call(
            functools.partial(backward_kernel, True),
            out_shape=block_shape,
            in_specs=[SMEM, VMEM, ANY, ANY, VMEM, VMEM],
            out_specs=ANY,
            scratch_shapes=streams,
            name="backward",
            **common,
        )(jnp.stack([code_at, at]), grad_out, codebook, codes, operands, inners)

    blocks = [swap(first, "dp", n_dp, n_dp - 1)]
    blocks += [swap(backward(dp_at ^ d), "dp", n_dp, d) for d in range(1, n_dp - 1)]
    blocks.append(backward(dp_at))
    rows_spec = pl.BlockSpec((min(1024, block), dim), lambda i: (i, 0))
    own_rows = pl.pallas_call(
        add_kernel,
        out_shape=jax.ShapeDtypeStruct((block, dim), F32),
        grid=(block // min(1024, block),),
        in_specs=[rows_spec] * n_dp,
        out_specs=rows_spec,
        cost_estimate=pl.CostEstimate(
            flops=0, bytes_accessed=(2 * n_dp + 4) * block * dim, transcendentals=0
        ),
        name="add",
    )(*blocks)
    return quantized, token_gradient, own_rows[None]


def solution(mesh):
    n_dp, n_code = mesh.shape["dp"], mesh.shape["code"]
    in_specs = (P("dp", None), P("code", None), P("dp", "code"), P("dp", None))
    out_specs = (P("dp", None), P("dp", None), P("code", "dp", None))
    return jax.shard_map(
        functools.partial(local, n_dp, n_code),
        mesh=mesh, in_specs=in_specs, out_specs=out_specs, check_vma=False,
    )
```

time: 91.6 us -> 99.4 us (1.085)
  Pallas kernels: 41.6 us -> 58.7 us
  waiting for transfers between devices: 31.6 us -> 22.4 us
    pallas_call x1, Pallas kernels: 16.8 us -> 29.9 us  [local(): pl.pallas_call(functools.partial(forward_kernel, n_code), out_shape=(pltp...]
    all_to_all x1, waiting for transfers between devices: 14.9 us -> 5.57 us  [local(): gathered = lax.all_to_all(spread, 'code', 0, 0, tiled=True)]
    pallas_call x2 -> x3, Pallas kernels: 20.3 us -> 24.3 us  [the longest x1 10.3 us: local(): pl.pallas_call(functools.partial(backward_kernel, False), out_shape=(bloc...]
  transfers between devices with their start and end apart: 3 -> 3, of which waited for: 2 -> 2; matrix products, arithmetic and copies ran while one was open for 1% -> 1% of each run, Pallas kernels for 2% -> 11%
where the time goes in v5:
time: 99.4 us; the launch traced here: 98.9 us
  Pallas kernels  58.7 us (59%)
  waiting for transfers between devices  22.4 us (23%)
  starting transfers between devices  12.8 us (13%)
  local copies, waits for them, and re-layouts  3.01 us (3%)
  other arithmetic  1.26 us (1%)
    pallas_call x1, Pallas kernels, local(): pl.pallas_call(functools.partial(forward_kernel, n_code), out_shape=(pltp...  29.9 us
    all_to_all x1, waiting for transfers between devices, local(): received = lax.all_to_all(sent, 'code', 0, 0, tiled=True)  16.8 us
    pallas_call x1, Pallas kernels, local(): pl.pallas_call(functools.partial(backward_kernel, False), out_shape=(bloc...  10.3 us
    pallas_call x1, Pallas kernels, backward(): pl.pallas_call(functools.partial(backward_kernel, True), out_shape=block_...  9.23 us
    all_to_all x1, starting transfers between devices, local(): received = lax.all_to_all(sent, 'code', 0, 0, tiled=True)  8.33 us
    all_to_all x1, waiting for transfers between devices, local(): gathered = lax.all_to_all(spread, 'code', 0, 0, tiled=True)  5.57 us
    pallas_call x1, Pallas kernels, local(): pl.pallas_call(add_kernel, out_shape=jax.ShapeDtypeStruct((block, dim), F...  4.74 us
    all_to_all x1, starting transfers between devices, local(): gathered = lax.all_to_all(spread, 'code', 0, 0, tiled=True)  4.43 us
  transfers between devices with their start and end apart: 3, of which 2 were waited for; matrix products, arithmetic and copies ran while one was open for 1% of the time, Pallas kernels for 11%

profile of v5, /device:TPU:0, one launch (start us, length us, event | category | flops | bytes accessed | tf_op | source)
XLA Modules:
  0.0 98.9 jit_solution(3760289231087501647)
XLA Ops:
  0.6 29.9 %forward.1 = (bf16[8,512,1024]{2,1,0:T(8,128)(2,1)}, bf16[16,32,640]{2,1,0:T(8,128)(2,1)}) custom-call(bf16[512,256]{1,0:T(8,128)(2,1)} %rest_0_.2, bf16[512,256]{1,0:T(8,128)(2,1)} %rest_0_.3, bf16[8192,256]{1,0:T(8,128)(2,1)} %rest_1_.3, bf16[512,8192]{1,0:T(8,128)(2,1)} %noise.1), custom_call_target="tpu_custom_call" | custom-call | flops 8589934592 | bytes 25165824 | tf_op jit(solution)/shard_map/forward/pallas_call | solution.py:323
  30.5 8.3 %all-to-all-start = ((bf16[16,32,640]{2,1,0:T(8,128)(2,1)}), bf16[16,32,640]{2,1,0:T(8,128)(2,1)S(1)}, u32[]{:S(2)}, u32[]{:S(2)}) async-start(bf16[16,32,640]{2,1,0:T(8,128)(2,1)} %get-tuple-element.12), calls=%async_computation | async-start | bytes 1310720 | tf_op jit(solution)/shard_map/all_to_all | solution.py:351
  38.9 0.6 pad_add_fusion.where
  39.4 16.8 %all-to-all-done.received.rest_4_ = bf16[16,32,640]{2,1,0:T(8,128)(2,1)S(1)} async-done(((bf16[16,32,640]{2,1,0:T(8,128)(2,1)}), bf16[16,32,640]{2,1,0:T(8,128)(2,1)S(1)}, u32[]{:S(2)}, u32[]{:S(2)}) %all-to-all-start) | async-done | bytes 655392 | tf_op jit(solution)/shard_map/all_to_all | solution.py:351
  56.3 0.0 copy-start
  56.3 0.9 copy-done
  57.1 2.4 %merge.1 = bf16[16,32,512]{2,1,0:T(8,128)(2,1)} custom-call(s32[1]{0:T(128)} %bitcast.me, bf16[16,32,640]{2,1,0:T(8,128)(2,1)} %copy-done), custom_call_target="tpu_custom_call" | custom-call | tf_op jit(solution)/shard_map/merge/pallas_call | solution.py:353
  59.6 10.3 %backward_first.1 = (bf16[4096,256]{1,0:T(8,128)(2,1)}, bf16[2,256,512]{2,1,0:T(8,128)(2,1)}, f32[512,128]{1,0:T(8,128)}) custom-call(s32[2]{0:T(128)} %pad_add_fusion.where, bf16[512,256]{1,0:T(8,128)(2,1)} %rest_0_.2, bf16[512,256]{1,0:T(8,128)(2,1)} %rest_0_.3, bf16[8192,256]{1,0:T(8,128)(2,1)} %rest_1_.3, ...), custom_call_target="tpu_custom_call" | custom-call | flops 3221225472 | bytes 8388608 | tf_op jit(solution)/shard_map/backward_first/pallas_call | solution.py:388
  69.9 0.1 collective-permute-start
  70.0 4.4 %all-to-all-start.1 = ((bf16[16,32,512]{2,1,0:T(8,128)(2,1)}), bf16[16,32,512]{2,1,0:T(8,128)(2,1)S(1)}, u32[]{:S(2)}, u32[]{:S(2)}) async-start(bf16[16,32,512]{2,1,0:T(8,128)(2,1)} %merge.1), calls=%async_computation.1 | async-start | bytes 1048576 | tf_op jit(solution)/shard_map/all_to_all | solution.py:361
  74.5 0.7 pad_add_fusion.1.where
  75.1 9.2 %backward.1.refs_1_ = bf16[4096,256]{1,0:T(8,128)(2,1)} custom-call(s32[2]{0:T(128)} %pad_add_fusion.1.where, bf16[512,256]{1,0:T(8,128)(2,1)} %rest_0_.3, bf16[8192,256]{1,0:T(8,128)(2,1)} %rest_1_.3, bf16[8,512,1024]{2,1,0:T(8,128)(2,1)} %get-tuple-element.16.rest_3_.rest_2_, bf16[2,256,512]{2,1,0:T(8,128)(2,1)} %get-tuple-element.19.rest_3_, ...), custom_call_target="tpu_custom_call" | custom-call | flops 3221225472 | bytes 8388608 | tf_op jit(solution)/shard_map/backward/pallas_call | solution.py:405
  84.3 5.6 %all-to-all-done.1.gathered = bf16[16,32,512]{2,1,0:T(8,128)(2,1)S(1)} async-done(((bf16[16,32,512]{2,1,0:T(8,128)(2,1)}), bf16[16,32,512]{2,1,0:T(8,128)(2,1)S(1)}, u32[]{:S(2)}, u32[]{:S(2)}) %all-to-all-start.1) | async-done | bytes 524320 | tf_op jit(solution)/shard_map/all_to_all | solution.py:361
  89.9 0.0 copy-start.1
  89.9 0.8 copy-done.1
  90.7 2.1 %unpack.1 = (f32[512,256]{1,0:T(8,128)}, f32[512,256]{1,0:T(8,128)}) custom-call(bf16[16,32,512]{2,1,0:T(8,128)(2,1)} %copy-done.1), custom_call_target="tpu_custom_call" | custom-call | bytes 67108864 | tf_op jit(solution)/shard_map/unpack/pallas_call | solution.py:362
  92.8 0.0 collective-permute-done.refs_0_
  92.8 0.0 copy-start.2
  92.8 1.3 %copy-done.2 = bf16[4096,256]{1,0:T(8,128)(2,1)} copy-done((bf16[4096,256]{1,0:T(8,128)(2,1)}, bf16[4096,256]{1,0:T(8,128)(2,1)S(1)}, u32[]{:S(2)}) %copy-start.2) | copy-done | bytes 2097176
  94.1 4.7 %add.5 = f32[4096,256]{1,0:T(8,128)} custom-call(bf16[4096,256]{1,0:T(8,128)(2,1)} %copy-done.2, bf16[4096,256]{1,0:T(8,128)(2,1)} %backward.1.refs_1_), custom_call_target="tpu_custom_call" | custom-call | bytes 8388608 | tf_op jit(solution)/shard_map/add/pallas_call | solution.py:419
Async XLA Ops:
  30.5 25.7 %all-to-all-start = ((bf16[16,32,640]{2,1,0:T(8,128)(2,1)}), bf16[16,32,640]{2,1,0:T(8,128)(2,1)S(1)}, u32[]{:S(2)}, u32[]{:S(2)}) async-start(bf16[16,32,640]{2,1,0:T(8,128)(2,1)} %get-tuple-element.12), calls=%async_computation | async-start | bytes 1310720 | tf_op jit(solution)/shard_map/all_to_all | solution.py:351
  56.3 0.9 copy-start
  69.9 22.8 %collective-permute-start = (bf16[4096,256]{1,0:T(8,128)(2,1)}, bf16[4096,256]{1,0:T(8,128)(2,1)S(1)}, u32[]{:S(2)}, u32[]{:S(2)}) collective-permute-start(bf16[4096,256]{1,0:T(8,128)(2,1)} %get-tuple-element.18), channel_id=1, source_target_pairs={{0,16},{16,0},{1,17},{17,1},{2,18},{18,2},{3,19},{19,3},{4,20},{20... | collective-permute-start | bytes 6291464 | tf_op jit(solution)/shard_map/ppermute | solution.py:310
  70.0 19.9 %all-to-all-start.1 = ((bf16[16,32,512]{2,1,0:T(8,128)(2,1)}), bf16[16,32,512]{2,1,0:T(8,128)(2,1)S(1)}, u32[]{:S(2)}, u32[]{:S(2)}) async-start(bf16[16,32,512]{2,1,0:T(8,128)(2,1)} %merge.1), calls=%async_computation.1 | async-start | bytes 1048576 | tf_op jit(solution)/shard_map/all_to_all | solution.py:361
  89.9 0.8 copy-start.1
  92.8 1.3 %copy-start.2 = (bf16[4096,256]{1,0:T(8,128)(2,1)}, bf16[4096,256]{1,0:T(8,128)(2,1)S(1)}, u32[]{:S(2)}) copy-start(bf16[4096,256]{1,0:T(8,128)(2,1)S(1)} %collective-permute-done.refs_0_) | copy-start | bytes 6291460

commit v6 on v5

--- a/solution.py
+++ b/solution.py
@@ -20,6 +20,7 @@
 VMEM = pl.BlockSpec(memory_space=pltpu.VMEM)
 SMEM = pl.BlockSpec(memory_space=pltpu.SMEM)
 ANY = pl.BlockSpec(memory_space=pl.ANY)
+FULL = pltpu.CompilerParams(vmem_limit_bytes=60 * MIB)
 
 
 def dot(left, right, left_dim=1, right_dim=0):
@@ -43,7 +44,8 @@
 
 def forward_kernel(
     n_code, tokens, grad_out, codebook, noise, codes, sent,
-    pair, book, noise_in, slot_a, slot_b, shifts, total, sums, book_sem, noise_sem, code_sem,
+    pair, book, noise_in, slot_a, slot_b, shifts, total, sums,
+    pair_sem, book_sem, noise_sem, code_sem,
 ):
     tiles, n_tokens, width = codes.shape
     dim = tokens.shape[1]
@@ -65,16 +67,31 @@
         for copy in fetch(t):
             copy.wait()
 
-    for t in range(min(AHEAD + 1, tiles)):
+    pair_copies = []
+    for r in range(0, n_tokens, ROWS):
+        for half, source in enumerate((tokens, grad_out)):
+            pair_copies.append(
+                pltpu.make_async_copy(
+                    source.at[pl.ds(r, ROWS)],
+                    pair.at[pl.ds(2 * r + half * ROWS, ROWS)],
+                    pair_sem.at[len(pair_copies)],
+                )
+            )
+    start(0)
+    for copy in pair_copies:
+        copy.start()
+    for t in range(1, min(AHEAD + 1, tiles)):
         start(t)
-    for r in range(0, n_tokens, ROWS):
-        pair[2 * r : 2 * r + ROWS] = tokens[r : r + ROWS]
-        pair[2 * r + ROWS : 2 * r + 2 * ROWS] = grad_out[r : r + ROWS]
 
     def raise_shift(t, some):
         for c in some:
-            value = (dot(tokens[...], book[t, c], 1, 1) + noise_in[t, :, c].astype(F32)) * TO_LOG2
-            shifts[...] = functools.reduce(jnp.maximum, lane_groups(value), shifts[...])
+            both = dot(pair[...], book[t, c], 1, 1)
+            for r in range(0, n_tokens, ROWS):
+                at = slice(r, r + ROWS)
+                score = both[2 * r : 2 * r + ROWS] + noise_in[t, at, c].astype(F32)
+                shifts[at] = functools.reduce(
+                    jnp.maximum, lane_groups(score * TO_LOG2), shifts[at]
+                )
 
     def store(t, s):
         return pltpu.make_async_copy(
@@ -154,6 +171,8 @@
         fits = jnp.max(total[...]) < LARGEST
         return again + 1, jnp.logical_and(fresh, jnp.logical_not(fits))
 
+    for copy in pair_copies:
+        copy.wait()
     arrive(0)
     lax.while_loop(lambda state: state[1], attempt, (jnp.int32(0), jnp.bool_(True)))
 
@@ -161,7 +180,10 @@
     mix = sums[:n_tokens]
     pulled = sums[n_tokens:]
     own_total = jnp.sum(total[...], axis=1, keepdims=True)
-    own_inner = jnp.sum(grad_out[...].astype(F32) * mix, axis=1, keepdims=True)
+    own_grad = jnp.concatenate(
+        [pair[2 * r + ROWS : 2 * r + 2 * ROWS] for r in range(0, n_tokens, ROWS)], axis=0
+    )
+    own_inner = jnp.sum(own_grad.astype(F32) * mix, axis=1, keepdims=True)
     mean = own_inner / own_total
     rows = n_tokens // n_code
     lanes = stat_lanes(n_code)
@@ -269,32 +291,59 @@
             result.at[t], out.at[pl.ds(pl.multiple_of(t * width, width), width)], out_sem.at[t]
         )
 
-    def block(t, carry):
-        for copy in fetch(t):
-            copy.wait()
-
-        @pl.when(t + AHEAD < tiles)
-        def _():
-            start(t + AHEAD)
-
-        for c in range(0, width, CHUNK):
-            gradient = dot(grad_out[...], book[t, c : c + CHUNK], 1, 1)
-            code = code_in[t, :, c : c + CHUNK]
-            inner = jnp.concatenate([inners[...]] * (CHUNK // 128), axis=1)
-            score_gradient = (code.astype(F32) * (gradient - inner)).astype(BF16)
-            value = dot(operands[0], code) + dot(operands[1], score_gradient)
-            result[t, c : c + CHUNK] = value.astype(BF16).T
-        send(t).start()
-        return carry
-
-    lax.fori_loop(0, tiles, block, 0)
+    chunk = min(CHUNK, width)
+    steps = [(t, slice(c, c + chunk)) for t in range(tiles) for c in range(0, width, chunk)]
+
+    def gradient_of(step):
+        t, c = step
+        if c.start == 0:
+            for copy in fetch(t):
+                copy.wait()
+            if t + AHEAD < tiles:
+                start(t + AHEAD)
+        return dot(grad_out[...], book[t, c], 1, 1)
+
+    ahead = gradient_of(steps[0])
+    for k, (t, c) in enumerate(steps):
+        gradient = ahead
+        if k + 1 < len(steps):
+            ahead = gradient_of(steps[k + 1])
+        code = code_in[t, :, c]
+        inner = jnp.concatenate([inners[...]] * (chunk // 128), axis=1)
+        score_gradient = (code.astype(F32) * (gradient - inner)).astype(BF16)
+        value = dot(operands[0], code) + dot(operands[1], score_gradient)
+        result[t, c] = value.astype(BF16).T
+        if c.stop == width:
+            send(t).start()
     for t in range(tiles):
         send(t).wait()
 
 
-def add_kernel(*refs):
-    out = refs[-1]
-    out[...] = sum(ref[...].astype(F32) for ref in refs[:-1])
+def add_kernel(n_parts, *refs):
+    parts, out = refs[:n_parts], refs[n_parts]
+    held, result, in_sem, out_sem = refs[n_parts + 1 :]
+    steps, rows, _ = result.shape
+
+    def fetch(i):
+        at = pl.ds(i * rows, rows)
+        return [
+            pltpu.make_async_copy(part.at[at], held.at[j, i], in_sem.at[j, i])
+            for j, part in enumerate(parts)
+        ]
+
+    def send(i):
+        return pltpu.make_async_copy(result.at[i], out.at[pl.ds(i * rows, rows)], out_sem.at[i])
+
+    for i in range(steps):
+        for copy in fetch(i):
+            copy.start()
+    for i in range(steps):
+        for copy in fetch(i):
+            copy.wait()
+        result[i] = sum(held[j, i].astype(F32) for j in range(n_parts))
+        send(i).start()
+    for i in range(steps):
+        send(i).wait()
 
 
 def unpack_kernel(gathered, quantized, gradient):
@@ -326,7 +375,7 @@
             pltpu.HBM((tiles, n_tokens, width), BF16),
             jax.ShapeDtypeStruct((n_code, rows, 2 * dim + lanes), BF16),
         ),
-        in_specs=[VMEM, VMEM, ANY, ANY],
+        in_specs=[ANY, ANY, ANY, ANY],
         out_specs=(ANY, VMEM),
         scratch_shapes=[
             pltpu.VMEM((2 * n_tokens, dim), BF16),
@@ -337,11 +386,12 @@
             pltpu.VMEM((n_tokens, 128), F32),
             pltpu.VMEM((n_tokens, 128), F32),
             pltpu.VMEM((2 * n_tokens, dim), F32),
+            pltpu.SemaphoreType.DMA((2 * n_tokens // ROWS,)),
             pltpu.SemaphoreType.DMA((tiles,)),
             pltpu.SemaphoreType.DMA((tiles,)),
             pltpu.SemaphoreType.DMA((2,)),
         ],
-        compiler_params=pltpu.CompilerParams(vmem_limit_bytes=60 * MIB),
+        compiler_params=FULL,
         cost_estimate=pl.CostEstimate(
             flops=4 * products, bytes_accessed=24 * MIB, transcendentals=n_tokens * n_codes
         ),
@@ -355,6 +405,7 @@
         out_shape=jax.ShapeDtypeStruct((n_code, rows, 2 * dim), BF16),
         in_specs=[SMEM, VMEM],
         out_specs=VMEM,
+        compiler_params=FULL,
         name="merge",
     )(code_at[None], received)
     received, spread = lax.optimization_barrier((received, spread))
@@ -364,6 +415,7 @@
         out_shape=(jax.ShapeDtypeStruct((n_tokens, dim), F32),) * 2,
         in_specs=[VMEM],
         out_specs=(VMEM, VMEM),
+        compiler_params=FULL,
         cost_estimate=pl.CostEstimate(flops=0, bytes_accessed=64 * MIB, transcendentals=0),
         name="unpack",
     )(gathered)
@@ -379,10 +431,8 @@
     ]
     block_shape = jax.ShapeDtypeStruct((block, dim), BF16)
     common = dict(
-        compiler_params=pltpu.CompilerParams(vmem_limit_bytes=60 * MIB),
-        cost_estimate=pl.CostEstimate(
-            flops=3 * products // n_dp, bytes_accessed=16 * MIB // n_dp, transcendentals=0
-        ),
+        compiler_params=FULL,
+        cost_estimate=pl.CostEstimate(flops=1, bytes_accessed=1, transcendentals=0),
     )
     dp_at = lax.axis_index("dp")
     first, operands, inners = pl.pallas_call(
@@ -415,13 +465,19 @@
     blocks = [swap(first, "dp", n_dp, n_dp - 1)]
     blocks += [swap(backward(dp_at ^ d), "dp", n_dp, d) for d in range(1, n_dp - 1)]
     blocks.append(backward(dp_at))
-    rows_spec = pl.BlockSpec((min(1024, block), dim), lambda i: (i, 0))
+    steps = max(block // 512, 1)
     own_rows = pl.pallas_call(
-        add_kernel,
+        functools.partial(add_kernel, n_dp),
         out_shape=jax.ShapeDtypeStruct((block, dim), F32),
-        grid=(block // min(1024, block),),
-        in_specs=[rows_spec] * n_dp,
-        out_specs=rows_spec,
+        in_specs=[ANY] * n_dp,
+        out_specs=ANY,
+        scratch_shapes=[
+            pltpu.VMEM((n_dp, steps, block // steps, dim), BF16),
+            pltpu.VMEM((steps, block // steps, dim), F32),
+            pltpu.SemaphoreType.DMA((n_dp, steps)),
+            pltpu.SemaphoreType.DMA((steps,)),
+        ],
+        compiler_params=FULL,
         cost_estimate=pl.CostEstimate(
             flops=0, bytes_accessed=(2 * n_dp + 4) * block * dim, transcendentals=0
         ),

time: 99.4 us -> 99.8 us (level)
  waiting for transfers between devices: 22.4 us -> 23.4 us
    pallas_call x1, Pallas kernels: 29.9 us -> 32.3 us  [local(): pl.pallas_call(functools.partial(forward_kernel, n_code), out_shape=(pltp...]
    pallas_call x1, Pallas kernels: 4.74 us -> 3.59 us  [local(): pl.pallas_call(functools.partial(add_kernel, n_dp), out_shape=jax.ShapeDt...]
  transfers between devices with their start and end apart: 3 -> 3, of which waited for: 2 -> 2; matrix products, arithmetic and copies ran while one was open for 1% -> 1% of each run, Pallas kernels for 11% -> 10%
where the time goes in v6:
time: 99.8 us; the launch traced here: 99.3 us
  Pallas kernels  58 us (58%)
  waiting for transfers between devices  23.4 us (23%)
  starting transfers between devices  12.8 us (13%)
  local copies, waits for them, and re-layouts  3.01 us (3%)
  other arithmetic  1.26 us (1%)
    pallas_call x1, Pallas kernels, local(): pl.pallas_call(functools.partial(forward_kernel, n_code), out_shape=(pltp...  32.3 us
    all_to_all x1, waiting for transfers between devices, local(): received = lax.all_to_all(sent, 'code', 0, 0, tiled=True)  16.8 us
    pallas_call x1, Pallas kernels, local(): pl.pallas_call(functools.partial(backward_kernel, False), out_shape=(bloc...  9.37 us
    all_to_all x1, starting transfers between devices, local(): received = lax.all_to_all(sent, 'code', 0, 0, tiled=True)  8.33 us
    pallas_call x1, Pallas kernels, backward(): pl.pallas_call(functools.partial(backward_kernel, True), out_shape=block_...  8.23 us
    all_to_all x1, waiting for transfers between devices, local(): gathered = lax.all_to_all(spread, 'code', 0, 0, tiled=True)  6.56 us
    all_to_all x1, starting transfers between devices, local(): gathered = lax.all_to_all(spread, 'code', 0, 0, tiled=True)  4.44 us
    pallas_call x1, Pallas kernels, local(): pl.pallas_call(functools.partial(add_kernel, n_dp), out_shape=jax.ShapeDt...  3.59 us
  transfers between devices with their start and end apart: 3, of which 2 were waited for; matrix products, arithmetic and copies ran while one was open for 1% of the time, Pallas kernels for 10%

profile of v6, /device:TPU:0, one launch (start us, length us, event | category | flops | bytes accessed | tf_op | source)
XLA Modules:
  0.0 99.3 jit_solution(7388202746868633864)
XLA Ops:
  0.6 32.3 %forward.1 = (bf16[8,512,1024]{2,1,0:T(8,128)(2,1)}, bf16[16,32,640]{2,1,0:T(8,128)(2,1)}) custom-call(bf16[512,256]{1,0:T(8,128)(2,1)} %rest_0_.2, bf16[512,256]{1,0:T(8,128)(2,1)} %rest_0_.3, bf16[8192,256]{1,0:T(8,128)(2,1)} %rest_1_.3, bf16[512,8192]{1,0:T(8,128)(2,1)} %noise.1), custom_call_target="tpu_custom_call" | custom-call | flops 8589934592 | bytes 25165824 | tf_op jit(solution)/shard_map/forward/pallas_call | solution.py:372
  32.9 8.3 %all-to-all-start = ((bf16[16,32,640]{2,1,0:T(8,128)(2,1)}), bf16[16,32,640]{2,1,0:T(8,128)(2,1)S(1)}, u32[]{:S(2)}, u32[]{:S(2)}) async-start(bf16[16,32,640]{2,1,0:T(8,128)(2,1)} %get-tuple-element.12), calls=%async_computation | async-start | bytes 1310720 | tf_op jit(solution)/shard_map/all_to_all | solution.py:401
  41.3 0.6 pad_add_fusion.where
  41.9 16.8 %all-to-all-done.received.rest_4_ = bf16[16,32,640]{2,1,0:T(8,128)(2,1)S(1)} async-done(((bf16[16,32,640]{2,1,0:T(8,128)(2,1)}), bf16[16,32,640]{2,1,0:T(8,128)(2,1)S(1)}, u32[]{:S(2)}, u32[]{:S(2)}) %all-to-all-start) | async-done | bytes 655392 | tf_op jit(solution)/shard_map/all_to_all | solution.py:401
  58.7 0.0 copy-start
  58.7 0.9 copy-done
  59.5 2.4 %merge.1 = bf16[16,32,512]{2,1,0:T(8,128)(2,1)} custom-call(s32[1]{0:T(128)} %bitcast.me, bf16[16,32,640]{2,1,0:T(8,128)(2,1)} %copy-done), custom_call_target="tpu_custom_call" | custom-call | tf_op jit(solution)/shard_map/merge/pallas_call | solution.py:403
  62.0 9.4 %backward_first.1 = (bf16[4096,256]{1,0:T(8,128)(2,1)}, bf16[2,256,512]{2,1,0:T(8,128)(2,1)}, f32[512,128]{1,0:T(8,128)}) custom-call(s32[2]{0:T(128)} %pad_add_fusion.where, bf16[512,256]{1,0:T(8,128)(2,1)} %rest_0_.2, bf16[512,256]{1,0:T(8,128)(2,1)} %rest_0_.3, bf16[8192,256]{1,0:T(8,128)(2,1)} %rest_1_.3, ...), custom_call_target="tpu_custom_call" | custom-call | flops 1 | bytes 1 | tf_op jit(solution)/shard_map/backward_first/pallas_call | solution.py:438
  71.4 0.1 collective-permute-start
  71.5 4.4 %all-to-all-start.1 = ((bf16[16,32,512]{2,1,0:T(8,128)(2,1)}), bf16[16,32,512]{2,1,0:T(8,128)(2,1)S(1)}, u32[]{:S(2)}, u32[]{:S(2)}) async-start(bf16[16,32,512]{2,1,0:T(8,128)(2,1)} %merge.1), calls=%async_computation.1 | async-start | bytes 1048576 | tf_op jit(solution)/shard_map/all_to_all | solution.py:412
  75.9 0.7 pad_add_fusion.1.where
  76.6 8.2 %backward.1.refs_1_ = bf16[4096,256]{1,0:T(8,128)(2,1)} custom-call(s32[2]{0:T(128)} %pad_add_fusion.1.where, bf16[512,256]{1,0:T(8,128)(2,1)} %rest_0_.3, bf16[8192,256]{1,0:T(8,128)(2,1)} %rest_1_.3, bf16[8,512,1024]{2,1,0:T(8,128)(2,1)} %get-tuple-element.16.rest_3_.rest_2_, bf16[2,256,512]{2,1,0:T(8,128)(2,1)} %get-tuple-element.19.rest_3_, ...), custom_call_target="tpu_custom_call" | custom-call | flops 1 | bytes 1 | tf_op jit(solution)/shard_map/backward/pallas_call | solution.py:455
  84.8 6.6 %all-to-all-done.1.gathered = bf16[16,32,512]{2,1,0:T(8,128)(2,1)S(1)} async-done(((bf16[16,32,512]{2,1,0:T(8,128)(2,1)}), bf16[16,32,512]{2,1,0:T(8,128)(2,1)S(1)}, u32[]{:S(2)}, u32[]{:S(2)}) %all-to-all-start.1) | async-done | bytes 524320 | tf_op jit(solution)/shard_map/all_to_all | solution.py:412
  91.4 0.0 copy-start.1
  91.4 0.8 copy-done.1
  92.2 2.1 %unpack.1 = (f32[512,256]{1,0:T(8,128)}, f32[512,256]{1,0:T(8,128)}) custom-call(bf16[16,32,512]{2,1,0:T(8,128)(2,1)} %copy-done.1), custom_call_target="tpu_custom_call" | custom-call | bytes 67108864 | tf_op jit(solution)/shard_map/unpack/pallas_call | solution.py:413
  94.2 0.0 collective-permute-done.refs_0_
  94.2 0.0 copy-start.2
  94.2 1.3 %copy-done.2 = bf16[4096,256]{1,0:T(8,128)(2,1)} copy-done((bf16[4096,256]{1,0:T(8,128)(2,1)}, bf16[4096,256]{1,0:T(8,128)(2,1)S(1)}, u32[]{:S(2)}) %copy-start.2) | copy-done | bytes 2097176
  95.6 3.6 %add.5 = f32[4096,256]{1,0:T(8,128)} custom-call(bf16[4096,256]{1,0:T(8,128)(2,1)} %copy-done.2, bf16[4096,256]{1,0:T(8,128)(2,1)} %backward.1.refs_1_), custom_call_target="tpu_custom_call" | custom-call | bytes 8388608 | tf_op jit(solution)/shard_map/add/pallas_call | solution.py:469
Async XLA Ops:
  32.9 25.7 %all-to-all-start = ((bf16[16,32,640]{2,1,0:T(8,128)(2,1)}), bf16[16,32,640]{2,1,0:T(8,128)(2,1)S(1)}, u32[]{:S(2)}, u32[]{:S(2)}) async-start(bf16[16,32,640]{2,1,0:T(8,128)(2,1)} %get-tuple-element.12), calls=%async_computation | async-start | bytes 1310720 | tf_op jit(solution)/shard_map/all_to_all | solution.py:401
  58.7 0.9 copy-start
  71.4 22.9 %collective-permute-start = (bf16[4096,256]{1,0:T(8,128)(2,1)}, bf16[4096,256]{1,0:T(8,128)(2,1)S(1)}, u32[]{:S(2)}, u32[]{:S(2)}) collective-permute-start(bf16[4096,256]{1,0:T(8,128)(2,1)} %get-tuple-element.18), channel_id=1, source_target_pairs={{0,16},{16,0},{1,17},{17,1},{2,18},{18,2},{3,19},{19,3},{4,20},{20... | collective-permute-start | bytes 6291464 | tf_op jit(solution)/shard_map/ppermute | solution.py:359
  71.5 19.9 %all-to-all-start.1 = ((bf16[16,32,512]{2,1,0:T(8,128)(2,1)}), bf16[16,32,512]{2,1,0:T(8,128)(2,1)S(1)}, u32[]{:S(2)}, u32[]{:S(2)}) async-start(bf16[16,32,512]{2,1,0:T(8,128)(2,1)} %merge.1), calls=%async_computation.1 | async-start | bytes 1048576 | tf_op jit(solution)/shard_map/all_to_all | solution.py:412
  91.4 0.8 copy-start.1
  94.2 1.3 %copy-start.2 = (bf16[4096,256]{1,0:T(8,128)(2,1)}, bf16[4096,256]{1,0:T(8,128)(2,1)S(1)}, u32[]{:S(2)}) copy-start(bf16[4096,256]{1,0:T(8,128)(2,1)S(1)} %collective-permute-done.refs_0_) | copy-start | bytes 6291460

commit v7 on v6

--- a/solution.py
+++ b/solution.py
@@ -15,12 +15,15 @@
 MIB = 1 << 20
 CHUNK = 256
 AHEAD = 3
+PARTS = 4
 ROWS = 64
 LARGEST = 2.0**60
 VMEM = pl.BlockSpec(memory_space=pltpu.VMEM)
 SMEM = pl.BlockSpec(memory_space=pltpu.SMEM)
 ANY = pl.BlockSpec(memory_space=pl.ANY)
 FULL = pltpu.CompilerParams(vmem_limit_bytes=60 * MIB)
+MOST = pltpu.CompilerParams(vmem_limit_bytes=56 * MIB)
+SOME = pltpu.CompilerParams(vmem_limit_bytes=24 * MIB)
 
 
 def dot(left, right, left_dim=1, right_dim=0):
@@ -60,8 +63,13 @@
         )
 
     def start(t):
-        for copy in fetch(t):
-            copy.start()
+        fetch(t)[0].start()
+        at = pl.ds(pl.multiple_of(t * width, width), width)
+        for r in range(0, n_tokens, n_tokens // PARTS):
+            part = pl.ds(r, n_tokens // PARTS)
+            pltpu.make_async_copy(
+                noise.at[part, at], noise_in.at[t, part], noise_sem.at[t]
+            ).start()
 
     def arrive(t):
         for copy in fetch(t):
@@ -405,7 +413,7 @@
         out_shape=jax.ShapeDtypeStruct((n_code, rows, 2 * dim), BF16),
         in_specs=[SMEM, VMEM],
         out_specs=VMEM,
-        compiler_params=FULL,
+        compiler_params=SOME,
         name="merge",
     )(code_at[None], received)
     received, spread = lax.optimization_barrier((received, spread))
@@ -415,8 +423,10 @@
         out_shape=(jax.ShapeDtypeStruct((n_tokens, dim), F32),) * 2,
         in_specs=[VMEM],
         out_specs=(VMEM, VMEM),
-        compiler_params=FULL,
-        cost_estimate=pl.CostEstimate(flops=0, bytes_accessed=64 * MIB, transcendentals=0),
+        compiler_params=SOME,
+        cost_estimate=pl.CostEstimate(
+            flops=100 * products, bytes_accessed=400 * MIB, transcendentals=0
+        ),
         name="unpack",
     )(gathered)
 
@@ -431,7 +441,7 @@
     ]
     block_shape = jax.ShapeDtypeStruct((block, dim), BF16)
     common = dict(
-        compiler_params=FULL,
+        compiler_params=MOST,
         cost_estimate=pl.CostEstimate(flops=1, bytes_accessed=1, transcendentals=0),
     )
     dp_at = lax.axis_index("dp")
@@ -477,7 +487,7 @@
             pltpu.SemaphoreType.DMA((n_dp, steps)),
             pltpu.SemaphoreType.DMA((steps,)),
         ],
-        compiler_params=FULL,
+        compiler_params=SOME,
         cost_estimate=pl.CostEstimate(
             flops=0, bytes_accessed=(2 * n_dp + 4) * block * dim, transcendentals=0
         ),

time: 99.8 us -> 89.4 us (0.90)
  waiting for transfers between devices: 23.4 us -> 17.4 us
  Pallas kernels: 58 us -> 55.7 us
  local copies, waits for them, and re-layouts: 3.01 us -> 0.93 us
    all_to_all x1, waiting for transfers between devices: 6.56 us -> 0.01 us  [local(): gathered = lax.all_to_all(spread, 'code', 0, 0, tiled=True)]
    unnamed x6 -> x4, local copies, waits for them, and re-layouts: 3.01 us -> 0.93 us
    pallas_call x1, Pallas kernels: 2.45 us -> 1.36 us  [local(): pl.pallas_call(merge_kernel, out_shape=jax.ShapeDtypeStruct((n_code, rows...]
    pallas_call x1, Pallas kernels: 2.07 us -> 1.03 us  [local(): pl.pallas_call(unpack_kernel, out_shape=(jax.ShapeDtypeStruct((n_tokens,...]
  transfers between devices with their start and end apart: 3 -> 3, of which waited for: 2 -> 1; matrix products, arithmetic and copies ran while one was open for 1% -> 1% of each run, Pallas kernels for 10% -> 21%
where the time goes in v7:
time: 89.4 us; the launch traced here: 88.9 us
  Pallas kernels  55.7 us (62%)
  waiting for transfers between devices  17.4 us (19%)
  starting transfers between devices  12.8 us (14%)
  other arithmetic  1.24 us (1%)
  local copies, waits for them, and re-layouts  0.93 us (1%)
    pallas_call x1, Pallas kernels, local(): pl.pallas_call(functools.partial(forward_kernel, n_code), out_shape=(pltp...  32.4 us
    all_to_all x1, waiting for transfers between devices, local(): received = lax.all_to_all(sent, 'code', 0, 0, tiled=True)  17.4 us
    pallas_call x1, Pallas kernels, local(): pl.pallas_call(functools.partial(backward_kernel, False), out_shape=(bloc...  9.38 us
    all_to_all x1, starting transfers between devices, local(): received = lax.all_to_all(sent, 'code', 0, 0, tiled=True)  8.33 us
    pallas_call x1, Pallas kernels, backward(): pl.pallas_call(functools.partial(backward_kernel, True), out_shape=block_...  8.24 us
    all_to_all x1, starting transfers between devices, local(): gathered = lax.all_to_all(spread, 'code', 0, 0, tiled=True)  4.43 us
    pallas_call x1, Pallas kernels, local(): pl.pallas_call(functools.partial(add_kernel, n_dp), out_shape=jax.ShapeDt...  3.21 us
  transfers between devices with their start and end apart: 3, of which 1 were waited for; matrix products, arithmetic and copies ran while one was open for 1% of the time, Pallas kernels for 21%

profile of v7, /device:TPU:0, one launch (start us, length us, event | category | flops | bytes accessed | tf_op | source)
XLA Modules:
  0.0 88.9 jit_solution(14662281308312899552)
XLA Ops:
  0.6 32.4 %forward.1 = (bf16[8,512,1024]{2,1,0:T(8,128)(2,1)}, bf16[16,32,640]{2,1,0:T(8,128)(2,1)}) custom-call(bf16[512,256]{1,0:T(8,128)(2,1)} %rest_0_.2, bf16[512,256]{1,0:T(8,128)(2,1)} %rest_0_.3, bf16[8192,256]{1,0:T(8,128)(2,1)} %rest_1_.3, bf16[512,8192]{1,0:T(8,128)(2,1)} %noise.1), custom_call_target="tpu_custom_call" | custom-call | flops 8589934592 | bytes 25165824 | tf_op jit(solution)/shard_map/forward/pallas_call | solution.py:380
  33.1 8.3 %all-to-all-start = ((bf16[16,32,640]{2,1,0:T(8,128)(2,1)}), bf16[16,32,640]{2,1,0:T(8,128)(2,1)S(1)}, u32[]{:S(2)}, u32[]{:S(2)}) async-start(bf16[16,32,640]{2,1,0:T(8,128)(2,1)} %get-tuple-element.12), calls=%async_computation | async-start | bytes 1310720 | tf_op jit(solution)/shard_map/all_to_all | solution.py:409
  41.4 17.4 %all-to-all-done.received.rest_4_ = bf16[16,32,640]{2,1,0:T(8,128)(2,1)S(1)} async-done(((bf16[16,32,640]{2,1,0:T(8,128)(2,1)}), bf16[16,32,640]{2,1,0:T(8,128)(2,1)S(1)}, u32[]{:S(2)}, u32[]{:S(2)}) %all-to-all-start) | async-done | bytes 655392 | tf_op jit(solution)/shard_map/all_to_all | solution.py:409
  58.8 0.0 copy-start.1
  58.8 1.4 %merge.1 = bf16[16,32,512]{2,1,0:T(8,128)(2,1)} custom-call(s32[1]{0:T(128)} %bitcast.me, bf16[16,32,640]{2,1,0:T(8,128)(2,1)S(1)} %all-to-all-done.received.rest_4_), custom_call_target="tpu_custom_call" | custom-call | tf_op jit(solution)/shard_map/merge/pallas_call | solution.py:411
  60.2 4.4 %all-to-all-start.1 = ((bf16[16,32,512]{2,1,0:T(8,128)(2,1)}), bf16[16,32,512]{2,1,0:T(8,128)(2,1)S(1)}, u32[]{:S(2)}, u32[]{:S(2)}) async-start(bf16[16,32,512]{2,1,0:T(8,128)(2,1)} %merge.1), calls=%async_computation.1 | async-start | bytes 1048576 | tf_op jit(solution)/shard_map/all_to_all | solution.py:420
  64.6 0.7 pad_add_fusion.where
  65.3 0.6 pad_add_fusion.1.where
  65.9 0.0 copy-done.1
  65.9 9.4 %backward_first.1 = (bf16[4096,256]{1,0:T(8,128)(2,1)}, bf16[2,256,512]{2,1,0:T(8,128)(2,1)}, f32[512,128]{1,0:T(8,128)}) custom-call(s32[2]{0:T(128)} %pad_add_fusion.where, bf16[512,256]{1,0:T(8,128)(2,1)} %rest_0_.2, bf16[512,256]{1,0:T(8,128)(2,1)} %rest_0_.3, bf16[8192,256]{1,0:T(8,128)(2,1)} %rest_1_.3, ...), custom_call_target="tpu_custom_call" | custom-call | flops 1 | bytes 1 | tf_op jit(solution)/shard_map/backward_first/pallas_call | solution.py:448
  75.3 0.1 collective-permute-start
  75.3 8.2 %backward.1.refs_1_ = bf16[4096,256]{1,0:T(8,128)(2,1)} custom-call(s32[2]{0:T(128)} %pad_add_fusion.1.where, bf16[512,256]{1,0:T(8,128)(2,1)} %rest_0_.3, bf16[8192,256]{1,0:T(8,128)(2,1)} %rest_1_.3, bf16[8,512,1024]{2,1,0:T(8,128)(2,1)} %get-tuple-element.16.rest_3_.rest_2_, bf16[2,256,512]{2,1,0:T(8,128)(2,1)} %get-tuple-element.19.rest_3_, ...), custom_call_target="tpu_custom_call" | custom-call | flops 1 | bytes 1 | tf_op jit(solution)/shard_map/backward/pallas_call | solution.py:465
  83.6 0.0 all-to-all-done.1.gathered
  83.6 0.0 copy-start
  83.6 1.0 %unpack.1 = (f32[512,256]{1,0:T(8,128)}, f32[512,256]{1,0:T(8,128)}) custom-call(bf16[16,32,512]{2,1,0:T(8,128)(2,1)S(1)} %all-to-all-done.1.gathered), custom_call_target="tpu_custom_call" | custom-call | flops 214748364800 | bytes 419430400 | tf_op jit(solution)/shard_map/unpack/pallas_call | solution.py:421
  84.6 0.0 collective-permute-done.refs_0_
  84.6 0.9 %copy-done = bf16[4096,256]{1,0:T(8,128)(2,1)S(1)} copy-done((bf16[4096,256]{1,0:T(8,128)(2,1)S(1)}, bf16[4096,256]{1,0:T(8,128)(2,1)}, u32[]{:S(2)}) %copy-start) | copy-done | bytes 2097176
  85.6 3.2 %add.5 = f32[4096,256]{1,0:T(8,128)} custom-call(bf16[4096,256]{1,0:T(8,128)(2,1)} %collective-permute-done.refs_0_, bf16[4096,256]{1,0:T(8,128)(2,1)S(1)} %copy-done), custom_call_target="tpu_custom_call" | custom-call | bytes 8388608 | tf_op jit(solution)/shard_map/add/pallas_call | solution.py:479
Async XLA Ops:
  33.1 25.8 %all-to-all-start = ((bf16[16,32,640]{2,1,0:T(8,128)(2,1)}), bf16[16,32,640]{2,1,0:T(8,128)(2,1)S(1)}, u32[]{:S(2)}, u32[]{:S(2)}) async-start(bf16[16,32,640]{2,1,0:T(8,128)(2,1)} %get-tuple-element.12), calls=%async_computation | async-start | bytes 1310720 | tf_op jit(solution)/shard_map/all_to_all | solution.py:409
  58.8 7.1 %copy-start.1 = (bf16[16,32,640]{2,1,0:T(8,128)(2,1)}, bf16[16,32,640]{2,1,0:T(8,128)(2,1)S(1)}, u32[]{:S(2)}) copy-start(bf16[16,32,640]{2,1,0:T(8,128)(2,1)S(1)} %all-to-all-done.received.rest_4_) | copy-start | bytes 1966084
  60.2 23.4 %all-to-all-start.1 = ((bf16[16,32,512]{2,1,0:T(8,128)(2,1)}), bf16[16,32,512]{2,1,0:T(8,128)(2,1)S(1)}, u32[]{:S(2)}, u32[]{:S(2)}) async-start(bf16[16,32,512]{2,1,0:T(8,128)(2,1)} %merge.1), calls=%async_computation.1 | async-start | bytes 1048576 | tf_op jit(solution)/shard_map/all_to_all | solution.py:420
  75.3 9.4 %collective-permute-start = (bf16[4096,256]{1,0:T(8,128)(2,1)}, bf16[4096,256]{1,0:T(8,128)(2,1)}, u32[]{:S(2)}, u32[]{:S(2)}) collective-permute-start(bf16[4096,256]{1,0:T(8,128)(2,1)} %get-tuple-element.18), channel_id=1, source_target_pairs={{0,16},{16,0},{1,17},{17,1},{2,18},{18,2},{3,19},{19,3},{4,20},{20... | collective-permute-start | bytes 6291464 | tf_op jit(solution)/shard_map/ppermute | solution.py:367
  83.6 2.0 %copy-start = (bf16[4096,256]{1,0:T(8,128)(2,1)S(1)}, bf16[4096,256]{1,0:T(8,128)(2,1)}, u32[]{:S(2)}) copy-start(bf16[4096,256]{1,0:T(8,128)(2,1)} %backward.1.refs_1_) | copy-start | bytes 6291460

commit v8 on v7

--- a/solution.py
+++ b/solution.py
@@ -1,5 +1,4 @@
 import functools
-import math
 
 import jax
 import jax.numpy as jnp
@@ -9,11 +8,12 @@
 from jax.sharding import PartitionSpec as P
 
 SOFTMAX_HEAT = 0.5
-TO_LOG2 = math.log2(math.e) / SOFTMAX_HEAT
+SHARPNESS = 1.0 / SOFTMAX_HEAT
 BF16 = jnp.bfloat16
 F32 = jnp.float32
 MIB = 1 << 20
 CHUNK = 256
+HIGH = 512
 AHEAD = 3
 PARTS = 4
 ROWS = 64
@@ -91,14 +91,17 @@
     for t in range(1, min(AHEAD + 1, tiles)):
         start(t)
 
+    def logits(both, t, r, c):
+        noise_part = (noise_in[t, r : r + ROWS, c] * BF16(SHARPNESS)).astype(F32)
+        return both[2 * r : 2 * r + ROWS] + noise_part
+
     def raise_shift(t, some):
         for c in some:
             both = dot(pair[...], book[t, c], 1, 1)
             for r in range(0, n_tokens, ROWS):
                 at = slice(r, r + ROWS)
-                score = both[2 * r : 2 * r + ROWS] + noise_in[t, at, c].astype(F32)
                 shifts[at] = functools.reduce(
-                    jnp.maximum, lane_groups(score * TO_LOG2), shifts[at]
+                    jnp.maximum, lane_groups(logits(both, t, r, c)), shifts[at]
                 )
 
     def store(t, s):
@@ -106,7 +109,7 @@
             slots[s].at[pl.ds(0, n_tokens)], codes.at[t], code_sem.at[s]
         )
 
-    def soften(t, s, fresh):
+    def soften(t, s, fresh, last=None):
         if fresh is not None:
             @pl.when(fresh)
             def _():
@@ -117,13 +120,17 @@
                     start(t + AHEAD)
 
         slot = slots[s]
-        for c in columns:
-            both = dot(pair[...], book[t, c], 1, 1)
+        ahead = dot(pair[...], book[t, columns[0]], 1, 1)
+        for k, c in enumerate(columns):
+            both = ahead
+            if k + 1 < len(columns):
+                ahead = dot(pair[...], book[t, columns[k + 1]], 1, 1)
+            elif last is not None:
+                last()
             for r in range(0, n_tokens, ROWS):
                 at = slice(r, r + ROWS)
-                score = both[2 * r : 2 * r + ROWS] + noise_in[t, at, c].astype(F32)
                 shift = jnp.concatenate([shifts[at]] * (CHUNK // 128), axis=1)
-                weight = jnp.exp2(score * TO_LOG2 - shift)
+                weight = jnp.exp(logits(both, t, r, c) - shift)
                 total[at] += sum(lane_groups(weight))
                 slot[at, c] = weight.astype(BF16)
                 gradient = both[2 * r + ROWS : 2 * r + 2 * ROWS]
@@ -161,18 +168,15 @@
             def _():
                 store(2 * i - 1, 1).wait()
 
-            soften(2 * i + 1, 1, fresh)
-            accumulate(2 * i, 0)
+            soften(2 * i + 1, 1, fresh, lambda: accumulate(2 * i, 0))
             store(2 * i, 0).wait()
-            soften(2 * i + 2, 0, fresh)
-            accumulate(2 * i + 1, 1)
+            soften(2 * i + 2, 0, fresh, lambda: accumulate(2 * i + 1, 1))
             return carry
 
         lax.fori_loop(0, tiles // 2 - 1, soften_pair, 0)
         if tiles > 2:
             store(tiles - 3, 1).wait()
-        soften(tiles - 1, 1, fresh)
-        accumulate(tiles - 2, 0)
+        soften(tiles - 1, 1, fresh, lambda: accumulate(tiles - 2, 0))
         accumulate(tiles - 1, 1)
         store(tiles - 2, 0).wait()
         store(tiles - 1, 1).wait()
@@ -181,6 +185,8 @@
 
     for copy in pair_copies:
         copy.wait()
+    for r in range(0, n_tokens, ROWS):
+        pair[2 * r : 2 * r + ROWS] = pair[2 * r : 2 * r + ROWS] * BF16(SHARPNESS)
     arrive(0)
     lax.while_loop(lambda state: state[1], attempt, (jnp.int32(0), jnp.bool_(True)))
 
@@ -221,7 +227,7 @@
     lanes = stat_lanes(n_code)
     stats = [received[p, :, received.shape[2] - lanes :].astype(F32) for p in range(n_code)]
     top = functools.reduce(jnp.maximum, stats)
-    scales = [roll_left(jnp.exp2(s - top), lanes // 2) for s in stats]
+    scales = [roll_left(jnp.exp(s - top), lanes // 2) for s in stats]
     pairs = [s + roll_left(s, 1) for s in stats]
     inners = [roll_left(s, 2) for s in pairs]
     total = sum(a * s for a, s in zip(scales, pairs))
@@ -255,21 +261,47 @@
         spread[p, :, dim:] = gradient
 
 
-def backward_kernel(prepared, where, *rest):
+def turn_kernel(grad_out, codes, turned, turned_grad, held, result, in_sem, out_sem):
+    tiles, _, width = held.shape
+
+    def fetch(t):
+        return pltpu.make_async_copy(codes.at[t], held.at[t], in_sem.at[t])
+
+    def send(t):
+        at = pl.ds(pl.multiple_of(t * width, width), width)
+        return pltpu.make_async_copy(result.at[t], turned.at[at], out_sem.at[t])
+
+    for t in range(tiles):
+        fetch(t).start()
+    turned_grad[...] = grad_out[...].T
+
+    def turn(t, carry):
+        fetch(t).wait()
+        for c in range(0, width, CHUNK):
+            result[t, c : c + CHUNK] = held[t, :, c : c + CHUNK].T
+        send(t).start()
+        return carry
+
+    lax.fori_loop(0, tiles, turn, 0)
+    for t in range(tiles):
+        send(t).wait()
+
+
+def backward_kernel(prepared, block, *rest):
     if prepared:
-        grad_out, codebook, codes, operands, inners, out, *rest = rest
+        turned_grad, codebook, turned, operands, inners, out, *rest = rest
     else:
-        tokens, grad_out, codebook, codes, received, out, operands, inners, upper, lower, *rest = rest
+        code_at, tokens, grad_out, turned_grad, codebook, turned, received, *rest = rest
+        out, operands, inners, spread_inner, *rest = rest
     book, code_in, result, book_sem, code_sem, out_sem = rest
     tiles, width, dim = book.shape
-    n_tokens = grad_out.shape[0]
-    first = where[1] * tiles
+    n_tokens = turned_grad.shape[1]
 
     def fetch(t):
-        at = pl.multiple_of((first + t) * width, width)
+        at = pl.ds(pl.multiple_of((block[0] * tiles + t) * width, width), width)
         return (
-            pltpu.make_async_copy(codebook.at[pl.ds(at, width)], book.at[t], book_sem.at[t]),
-            pltpu.make_async_copy(codes.at[first + t], code_in.at[t], code_sem.at[t]),
+            pltpu.make_async_copy(codebook.at[at], book.at[t], book_sem.at[t]),
+            pltpu.make_async_copy(turned.at[at], code_in.at[t], code_sem.at[t]),
         )
 
     def start(t):
@@ -284,23 +316,22 @@
         scales, _, inner = merged_stats(received)
         scale = jnp.zeros(inner.shape, F32)
         for p in range(n_code):
-            scale = jnp.where(where[0] == p, scales[p], scale)
+            scale = jnp.where(code_at[0] == p, scales[p], scale)
         for g in range(n_code):
             part = slice(g * rows, (g + 1) * rows)
             column = scale[:, 4 * g : 4 * g + 1]
-            upper[part] = column * grad_out[part].astype(F32)
-            lower[part] = column * (tokens[part].astype(F32) / SOFTMAX_HEAT)
-            inners[part] = jnp.broadcast_to(inner[:, 4 * g : 4 * g + 1], (rows, 128))
-        operands[0] = upper[...].T.astype(BF16)
-        operands[1] = lower[...].T.astype(BF16)
+            operands[0, part] = (column * grad_out[part].astype(F32)).astype(BF16)
+            operands[1, part] = (column * (tokens[part].astype(F32) / SOFTMAX_HEAT)).astype(BF16)
+            spread_inner[part] = jnp.broadcast_to(inner[:, 4 * g : 4 * g + 1], (rows, 128))
+        inners[...] = spread_inner[...].T[:8]
 
     def send(t):
         return pltpu.make_async_copy(
             result.at[t], out.at[pl.ds(pl.multiple_of(t * width, width), width)], out_sem.at[t]
         )
 
-    chunk = min(CHUNK, width)
-    steps = [(t, slice(c, c + chunk)) for t in range(tiles) for c in range(0, width, chunk)]
+    high = min(HIGH, width)
+    steps = [(t, slice(c, c + high)) for t in range(tiles) for c in range(0, width, high)]
 
     def gradient_of(step):
         t, c = step
@@ -309,18 +340,17 @@
                 copy.wait()
             if t + AHEAD < tiles:
                 start(t + AHEAD)
-        return dot(grad_out[...], book[t, c], 1, 1)
+        return dot(book[t, c], turned_grad[...])
 
     ahead = gradient_of(steps[0])
     for k, (t, c) in enumerate(steps):
         gradient = ahead
         if k + 1 < len(steps):
             ahead = gradient_of(steps[k + 1])
-        code = code_in[t, :, c]
-        inner = jnp.concatenate([inners[...]] * (chunk // 128), axis=1)
-        score_gradient = (code.astype(F32) * (gradient - inner)).astype(BF16)
-        value = dot(operands[0], code) + dot(operands[1], score_gradient)
-        result[t, c] = value.astype(BF16).T
+        code = code_in[t, c]
+        score_gradient = (code.astype(F32) * (gradient - inners[:1])).astype(BF16)
+        value = dot(code, operands[0]) + dot(score_gradient, operands[1])
+        result[t, c] = value.astype(BF16)
         if c.stop == width:
             send(t).start()
     for t in range(tiles):
@@ -407,6 +437,27 @@
     )(tokens, grad_out, codebook, noise)
 
     received = lax.all_to_all(sent, "code", 0, 0, tiled=True)
+    turned, turned_grad = pl.pallas_call(
+        turn_kernel,
+        out_shape=(
+            pltpu.HBM((n_codes, n_tokens), BF16),
+            jax.ShapeDtypeStruct((dim, n_tokens), BF16),
+        ),
+        in_specs=[VMEM, ANY],
+        out_specs=(ANY, VMEM),
+        scratch_shapes=[
+            pltpu.VMEM((tiles, n_tokens, width), BF16),
+            pltpu.VMEM((tiles, width, n_tokens), BF16),
+            pltpu.SemaphoreType.DMA((tiles,)),
+            pltpu.SemaphoreType.DMA((tiles,)),
+        ],
+        compiler_params=FULL,
+        cost_estimate=pl.CostEstimate(
+            flops=0, bytes_accessed=4 * n_tokens * n_codes, transcendentals=0
+        ),
+        name="turn",
+    )(grad_out, codes)
+    received, turned, turned_grad = lax.optimization_barrier((received, turned, turned_grad))
     code_at = lax.axis_index("code")
     spread = pl.pallas_call(
         merge_kernel,
@@ -433,7 +484,7 @@
     block_tiles = block // width
     streams = [
         pltpu.VMEM((block_tiles, width, dim), BF16),
-        pltpu.VMEM((block_tiles, n_tokens, width), BF16),
+        pltpu.VMEM((block_tiles, width, n_tokens), BF16),
         pltpu.VMEM((block_tiles, width, dim), BF16),
         pltpu.SemaphoreType.DMA((block_tiles,)),
         pltpu.SemaphoreType.DMA((block_tiles,)),
@@ -449,17 +500,18 @@
         functools.partial(backward_kernel, False),
         out_shape=(
             block_shape,
-            jax.ShapeDtypeStruct((2, dim, n_tokens), BF16),
-            jax.ShapeDtypeStruct((n_tokens, 128), F32),
-        ),
-        in_specs=[SMEM, VMEM, VMEM, ANY, ANY, VMEM],
+            jax.ShapeDtypeStruct((2, n_tokens, dim), BF16),
+            jax.ShapeDtypeStruct((8, n_tokens), F32),
+        ),
+        in_specs=[SMEM, SMEM, VMEM, VMEM, VMEM, ANY, ANY, VMEM],
         out_specs=(ANY, VMEM, VMEM),
-        scratch_shapes=[
-            pltpu.VMEM((n_tokens, dim), F32), pltpu.VMEM((n_tokens, dim), F32),
-        ] + streams,
+        scratch_shapes=[pltpu.VMEM((n_tokens, 128), F32)] + streams,
         name="backward_first",
         **common,
-    )(jnp.stack([code_at, dp_at ^ (n_dp - 1)]), tokens, grad_out, codebook, codes, received)
+    )(
+        (dp_at ^ (n_dp - 1))[None], code_at[None], tokens, grad_out, turned_grad, codebook,
+        turned, received,
+    )
 
     def backward(at):
         return pl.pallas_call(
@@ -470,7 +522,7 @@
             scratch_shapes=streams,
             name="backward",
             **common,
-        )(jnp.stack([code_at, at]), grad_out, codebook, codes, operands, inners)
+        )(at[None], turned_grad, codebook, turned, operands, inners)
 
     blocks = [swap(first, "dp", n_dp, n_dp - 1)]
     blocks += [swap(backward(dp_at ^ d), "dp", n_dp, d) for d in range(1, n_dp - 1)]

time: 89.4 us -> 87.7 us (0.981)
  waiting for transfers between devices: 17.4 us -> 8.64 us
  Pallas kernels: 55.7 us -> 63.9 us
  other arithmetic: 1.24 us -> 0 us
    pallas_call x0 -> x1, Pallas kernels: none -> 8.79 us  [local(): pl.pallas_call(turn_kernel, out_shape=(pltpu.HBM((n_codes, n_tokens), BF1...]
    all_to_all x1, waiting for transfers between devices: 17.4 us -> 8.63 us  [local(): received = lax.all_to_all(sent, 'code', 0, 0, tiled=True)]
    another operation x2 -> x0, other arithmetic: 1.24 us -> none  [the longest x1 0.66 us: local(): jnp.stack([code_at, dp_at ^ n_dp - 1])]
  transfers between devices with their start and end apart: 3 -> 3, of which waited for: 1 -> 1; matrix products, arithmetic and copies ran while one was open for 1% -> 0% of each run, Pallas kernels for 21% -> 31%
where the time goes in v8:
time: 87.7 us; the launch traced here: 87.1 us
  Pallas kernels  63.9 us (73%)
  starting transfers between devices  12.8 us (15%)
  waiting for transfers between devices  8.64 us (10%)
  local copies, waits for them, and re-layouts  0.93 us (1%)
  between operations  0.88 us (1%)
    pallas_call x1, Pallas kernels, local(): pl.pallas_call(functools.partial(forward_kernel, n_code), out_shape=(pltp...  32.4 us
    pallas_call x1, Pallas kernels, local(): pl.pallas_call(functools.partial(backward_kernel, False), out_shape=(bloc...  9.15 us
    pallas_call x1, Pallas kernels, local(): pl.pallas_call(turn_kernel, out_shape=(pltpu.HBM((n_codes, n_tokens), BF1...  8.79 us
    all_to_all x1, waiting for transfers between devices, local(): received = lax.all_to_all(sent, 'code', 0, 0, tiled=True)  8.63 us
    all_to_all x1, starting transfers between devices, local(): received = lax.all_to_all(sent, 'code', 0, 0, tiled=True)  8.32 us
    pallas_call x1, Pallas kernels, backward(): pl.pallas_call(functools.partial(backward_kernel, True), out_shape=block_...  7.93 us
    all_to_all x1, starting transfers between devices, local(): gathered = lax.all_to_all(spread, 'code', 0, 0, tiled=True)  4.43 us
    pallas_call x1, Pallas kernels, local(): pl.pallas_call(functools.partial(add_kernel, n_dp), out_shape=jax.ShapeDt...  3.21 us
  transfers between devices with their start and end apart: 3, of which 1 were waited for; matrix products, arithmetic and copies ran while one was open for 0% of the time, Pallas kernels for 31%

profile of v8, /device:TPU:0, one launch (start us, length us, event | category | flops | bytes accessed | tf_op | source)
XLA Modules:
  0.0 87.1 jit_solution(14436019444874597778)
XLA Ops:
  0.6 32.4 %forward.1 = (bf16[8,512,1024]{2,1,0:T(8,128)(2,1)}, bf16[16,32,640]{2,1,0:T(8,128)(2,1)}) custom-call(bf16[512,256]{1,0:T(8,128)(2,1)} %rest_1_.2, bf16[512,256]{1,0:T(8,128)(2,1)} %rest_2_.1, bf16[8192,256]{1,0:T(8,128)(2,1)} %rest_1_.3, bf16[512,8192]{1,0:T(8,128)(2,1)} %noise.1), custom_call_target="tpu_custom_call" | custom-call | flops 8589934592 | bytes 25165824 | tf_op jit(solution)/shard_map/forward/pallas_call | solution.py:410
  33.0 8.3 %all-to-all-start = ((bf16[16,32,640]{2,1,0:T(8,128)(2,1)}), bf16[16,32,640]{2,1,0:T(8,128)(2,1)S(1)}, u32[]{:S(2)}, u32[]{:S(2)}) async-start(bf16[16,32,640]{2,1,0:T(8,128)(2,1)} %get-tuple-element.17), calls=%async_computation | async-start | bytes 1310720 | tf_op jit(solution)/shard_map/all_to_all | solution.py:439
  41.4 8.8 %turn.1 = (bf16[8192,512]{1,0:T(8,128)(2,1)}, bf16[256,512]{1,0:T(8,128)(2,1)}) custom-call(bf16[512,256]{1,0:T(8,128)(2,1)} %rest_2_.1, bf16[8,512,1024]{2,1,0:T(8,128)(2,1)} %get-tuple-element.18.codes), custom_call_target="tpu_custom_call" | custom-call | bytes 16777216 | tf_op jit(solution)/shard_map/turn/pallas_call | solution.py:440
  50.2 8.6 %all-to-all-done.received.rest_6_ = bf16[16,32,640]{2,1,0:T(8,128)(2,1)S(1)} async-done(((bf16[16,32,640]{2,1,0:T(8,128)(2,1)}), bf16[16,32,640]{2,1,0:T(8,128)(2,1)S(1)}, u32[]{:S(2)}, u32[]{:S(2)}) %all-to-all-start) | async-done | bytes 655392 | tf_op jit(solution)/shard_map/all_to_all | solution.py:439
  58.8 0.0 copy-start.1
  58.8 1.4 %merge.1 = bf16[16,32,512]{2,1,0:T(8,128)(2,1)} custom-call(s32[1]{0:T(128)} %bitcast.me.rest_0_, bf16[16,32,640]{2,1,0:T(8,128)(2,1)S(1)} %all-to-all-done.received.rest_6_), custom_call_target="tpu_custom_call" | custom-call | tf_op jit(solution)/shard_map/merge/pallas_call | solution.py:462
  60.2 4.4 %all-to-all-start.1 = ((bf16[16,32,512]{2,1,0:T(8,128)(2,1)}), bf16[16,32,512]{2,1,0:T(8,128)(2,1)S(1)}, u32[]{:S(2)}, u32[]{:S(2)}) async-start(bf16[16,32,512]{2,1,0:T(8,128)(2,1)} %merge.1), calls=%async_computation.1 | async-start | bytes 1048576 | tf_op jit(solution)/shard_map/all_to_all | solution.py:471
  64.6 0.0 copy-done.1
  64.6 9.1 %backward_first.1 = (bf16[4096,256]{1,0:T(8,128)(2,1)}, bf16[2,512,256]{2,1,0:T(8,128)(2,1)}, f32[8,512]{1,0:T(8,128)}) custom-call(s32[1]{0:T(128)} %bitcast.1.block, s32[1]{0:T(128)} %bitcast.me.rest_0_, bf16[512,256]{1,0:T(8,128)(2,1)} %rest_1_.2, bf16[512,256]{1,0:T(8,128)(2,1)} %rest_2_.1, bf16[256,512]{1,0:T(8,128)(2,1)} %get-tuple-element.25.rest_3_.rest_0_, ...), custom_call_target="tpu_custom_call" | custom-call | flops 1 | bytes 1 | tf_op jit(solution)/shard_map/backward_first/pallas_call | solution.py:499
  73.8 0.1 collective-permute-start
  73.9 7.9 %backward.1.refs_1_ = bf16[4096,256]{1,0:T(8,128)(2,1)} custom-call(s32[1]{0:T(128)} %bitcast.2.block, bf16[256,512]{1,0:T(8,128)(2,1)} %get-tuple-element.25.rest_3_.rest_0_, bf16[8192,256]{1,0:T(8,128)(2,1)} %rest_1_.3, bf16[8192,512]{1,0:T(8,128)(2,1)} %get-tuple-element.26.rest_5_.rest_2_, bf16[2,512,256]{2,1,0:T(8,128)(2,1)} %get-tuple-element.29.rest_3_, ...), custom_call_target="tpu_custom_call" | custom-call | flops 1 | bytes 1 | tf_op jit(solution)/shard_map/backward/pallas_call | solution.py:517
  81.8 0.0 all-to-all-done.1.gathered
  81.8 0.0 copy-start
  81.8 1.0 %unpack.1 = (f32[512,256]{1,0:T(8,128)}, f32[512,256]{1,0:T(8,128)}) custom-call(bf16[16,32,512]{2,1,0:T(8,128)(2,1)S(1)} %all-to-all-done.1.gathered), custom_call_target="tpu_custom_call" | custom-call | flops 214748364800 | bytes 419430400 | tf_op jit(solution)/shard_map/unpack/pallas_call | solution.py:472
  82.8 0.0 collective-permute-done.refs_0_
  82.8 0.9 %copy-done = bf16[4096,256]{1,0:T(8,128)(2,1)S(1)} copy-done((bf16[4096,256]{1,0:T(8,128)(2,1)S(1)}, bf16[4096,256]{1,0:T(8,128)(2,1)}, u32[]{:S(2)}) %copy-start) | copy-done | bytes 2097176
  83.8 3.2 %add.1 = f32[4096,256]{1,0:T(8,128)} custom-call(bf16[4096,256]{1,0:T(8,128)(2,1)} %collective-permute-done.refs_0_, bf16[4096,256]{1,0:T(8,128)(2,1)S(1)} %copy-done), custom_call_target="tpu_custom_call" | custom-call | bytes 8388608 | tf_op jit(solution)/shard_map/add/pallas_call | solution.py:531
Async XLA Ops:
  33.0 25.8 %all-to-all-start = ((bf16[16,32,640]{2,1,0:T(8,128)(2,1)}), bf16[16,32,640]{2,1,0:T(8,128)(2,1)S(1)}, u32[]{:S(2)}, u32[]{:S(2)}) async-start(bf16[16,32,640]{2,1,0:T(8,128)(2,1)} %get-tuple-element.17), calls=%async_computation | async-start | bytes 1310720 | tf_op jit(solution)/shard_map/all_to_all | solution.py:439
  58.8 5.8 %copy-start.1 = (bf16[16,32,640]{2,1,0:T(8,128)(2,1)}, bf16[16,32,640]{2,1,0:T(8,128)(2,1)S(1)}, u32[]{:S(2)}) copy-start(bf16[16,32,640]{2,1,0:T(8,128)(2,1)S(1)} %all-to-all-done.received.rest_6_) | copy-start | bytes 1966084
  60.2 21.6 %all-to-all-start.1 = ((bf16[16,32,512]{2,1,0:T(8,128)(2,1)}), bf16[16,32,512]{2,1,0:T(8,128)(2,1)S(1)}, u32[]{:S(2)}, u32[]{:S(2)}) async-start(bf16[16,32,512]{2,1,0:T(8,128)(2,1)} %merge.1), calls=%async_computation.1 | async-start | bytes 1048576 | tf_op jit(solution)/shard_map/all_to_all | solution.py:471
  73.8 9.1 %collective-permute-start = (bf16[4096,256]{1,0:T(8,128)(2,1)}, bf16[4096,256]{1,0:T(8,128)(2,1)}, u32[]{:S(2)}, u32[]{:S(2)}) collective-permute-start(bf16[4096,256]{1,0:T(8,128)(2,1)} %get-tuple-element.28), channel_id=1, source_target_pairs={{0,16},{16,0},{1,17},{17,1},{2,18},{18,2},{3,19},{19,3},{4,20},{20... | collective-permute-start | bytes 6291464 | tf_op jit(solution)/shard_map/ppermute | solution.py:397
  81.8 2.0 %copy-start = (bf16[4096,256]{1,0:T(8,128)(2,1)S(1)}, bf16[4096,256]{1,0:T(8,128)(2,1)}, u32[]{:S(2)}) copy-start(bf16[4096,256]{1,0:T(8,128)(2,1)} %backward.1.refs_1_) | copy-start | bytes 6291460

commit v9 on v6

--- a/solution.py
+++ b/solution.py
@@ -1,5 +1,4 @@
 import functools
-import math
 
 import jax
 import jax.numpy as jnp
@@ -9,11 +8,11 @@
 from jax.sharding import PartitionSpec as P
 
 SOFTMAX_HEAT = 0.5
-TO_LOG2 = math.log2(math.e) / SOFTMAX_HEAT
+SHARPNESS = 1.0 / SOFTMAX_HEAT
 BF16 = jnp.bfloat16
 F32 = jnp.float32
 MIB = 1 << 20
-CHUNK = 256
+CHUNK = 512
 AHEAD = 3
 ROWS = 64
 LARGEST = 2.0**60
@@ -21,6 +20,8 @@
 SMEM = pl.BlockSpec(memory_space=pltpu.SMEM)
 ANY = pl.BlockSpec(memory_space=pl.ANY)
 FULL = pltpu.CompilerParams(vmem_limit_bytes=60 * MIB)
+MOST = pltpu.CompilerParams(vmem_limit_bytes=56 * MIB)
+SOME = pltpu.CompilerParams(vmem_limit_bytes=24 * MIB)
 
 
 def dot(left, right, left_dim=1, right_dim=0):
@@ -43,9 +44,9 @@
 
 
 def forward_kernel(
-    n_code, tokens, grad_out, codebook, noise, codes, sent,
-    pair, book, noise_in, slot_a, slot_b, shifts, total, sums,
-    pair_sem, book_sem, noise_sem, code_sem,
+    n_code, tokens, grad_out, codebook, noise, codes, sent, mix, mean,
+    own_tokens, own_grad, book, noise_in, slot_a, slot_b, shifts, total,
+    own_sem, book_sem, noise_sem, code_sem,
 ):
     tiles, n_tokens, width = codes.shape
     dim = tokens.shape[1]
@@ -67,38 +68,35 @@
         for copy in fetch(t):
             copy.wait()
 
-    pair_copies = []
-    for r in range(0, n_tokens, ROWS):
-        for half, source in enumerate((tokens, grad_out)):
-            pair_copies.append(
-                pltpu.make_async_copy(
-                    source.at[pl.ds(r, ROWS)],
-                    pair.at[pl.ds(2 * r + half * ROWS, ROWS)],
-                    pair_sem.at[len(pair_copies)],
-                )
-            )
-    start(0)
-    for copy in pair_copies:
-        copy.start()
-    for t in range(1, min(AHEAD + 1, tiles)):
+    own_copies = (
+        pltpu.make_async_copy(tokens, own_tokens, own_sem.at[0]),
+        pltpu.make_async_copy(grad_out, own_grad, own_sem.at[1]),
+    )
+    own_copies[0].start()
+    for t in range(min(AHEAD + 1, tiles)):
         start(t)
+    own_copies[1].start()
+
+    def score(t, c):
+        return dot(own_tokens[...], book[t, c], 1, 1)
+
+    def logits(scores, t, at, c):
+        return scores[at] + (noise_in[t, at, c] * BF16(SHARPNESS)).astype(F32)
+
+    row_parts = [slice(r, r + ROWS) for r in range(0, n_tokens, ROWS)]
 
     def raise_shift(t, some):
         for c in some:
-            both = dot(pair[...], book[t, c], 1, 1)
-            for r in range(0, n_tokens, ROWS):
-                at = slice(r, r + ROWS)
-                score = both[2 * r : 2 * r + ROWS] + noise_in[t, at, c].astype(F32)
+            scores = score(t, c)
+            for at in row_parts:
                 shifts[at] = functools.reduce(
-                    jnp.maximum, lane_groups(score * TO_LOG2), shifts[at]
+                    jnp.maximum, lane_groups(logits(scores, t, at, c)), shifts[at]
                 )
 
     def store(t, s):
-        return pltpu.make_async_copy(
-            slots[s].at[pl.ds(0, n_tokens)], codes.at[t], code_sem.at[s]
-        )
-
-    def soften(t, s, fresh):
+        return pltpu.make_async_copy(slots[s], codes.at[t], code_sem.at[s])
+
+    def soften(t, s, fresh, last=None):
         if fresh is not None:
             @pl.when(fresh)
             def _():
@@ -109,21 +107,22 @@
                     start(t + AHEAD)
 
         slot = slots[s]
-        for c in columns:
-            both = dot(pair[...], book[t, c], 1, 1)
-            for r in range(0, n_tokens, ROWS):
-                at = slice(r, r + ROWS)
-                score = both[2 * r : 2 * r + ROWS] + noise_in[t, at, c].astype(F32)
+        ahead = score(t, columns[0])
+        for k, c in enumerate(columns):
+            scores = ahead
+            if k + 1 < len(columns):
+                ahead = score(t, columns[k + 1])
+            elif last is not None:
+                last()
+            for at in row_parts:
                 shift = jnp.concatenate([shifts[at]] * (CHUNK // 128), axis=1)
-                weight = jnp.exp2(score * TO_LOG2 - shift)
+                weight = jnp.exp(logits(scores, t, at, c) - shift)
                 total[at] += sum(lane_groups(weight))
                 slot[at, c] = weight.astype(BF16)
-                gradient = both[2 * r + ROWS : 2 * r + 2 * ROWS]
-                slot[n_tokens + r : n_tokens + r + ROWS, c] = (weight * gradient).astype(BF16)
         store(t, s).start()
 
     def accumulate(t, s):
-        sums[...] += dot(slots[s][...], book[t])
+        mix[...] += dot(slots[s][...], book[t])
 
     def attempt(state):
         again, _ = state
@@ -132,7 +131,7 @@
 
         @pl.when(fresh)
         def _():
-            raise_shift(0, columns[:2])
+            raise_shift(0, columns[:1])
 
         @pl.when(jnp.logical_not(fresh))
         def _():
@@ -145,7 +144,7 @@
         shift = jnp.max(shifts[...], axis=1, keepdims=True).astype(BF16).astype(F32)
         shifts[...] = jnp.broadcast_to(shift, shifts.shape)
         total[...] = jnp.zeros(total.shape, F32)
-        sums[...] = jnp.zeros(sums.shape, F32)
+        mix[...] = jnp.zeros(mix.shape, F32)
         soften(0, 0, None)
 
         def soften_pair(i, carry):
@@ -153,38 +152,31 @@
             def _():
                 store(2 * i - 1, 1).wait()
 
-            soften(2 * i + 1, 1, fresh)
-            accumulate(2 * i, 0)
+            soften(2 * i + 1, 1, fresh, lambda: accumulate(2 * i, 0))
             store(2 * i, 0).wait()
-            soften(2 * i + 2, 0, fresh)
-            accumulate(2 * i + 1, 1)
+            soften(2 * i + 2, 0, fresh, lambda: accumulate(2 * i + 1, 1))
             return carry
 
         lax.fori_loop(0, tiles // 2 - 1, soften_pair, 0)
         if tiles > 2:
             store(tiles - 3, 1).wait()
-        soften(tiles - 1, 1, fresh)
-        accumulate(tiles - 2, 0)
+        soften(tiles - 1, 1, fresh, lambda: accumulate(tiles - 2, 0))
         accumulate(tiles - 1, 1)
         store(tiles - 2, 0).wait()
         store(tiles - 1, 1).wait()
         fits = jnp.max(total[...]) < LARGEST
         return again + 1, jnp.logical_and(fresh, jnp.logical_not(fits))
 
-    for copy in pair_copies:
-        copy.wait()
+    own_copies[0].wait()
+    own_tokens[...] = own_tokens[...] * BF16(SHARPNESS)
     arrive(0)
     lax.while_loop(lambda state: state[1], attempt, (jnp.int32(0), jnp.bool_(True)))
 
+    own_copies[1].wait()
     shift = shifts[:, :1]
-    mix = sums[:n_tokens]
-    pulled = sums[n_tokens:]
     own_total = jnp.sum(total[...], axis=1, keepdims=True)
-    own_grad = jnp.concatenate(
-        [pair[2 * r + ROWS : 2 * r + 2 * ROWS] for r in range(0, n_tokens, ROWS)], axis=0
-    )
-    own_inner = jnp.sum(own_grad.astype(F32) * mix, axis=1, keepdims=True)
-    mean = own_inner / own_total
+    own_inner = jnp.sum(own_grad[...].astype(F32) * mix[...], axis=1, keepdims=True)
+    mean[...] = jnp.broadcast_to(own_inner / own_total, mean.shape)
     rows = n_tokens // n_code
     lanes = stat_lanes(n_code)
     half = lanes // 2
@@ -198,10 +190,55 @@
         stats = jnp.where((lane - half) // 4 == g, shift[at], stats)
     stats = stats.astype(BF16)
     for g in range(n_code):
+        sent[g, :, :dim] = mix[g * rows : (g + 1) * rows].astype(BF16)
+        sent[g, :, dim:] = stats
+
+
+def pull_kernel(
+    grad_out, codebook, codes, mix, mean, sent,
+    book, code_in, slot_a, slot_b, pulled, book_sem, code_sem,
+):
+    tiles, width, dim = book.shape
+    n_code, rows, _ = sent.shape
+    slots = (slot_a, slot_b)
+    steps = [(t, slice(c, c + CHUNK)) for t in range(tiles) for c in range(0, width, CHUNK)]
+
+    def fetch(t):
+        at = pl.ds(t * width, width)
+        return (
+            pltpu.make_async_copy(codebook.at[at], book.at[t], book_sem.at[t]),
+            pltpu.make_async_copy(codes.at[t], code_in.at[t], code_sem.at[t]),
+        )
+
+    def start(t):
+        for copy in fetch(t):
+            copy.start()
+
+    def gradient_of(step):
+        t, c = step
+        if c.start == 0:
+            for copy in fetch(t):
+                copy.wait()
+            if t + AHEAD < tiles:
+                start(t + AHEAD)
+        return dot(grad_out[...], book[t, c], 1, 1)
+
+    for t in range(min(AHEAD, tiles)):
+        start(t)
+    pulled[...] = jnp.zeros(pulled.shape, F32)
+    ahead = gradient_of(steps[0])
+    for k, (t, c) in enumerate(steps):
+        gradient = ahead
+        if k + 1 < len(steps):
+            ahead = gradient_of(steps[k + 1])
+        if c.start == 0 and t > 0:
+            pulled[...] += dot(slots[(t - 1) % 2][...], book[t - 1])
+        slots[t % 2][:, c] = (code_in[t, :, c].astype(F32) * gradient).astype(BF16)
+    pulled[...] += dot(slots[(tiles - 1) % 2][...], book[tiles - 1])
+    for g in range(n_code):
         at = slice(g * rows, (g + 1) * rows)
-        sent[g, :, :dim] = mix[at].astype(BF16)
-        sent[g, :, dim : 2 * dim] = (pulled[at] - mean[at] * mix[at]).astype(BF16)
-        sent[g, :, 2 * dim :] = stats
+        means = jnp.concatenate([mean[at]] * (dim // 128), axis=1)
+        sent[g] = (pulled[at] - means * mix[at]).astype(BF16)
 
 
 def roll_left(value, by):
@@ -213,7 +250,7 @@
     lanes = stat_lanes(n_code)
     stats = [received[p, :, received.shape[2] - lanes :].astype(F32) for p in range(n_code)]
     top = functools.reduce(jnp.maximum, stats)
-    scales = [roll_left(jnp.exp2(s - top), lanes // 2) for s in stats]
+    scales = [roll_left(jnp.exp(s - top), lanes // 2) for s in stats]
     pairs = [s + roll_left(s, 1) for s in stats]
     inners = [roll_left(s, 2) for s in pairs]
     total = sum(a * s for a, s in zip(scales, pairs))
@@ -222,7 +259,7 @@
     return [a / total for a in scales], means, inner
 
 
-def merge_kernel(me, received, spread):
+def merge_kernel(me, received, received_pulled, spread):
     n_code, rows, _ = received.shape
     dim = spread.shape[2] // 2
     scales, means, inner = merged_stats(received)
@@ -239,7 +276,7 @@
         offset = column(scales[p] * (means[p] - inner))
         mix = received[p, :, :dim].astype(F32)
         quantized += scale * mix
-        gradient += scale * received[p, :, dim : 2 * dim].astype(F32) + offset * mix
+        gradient += scale * received_pulled[p].astype(F32) + offset * mix
     quantized = quantized.astype(BF16)
     gradient = (gradient / SOFTMAX_HEAT).astype(BF16)
     for p in range(n_code):
@@ -247,15 +284,15 @@
         spread[p, :, dim:] = gradient
 
 
-def backward_kernel(prepared, where, *rest):
+def backward_kernel(prepared, block, *rest):
     if prepared:
         grad_out, codebook, codes, operands, inners, out, *rest = rest
     else:
-        tokens, grad_out, codebook, codes, received, out, operands, inners, upper, lower, *rest = rest
+        code_at, tokens, grad_out, codebook, codes, received, out, operands, inners, upper, lower, *rest = rest
     book, code_in, result, book_sem, code_sem, out_sem = rest
     tiles, width, dim = book.shape
     n_tokens = grad_out.shape[0]
-    first = where[1] * tiles
+    first = block[0] * tiles
 
     def fetch(t):
         at = pl.multiple_of((first + t) * width, width)
@@ -276,7 +313,7 @@
         scales, _, inner = merged_stats(received)
         scale = jnp.zeros(inner.shape, F32)
         for p in range(n_code):
-            scale = jnp.where(where[0] == p, scales[p], scale)
+            scale = jnp.where(code_at[0] == p, scales[p], scale)
         for g in range(n_code):
             part = slice(g * rows, (g + 1) * rows)
             column = scale[:, 4 * g : 4 * g + 1]
@@ -369,57 +406,62 @@
     lanes = stat_lanes(n_code)
     products = 2 * n_tokens * n_codes * dim
 
-    codes, sent = pl.pallas_call(
+    codes, sent, mix, mean = pl.pallas_call(
         functools.partial(forward_kernel, n_code),
         out_shape=(
             pltpu.HBM((tiles, n_tokens, width), BF16),
-            jax.ShapeDtypeStruct((n_code, rows, 2 * dim + lanes), BF16),
+            jax.ShapeDtypeStruct((n_code, rows, dim + lanes), BF16),
+            jax.ShapeDtypeStruct((n_tokens, dim), F32),
+            jax.ShapeDtypeStruct((n_tokens, 128), F32),
         ),
         in_specs=[ANY, ANY, ANY, ANY],
-        out_specs=(ANY, VMEM),
+        out_specs=(ANY, VMEM, VMEM, VMEM),
         scratch_shapes=[
-            pltpu.VMEM((2 * n_tokens, dim), BF16),
+            pltpu.VMEM((n_tokens, dim), BF16),
+            pltpu.VMEM((n_tokens, dim), BF16),
             pltpu.VMEM((tiles, width, dim), BF16),
             pltpu.VMEM((tiles, n_tokens, width), BF16),
-            pltpu.VMEM((2 * n_tokens, width), BF16),
-            pltpu.VMEM((2 * n_tokens, width), BF16),
+            pltpu.VMEM((n_tokens, width), BF16),
+            pltpu.VMEM((n_tokens, width), BF16),
             pltpu.VMEM((n_tokens, 128), F32),
             pltpu.VMEM((n_tokens, 128), F32),
-            pltpu.VMEM((2 * n_tokens, dim), F32),
-            pltpu.SemaphoreType.DMA((2 * n_tokens // ROWS,)),
+            pltpu.SemaphoreType.DMA((2,)),
             pltpu.SemaphoreType.DMA((tiles,)),
             pltpu.SemaphoreType.DMA((tiles,)),
             pltpu.SemaphoreType.DMA((2,)),
         ],
         compiler_params=FULL,
         cost_estimate=pl.CostEstimate(
-            flops=4 * products, bytes_accessed=24 * MIB, transcendentals=n_tokens * n_codes
+            flops=2 * products, bytes_accessed=20 * MIB, transcendentals=n_tokens * n_codes
         ),
         name="forward",
     )(tokens, grad_out, codebook, noise)
-
     received = lax.all_to_all(sent, "code", 0, 0, tiled=True)
+
+    sent_pulled = pl.pallas_call(
+        pull_kernel,
+        out_shape=jax.ShapeDtypeStruct((n_code, rows, dim), BF16),
+        in_specs=[VMEM, ANY, ANY, VMEM, VMEM],
+        out_specs=VMEM,
+        scratch_shapes=[
+            pltpu.VMEM((tiles, width, dim), BF16),
+            pltpu.VMEM((tiles, n_tokens, width), BF16),
+            pltpu.VMEM((n_tokens, width), BF16),
+            pltpu.VMEM((n_tokens, width), BF16),
+            pltpu.VMEM((n_tokens, dim), F32),
+            pltpu.SemaphoreType.DMA((tiles,)),
+            pltpu.SemaphoreType.DMA((tiles,)),
+        ],
+        compiler_params=FULL,
+        cost_estimate=pl.CostEstimate(
+            flops=2 * products, bytes_accessed=12 * MIB, transcendentals=0
+        ),
+        name="pull",
+    )(grad_out, codebook, codes, mix, mean)
+    received_pulled = lax.all_to_all(sent_pulled, "code", 0, 0, tiled=True)
+
     code_at = lax.axis_index("code")
-    spread = pl.pallas_call(
-        merge_kernel,
-        out_shape=jax.ShapeDtypeStruct((n_code, rows, 2 * dim), BF16),
-        in_specs=[SMEM, VMEM],
-        out_specs=VMEM,
-        compiler_params=FULL,
-        name="merge",
-    )(code_at[None], received)
-    received, spread = lax.optimization_barrier((received, spread))
-    gathered = lax.all_to_all(spread, "code", 0, 0, tiled=True)
-    quantized, token_gradient = pl.pallas_call(
-        unpack_kernel,
-        out_shape=(jax.ShapeDtypeStruct((n_tokens, dim), F32),) * 2,
-        in_specs=[VMEM],
-        out_specs=(VMEM, VMEM),
-        compiler_params=FULL,
-        cost_estimate=pl.CostEstimate(flops=0, bytes_accessed=64 * MIB, transcendentals=0),
-        name="unpack",
-    )(gathered)
-
+    dp_at = lax.axis_index("dp")
     block_tiles = block // width
     streams = [
         pltpu.VMEM((block_tiles, width, dim), BF16),
@@ -431,10 +473,11 @@
     ]
     block_shape = jax.ShapeDtypeStruct((block, dim), BF16)
     common = dict(
-        compiler_params=FULL,
-        cost_estimate=pl.CostEstimate(flops=1, bytes_accessed=1, transcendentals=0),
+        compiler_params=MOST,
+        cost_estimate=pl.CostEstimate(
+            flops=3 * products // n_dp, bytes_accessed=16 * MIB // n_dp, transcendentals=0
+        ),
     )
-    dp_at = lax.axis_index("dp")
     first, operands, inners = pl.pallas_call(
         functools.partial(backward_kernel, False),
         out_shape=(
@@ -442,14 +485,27 @@
             jax.ShapeDtypeStruct((2, dim, n_tokens), BF16),
             jax.ShapeDtypeStruct((n_tokens, 128), F32),
         ),
-        in_specs=[SMEM, VMEM, VMEM, ANY, ANY, VMEM],
+        in_specs=[SMEM, SMEM, VMEM, VMEM, ANY, ANY, VMEM],
         out_specs=(ANY, VMEM, VMEM),
         scratch_shapes=[
             pltpu.VMEM((n_tokens, dim), F32), pltpu.VMEM((n_tokens, dim), F32),
         ] + streams,
         name="backward_first",
         **common,
-    )(jnp.stack([code_at, dp_at ^ (n_dp - 1)]), tokens, grad_out, codebook, codes, received)
+    )(
+        (dp_at ^ (n_dp - 1))[None], code_at[None], tokens, grad_out, codebook, codes, received
+    )
+    received_pulled, operands = lax.optimization_barrier((received_pulled, operands))
+    spread = pl.pallas_call(
+        merge_kernel,
+        out_shape=jax.ShapeDtypeStruct((n_code, rows, 2 * dim), BF16),
+        in_specs=[SMEM, VMEM, VMEM],
+        out_specs=VMEM,
+        compiler_params=SOME,
+        name="merge",
+    )(code_at[None], received, received_pulled)
+    spread, operands = lax.optimization_barrier((spread, operands))
+    gathered = lax.all_to_all(spread, "code", 0, 0, tiled=True)
 
     def backward(at):
         return pl.pallas_call(
@@ -460,7 +516,7 @@
             scratch_shapes=streams,
             name="backward",
             **common,
-        )(jnp.stack([code_at, at]), grad_out, codebook, codes, operands, inners)
+        )(at[None], grad_out, codebook, codes, operands, inners)
 
     blocks = [swap(first, "dp", n_dp, n_dp - 1)]
     blocks += [swap(backward(dp_at ^ d), "dp", n_dp, d) for d in range(1, n_dp - 1)]
@@ -477,12 +533,24 @@
             pltpu.SemaphoreType.DMA((n_dp, steps)),
             pltpu.SemaphoreType.DMA((steps,)),
         ],
-        compiler_params=FULL,
+        compiler_params=SOME,
         cost_estimate=pl.CostEstimate(
             flops=0, bytes_accessed=(2 * n_dp + 4) * block * dim, transcendentals=0
         ),
         name="add",
     )(*blocks)
+    gathered, own_rows = lax.optimization_barrier((gathered, own_rows))
+    quantized, token_gradient = pl.pallas_call(
+        unpack_kernel,
+        out_shape=(jax.ShapeDtypeStruct((n_tokens, dim), F32),) * 2,
+        in_specs=[VMEM],
+        out_specs=(VMEM, VMEM),
+        compiler_params=SOME,
+        cost_estimate=pl.CostEstimate(
+            flops=0, bytes_accessed=12 * n_tokens * dim, transcendentals=0
+        ),
+        name="unpack",
+    )(gathered)
     return quantized, token_gradient, own_rows[None]
 
 

time: 99.8 us -> 99.9 us (level)
  blocking collectives: 0 us -> 14.3 us
  waiting for transfers between devices: 23.4 us -> 15 us
  Pallas kernels: 58 us -> 54.8 us
  other arithmetic: 1.26 us -> 0 us
    all_to_all x0 -> x1, blocking collectives: none -> 14.3 us  [local(): received_pulled = lax.all_to_all(sent_pulled, 'code', 0, 0, tiled=True)]
    pallas_call x0 -> x1, Pallas kernels: none -> 9.88 us  [local(): pl.pallas_call(pull_kernel, out_shape=jax.ShapeDtypeStruct((n_code, rows,...]
    pallas_call x1, Pallas kernels: 32.3 us -> 23 us  [local(): pl.pallas_call(functools.partial(forward_kernel, n_code), out_shape=(pltp...]
    all_to_all x1, waiting for transfers between devices: 6.56 us -> 2.34 us  [local(): gathered = lax.all_to_all(spread, 'code', 0, 0, tiled=True)]
    all_to_all x1, waiting for transfers between devices: 16.8 us -> 12.6 us  [local(): received = lax.all_to_all(sent, 'code', 0, 0, tiled=True)]
    another operation x2 -> x0, other arithmetic: 1.26 us -> none  [the longest x1 0.66 us: backward(): jnp.stack([code_at, at])]
    pallas_call x1, Pallas kernels: 2.45 us -> 1.37 us  [local(): pl.pallas_call(merge_kernel, out_shape=jax.ShapeDtypeStruct((n_code, rows...]
    pallas_call x1, Pallas kernels: 2.07 us -> 1.03 us  [local(): pl.pallas_call(unpack_kernel, out_shape=(jax.ShapeDtypeStruct((n_tokens,...]
  transfers between devices with their start and end apart: 3 -> 3, of which waited for: 2 -> 2; matrix products, arithmetic and copies ran while one was open for 1% -> 0% of each run, Pallas kernels for 10% -> 22%
where the time goes in v9:
time: 99.9 us; the launch traced here: 99.4 us
  Pallas kernels  54.8 us (55%)
  waiting for transfers between devices  15 us (15%)
  blocking collectives  14.3 us (14%)
  starting transfers between devices  12.2 us (12%)
  local copies, waits for them, and re-layouts  2.38 us (2%)
    pallas_call x1, Pallas kernels, local(): pl.pallas_call(functools.partial(forward_kernel, n_code), out_shape=(pltp...  23 us
    all_to_all x1, blocking collectives, local(): received_pulled = lax.all_to_all(sent_pulled, 'code', 0, 0, tiled=True)  14.3 us
    all_to_all x1, waiting for transfers between devices, local(): received = lax.all_to_all(sent, 'code', 0, 0, tiled=True)  12.6 us
    pallas_call x1, Pallas kernels, local(): pl.pallas_call(pull_kernel, out_shape=jax.ShapeDtypeStruct((n_code, rows,...  9.88 us
    pallas_call x1, Pallas kernels, local(): pl.pallas_call(functools.partial(backward_kernel, False), out_shape=(bloc...  8.98 us
    all_to_all x1, starting transfers between devices, local(): received = lax.all_to_all(sent, 'code', 0, 0, tiled=True)  8.33 us
    pallas_call x1, Pallas kernels, backward(): pl.pallas_call(functools.partial(backward_kernel, True), out_shape=block_...  7.94 us
    all_to_all x1, starting transfers between devices, local(): gathered = lax.all_to_all(spread, 'code', 0, 0, tiled=True)  3.79 us
  transfers between devices with their start and end apart: 3, of which 2 were waited for; matrix products, arithmetic and copies ran while one was open for 0% of the time, Pallas kernels for 22%

profile of v9, /device:TPU:0, one launch (start us, length us, event | category | flops | bytes accessed | tf_op | source)
XLA Modules:
  0.0 99.4 jit_solution(7933593730457177098)
XLA Ops:
  0.6 23.0 %forward.1 = (bf16[8,512,1024]{2,1,0:T(8,128)(2,1)}, bf16[16,32,384]{2,1,0:T(8,128)(2,1)}, f32[512,256]{1,0:T(8,128)}, f32[512,128]{1,0:T(8,128)}) custom-call(bf16[512,256]{1,0:T(8,128)(2,1)} %rest_1_.2, bf16[512,256]{1,0:T(8,128)(2,1)} %rest_0_.1, bf16[8192,256]{1,0:T(8,128)(2,1)} %rest_1_.3, bf16[512,8192]{1,0:T(8,128)(2,1)} %noise.1), custom_call_target="tpu_custom_call" | custom-call | flops 4294967296 | bytes 20971520 | tf_op jit(solution)/shard_map/forward/pallas_call | solution.py:409
  23.7 8.3 %all-to-all-start = ((bf16[16,32,384]{2,1,0:T(8,128)(2,1)}), bf16[16,32,384]{2,1,0:T(8,128)(2,1)S(1)}, u32[]{:S(2)}, u32[]{:S(2)}) async-start(bf16[16,32,384]{2,1,0:T(8,128)(2,1)} %get-tuple-element.18), calls=%async_computation | async-start | bytes 786432 | tf_op jit(solution)/shard_map/all_to_all | solution.py:439
  32.0 12.6 %all-to-all-done.rest_5_.received = bf16[16,32,384]{2,1,0:T(8,128)(2,1)S(1)} async-done(((bf16[16,32,384]{2,1,0:T(8,128)(2,1)}), bf16[16,32,384]{2,1,0:T(8,128)(2,1)S(1)}, u32[]{:S(2)}, u32[]{:S(2)}) %all-to-all-start) | async-done | bytes 393248 | tf_op jit(solution)/shard_map/all_to_all | solution.py:439
  44.7 0.0 copy-start.1
  44.7 0.8 copy-done.1
  45.4 9.0 %backward_first.1 = (bf16[4096,256]{1,0:T(8,128)(2,1)}, bf16[2,256,512]{2,1,0:T(8,128)(2,1)}, f32[512,128]{1,0:T(8,128)}) custom-call(s32[1]{0:T(128)} %bitcast.1.block, s32[1]{0:T(128)} %bitcast.rest_0_.me, bf16[512,256]{1,0:T(8,128)(2,1)} %rest_1_.2, bf16[512,256]{1,0:T(8,128)(2,1)} %rest_0_.1, bf16[8192,256]{1,0:T(8,128)(2,1)} %rest_1_.3, ...), custom_call_target="tpu_custom_call" | custom-call | flops 3221225472 | bytes 8388608 | tf_op jit(solution)/shard_map/backward_first/pallas_call | solution.py:481
  54.4 0.1 collective-permute-start
  54.5 0.0 copy-start.2
  54.5 9.9 %pull.1 = bf16[16,32,256]{2,1,0:T(8,128)(2,1)} custom-call(bf16[512,256]{1,0:T(8,128)(2,1)} %rest_0_.1, bf16[8192,256]{1,0:T(8,128)(2,1)} %rest_1_.3, bf16[8,512,1024]{2,1,0:T(8,128)(2,1)} %get-tuple-element.19.codes.rest_4_.rest_2_, f32[512,256]{1,0:T(8,128)} %get-tuple-element.20.mix, f32[512,128]{1,0:T(8,128)} %get-tuple-element.21.mean), custom_call_target="tpu_custom_call" | custom-call | flops 4294967296 | bytes 12582912 | tf_op jit(solution)/shard_map/pull/pallas_call | solution.py:441
  64.4 14.3 %all_to_all.15.received_pulled = bf16[16,32,256]{2,1,0:T(8,128)(2,1)S(1)} all-to-all(bf16[16,32,256]{2,1,0:T(8,128)(2,1)} %pull.1), channel_id=1, replica_groups=mesh['dp'=2,'code'=16] {'code'}, dimensions={0} | all-to-all | bytes 524288 | tf_op jit(solution)/shard_map/all_to_all | solution.py:461
  78.7 0.0 copy-done.2
  78.7 1.4 %merge.1 = bf16[16,32,512]{2,1,0:T(8,128)(2,1)} custom-call(s32[1]{0:T(128)} %bitcast.rest_0_.me, bf16[16,32,384]{2,1,0:T(8,128)(2,1)S(1)} %copy-done.2, bf16[16,32,256]{2,1,0:T(8,128)(2,1)S(1)} %all_to_all.15.received_pulled), custom_call_target="tpu_custom_call" | custom-call | tf_op jit(solution)/shard_map/merge/pallas_call | solution.py:499
  80.1 3.8 %all-to-all-start.2 = ((bf16[16,32,512]{2,1,0:T(8,128)(2,1)}), bf16[16,32,512]{2,1,0:T(8,128)(2,1)S(1)}, u32[]{:S(2)}, u32[]{:S(2)}) async-start(bf16[16,32,512]{2,1,0:T(8,128)(2,1)} %merge.1), calls=%async_computation.2 | async-start | bytes 1048576 | tf_op jit(solution)/shard_map/all_to_all | solution.py:508
  83.9 7.9 %backward.1.refs_1_ = bf16[4096,256]{1,0:T(8,128)(2,1)} custom-call(s32[1]{0:T(128)} %bitcast.2.block, bf16[512,256]{1,0:T(8,128)(2,1)} %rest_0_.1, bf16[8192,256]{1,0:T(8,128)(2,1)} %rest_1_.3, bf16[8,512,1024]{2,1,0:T(8,128)(2,1)} %get-tuple-element.19.codes.rest_4_.rest_2_, bf16[2,256,512]{2,1,0:T(8,128)(2,1)} %get-tuple-element.27.rest_3_, ...), custom_call_target="tpu_custom_call" | custom-call | flops 3221225472 | bytes 8388608 | tf_op jit(solution)/shard_map/backward/pallas_call | solution.py:511
  91.8 0.0 collective-permute-done.refs_0_
  91.8 0.0 copy-start
  91.8 1.6 %copy-done = bf16[4096,256]{1,0:T(8,128)(2,1)S(1)} copy-done((bf16[4096,256]{1,0:T(8,128)(2,1)S(1)}, bf16[4096,256]{1,0:T(8,128)(2,1)}, u32[]{:S(2)}) %copy-start) | copy-done | bytes 2097176
  93.4 2.6 %add.1 = f32[4096,256]{1,0:T(8,128)} custom-call(bf16[4096,256]{1,0:T(8,128)(2,1)S(1)} %collective-permute-done.refs_0_, bf16[4096,256]{1,0:T(8,128)(2,1)S(1)} %copy-done), custom_call_target="tpu_custom_call" | custom-call | bytes 8388608 | tf_op jit(solution)/shard_map/add/pallas_call | solution.py:525
  96.0 2.3 %all-to-all-done.2.gathered = bf16[16,32,512]{2,1,0:T(8,128)(2,1)S(1)} async-done(((bf16[16,32,512]{2,1,0:T(8,128)(2,1)}), bf16[16,32,512]{2,1,0:T(8,128)(2,1)S(1)}, u32[]{:S(2)}, u32[]{:S(2)}) %all-to-all-start.2) | async-done | bytes 524320 | tf_op jit(solution)/shard_map/all_to_all | solution.py:508
  98.3 1.0 %unpack.1 = (f32[512,256]{1,0:T(8,128)}, f32[512,256]{1,0:T(8,128)}) custom-call(bf16[16,32,512]{2,1,0:T(8,128)(2,1)S(1)} %all-to-all-done.2.gathered), custom_call_target="tpu_custom_call" | custom-call | bytes 1572864 | tf_op jit(solution)/shard_map/unpack/pallas_call | solution.py:543
Async XLA Ops:
  23.7 21.0 %all-to-all-start = ((bf16[16,32,384]{2,1,0:T(8,128)(2,1)}), bf16[16,32,384]{2,1,0:T(8,128)(2,1)S(1)}, u32[]{:S(2)}, u32[]{:S(2)}) async-start(bf16[16,32,384]{2,1,0:T(8,128)(2,1)} %get-tuple-element.18), calls=%async_computation | async-start | bytes 786432 | tf_op jit(solution)/shard_map/all_to_all | solution.py:439
  44.7 0.8 copy-start.1
  54.4 37.4 %collective-permute-start = (bf16[4096,256]{1,0:T(8,128)(2,1)}, bf16[4096,256]{1,0:T(8,128)(2,1)S(1)}, u32[]{:S(2)}, u32[]{:S(2)}) collective-permute-start(bf16[4096,256]{1,0:T(8,128)(2,1)} %get-tuple-element.26), channel_id=1, source_target_pairs={{0,16},{16,0},{1,17},{17,1},{2,18},{18,2},{3,19},{19,3},{4,20},{20... | collective-permute-start | bytes 6291464 | tf_op jit(solution)/shard_map/ppermute | solution.py:396
  54.5 24.2 %copy-start.2 = (bf16[16,32,384]{2,1,0:T(8,128)(2,1)S(1)}, bf16[16,32,384]{2,1,0:T(8,128)(2,1)}, u32[]{:S(2)}) copy-start(bf16[16,32,384]{2,1,0:T(8,128)(2,1)} %copy-done.1) | copy-start | bytes 1179652
  80.1 18.3 %all-to-all-start.2 = ((bf16[16,32,512]{2,1,0:T(8,128)(2,1)}), bf16[16,32,512]{2,1,0:T(8,128)(2,1)S(1)}, u32[]{:S(2)}, u32[]{:S(2)}) async-start(bf16[16,32,512]{2,1,0:T(8,128)(2,1)} %merge.1), calls=%async_computation.2 | async-start | bytes 1048576 | tf_op jit(solution)/shard_map/all_to_all | solution.py:508
  91.8 1.6 %copy-start = (bf16[4096,256]{1,0:T(8,128)(2,1)S(1)}, bf16[4096,256]{1,0:T(8,128)(2,1)}, u32[]{:S(2)}) copy-start(bf16[4096,256]{1,0:T(8,128)(2,1)} %backward.1.refs_1_) | copy-start | bytes 6291460

commit v10 on v8

--- a/solution.py
+++ b/solution.py
@@ -13,9 +13,8 @@
 F32 = jnp.float32
 MIB = 1 << 20
 CHUNK = 256
-HIGH = 512
-AHEAD = 3
-PARTS = 4
+WIDE = 512
+AHEAD = 2
 ROWS = 64
 LARGEST = 2.0**60
 VMEM = pl.BlockSpec(memory_space=pltpu.VMEM)
@@ -46,7 +45,7 @@
 
 
 def forward_kernel(
-    n_code, tokens, grad_out, codebook, noise, codes, sent,
+    n_code, tokens, grad_out, codebook, noise, codes, sent, means,
     pair, book, noise_in, slot_a, slot_b, shifts, total, sums,
     pair_sem, book_sem, noise_sem, code_sem,
 ):
@@ -63,13 +62,8 @@
         )
 
     def start(t):
-        fetch(t)[0].start()
-        at = pl.ds(pl.multiple_of(t * width, width), width)
-        for r in range(0, n_tokens, n_tokens // PARTS):
-            part = pl.ds(r, n_tokens // PARTS)
-            pltpu.make_async_copy(
-                noise.at[part, at], noise_in.at[t, part], noise_sem.at[t]
-            ).start()
+        for copy in fetch(t):
+            copy.start()
 
     def arrive(t):
         for copy in fetch(t):
@@ -199,6 +193,7 @@
     )
     own_inner = jnp.sum(own_grad.astype(F32) * mix, axis=1, keepdims=True)
     mean = own_inner / own_total
+    means[...] = jnp.broadcast_to(mean, means.shape)
     rows = n_tokens // n_code
     lanes = stat_lanes(n_code)
     half = lanes // 2
@@ -261,77 +256,25 @@
         spread[p, :, dim:] = gradient
 
 
-def turn_kernel(grad_out, codes, turned, turned_grad, held, result, in_sem, out_sem):
-    tiles, _, width = held.shape
+def weigh_kernel(
+    grad_out, codebook, codes, means, weighed, book, code_in, result, book_sem, code_sem, out_sem
+):
+    tiles, width, _ = book.shape
+    steps = [(t, slice(c, c + WIDE)) for t in range(tiles) for c in range(0, width, WIDE)]
 
     def fetch(t):
-        return pltpu.make_async_copy(codes.at[t], held.at[t], in_sem.at[t])
-
-    def send(t):
-        at = pl.ds(pl.multiple_of(t * width, width), width)
-        return pltpu.make_async_copy(result.at[t], turned.at[at], out_sem.at[t])
-
-    for t in range(tiles):
-        fetch(t).start()
-    turned_grad[...] = grad_out[...].T
-
-    def turn(t, carry):
-        fetch(t).wait()
-        for c in range(0, width, CHUNK):
-            result[t, c : c + CHUNK] = held[t, :, c : c + CHUNK].T
-        send(t).start()
-        return carry
-
-    lax.fori_loop(0, tiles, turn, 0)
-    for t in range(tiles):
-        send(t).wait()
-
-
-def backward_kernel(prepared, block, *rest):
-    if prepared:
-        turned_grad, codebook, turned, operands, inners, out, *rest = rest
-    else:
-        code_at, tokens, grad_out, turned_grad, codebook, turned, received, *rest = rest
-        out, operands, inners, spread_inner, *rest = rest
-    book, code_in, result, book_sem, code_sem, out_sem = rest
-    tiles, width, dim = book.shape
-    n_tokens = turned_grad.shape[1]
-
-    def fetch(t):
-        at = pl.ds(pl.multiple_of((block[0] * tiles + t) * width, width), width)
+        at = pl.ds(t * width, width)
         return (
             pltpu.make_async_copy(codebook.at[at], book.at[t], book_sem.at[t]),
-            pltpu.make_async_copy(turned.at[at], code_in.at[t], code_sem.at[t]),
+            pltpu.make_async_copy(codes.at[t], code_in.at[t], code_sem.at[t]),
         )
 
     def start(t):
         for copy in fetch(t):
             copy.start()
 
-    for t in range(min(AHEAD, tiles)):
-        start(t)
-
-    if not prepared:
-        n_code, rows, _ = received.shape
-        scales, _, inner = merged_stats(received)
-        scale = jnp.zeros(inner.shape, F32)
-        for p in range(n_code):
-            scale = jnp.where(code_at[0] == p, scales[p], scale)
-        for g in range(n_code):
-            part = slice(g * rows, (g + 1) * rows)
-            column = scale[:, 4 * g : 4 * g + 1]
-            operands[0, part] = (column * grad_out[part].astype(F32)).astype(BF16)
-            operands[1, part] = (column * (tokens[part].astype(F32) / SOFTMAX_HEAT)).astype(BF16)
-            spread_inner[part] = jnp.broadcast_to(inner[:, 4 * g : 4 * g + 1], (rows, 128))
-        inners[...] = spread_inner[...].T[:8]
-
     def send(t):
-        return pltpu.make_async_copy(
-            result.at[t], out.at[pl.ds(pl.multiple_of(t * width, width), width)], out_sem.at[t]
-        )
-
-    high = min(HIGH, width)
-    steps = [(t, slice(c, c + high)) for t in range(tiles) for c in range(0, width, high)]
+        return pltpu.make_async_copy(result.at[t], weighed.at[t], out_sem.at[t])
 
     def gradient_of(step):
         t, c = step
@@ -340,17 +283,91 @@
                 copy.wait()
             if t + AHEAD < tiles:
                 start(t + AHEAD)
-        return dot(book[t, c], turned_grad[...])
-
+        return dot(grad_out[...], book[t, c], 1, 1)
+
+    for t in range(min(AHEAD, tiles)):
+        start(t)
     ahead = gradient_of(steps[0])
     for k, (t, c) in enumerate(steps):
         gradient = ahead
         if k + 1 < len(steps):
             ahead = gradient_of(steps[k + 1])
-        code = code_in[t, c]
-        score_gradient = (code.astype(F32) * (gradient - inners[:1])).astype(BF16)
-        value = dot(code, operands[0]) + dot(score_gradient, operands[1])
-        result[t, c] = value.astype(BF16)
+        mean = jnp.concatenate([means[...]] * (WIDE // 128), axis=1)
+        result[t, :, c] = (code_in[t, :, c].astype(F32) * (gradient - mean)).astype(BF16)
+        if c.stop == width:
+            send(t).start()
+    for t in range(tiles):
+        send(t).wait()
+
+
+def backward_kernel(prepared, block, *rest):
+    if prepared:
+        codes, weighed, operands, out, *rest = rest
+    else:
+        code_at, tokens, grad_out, codes, weighed, received, out, operands, *rest = rest
+        upper, lower, *rest = rest
+    both_in, result, in_sem, out_sem = rest
+    tiles, width, dim = result.shape
+    n_tokens = both_in.shape[1] // 2
+
+    def fetch(t):
+        return [
+            pltpu.make_async_copy(
+                source.at[block[0] * tiles + t],
+                both_in.at[t, pl.ds(half * n_tokens, n_tokens)],
+                in_sem.at[half, t],
+            )
+            for half, source in enumerate((codes, weighed))
+        ]
+
+    def start(t):
+        for copy in fetch(t):
+            copy.start()
+
+    for t in range(min(AHEAD, tiles)):
+        start(t)
+
+    if not prepared:
+        n_code, rows, _ = received.shape
+        scales, means, inner = merged_stats(received)
+        scale = jnp.zeros(inner.shape, F32)
+        mean = jnp.zeros(inner.shape, F32)
+        for p in range(n_code):
+            scale = jnp.where(code_at[0] == p, scales[p], scale)
+            mean = jnp.where(code_at[0] == p, means[p], mean)
+        offset = mean - inner
+        for g in range(n_code):
+            part = slice(g * rows, (g + 1) * rows)
+            at = slice(4 * g, 4 * g + 1)
+            token = scale[:, at] * (tokens[part].astype(F32) / SOFTMAX_HEAT)
+            upper[part] = scale[:, at] * grad_out[part].astype(F32) + offset[:, at] * token
+            lower[part] = token
+        operands[:, :n_tokens] = upper[...].T.astype(BF16)
+        operands[:, n_tokens:] = lower[...].T.astype(BF16)
+
+    def send(t):
+        return pltpu.make_async_copy(
+            result.at[t], out.at[pl.ds(t * width, width)], out_sem.at[t]
+        )
+
+    wide = min(WIDE, width)
+    steps = [(t, slice(c, c + wide)) for t in range(tiles) for c in range(0, width, wide)]
+
+    def product(step):
+        t, c = step
+        if c.start == 0:
+            for copy in fetch(t):
+                copy.wait()
+            if t + AHEAD < tiles:
+                start(t + AHEAD)
+        return dot(operands[...], both_in[t, :, c])
+
+    ahead = product(steps[0])
+    for k, (t, c) in enumerate(steps):
+        value = ahead
+        if k + 1 < len(steps):
+            ahead = product(steps[k + 1])
+        result[t, c] = value.astype(BF16).T
         if c.stop == width:
             send(t).start()
     for t in range(tiles):
@@ -407,14 +424,15 @@
     lanes = stat_lanes(n_code)
     products = 2 * n_tokens * n_codes * dim
 
-    codes, sent = pl.pallas_call(
+    codes, sent, means = pl.pallas_call(
         functools.partial(forward_kernel, n_code),
         out_shape=(
             pltpu.HBM((tiles, n_tokens, width), BF16),
             jax.ShapeDtypeStruct((n_code, rows, 2 * dim + lanes), BF16),
+            jax.ShapeDtypeStruct((n_tokens, 128), F32),
         ),
         in_specs=[ANY, ANY, ANY, ANY],
-        out_specs=(ANY, VMEM),
+        out_specs=(ANY, VMEM, VMEM),
         scratch_shapes=[
             pltpu.VMEM((2 * n_tokens, dim), BF16),
             pltpu.VMEM((tiles, width, dim), BF16),
@@ -437,27 +455,26 @@
     )(tokens, grad_out, codebook, noise)
 
     received = lax.all_to_all(sent, "code", 0, 0, tiled=True)
-    turned, turned_grad = pl.pallas_call(
-        turn_kernel,
-        out_shape=(
-            pltpu.HBM((n_codes, n_tokens), BF16),
-            jax.ShapeDtypeStruct((dim, n_tokens), BF16),
-        ),
-        in_specs=[VMEM, ANY],
-        out_specs=(ANY, VMEM),
+    weighed = pl.pallas_call(
+        weigh_kernel,
+        out_shape=pltpu.HBM((tiles, n_tokens, width), BF16),
+        in_specs=[VMEM, ANY, ANY, VMEM],
+        out_specs=ANY,
         scratch_shapes=[
+            pltpu.VMEM((tiles, width, dim), BF16),
             pltpu.VMEM((tiles, n_tokens, width), BF16),
-            pltpu.VMEM((tiles, width, n_tokens), BF16),
+            pltpu.VMEM((tiles, n_tokens, width), BF16),
+            pltpu.SemaphoreType.DMA((tiles,)),
             pltpu.SemaphoreType.DMA((tiles,)),
             pltpu.SemaphoreType.DMA((tiles,)),
         ],
         compiler_params=FULL,
         cost_estimate=pl.CostEstimate(
-            flops=0, bytes_accessed=4 * n_tokens * n_codes, transcendentals=0
+            flops=products, bytes_accessed=20 * MIB, transcendentals=0
         ),
-        name="turn",
-    )(grad_out, codes)
-    received, turned, turned_grad = lax.optimization_barrier((received, turned, turned_grad))
+        name="weigh",
+    )(grad_out, codebook, codes, means)
+    received, weighed = lax.optimization_barrier((received, weighed))
     code_at = lax.axis_index("code")
     spread = pl.pallas_call(
         merge_kernel,
@@ -483,11 +500,9 @@
 
     block_tiles = block // width
     streams = [
+        pltpu.VMEM((block_tiles, 2 * n_tokens, width), BF16),
         pltpu.VMEM((block_tiles, width, dim), BF16),
-        pltpu.VMEM((block_tiles, width, n_tokens), BF16),
-        pltpu.VMEM((block_tiles, width, dim), BF16),
-        pltpu.SemaphoreType.DMA((block_tiles,)),
-        pltpu.SemaphoreType.DMA((block_tiles,)),
+        pltpu.SemaphoreType.DMA((2, block_tiles)),
         pltpu.SemaphoreType.DMA((block_tiles,)),
     ]
     block_shape = jax.ShapeDtypeStruct((block, dim), BF16)
@@ -496,33 +511,30 @@
         cost_estimate=pl.CostEstimate(flops=1, bytes_accessed=1, transcendentals=0),
     )
     dp_at = lax.axis_index("dp")
-    first, operands, inners = pl.pallas_call(
+    first, operands = pl.pallas_call(
         functools.partial(backward_kernel, False),
-        out_shape=(
-            block_shape,
-            jax.ShapeDtypeStruct((2, n_tokens, dim), BF16),
-            jax.ShapeDtypeStruct((8, n_tokens), F32),
-        ),
-        in_specs=[SMEM, SMEM, VMEM, VMEM, VMEM, ANY, ANY, VMEM],
-        out_specs=(ANY, VMEM, VMEM),
-        scratch_shapes=[pltpu.VMEM((n_tokens, 128), F32)] + streams,
+        out_shape=(block_shape, jax.ShapeDtypeStruct((dim, 2 * n_tokens), BF16)),
+        in_specs=[SMEM, SMEM, VMEM, VMEM, ANY, ANY, VMEM],
+        out_specs=(ANY, VMEM),
+        scratch_shapes=[
+            pltpu.VMEM((n_tokens, dim), F32), pltpu.VMEM((n_tokens, dim), F32),
+        ] + streams,
         name="backward_first",
         **common,
     )(
-        (dp_at ^ (n_dp - 1))[None], code_at[None], tokens, grad_out, turned_grad, codebook,
-        turned, received,
+        (dp_at ^ (n_dp - 1))[None], code_at[None], tokens, grad_out, codes, weighed, received
     )
 
     def backward(at):
         return pl.pallas_call(
             functools.partial(backward_kernel, True),
             out_shape=block_shape,
-            in_specs=[SMEM, VMEM, ANY, ANY, VMEM, VMEM],
+            in_specs=[SMEM, ANY, ANY, VMEM],
             out_specs=ANY,
             scratch_shapes=streams,
             name="backward",
             **common,
-        )(at[None], turned_grad, codebook, turned, operands, inners)
+        )(at[None], codes, weighed, operands)
 
     blocks = [swap(first, "dp", n_dp, n_dp - 1)]
     blocks += [swap(backward(dp_at ^ d), "dp", n_dp, d) for d in range(1, n_dp - 1)]

time: 87.7 us -> 85.1 us (0.970)
  Pallas kernels: 63.9 us -> 62.5 us
  waiting for transfers between devices: 8.64 us -> 7.31 us
    all_to_all x1, waiting for transfers between devices: 8.63 us -> 7.3 us  [local(): received = lax.all_to_all(sent, 'code', 0, 0, tiled=True)]
    pallas_call x1, Pallas kernels: 8.79 us -> 10.1 us  [local(): pl.pallas_call(weigh_kernel, out_shape=pltpu.HBM((tiles, n_tokens, width)...]
    pallas_call x1, Pallas kernels: 9.15 us -> 8.06 us  [local(): pl.pallas_call(functools.partial(backward_kernel, False), out_shape=(bloc...]
    pallas_call x1, Pallas kernels: 7.93 us -> 6.84 us  [backward(): pl.pallas_call(functools.partial(backward_kernel, True), out_shape=block_...]
where the time goes in v10:
time: 85.1 us; the launch traced here: 84.4 us
  Pallas kernels  62.5 us (73%)
  starting transfers between devices  12.8 us (15%)
  waiting for transfers between devices  7.31 us (9%)
  local copies, waits for them, and re-layouts  0.93 us (1%)
  between operations  0.88 us (1%)
    pallas_call x1, Pallas kernels, local(): pl.pallas_call(functools.partial(forward_kernel, n_code), out_shape=(pltp...  31.8 us
    pallas_call x1, Pallas kernels, local(): pl.pallas_call(weigh_kernel, out_shape=pltpu.HBM((tiles, n_tokens, width)...  10.1 us
    all_to_all x1, starting transfers between devices, local(): received = lax.all_to_all(sent, 'code', 0, 0, tiled=True)  8.33 us
    pallas_call x1, Pallas kernels, local(): pl.pallas_call(functools.partial(backward_kernel, False), out_shape=(bloc...  8.06 us
    all_to_all x1, waiting for transfers between devices, local(): received = lax.all_to_all(sent, 'code', 0, 0, tiled=True)  7.3 us
    pallas_call x1, Pallas kernels, backward(): pl.pallas_call(functools.partial(backward_kernel, True), out_shape=block_...  6.84 us
    all_to_all x1, starting transfers between devices, local(): gathered = lax.all_to_all(spread, 'code', 0, 0, tiled=True)  4.42 us
    pallas_call x1, Pallas kernels, local(): pl.pallas_call(functools.partial(add_kernel, n_dp), out_shape=jax.ShapeDt...  3.21 us
  transfers between devices with their start and end apart: 3, of which 1 were waited for; matrix products, arithmetic and copies ran while one was open for 0% of the time, Pallas kernels for 31%

profile of v10, /device:TPU:0, one launch (start us, length us, event | category | flops | bytes accessed | tf_op | source)
XLA Modules:
  0.0 84.4 jit_solution(7883072101084213316)
XLA Ops:
  0.6 31.8 %forward.1 = (bf16[8,512,1024]{2,1,0:T(8,128)(2,1)}, bf16[16,32,640]{2,1,0:T(8,128)(2,1)}, f32[512,128]{1,0:T(8,128)}) custom-call(bf16[512,256]{1,0:T(8,128)(2,1)} %rest_1_.1, bf16[512,256]{1,0:T(8,128)(2,1)} %rest_2_.1, bf16[8192,256]{1,0:T(8,128)(2,1)} %codebook.3, bf16[512,8192]{1,0:T(8,128)(2,1)} %noise.1), custom_call_target="tpu_custom_call" | custom-call | flops 8589934592 | bytes 25165824 | tf_op jit(solution)/shard_map/forward/pallas_call | solution.py:427
  32.5 8.3 %all-to-all-start = ((bf16[16,32,640]{2,1,0:T(8,128)(2,1)}), bf16[16,32,640]{2,1,0:T(8,128)(2,1)S(1)}, u32[]{:S(2)}, u32[]{:S(2)}) async-start(bf16[16,32,640]{2,1,0:T(8,128)(2,1)} %get-tuple-element.14), calls=%async_computation | async-start | bytes 1310720 | tf_op jit(solution)/shard_map/all_to_all | solution.py:457
  40.8 10.1 %weigh.1.rest_4_.rest_1_ = bf16[8,512,1024]{2,1,0:T(8,128)(2,1)} custom-call(bf16[512,256]{1,0:T(8,128)(2,1)} %rest_2_.1, bf16[8192,256]{1,0:T(8,128)(2,1)} %codebook.3, bf16[8,512,1024]{2,1,0:T(8,128)(2,1)} %get-tuple-element.15.codes.rest_3_.rest_0_, f32[512,128]{1,0:T(8,128)} %get-tuple-element.16.means), custom_call_target="tpu_custom_call" | custom-call | flops 2147483648 | bytes 20971520 | tf_op jit(solution)/shard_map/weigh/pallas_call | solution.py:458
  50.9 7.3 %all-to-all-done.received.rest_5_ = bf16[16,32,640]{2,1,0:T(8,128)(2,1)S(1)} async-done(((bf16[16,32,640]{2,1,0:T(8,128)(2,1)}), bf16[16,32,640]{2,1,0:T(8,128)(2,1)S(1)}, u32[]{:S(2)}, u32[]{:S(2)}) %all-to-all-start) | async-done | bytes 655392 | tf_op jit(solution)/shard_map/all_to_all | solution.py:457
  58.2 0.0 copy-start.1
  58.2 1.4 %merge.1 = bf16[16,32,512]{2,1,0:T(8,128)(2,1)} custom-call(s32[1]{0:T(128)} %bitcast.me.rest_0_, bf16[16,32,640]{2,1,0:T(8,128)(2,1)S(1)} %all-to-all-done.received.rest_5_), custom_call_target="tpu_custom_call" | custom-call | tf_op jit(solution)/shard_map/merge/pallas_call | solution.py:479
  59.6 4.4 %all-to-all-start.1 = ((bf16[16,32,512]{2,1,0:T(8,128)(2,1)}), bf16[16,32,512]{2,1,0:T(8,128)(2,1)S(1)}, u32[]{:S(2)}, u32[]{:S(2)}) async-start(bf16[16,32,512]{2,1,0:T(8,128)(2,1)} %merge.1), calls=%async_computation.1 | async-start | bytes 1048576 | tf_op jit(solution)/shard_map/all_to_all | solution.py:488
  64.0 0.0 copy-done.1
  64.0 8.1 %backward_first.1 = (bf16[4096,256]{1,0:T(8,128)(2,1)}, bf16[256,1024]{1,0:T(8,128)(2,1)}) custom-call(s32[1]{0:T(128)} %bitcast.1.block, s32[1]{0:T(128)} %bitcast.me.rest_0_, bf16[512,256]{1,0:T(8,128)(2,1)} %rest_1_.1, bf16[512,256]{1,0:T(8,128)(2,1)} %rest_2_.1, bf16[8,512,1024]{2,1,0:T(8,128)(2,1)} %get-tuple-element.15.codes.rest_3_.rest_0_, ...), custom_call_target="tpu_custom_call" | custom-call | flops 1 | bytes 1 | tf_op jit(solution)/shard_map/backward_first/pallas_call | solution.py:514
  72.1 0.1 collective-permute-start
  72.2 6.8 %backward.1.refs_1_ = bf16[4096,256]{1,0:T(8,128)(2,1)} custom-call(s32[1]{0:T(128)} %bitcast.2.block, bf16[8,512,1024]{2,1,0:T(8,128)(2,1)} %get-tuple-element.15.codes.rest_3_.rest_0_, bf16[8,512,1024]{2,1,0:T(8,128)(2,1)} %weigh.1.rest_4_.rest_1_, bf16[256,1024]{1,0:T(8,128)(2,1)} %get-tuple-element.24.rest_2_), custom_call_target="tpu_custom_call" | custom-call | flops 1 | bytes 1 | tf_op jit(solution)/shard_map/backward/pallas_call | solution.py:529
  79.0 0.0 all-to-all-done.1.gathered
  79.0 0.0 copy-start
  79.1 1.0 %unpack.1 = (f32[512,256]{1,0:T(8,128)}, f32[512,256]{1,0:T(8,128)}) custom-call(bf16[16,32,512]{2,1,0:T(8,128)(2,1)S(1)} %all-to-all-done.1.gathered), custom_call_target="tpu_custom_call" | custom-call | flops 214748364800 | bytes 419430400 | tf_op jit(solution)/shard_map/unpack/pallas_call | solution.py:489
  80.1 0.0 collective-permute-done.refs_0_
  80.1 0.9 %copy-done = bf16[4096,256]{1,0:T(8,128)(2,1)S(1)} copy-done((bf16[4096,256]{1,0:T(8,128)(2,1)S(1)}, bf16[4096,256]{1,0:T(8,128)(2,1)}, u32[]{:S(2)}) %copy-start) | copy-done | bytes 2097176
  81.0 3.2 %add.1 = f32[4096,256]{1,0:T(8,128)} custom-call(bf16[4096,256]{1,0:T(8,128)(2,1)} %collective-permute-done.refs_0_, bf16[4096,256]{1,0:T(8,128)(2,1)S(1)} %copy-done), custom_call_target="tpu_custom_call" | custom-call | bytes 8388608 | tf_op jit(solution)/shard_map/add/pallas_call | solution.py:543
Async XLA Ops:
  32.5 25.8 %all-to-all-start = ((bf16[16,32,640]{2,1,0:T(8,128)(2,1)}), bf16[16,32,640]{2,1,0:T(8,128)(2,1)S(1)}, u32[]{:S(2)}, u32[]{:S(2)}) async-start(bf16[16,32,640]{2,1,0:T(8,128)(2,1)} %get-tuple-element.14), calls=%async_computation | async-start | bytes 1310720 | tf_op jit(solution)/shard_map/all_to_all | solution.py:457
  58.2 5.8 %copy-start.1 = (bf16[16,32,640]{2,1,0:T(8,128)(2,1)}, bf16[16,32,640]{2,1,0:T(8,128)(2,1)S(1)}, u32[]{:S(2)}) copy-start(bf16[16,32,640]{2,1,0:T(8,128)(2,1)S(1)} %all-to-all-done.received.rest_5_) | copy-start | bytes 1966084
  59.6 19.4 %all-to-all-start.1 = ((bf16[16,32,512]{2,1,0:T(8,128)(2,1)}), bf16[16,32,512]{2,1,0:T(8,128)(2,1)S(1)}, u32[]{:S(2)}, u32[]{:S(2)}) async-start(bf16[16,32,512]{2,1,0:T(8,128)(2,1)} %merge.1), calls=%async_computation.1 | async-start | bytes 1048576 | tf_op jit(solution)/shard_map/all_to_all | solution.py:488
  72.1 8.0 %collective-permute-start = (bf16[4096,256]{1,0:T(8,128)(2,1)}, bf16[4096,256]{1,0:T(8,128)(2,1)}, u32[]{:S(2)}, u32[]{:S(2)}) collective-permute-start(bf16[4096,256]{1,0:T(8,128)(2,1)} %get-tuple-element.23), channel_id=1, source_target_pairs={{0,16},{16,0},{1,17},{17,1},{2,18},{18,2},{3,19},{19,3},{4,20},{20... | collective-permute-start | bytes 6291464 | tf_op jit(solution)/shard_map/ppermute | solution.py:414
  79.0 2.0 %copy-start = (bf16[4096,256]{1,0:T(8,128)(2,1)S(1)}, bf16[4096,256]{1,0:T(8,128)(2,1)}, u32[]{:S(2)}) copy-start(bf16[4096,256]{1,0:T(8,128)(2,1)} %backward.1.refs_1_) | copy-start | bytes 6291460

commit v11 on v10

--- a/solution.py
+++ b/solution.py
@@ -15,6 +15,7 @@
 CHUNK = 256
 WIDE = 512
 AHEAD = 2
+NEAR = 3
 ROWS = 64
 LARGEST = 2.0**60
 VMEM = pl.BlockSpec(memory_space=pltpu.VMEM)
@@ -49,8 +50,9 @@
     pair, book, noise_in, slot_a, slot_b, shifts, total, sums,
     pair_sem, book_sem, noise_sem, code_sem,
 ):
-    tiles, n_tokens, width = codes.shape
-    dim = tokens.shape[1]
+    tiles, width, dim = book.shape
+    n_tokens = tokens.shape[0]
+    wide = codes.shape[2]
     columns = [slice(c, c + CHUNK) for c in range(0, width, CHUNK)]
     slots = (slot_a, slot_b)
 
@@ -79,11 +81,9 @@
                     pair_sem.at[len(pair_copies)],
                 )
             )
-    start(0)
     for copy in pair_copies:
         copy.start()
-    for t in range(1, min(AHEAD + 1, tiles)):
-        start(t)
+    start(0)
 
     def logits(both, t, r, c):
         noise_part = (noise_in[t, r : r + ROWS, c] * BF16(SHARPNESS)).astype(F32)
@@ -99,9 +99,18 @@
                 )
 
     def store(t, s):
-        return pltpu.make_async_copy(
-            slots[s].at[pl.ds(0, n_tokens)], codes.at[t], code_sem.at[s]
-        )
+        return [
+            pltpu.make_async_copy(
+                slots[s].at[pl.ds(0, n_tokens), pl.ds(j * wide, wide)],
+                codes.at[t * (width // wide) + j],
+                code_sem.at[s, j],
+            )
+            for j in range(width // wide)
+        ]
+
+    def stored(t, s):
+        for copy in store(t, s):
+            copy.wait()
 
     def soften(t, s, fresh, last=None):
         if fresh is not None:
@@ -129,7 +138,8 @@
                 slot[at, c] = weight.astype(BF16)
                 gradient = both[2 * r + ROWS : 2 * r + 2 * ROWS]
                 slot[n_tokens + r : n_tokens + r + ROWS, c] = (weight * gradient).astype(BF16)
-        store(t, s).start()
+        for copy in store(t, s):
+            copy.start()
 
     def accumulate(t, s):
         sums[...] += dot(slots[s][...], book[t])
@@ -141,10 +151,13 @@
 
         @pl.when(fresh)
         def _():
-            raise_shift(0, columns[:2])
+            raise_shift(0, columns[:1])
 
         @pl.when(jnp.logical_not(fresh))
         def _():
+            stored(tiles - 2, 0)
+            stored(tiles - 1, 1)
+
             def over(t, carry):
                 raise_shift(t, columns)
                 return carry
@@ -160,20 +173,18 @@
         def soften_pair(i, carry):
             @pl.when(i > 0)
             def _():
-                store(2 * i - 1, 1).wait()
+                stored(2 * i - 1, 1)
 
             soften(2 * i + 1, 1, fresh, lambda: accumulate(2 * i, 0))
-            store(2 * i, 0).wait()
+            stored(2 * i, 0)
             soften(2 * i + 2, 0, fresh, lambda: accumulate(2 * i + 1, 1))
             return carry
 
         lax.fori_loop(0, tiles // 2 - 1, soften_pair, 0)
         if tiles > 2:
-            store(tiles - 3, 1).wait()
+            stored(tiles - 3, 1)
         soften(tiles - 1, 1, fresh, lambda: accumulate(tiles - 2, 0))
         accumulate(tiles - 1, 1)
-        store(tiles - 2, 0).wait()
-        store(tiles - 1, 1).wait()
         fits = jnp.max(total[...]) < LARGEST
         return again + 1, jnp.logical_and(fresh, jnp.logical_not(fits))
 
@@ -182,6 +193,8 @@
     for r in range(0, n_tokens, ROWS):
         pair[2 * r : 2 * r + ROWS] = pair[2 * r : 2 * r + ROWS] * BF16(SHARPNESS)
     arrive(0)
+    for t in range(1, min(AHEAD + 1, tiles)):
+        start(t)
     lax.while_loop(lambda state: state[1], attempt, (jnp.int32(0), jnp.bool_(True)))
 
     shift = shifts[:, :1]
@@ -211,6 +224,8 @@
         sent[g, :, :dim] = mix[at].astype(BF16)
         sent[g, :, dim : 2 * dim] = (pulled[at] - mean[at] * mix[at]).astype(BF16)
         sent[g, :, 2 * dim :] = stats
+    stored(tiles - 2, 0)
+    stored(tiles - 1, 1)
 
 
 def roll_left(value, by):
@@ -281,11 +296,11 @@
         if c.start == 0:
             for copy in fetch(t):
                 copy.wait()
-            if t + AHEAD < tiles:
-                start(t + AHEAD)
+            if t + NEAR < tiles:
+                start(t + NEAR)
         return dot(grad_out[...], book[t, c], 1, 1)
 
-    for t in range(min(AHEAD, tiles)):
+    for t in range(min(NEAR, tiles)):
         start(t)
     ahead = gradient_of(steps[0])
     for k, (t, c) in enumerate(steps):
@@ -324,7 +339,7 @@
         for copy in fetch(t):
             copy.start()
 
-    for t in range(min(AHEAD, tiles)):
+    for t in range(min(NEAR, tiles)):
         start(t)
 
     if not prepared:
@@ -358,8 +373,8 @@
         if c.start == 0:
             for copy in fetch(t):
                 copy.wait()
-            if t + AHEAD < tiles:
-                start(t + AHEAD)
+            if t + NEAR < tiles:
+                start(t + NEAR)
         return dot(operands[...], both_in[t, :, c])
 
     ahead = product(steps[0])
@@ -420,6 +435,8 @@
     rows = n_tokens // n_code
     block = n_codes // n_dp
     width = min(1024, block)
+    wide = min(WIDE, width)
+    tiles_in = n_codes // wide
     tiles = n_codes // width
     lanes = stat_lanes(n_code)
     products = 2 * n_tokens * n_codes * dim
@@ -427,7 +444,7 @@
     codes, sent, means = pl.pallas_call(
         functools.partial(forward_kernel, n_code),
         out_shape=(
-            pltpu.HBM((tiles, n_tokens, width), BF16),
+            pltpu.HBM((n_codes // wide, n_tokens, wide), BF16),
             jax.ShapeDtypeStruct((n_code, rows, 2 * dim + lanes), BF16),
             jax.ShapeDtypeStruct((n_tokens, 128), F32),
         ),
@@ -445,7 +462,7 @@
             pltpu.SemaphoreType.DMA((2 * n_tokens // ROWS,)),
             pltpu.SemaphoreType.DMA((tiles,)),
             pltpu.SemaphoreType.DMA((tiles,)),
-            pltpu.SemaphoreType.DMA((2,)),
+            pltpu.SemaphoreType.DMA((2, width // wide)),
         ],
         compiler_params=FULL,
         cost_estimate=pl.CostEstimate(
@@ -457,16 +474,16 @@
     received = lax.all_to_all(sent, "code", 0, 0, tiled=True)
     weighed = pl.pallas_call(
         weigh_kernel,
-        out_shape=pltpu.HBM((tiles, n_tokens, width), BF16),
+        out_shape=pltpu.HBM((tiles_in, n_tokens, wide), BF16),
         in_specs=[VMEM, ANY, ANY, VMEM],
         out_specs=ANY,
         scratch_shapes=[
-            pltpu.VMEM((tiles, width, dim), BF16),
-            pltpu.VMEM((tiles, n_tokens, width), BF16),
-            pltpu.VMEM((tiles, n_tokens, width), BF16),
-            pltpu.SemaphoreType.DMA((tiles,)),
-            pltpu.SemaphoreType.DMA((tiles,)),
-            pltpu.SemaphoreType.DMA((tiles,)),
+            pltpu.VMEM((tiles_in, wide, dim), BF16),
+            pltpu.VMEM((tiles_in, n_tokens, wide), BF16),
+            pltpu.VMEM((tiles_in, n_tokens, wide), BF16),
+            pltpu.SemaphoreType.DMA((tiles_in,)),
+            pltpu.SemaphoreType.DMA((tiles_in,)),
+            pltpu.SemaphoreType.DMA((tiles_in,)),
         ],
         compiler_params=FULL,
         cost_estimate=pl.CostEstimate(
@@ -498,10 +515,10 @@
         name="unpack",
     )(gathered)
 
-    block_tiles = block // width
+    block_tiles = block // wide
     streams = [
-        pltpu.VMEM((block_tiles, 2 * n_tokens, width), BF16),
-        pltpu.VMEM((block_tiles, width, dim), BF16),
+        pltpu.VMEM((block_tiles, 2 * n_tokens, wide), BF16),
+        pltpu.VMEM((block_tiles, wide, dim), BF16),
         pltpu.SemaphoreType.DMA((2, block_tiles)),
         pltpu.SemaphoreType.DMA((block_tiles,)),
     ]

time: 85.1 us -> 84.3 us (level)
  waiting for transfers between devices: 7.31 us -> 5.57 us
  Pallas kernels: 62.5 us -> 63.4 us
    all_to_all x1, waiting for transfers between devices: 7.3 us -> 5.57 us  [local(): received = lax.all_to_all(sent, 'code', 0, 0, tiled=True)]
    pallas_call x1, Pallas kernels: 10.1 us -> 11.8 us  [local(): pl.pallas_call(weigh_kernel, out_shape=pltpu.HBM((tiles_in, n_tokens, wid...]
  transfers between devices with their start and end apart: 3 -> 3, of which waited for: 1 -> 1; matrix products, arithmetic and copies ran while one was open for 0% -> 0% of each run, Pallas kernels for 31% -> 33%
where the time goes in v11:
time: 84.3 us; the launch traced here: 83.6 us
  Pallas kernels  63.4 us (75%)
  starting transfers between devices  12.8 us (15%)
  waiting for transfers between devices  5.57 us (7%)
  local copies, waits for them, and re-layouts  0.93 us (1%)
  between operations  0.9 us (1%)
    pallas_call x1, Pallas kernels, local(): pl.pallas_call(functools.partial(forward_kernel, n_code), out_shape=(pltp...  31.1 us
    pallas_call x1, Pallas kernels, local(): pl.pallas_call(weigh_kernel, out_shape=pltpu.HBM((tiles_in, n_tokens, wid...  11.8 us
    all_to_all x1, starting transfers between devices, local(): received = lax.all_to_all(sent, 'code', 0, 0, tiled=True)  8.32 us
    pallas_call x1, Pallas kernels, local(): pl.pallas_call(functools.partial(backward_kernel, False), out_shape=(bloc...  8.03 us
    pallas_call x1, Pallas kernels, backward(): pl.pallas_call(functools.partial(backward_kernel, True), out_shape=block_...  6.81 us
    all_to_all x1, waiting for transfers between devices, local(): received = lax.all_to_all(sent, 'code', 0, 0, tiled=True)  5.57 us
    all_to_all x1, starting transfers between devices, local(): gathered = lax.all_to_all(spread, 'code', 0, 0, tiled=True)  4.43 us
    pallas_call x1, Pallas kernels, local(): pl.pallas_call(functools.partial(add_kernel, n_dp), out_shape=jax.ShapeDt...  3.21 us
  transfers between devices with their start and end apart: 3, of which 1 were waited for; matrix products, arithmetic and copies ran while one was open for 0% of the time, Pallas kernels for 33%

profile of v11, /device:TPU:0, one launch (start us, length us, event | category | flops | bytes accessed | tf_op | source)
XLA Modules:
  0.0 83.6 jit_solution(12498674814670272276)
XLA Ops:
  0.6 31.1 %forward.1 = (bf16[16,512,512]{2,1,0:T(8,128)(2,1)}, bf16[16,32,640]{2,1,0:T(8,128)(2,1)}, f32[512,128]{1,0:T(8,128)}) custom-call(bf16[512,256]{1,0:T(8,128)(2,1)} %rest_1_.1, bf16[512,256]{1,0:T(8,128)(2,1)} %rest_2_.1, bf16[8192,256]{1,0:T(8,128)(2,1)} %codebook.3, bf16[512,8192]{1,0:T(8,128)(2,1)} %noise.1), custom_call_target="tpu_custom_call" | custom-call | flops 8589934592 | bytes 25165824 | tf_op jit(solution)/shard_map/forward/pallas_call | solution.py:444
  31.8 8.3 %all-to-all-start = ((bf16[16,32,640]{2,1,0:T(8,128)(2,1)}), bf16[16,32,640]{2,1,0:T(8,128)(2,1)S(1)}, u32[]{:S(2)}, u32[]{:S(2)}) async-start(bf16[16,32,640]{2,1,0:T(8,128)(2,1)} %get-tuple-element.14), calls=%async_computation | async-start | bytes 1310720 | tf_op jit(solution)/shard_map/all_to_all | solution.py:474
  40.1 11.8 %weigh.1.rest_4_.rest_1_ = bf16[16,512,512]{2,1,0:T(8,128)(2,1)} custom-call(bf16[512,256]{1,0:T(8,128)(2,1)} %rest_2_.1, bf16[8192,256]{1,0:T(8,128)(2,1)} %codebook.3, bf16[16,512,512]{2,1,0:T(8,128)(2,1)} %get-tuple-element.15.codes.rest_3_.rest_0_, f32[512,128]{1,0:T(8,128)} %get-tuple-element.16.means), custom_call_target="tpu_custom_call" | custom-call | flops 2147483648 | bytes 20971520 | tf_op jit(solution)/shard_map/weigh/pallas_call | solution.py:475
  51.9 5.6 %all-to-all-done.received.rest_5_ = bf16[16,32,640]{2,1,0:T(8,128)(2,1)S(1)} async-done(((bf16[16,32,640]{2,1,0:T(8,128)(2,1)}), bf16[16,32,640]{2,1,0:T(8,128)(2,1)S(1)}, u32[]{:S(2)}, u32[]{:S(2)}) %all-to-all-start) | async-done | bytes 655392 | tf_op jit(solution)/shard_map/all_to_all | solution.py:474
  57.5 0.0 copy-start.1
  57.5 1.4 %merge.1 = bf16[16,32,512]{2,1,0:T(8,128)(2,1)} custom-call(s32[1]{0:T(128)} %bitcast.me.rest_0_, bf16[16,32,640]{2,1,0:T(8,128)(2,1)S(1)} %all-to-all-done.received.rest_5_), custom_call_target="tpu_custom_call" | custom-call | tf_op jit(solution)/shard_map/merge/pallas_call | solution.py:496
  58.9 4.4 %all-to-all-start.1 = ((bf16[16,32,512]{2,1,0:T(8,128)(2,1)}), bf16[16,32,512]{2,1,0:T(8,128)(2,1)S(1)}, u32[]{:S(2)}, u32[]{:S(2)}) async-start(bf16[16,32,512]{2,1,0:T(8,128)(2,1)} %merge.1), calls=%async_computation.1 | async-start | bytes 1048576 | tf_op jit(solution)/shard_map/all_to_all | solution.py:505
  63.3 0.0 copy-done.1
  63.3 8.0 %backward_first.1 = (bf16[4096,256]{1,0:T(8,128)(2,1)}, bf16[256,1024]{1,0:T(8,128)(2,1)}) custom-call(s32[1]{0:T(128)} %bitcast.1.block, s32[1]{0:T(128)} %bitcast.me.rest_0_, bf16[512,256]{1,0:T(8,128)(2,1)} %rest_1_.1, bf16[512,256]{1,0:T(8,128)(2,1)} %rest_2_.1, bf16[16,512,512]{2,1,0:T(8,128)(2,1)} %get-tuple-element.15.codes.rest_3_.rest_0_, ...), custom_call_target="tpu_custom_call" | custom-call | flops 1 | bytes 1 | tf_op jit(solution)/shard_map/backward_first/pallas_call | solution.py:531
  71.3 0.1 collective-permute-start
  71.4 6.8 %backward.1.refs_1_ = bf16[4096,256]{1,0:T(8,128)(2,1)} custom-call(s32[1]{0:T(128)} %bitcast.2.block, bf16[16,512,512]{2,1,0:T(8,128)(2,1)} %get-tuple-element.15.codes.rest_3_.rest_0_, bf16[16,512,512]{2,1,0:T(8,128)(2,1)} %weigh.1.rest_4_.rest_1_, bf16[256,1024]{1,0:T(8,128)(2,1)} %get-tuple-element.24.rest_2_), custom_call_target="tpu_custom_call" | custom-call | flops 1 | bytes 1 | tf_op jit(solution)/shard_map/backward/pallas_call | solution.py:546
  78.2 0.0 all-to-all-done.1.gathered
  78.3 0.0 copy-start
  78.3 1.0 %unpack.1 = (f32[512,256]{1,0:T(8,128)}, f32[512,256]{1,0:T(8,128)}) custom-call(bf16[16,32,512]{2,1,0:T(8,128)(2,1)S(1)} %all-to-all-done.1.gathered), custom_call_target="tpu_custom_call" | custom-call | flops 214748364800 | bytes 419430400 | tf_op jit(solution)/shard_map/unpack/pallas_call | solution.py:506
  79.3 0.0 collective-permute-done.refs_0_
  79.3 0.9 %copy-done = bf16[4096,256]{1,0:T(8,128)(2,1)S(1)} copy-done((bf16[4096,256]{1,0:T(8,128)(2,1)S(1)}, bf16[4096,256]{1,0:T(8,128)(2,1)}, u32[]{:S(2)}) %copy-start) | copy-done | bytes 2097176
  80.2 3.2 %add.1 = f32[4096,256]{1,0:T(8,128)} custom-call(bf16[4096,256]{1,0:T(8,128)(2,1)} %collective-permute-done.refs_0_, bf16[4096,256]{1,0:T(8,128)(2,1)S(1)} %copy-done), custom_call_target="tpu_custom_call" | custom-call | bytes 8388608 | tf_op jit(solution)/shard_map/add/pallas_call | solution.py:560
Async XLA Ops:
  31.8 25.7 %all-to-all-start = ((bf16[16,32,640]{2,1,0:T(8,128)(2,1)}), bf16[16,32,640]{2,1,0:T(8,128)(2,1)S(1)}, u32[]{:S(2)}, u32[]{:S(2)}) async-start(bf16[16,32,640]{2,1,0:T(8,128)(2,1)} %get-tuple-element.14), calls=%async_computation | async-start | bytes 1310720 | tf_op jit(solution)/shard_map/all_to_all | solution.py:474
  57.5 5.8 %copy-start.1 = (bf16[16,32,640]{2,1,0:T(8,128)(2,1)}, bf16[16,32,640]{2,1,0:T(8,128)(2,1)S(1)}, u32[]{:S(2)}) copy-start(bf16[16,32,640]{2,1,0:T(8,128)(2,1)S(1)} %all-to-all-done.received.rest_5_) | copy-start | bytes 1966084
  58.9 19.4 %all-to-all-start.1 = ((bf16[16,32,512]{2,1,0:T(8,128)(2,1)}), bf16[16,32,512]{2,1,0:T(8,128)(2,1)S(1)}, u32[]{:S(2)}, u32[]{:S(2)}) async-start(bf16[16,32,512]{2,1,0:T(8,128)(2,1)} %merge.1), calls=%async_computation.1 | async-start | bytes 1048576 | tf_op jit(solution)/shard_map/all_to_all | solution.py:505
  71.3 8.0 %collective-permute-start = (bf16[4096,256]{1,0:T(8,128)(2,1)}, bf16[4096,256]{1,0:T(8,128)(2,1)}, u32[]{:S(2)}, u32[]{:S(2)}) collective-permute-start(bf16[4096,256]{1,0:T(8,128)(2,1)} %get-tuple-element.23), channel_id=1, source_target_pairs={{0,16},{16,0},{1,17},{17,1},{2,18},{18,2},{3,19},{19,3},{4,20},{20... | collective-permute-start | bytes 6291464 | tf_op jit(solution)/shard_map/ppermute | solution.py:429
  78.3 2.0 %copy-start = (bf16[4096,256]{1,0:T(8,128)(2,1)S(1)}, bf16[4096,256]{1,0:T(8,128)(2,1)}, u32[]{:S(2)}) copy-start(bf16[4096,256]{1,0:T(8,128)(2,1)} %backward.1.refs_1_) | copy-start | bytes 6291460

commit v12 on v11

--- a/solution.py
+++ b/solution.py
@@ -23,6 +23,7 @@
 ANY = pl.BlockSpec(memory_space=pl.ANY)
 FULL = pltpu.CompilerParams(vmem_limit_bytes=60 * MIB)
 MOST = pltpu.CompilerParams(vmem_limit_bytes=56 * MIB)
+PART = pltpu.CompilerParams(vmem_limit_bytes=58 * MIB)
 SOME = pltpu.CompilerParams(vmem_limit_bytes=24 * MIB)
 
 
@@ -46,13 +47,11 @@
 
 
 def forward_kernel(
-    n_code, tokens, grad_out, codebook, noise, codes, sent, means,
-    pair, book, noise_in, slot_a, slot_b, shifts, total, sums,
-    pair_sem, book_sem, noise_sem, code_sem,
+    n_code, tokens, grad_out, codebook, noise, sent, means, shifts,
+    pair, book, noise_in, slot_a, slot_b, total, sums, pair_sem, book_sem, noise_sem,
 ):
     tiles, width, dim = book.shape
     n_tokens = tokens.shape[0]
-    wide = codes.shape[2]
     columns = [slice(c, c + CHUNK) for c in range(0, width, CHUNK)]
     slots = (slot_a, slot_b)
 
@@ -97,20 +96,6 @@
                 shifts[at] = functools.reduce(
                     jnp.maximum, lane_groups(logits(both, t, r, c)), shifts[at]
                 )
-
-    def store(t, s):
-        return [
-            pltpu.make_async_copy(
-                slots[s].at[pl.ds(0, n_tokens), pl.ds(j * wide, wide)],
-                codes.at[t * (width // wide) + j],
-                code_sem.at[s, j],
-            )
-            for j in range(width // wide)
-        ]
-
-    def stored(t, s):
-        for copy in store(t, s):
-            copy.wait()
 
     def soften(t, s, fresh, last=None):
         if fresh is not None:
@@ -138,8 +123,6 @@
                 slot[at, c] = weight.astype(BF16)
                 gradient = both[2 * r + ROWS : 2 * r + 2 * ROWS]
                 slot[n_tokens + r : n_tokens + r + ROWS, c] = (weight * gradient).astype(BF16)
-        for copy in store(t, s):
-            copy.start()
 
     def accumulate(t, s):
         sums[...] += dot(slots[s][...], book[t])
@@ -155,9 +138,6 @@
 
         @pl.when(jnp.logical_not(fresh))
         def _():
-            stored(tiles - 2, 0)
-            stored(tiles - 1, 1)
-
             def over(t, carry):
                 raise_shift(t, columns)
                 return carry
@@ -171,18 +151,11 @@
         soften(0, 0, None)
 
         def soften_pair(i, carry):
-            @pl.when(i > 0)
-            def _():
-                stored(2 * i - 1, 1)
-
             soften(2 * i + 1, 1, fresh, lambda: accumulate(2 * i, 0))
-            stored(2 * i, 0)
             soften(2 * i + 2, 0, fresh, lambda: accumulate(2 * i + 1, 1))
             return carry
 
         lax.fori_loop(0, tiles // 2 - 1, soften_pair, 0)
-        if tiles > 2:
-            stored(tiles - 3, 1)
         soften(tiles - 1, 1, fresh, lambda: accumulate(tiles - 2, 0))
         accumulate(tiles - 1, 1)
         fits = jnp.max(total[...]) < LARGEST
@@ -224,8 +197,6 @@
         sent[g, :, :dim] = mix[at].astype(BF16)
         sent[g, :, dim : 2 * dim] = (pulled[at] - mean[at] * mix[at]).astype(BF16)
         sent[g, :, 2 * dim :] = stats
-    stored(tiles - 2, 0)
-    stored(tiles - 1, 1)
 
 
 def roll_left(value, by):
@@ -272,47 +243,59 @@
 
 
 def weigh_kernel(
-    grad_out, codebook, codes, means, weighed, book, code_in, result, book_sem, code_sem, out_sem
+    tokens, grad_out, codebook, noise, means, shifts, codes, weighed,
+    book, noise_in, code_out, weighed_out, sharp, book_sem, noise_sem, out_sem,
 ):
     tiles, width, _ = book.shape
-    steps = [(t, slice(c, c + WIDE)) for t in range(tiles) for c in range(0, width, WIDE)]
+    wide = codes.shape[2]
+    steps = [(t, slice(c, c + wide)) for t in range(tiles) for c in range(0, width, wide)]
 
     def fetch(t):
         at = pl.ds(t * width, width)
         return (
             pltpu.make_async_copy(codebook.at[at], book.at[t], book_sem.at[t]),
-            pltpu.make_async_copy(codes.at[t], code_in.at[t], code_sem.at[t]),
+            pltpu.make_async_copy(noise.at[:, at], noise_in.at[t], noise_sem.at[t]),
         )
 
     def start(t):
         for copy in fetch(t):
             copy.start()
 
-    def send(t):
-        return pltpu.make_async_copy(result.at[t], weighed.at[t], out_sem.at[t])
-
-    def gradient_of(step):
+    def send(k):
+        return (
+            pltpu.make_async_copy(code_out.at[k], codes.at[k], out_sem.at[0, k]),
+            pltpu.make_async_copy(weighed_out.at[k], weighed.at[k], out_sem.at[1, k]),
+        )
+
+    def products_of(step):
         t, c = step
         if c.start == 0:
             for copy in fetch(t):
                 copy.wait()
             if t + NEAR < tiles:
                 start(t + NEAR)
-        return dot(grad_out[...], book[t, c], 1, 1)
+        keys = book[t, c]
+        return dot(sharp[...], keys, 1, 1), dot(grad_out[...], keys, 1, 1)
 
     for t in range(min(NEAR, tiles)):
         start(t)
-    ahead = gradient_of(steps[0])
+    sharp[...] = tokens[...] * BF16(SHARPNESS)
+    ahead = products_of(steps[0])
     for k, (t, c) in enumerate(steps):
-        gradient = ahead
+        score, gradient = ahead
         if k + 1 < len(steps):
-            ahead = gradient_of(steps[k + 1])
-        mean = jnp.concatenate([means[...]] * (WIDE // 128), axis=1)
-        result[t, :, c] = (code_in[t, :, c].astype(F32) * (gradient - mean)).astype(BF16)
-        if c.stop == width:
-            send(t).start()
-    for t in range(tiles):
-        send(t).wait()
+            ahead = products_of(steps[k + 1])
+        shift = jnp.concatenate([shifts[...]] * (wide // 128), axis=1)
+        mean = jnp.concatenate([means[...]] * (wide // 128), axis=1)
+        noise_part = (noise_in[t, :, c] * BF16(SHARPNESS)).astype(F32)
+        code = jnp.exp(score + noise_part - shift).astype(BF16)
+        code_out[k] = code
+        weighed_out[k] = (code.astype(F32) * (gradient - mean)).astype(BF16)
+        for copy in send(k):
+            copy.start()
+    for k in range(len(steps)):
+        for copy in send(k):
+            copy.wait()
 
 
 def backward_kernel(prepared, block, *rest):
@@ -441,15 +424,15 @@
     lanes = stat_lanes(n_code)
     products = 2 * n_tokens * n_codes * dim
 
-    codes, sent, means = pl.pallas_call(
+    sent, means, shifts = pl.pallas_call(
         functools.partial(forward_kernel, n_code),
         out_shape=(
-            pltpu.HBM((n_codes // wide, n_tokens, wide), BF16),
             jax.ShapeDtypeStruct((n_code, rows, 2 * dim + lanes), BF16),
+            jax.ShapeDtypeStruct((n_tokens, 128), F32),
             jax.ShapeDtypeStruct((n_tokens, 128), F32),
         ),
         in_specs=[ANY, ANY, ANY, ANY],
-        out_specs=(ANY, VMEM, VMEM),
+        out_specs=(VMEM, VMEM, VMEM),
         scratch_shapes=[
             pltpu.VMEM((2 * n_tokens, dim), BF16),
             pltpu.VMEM((tiles, width, dim), BF16),
@@ -457,40 +440,40 @@
             pltpu.VMEM((2 * n_tokens, width), BF16),
             pltpu.VMEM((2 * n_tokens, width), BF16),
             pltpu.VMEM((n_tokens, 128), F32),
-            pltpu.VMEM((n_tokens, 128), F32),
             pltpu.VMEM((2 * n_tokens, dim), F32),
             pltpu.SemaphoreType.DMA((2 * n_tokens // ROWS,)),
             pltpu.SemaphoreType.DMA((tiles,)),
             pltpu.SemaphoreType.DMA((tiles,)),
-            pltpu.SemaphoreType.DMA((2, width // wide)),
         ],
         compiler_params=FULL,
         cost_estimate=pl.CostEstimate(
-            flops=4 * products, bytes_accessed=24 * MIB, transcendentals=n_tokens * n_codes
+            flops=4 * products, bytes_accessed=12 * MIB, transcendentals=n_tokens * n_codes
         ),
         name="forward",
     )(tokens, grad_out, codebook, noise)
 
     received = lax.all_to_all(sent, "code", 0, 0, tiled=True)
-    weighed = pl.pallas_call(
+    codes, weighed = pl.pallas_call(
         weigh_kernel,
-        out_shape=pltpu.HBM((tiles_in, n_tokens, wide), BF16),
-        in_specs=[VMEM, ANY, ANY, VMEM],
-        out_specs=ANY,
+        out_shape=(pltpu.HBM((tiles_in, n_tokens, wide), BF16),) * 2,
+        in_specs=[VMEM, VMEM, ANY, ANY, VMEM, VMEM],
+        out_specs=(ANY, ANY),
         scratch_shapes=[
-            pltpu.VMEM((tiles_in, wide, dim), BF16),
+            pltpu.VMEM((tiles, width, dim), BF16),
+            pltpu.VMEM((tiles, n_tokens, width), BF16),
             pltpu.VMEM((tiles_in, n_tokens, wide), BF16),
             pltpu.VMEM((tiles_in, n_tokens, wide), BF16),
-            pltpu.SemaphoreType.DMA((tiles_in,)),
-            pltpu.SemaphoreType.DMA((tiles_in,)),
-            pltpu.SemaphoreType.DMA((tiles_in,)),
+            pltpu.VMEM((n_tokens, dim), BF16),
+            pltpu.SemaphoreType.DMA((tiles,)),
+            pltpu.SemaphoreType.DMA((tiles,)),
+            pltpu.SemaphoreType.DMA((2, tiles_in)),
         ],
         compiler_params=FULL,
         cost_estimate=pl.CostEstimate(
-            flops=products, bytes_accessed=20 * MIB, transcendentals=0
+            flops=2 * products, bytes_accessed=28 * MIB, transcendentals=n_tokens * n_codes
         ),
         name="weigh",
-    )(grad_out, codebook, codes, means)
+    )(tokens, grad_out, codebook, noise, means, shifts)
     received, weighed = lax.optimization_barrier((received, weighed))
     code_at = lax.axis_index("code")
     spread = pl.pallas_call(
@@ -568,7 +551,7 @@
             pltpu.SemaphoreType.DMA((n_dp, steps)),
             pltpu.SemaphoreType.DMA((steps,)),
         ],
-        compiler_params=SOME,
+        compiler_params=PART,
         cost_estimate=pl.CostEstimate(
             flops=0, bytes_accessed=(2 * n_dp + 4) * block * dim, transcendentals=0
         ),

time: 84.3 us -> 83.1 us (0.986)
  waiting for transfers between devices: 5.57 us -> 4.6 us
  local copies, waits for them, and re-layouts: 0.93 us -> 0.01 us
    all_to_all x1, waiting for transfers between devices: 5.57 us -> 4.59 us  [local(): received = lax.all_to_all(sent, 'code', 0, 0, tiled=True)]
    unnamed x4 -> x2, local copies, waits for them, and re-layouts: 0.93 us -> 0.01 us
  transfers between devices with their start and end apart: 3 -> 3, of which waited for: 1 -> 1; matrix products, arithmetic and copies ran while one was open for 0% -> 0% of each run, Pallas kernels for 33% -> 35%
where the time goes in v12:
time: 83.1 us; the launch traced here: 82.4 us
  Pallas kernels  64.1 us (77%)
  starting transfers between devices  12.8 us (15%)
  waiting for transfers between devices  4.6 us (6%)
  between operations  0.89 us (1%)
    pallas_call x1, Pallas kernels, local(): pl.pallas_call(functools.partial(forward_kernel, n_code), out_shape=(jax....  30.5 us
    pallas_call x1, Pallas kernels, local(): pl.pallas_call(weigh_kernel, out_shape=(pltpu.HBM((tiles_in, n_tokens, wi...  12.8 us
    all_to_all x1, starting transfers between devices, local(): received = lax.all_to_all(sent, 'code', 0, 0, tiled=True)  8.32 us
    pallas_call x1, Pallas kernels, local(): pl.pallas_call(functools.partial(backward_kernel, False), out_shape=(bloc...  8.03 us
    pallas_call x1, Pallas kernels, backward(): pl.pallas_call(functools.partial(backward_kernel, True), out_shape=block_...  6.81 us
    all_to_all x1, waiting for transfers between devices, local(): received = lax.all_to_all(sent, 'code', 0, 0, tiled=True)  4.59 us
    all_to_all x1, starting transfers between devices, local(): gathered = lax.all_to_all(spread, 'code', 0, 0, tiled=True)  4.43 us
    pallas_call x1, Pallas kernels, local(): pl.pallas_call(functools.partial(add_kernel, n_dp), out_shape=jax.ShapeDt...  3.59 us
  transfers between devices with their start and end apart: 3, of which 1 were waited for; matrix products, arithmetic and copies ran while one was open for 0% of the time, Pallas kernels for 35%

profile of v12, /device:TPU:0, one launch (start us, length us, event | category | flops | bytes accessed | tf_op | source)
XLA Modules:
  0.0 82.4 jit_solution(17109008442709350815)
XLA Ops:
  0.6 30.5 %forward.1 = (bf16[16,32,640]{2,1,0:T(8,128)(2,1)}, f32[512,128]{1,0:T(8,128)}, f32[512,128]{1,0:T(8,128)}) custom-call(bf16[512,256]{1,0:T(8,128)(2,1)} %rest_1_.1, bf16[512,256]{1,0:T(8,128)(2,1)} %rest_2_.1, bf16[8192,256]{1,0:T(8,128)(2,1)} %codebook.3, bf16[512,8192]{1,0:T(8,128)(2,1)} %noise.3), custom_call_target="tpu_custom_call" | custom-call | flops 8589934592 | bytes 12582912 | tf_op jit(solution)/shard_map/forward/pallas_call | solution.py:427
  31.1 8.3 %all-to-all-start = ((bf16[16,32,640]{2,1,0:T(8,128)(2,1)}), bf16[16,32,640]{2,1,0:T(8,128)(2,1)S(1)}, u32[]{:S(2)}, u32[]{:S(2)}) async-start(bf16[16,32,640]{2,1,0:T(8,128)(2,1)} %get-tuple-element.16), calls=%async_computation | async-start | bytes 1310720 | tf_op jit(solution)/shard_map/all_to_all | solution.py:455
  39.5 12.8 %weigh.1 = (bf16[16,512,512]{2,1,0:T(8,128)(2,1)}, bf16[16,512,512]{2,1,0:T(8,128)(2,1)}) custom-call(bf16[512,256]{1,0:T(8,128)(2,1)} %rest_1_.1, bf16[512,256]{1,0:T(8,128)(2,1)} %rest_2_.1, bf16[8192,256]{1,0:T(8,128)(2,1)} %codebook.3, bf16[512,8192]{1,0:T(8,128)(2,1)} %noise.3, f32[512,128]{1,0:T(8,128)} %get-tuple-element.17.means, ...), custom_call_target="tpu_custom_call" | custom-call | flops 4294967296 | bytes 29360128 | tf_op jit(solution)/shard_map/weigh/pallas_call | solution.py:456
  52.3 4.6 %all-to-all-done.received.rest_5_ = bf16[16,32,640]{2,1,0:T(8,128)(2,1)S(1)} async-done(((bf16[16,32,640]{2,1,0:T(8,128)(2,1)}), bf16[16,32,640]{2,1,0:T(8,128)(2,1)S(1)}, u32[]{:S(2)}, u32[]{:S(2)}) %all-to-all-start) | async-done | bytes 655392 | tf_op jit(solution)/shard_map/all_to_all | solution.py:455
  56.9 0.0 copy-start
  56.9 1.4 %merge.1 = bf16[16,32,512]{2,1,0:T(8,128)(2,1)} custom-call(s32[1]{0:T(128)} %bitcast.me.rest_0_, bf16[16,32,640]{2,1,0:T(8,128)(2,1)S(1)} %all-to-all-done.received.rest_5_), custom_call_target="tpu_custom_call" | custom-call | tf_op jit(solution)/shard_map/merge/pallas_call | solution.py:479
  58.2 4.4 %all-to-all-start.1 = ((bf16[16,32,512]{2,1,0:T(8,128)(2,1)}), bf16[16,32,512]{2,1,0:T(8,128)(2,1)S(1)}, u32[]{:S(2)}, u32[]{:S(2)}) async-start(bf16[16,32,512]{2,1,0:T(8,128)(2,1)} %merge.1), calls=%async_computation.1 | async-start | bytes 1048576 | tf_op jit(solution)/shard_map/all_to_all | solution.py:488
  62.7 0.0 copy-done
  62.7 8.0 %backward_first.1 = (bf16[4096,256]{1,0:T(8,128)(2,1)}, bf16[256,1024]{1,0:T(8,128)(2,1)}) custom-call(s32[1]{0:T(128)} %bitcast.1.block, s32[1]{0:T(128)} %bitcast.me.rest_0_, bf16[512,256]{1,0:T(8,128)(2,1)} %rest_1_.1, bf16[512,256]{1,0:T(8,128)(2,1)} %rest_2_.1, bf16[16,512,512]{2,1,0:T(8,128)(2,1)} %get-tuple-element.24.rest_3_.rest_0_, ...), custom_call_target="tpu_custom_call" | custom-call | flops 1 | bytes 1 | tf_op jit(solution)/shard_map/backward_first/pallas_call | solution.py:514
  70.7 0.1 collective-permute-start
  70.8 6.8 %backward.1.refs_1_ = bf16[4096,256]{1,0:T(8,128)(2,1)} custom-call(s32[1]{0:T(128)} %bitcast.2.block, bf16[16,512,512]{2,1,0:T(8,128)(2,1)} %get-tuple-element.24.rest_3_.rest_0_, bf16[16,512,512]{2,1,0:T(8,128)(2,1)} %get-tuple-element.25.rest_4_.rest_1_, bf16[256,1024]{1,0:T(8,128)(2,1)} %get-tuple-element.28.rest_2_), custom_call_target="tpu_custom_call" | custom-call | flops 1 | bytes 1 | tf_op jit(solution)/shard_map/backward/pallas_call | solution.py:529
  77.6 0.0 all-to-all-done.1.gathered
  77.6 1.0 %unpack.1 = (f32[512,256]{1,0:T(8,128)}, f32[512,256]{1,0:T(8,128)}) custom-call(bf16[16,32,512]{2,1,0:T(8,128)(2,1)S(1)} %all-to-all-done.1.gathered), custom_call_target="tpu_custom_call" | custom-call | flops 214748364800 | bytes 419430400 | tf_op jit(solution)/shard_map/unpack/pallas_call | solution.py:489
  78.7 0.0 collective-permute-done.refs_0_
  78.7 3.6 %add.1 = f32[4096,256]{1,0:T(8,128)} custom-call(bf16[4096,256]{1,0:T(8,128)(2,1)} %collective-permute-done.refs_0_, bf16[4096,256]{1,0:T(8,128)(2,1)} %backward.1.refs_1_), custom_call_target="tpu_custom_call" | custom-call | bytes 8388608 | tf_op jit(solution)/shard_map/add/pallas_call | solution.py:543
Async XLA Ops:
  31.1 25.7 %all-to-all-start = ((bf16[16,32,640]{2,1,0:T(8,128)(2,1)}), bf16[16,32,640]{2,1,0:T(8,128)(2,1)S(1)}, u32[]{:S(2)}, u32[]{:S(2)}) async-start(bf16[16,32,640]{2,1,0:T(8,128)(2,1)} %get-tuple-element.16), calls=%async_computation | async-start | bytes 1310720 | tf_op jit(solution)/shard_map/all_to_all | solution.py:455
  56.9 5.8 %copy-start = (bf16[16,32,640]{2,1,0:T(8,128)(2,1)}, bf16[16,32,640]{2,1,0:T(8,128)(2,1)S(1)}, u32[]{:S(2)}) copy-start(bf16[16,32,640]{2,1,0:T(8,128)(2,1)S(1)} %all-to-all-done.received.rest_5_) | copy-start | bytes 1966084
  58.2 19.4 %all-to-all-start.1 = ((bf16[16,32,512]{2,1,0:T(8,128)(2,1)}), bf16[16,32,512]{2,1,0:T(8,128)(2,1)S(1)}, u32[]{:S(2)}, u32[]{:S(2)}) async-start(bf16[16,32,512]{2,1,0:T(8,128)(2,1)} %merge.1), calls=%async_computation.1 | async-start | bytes 1048576 | tf_op jit(solution)/shard_map/all_to_all | solution.py:488
  70.7 8.0 %collective-permute-start = (bf16[4096,256]{1,0:T(8,128)(2,1)}, bf16[4096,256]{1,0:T(8,128)(2,1)}, u32[]{:S(2)}, u32[]{:S(2)}) collective-permute-start(bf16[4096,256]{1,0:T(8,128)(2,1)} %get-tuple-element.27), channel_id=1, source_target_pairs={{0,16},{16,0},{1,17},{17,1},{2,18},{18,2},{3,19},{19,3},{4,20},{20... | collective-permute-start | bytes 6291464 | tf_op jit(solution)/shard_map/ppermute | solution.py:412

commit v13 on v12

--- a/solution.py
+++ b/solution.py
@@ -12,7 +12,7 @@
 BF16 = jnp.bfloat16
 F32 = jnp.float32
 MIB = 1 << 20
-CHUNK = 256
+CHUNK = 512
 WIDE = 512
 AHEAD = 2
 NEAR = 3
@@ -125,7 +125,8 @@
                 slot[n_tokens + r : n_tokens + r + ROWS, c] = (weight * gradient).astype(BF16)
 
     def accumulate(t, s):
-        sums[...] += dot(slots[s][...], book[t])
+        for half in (slice(0, n_tokens), slice(n_tokens, 2 * n_tokens)):
+            sums[half] += dot(slots[s][half], book[t])
 
     def attempt(state):
         again, _ = state
@@ -322,7 +323,7 @@
         for copy in fetch(t):
             copy.start()
 
-    for t in range(min(NEAR, tiles)):
+    for t in range(tiles):
         start(t)
 
     if not prepared:
@@ -356,8 +357,6 @@
         if c.start == 0:
             for copy in fetch(t):
                 copy.wait()
-            if t + NEAR < tiles:
-                start(t + NEAR)
         return dot(operands[...], both_in[t, :, c])
 
     ahead = product(steps[0])

time: 83.1 us -> 83.3 us (level)
  transfers between devices with their start and end apart: 3 -> 3, of which waited for: 1 -> 1; matrix products, arithmetic and copies ran while one was open for 0% -> 0% of each run, Pallas kernels for 35% -> 34%
where the time goes in v13:
time: 83.3 us; the launch traced here: 82.8 us
  Pallas kernels  64.5 us (77%)
  starting transfers between devices  12.8 us (15%)
  waiting for transfers between devices  4.58 us (5%)
  between operations  0.89 us (1%)
    pallas_call x1, Pallas kernels, local(): pl.pallas_call(functools.partial(forward_kernel, n_code), out_shape=(jax....  31 us
    pallas_call x1, Pallas kernels, local(): pl.pallas_call(weigh_kernel, out_shape=(pltpu.HBM((tiles_in, n_tokens, wi...  12.8 us
    all_to_all x1, starting transfers between devices, local(): received = lax.all_to_all(sent, 'code', 0, 0, tiled=True)  8.33 us
    pallas_call x1, Pallas kernels, local(): pl.pallas_call(functools.partial(backward_kernel, False), out_shape=(bloc...  7.95 us
    pallas_call x1, Pallas kernels, backward(): pl.pallas_call(functools.partial(backward_kernel, True), out_shape=block_...  6.74 us
    all_to_all x1, waiting for transfers between devices, local(): received = lax.all_to_all(sent, 'code', 0, 0, tiled=True)  4.58 us
    all_to_all x1, starting transfers between devices, local(): gathered = lax.all_to_all(spread, 'code', 0, 0, tiled=True)  4.43 us
    pallas_call x1, Pallas kernels, local(): pl.pallas_call(functools.partial(add_kernel, n_dp), out_shape=jax.ShapeDt...  3.59 us
  transfers between devices with their start and end apart: 3, of which 1 were waited for; matrix products, arithmetic and copies ran while one was open for 0% of the time, Pallas kernels for 34%

profile of v13, /device:TPU:0, one launch (start us, length us, event | category | flops | bytes accessed | tf_op | source)
XLA Modules:
  0.0 82.8 jit_solution(8065762571741610761)
XLA Ops:
  0.6 31.0 %forward.1 = (bf16[16,32,640]{2,1,0:T(8,128)(2,1)}, f32[512,128]{1,0:T(8,128)}, f32[512,128]{1,0:T(8,128)}) custom-call(bf16[512,256]{1,0:T(8,128)(2,1)} %rest_1_.1, bf16[512,256]{1,0:T(8,128)(2,1)} %rest_2_.1, bf16[8192,256]{1,0:T(8,128)(2,1)} %codebook.3, bf16[512,8192]{1,0:T(8,128)(2,1)} %noise.3), custom_call_target="tpu_custom_call" | custom-call | flops 8589934592 | bytes 12582912 | tf_op jit(solution)/shard_map/forward/pallas_call | solution.py:426
  31.7 8.3 %all-to-all-start = ((bf16[16,32,640]{2,1,0:T(8,128)(2,1)}), bf16[16,32,640]{2,1,0:T(8,128)(2,1)S(1)}, u32[]{:S(2)}, u32[]{:S(2)}) async-start(bf16[16,32,640]{2,1,0:T(8,128)(2,1)} %get-tuple-element.16), calls=%async_computation | async-start | bytes 1310720 | tf_op jit(solution)/shard_map/all_to_all | solution.py:454
  40.0 12.8 %weigh.1 = (bf16[16,512,512]{2,1,0:T(8,128)(2,1)}, bf16[16,512,512]{2,1,0:T(8,128)(2,1)}) custom-call(bf16[512,256]{1,0:T(8,128)(2,1)} %rest_1_.1, bf16[512,256]{1,0:T(8,128)(2,1)} %rest_2_.1, bf16[8192,256]{1,0:T(8,128)(2,1)} %codebook.3, bf16[512,8192]{1,0:T(8,128)(2,1)} %noise.3, f32[512,128]{1,0:T(8,128)} %get-tuple-element.17.means, ...), custom_call_target="tpu_custom_call" | custom-call | flops 4294967296 | bytes 29360128 | tf_op jit(solution)/shard_map/weigh/pallas_call | solution.py:455
  52.8 4.6 %all-to-all-done.received.rest_5_ = bf16[16,32,640]{2,1,0:T(8,128)(2,1)S(1)} async-done(((bf16[16,32,640]{2,1,0:T(8,128)(2,1)}), bf16[16,32,640]{2,1,0:T(8,128)(2,1)S(1)}, u32[]{:S(2)}, u32[]{:S(2)}) %all-to-all-start) | async-done | bytes 655392 | tf_op jit(solution)/shard_map/all_to_all | solution.py:454
  57.4 0.0 copy-start
  57.4 1.4 %merge.1 = bf16[16,32,512]{2,1,0:T(8,128)(2,1)} custom-call(s32[1]{0:T(128)} %bitcast.me.rest_0_, bf16[16,32,640]{2,1,0:T(8,128)(2,1)S(1)} %all-to-all-done.received.rest_5_), custom_call_target="tpu_custom_call" | custom-call | tf_op jit(solution)/shard_map/merge/pallas_call | solution.py:478
  58.8 4.4 %all-to-all-start.1 = ((bf16[16,32,512]{2,1,0:T(8,128)(2,1)}), bf16[16,32,512]{2,1,0:T(8,128)(2,1)S(1)}, u32[]{:S(2)}, u32[]{:S(2)}) async-start(bf16[16,32,512]{2,1,0:T(8,128)(2,1)} %merge.1), calls=%async_computation.1 | async-start | bytes 1048576 | tf_op jit(solution)/shard_map/all_to_all | solution.py:487
  63.2 0.0 copy-done
  63.2 8.0 %backward_first.1 = (bf16[4096,256]{1,0:T(8,128)(2,1)}, bf16[256,1024]{1,0:T(8,128)(2,1)}) custom-call(s32[1]{0:T(128)} %bitcast.1.block, s32[1]{0:T(128)} %bitcast.me.rest_0_, bf16[512,256]{1,0:T(8,128)(2,1)} %rest_1_.1, bf16[512,256]{1,0:T(8,128)(2,1)} %rest_2_.1, bf16[16,512,512]{2,1,0:T(8,128)(2,1)} %get-tuple-element.24.rest_3_.rest_0_, ...), custom_call_target="tpu_custom_call" | custom-call | flops 1 | bytes 1 | tf_op jit(solution)/shard_map/backward_first/pallas_call | solution.py:513
  71.2 0.1 collective-permute-start
  71.3 6.7 %backward.1.refs_1_ = bf16[4096,256]{1,0:T(8,128)(2,1)} custom-call(s32[1]{0:T(128)} %bitcast.2.block, bf16[16,512,512]{2,1,0:T(8,128)(2,1)} %get-tuple-element.24.rest_3_.rest_0_, bf16[16,512,512]{2,1,0:T(8,128)(2,1)} %get-tuple-element.25.rest_4_.rest_1_, bf16[256,1024]{1,0:T(8,128)(2,1)} %get-tuple-element.28.rest_2_), custom_call_target="tpu_custom_call" | custom-call | flops 1 | bytes 1 | tf_op jit(solution)/shard_map/backward/pallas_call | solution.py:528
  78.0 0.0 all-to-all-done.1.gathered
  78.0 1.0 %unpack.1 = (f32[512,256]{1,0:T(8,128)}, f32[512,256]{1,0:T(8,128)}) custom-call(bf16[16,32,512]{2,1,0:T(8,128)(2,1)S(1)} %all-to-all-done.1.gathered), custom_call_target="tpu_custom_call" | custom-call | flops 214748364800 | bytes 419430400 | tf_op jit(solution)/shard_map/unpack/pallas_call | solution.py:488
  79.1 0.0 collective-permute-done.refs_0_
  79.1 3.6 %add.1 = f32[4096,256]{1,0:T(8,128)} custom-call(bf16[4096,256]{1,0:T(8,128)(2,1)} %collective-permute-done.refs_0_, bf16[4096,256]{1,0:T(8,128)(2,1)} %backward.1.refs_1_), custom_call_target="tpu_custom_call" | custom-call | bytes 8388608 | tf_op jit(solution)/shard_map/add/pallas_call | solution.py:542
Async XLA Ops:
  31.7 25.7 %all-to-all-start = ((bf16[16,32,640]{2,1,0:T(8,128)(2,1)}), bf16[16,32,640]{2,1,0:T(8,128)(2,1)S(1)}, u32[]{:S(2)}, u32[]{:S(2)}) async-start(bf16[16,32,640]{2,1,0:T(8,128)(2,1)} %get-tuple-element.16), calls=%async_computation | async-start | bytes 1310720 | tf_op jit(solution)/shard_map/all_to_all | solution.py:454
  57.4 5.8 %copy-start = (bf16[16,32,640]{2,1,0:T(8,128)(2,1)}, bf16[16,32,640]{2,1,0:T(8,128)(2,1)S(1)}, u32[]{:S(2)}) copy-start(bf16[16,32,640]{2,1,0:T(8,128)(2,1)S(1)} %all-to-all-done.received.rest_5_) | copy-start | bytes 1966084
  58.8 19.2 %all-to-all-start.1 = ((bf16[16,32,512]{2,1,0:T(8,128)(2,1)}), bf16[16,32,512]{2,1,0:T(8,128)(2,1)S(1)}, u32[]{:S(2)}, u32[]{:S(2)}) async-start(bf16[16,32,512]{2,1,0:T(8,128)(2,1)} %merge.1), calls=%async_computation.1 | async-start | bytes 1048576 | tf_op jit(solution)/shard_map/all_to_all | solution.py:487
  71.2 7.9 %collective-permute-start = (bf16[4096,256]{1,0:T(8,128)(2,1)}, bf16[4096,256]{1,0:T(8,128)(2,1)}, u32[]{:S(2)}, u32[]{:S(2)}) collective-permute-start(bf16[4096,256]{1,0:T(8,128)(2,1)} %get-tuple-element.27), channel_id=1, source_target_pairs={{0,16},{16,0},{1,17},{17,1},{2,18},{18,2},{3,19},{19,3},{4,20},{20... | collective-permute-start | bytes 6291464 | tf_op jit(solution)/shard_map/ppermute | solution.py:411

commit v14 on v12

--- a/solution.py
+++ b/solution.py
@@ -47,8 +47,9 @@
 
 
 def forward_kernel(
-    n_code, tokens, grad_out, codebook, noise, sent, means, shifts,
-    pair, book, noise_in, slot_a, slot_b, total, sums, pair_sem, book_sem, noise_sem,
+    n_code, tokens, grad_out, codebook, noise, sent, sides,
+    pair, book, noise_in, slot_a, slot_b, shifts, total, sums, sent_out, sides_out,
+    pair_sem, book_sem, noise_sem, first_sem, out_sem,
 ):
     tiles, width, dim = book.shape
     n_tokens = tokens.shape[0]
@@ -80,9 +81,19 @@
                     pair_sem.at[len(pair_copies)],
                 )
             )
+    halves = []
+    for h in range(2):
+        at = pl.ds(h * (width // 2), width // 2)
+        halves.append((
+            pltpu.make_async_copy(codebook.at[at], book.at[0, at], first_sem.at[h, 0]),
+            pltpu.make_async_copy(noise.at[:, at], noise_in.at[0, :, at], first_sem.at[h, 1]),
+        ))
+    halves[0][0].start()
     for copy in pair_copies:
         copy.start()
-    start(0)
+    halves[0][1].start()
+    for copy in halves[1]:
+        copy.start()
 
     def logits(both, t, r, c):
         noise_part = (noise_in[t, r : r + ROWS, c] * BF16(SHARPNESS)).astype(F32)
@@ -148,6 +159,12 @@
         shifts[...] = jnp.broadcast_to(shift, shifts.shape)
         total[...] = jnp.zeros(total.shape, F32)
         sums[...] = jnp.zeros(sums.shape, F32)
+
+        @pl.when(fresh)
+        def _():
+            for copy in halves[1]:
+                copy.wait()
+
         soften(0, 0, None)
 
         def soften_pair(i, carry):
@@ -165,7 +182,8 @@
         copy.wait()
     for r in range(0, n_tokens, ROWS):
         pair[2 * r : 2 * r + ROWS] = pair[2 * r : 2 * r + ROWS] * BF16(SHARPNESS)
-    arrive(0)
+    for copy in halves[0]:
+        copy.wait()
     for t in range(1, min(AHEAD + 1, tiles)):
         start(t)
     lax.while_loop(lambda state: state[1], attempt, (jnp.int32(0), jnp.bool_(True)))
@@ -179,7 +197,10 @@
     )
     own_inner = jnp.sum(own_grad.astype(F32) * mix, axis=1, keepdims=True)
     mean = own_inner / own_total
-    means[...] = jnp.broadcast_to(mean, means.shape)
+    side = lax.broadcasted_iota(jnp.int32, sides_out.shape, 1)
+    sides_out[...] = jnp.where(side < 64, mean, shift)
+    copies = [pltpu.make_async_copy(sides_out, sides, out_sem.at[0])]
+    copies[0].start()
     rows = n_tokens // n_code
     lanes = stat_lanes(n_code)
     half = lanes // 2
@@ -192,11 +213,20 @@
             stats = jnp.where(lane == 4 * g + i, part[at], stats)
         stats = jnp.where((lane - half) // 4 == g, shift[at], stats)
     stats = stats.astype(BF16)
+    group = n_code // min(n_code, 4)
     for g in range(n_code):
         at = slice(g * rows, (g + 1) * rows)
-        sent[g, :, :dim] = mix[at].astype(BF16)
-        sent[g, :, dim : 2 * dim] = (pulled[at] - mean[at] * mix[at]).astype(BF16)
-        sent[g, :, 2 * dim :] = stats
+        sent_out[g, :, :dim] = mix[at].astype(BF16)
+        sent_out[g, :, dim : 2 * dim] = (pulled[at] - mean[at] * mix[at]).astype(BF16)
+        sent_out[g, :, 2 * dim :] = stats
+        if (g + 1) % group == 0:
+            part = pl.ds(g + 1 - group, group)
+            copies.append(
+                pltpu.make_async_copy(sent_out.at[part], sent.at[part], out_sem.at[len(copies)])
+            )
+            copies[-1].start()
+    for copy in copies:
+        copy.wait()
 
 
 def roll_left(value, by):
@@ -243,8 +273,8 @@
 
 
 def weigh_kernel(
-    tokens, grad_out, codebook, noise, means, shifts, codes, weighed,
-    book, noise_in, code_out, weighed_out, sharp, book_sem, noise_sem, out_sem,
+    tokens, grad_out, codebook, noise, sides, codes, weighed,
+    book, noise_in, code_out, weighed_out, sharp, means, shifts, book_sem, noise_sem, out_sem,
 ):
     tiles, width, _ = book.shape
     wide = codes.shape[2]
@@ -280,6 +310,8 @@
     for t in range(min(NEAR, tiles)):
         start(t)
     sharp[...] = tokens[...] * BF16(SHARPNESS)
+    means[...] = jnp.broadcast_to(sides[:, :1], means.shape)
+    shifts[...] = jnp.broadcast_to(sides[:, 64:65], shifts.shape)
     ahead = products_of(steps[0])
     for k, (t, c) in enumerate(steps):
         score, gradient = ahead
@@ -300,11 +332,11 @@
 
 def backward_kernel(prepared, block, *rest):
     if prepared:
-        codes, weighed, operands, out, *rest = rest
+        codes, weighed, given, out, *rest = rest
     else:
-        code_at, tokens, grad_out, codes, weighed, received, out, operands, *rest = rest
-        upper, lower, *rest = rest
-    both_in, result, in_sem, out_sem = rest
+        code_at, tokens, grad_out, codes, weighed, received, out, kept, *rest = rest
+        own, upper, lower, *rest = rest
+    both_in, result, operands, in_sem, out_sem, own_sem = rest
     tiles, width, dim = result.shape
     n_tokens = both_in.shape[1] // 2
 
@@ -322,10 +354,22 @@
         for copy in fetch(t):
             copy.start()
 
-    for t in range(min(NEAR, tiles)):
+    start(0)
+    if prepared:
+        own_copies = [pltpu.make_async_copy(given, operands, own_sem.at[0])]
+    else:
+        own_copies = [
+            pltpu.make_async_copy(tokens, own.at[0], own_sem.at[0]),
+            pltpu.make_async_copy(grad_out, own.at[1], own_sem.at[1]),
+        ]
+    for copy in own_copies:
+        copy.start()
+    for t in range(1, min(NEAR, tiles)):
         start(t)
 
-    if not prepared:
+    if prepared:
+        own_copies[0].wait()
+    else:
         n_code, rows, _ = received.shape
         scales, means, inner = merged_stats(received)
         scale = jnp.zeros(inner.shape, F32)
@@ -334,14 +378,18 @@
             scale = jnp.where(code_at[0] == p, scales[p], scale)
             mean = jnp.where(code_at[0] == p, means[p], mean)
         offset = mean - inner
+        for copy in own_copies:
+            copy.wait()
         for g in range(n_code):
             part = slice(g * rows, (g + 1) * rows)
             at = slice(4 * g, 4 * g + 1)
-            token = scale[:, at] * (tokens[part].astype(F32) / SOFTMAX_HEAT)
-            upper[part] = scale[:, at] * grad_out[part].astype(F32) + offset[:, at] * token
+            token = scale[:, at] * (own[0, part].astype(F32) / SOFTMAX_HEAT)
+            upper[part] = scale[:, at] * own[1, part].astype(F32) + offset[:, at] * token
             lower[part] = token
         operands[:, :n_tokens] = upper[...].T.astype(BF16)
         operands[:, n_tokens:] = lower[...].T.astype(BF16)
+        keep = pltpu.make_async_copy(operands, kept, own_sem.at[0])
+        keep.start()
 
     def send(t):
         return pltpu.make_async_copy(
@@ -370,6 +418,8 @@
             send(t).start()
     for t in range(tiles):
         send(t).wait()
+    if not prepared:
+        keep.wait()
 
 
 def add_kernel(n_parts, *refs):
@@ -424,15 +474,14 @@
     lanes = stat_lanes(n_code)
     products = 2 * n_tokens * n_codes * dim
 
-    sent, means, shifts = pl.pallas_call(
+    sent, sides = pl.pallas_call(
         functools.partial(forward_kernel, n_code),
         out_shape=(
             jax.ShapeDtypeStruct((n_code, rows, 2 * dim + lanes), BF16),
             jax.ShapeDtypeStruct((n_tokens, 128), F32),
-            jax.ShapeDtypeStruct((n_tokens, 128), F32),
         ),
         in_specs=[ANY, ANY, ANY, ANY],
-        out_specs=(VMEM, VMEM, VMEM),
+        out_specs=(ANY, ANY),
         scratch_shapes=[
             pltpu.VMEM((2 * n_tokens, dim), BF16),
             pltpu.VMEM((tiles, width, dim), BF16),
@@ -440,10 +489,15 @@
             pltpu.VMEM((2 * n_tokens, width), BF16),
             pltpu.VMEM((2 * n_tokens, width), BF16),
             pltpu.VMEM((n_tokens, 128), F32),
+            pltpu.VMEM((n_tokens, 128), F32),
             pltpu.VMEM((2 * n_tokens, dim), F32),
+            pltpu.VMEM((n_code, rows, 2 * dim + lanes), BF16),
+            pltpu.VMEM((n_tokens, 128), F32),
             pltpu.SemaphoreType.DMA((2 * n_tokens // ROWS,)),
             pltpu.SemaphoreType.DMA((tiles,)),
             pltpu.SemaphoreType.DMA((tiles,)),
+            pltpu.SemaphoreType.DMA((2, 2)),
+            pltpu.SemaphoreType.DMA((1 + min(n_code, 4),)),
         ],
         compiler_params=FULL,
         cost_estimate=pl.CostEstimate(
@@ -456,7 +510,7 @@
     codes, weighed = pl.pallas_call(
         weigh_kernel,
         out_shape=(pltpu.HBM((tiles_in, n_tokens, wide), BF16),) * 2,
-        in_specs=[VMEM, VMEM, ANY, ANY, VMEM, VMEM],
+        in_specs=[VMEM, VMEM, ANY, ANY, VMEM],
         out_specs=(ANY, ANY),
         scratch_shapes=[
             pltpu.VMEM((tiles, width, dim), BF16),
@@ -464,6 +518,8 @@
             pltpu.VMEM((tiles_in, n_tokens, wide), BF16),
             pltpu.VMEM((tiles_in, n_tokens, wide), BF16),
             pltpu.VMEM((n_tokens, dim), BF16),
+            pltpu.VMEM((n_tokens, 128), F32),
+            pltpu.VMEM((n_tokens, 128), F32),
             pltpu.SemaphoreType.DMA((tiles,)),
             pltpu.SemaphoreType.DMA((tiles,)),
             pltpu.SemaphoreType.DMA((2, tiles_in)),
@@ -473,7 +529,7 @@
             flops=2 * products, bytes_accessed=28 * MIB, transcendentals=n_tokens * n_codes
         ),
         name="weigh",
-    )(tokens, grad_out, codebook, noise, means, shifts)
+    )(tokens, grad_out, codebook, noise, sides)
     received, weighed = lax.optimization_barrier((received, weighed))
     code_at = lax.axis_index("code")
     spread = pl.pallas_call(
@@ -502,8 +558,10 @@
     streams = [
         pltpu.VMEM((block_tiles, 2 * n_tokens, wide), BF16),
         pltpu.VMEM((block_tiles, wide, dim), BF16),
+        pltpu.VMEM((dim, 2 * n_tokens), BF16),
         pltpu.SemaphoreType.DMA((2, block_tiles)),
         pltpu.SemaphoreType.DMA((block_tiles,)),
+        pltpu.SemaphoreType.DMA((2,)),
     ]
     block_shape = jax.ShapeDtypeStruct((block, dim), BF16)
     common = dict(
@@ -514,10 +572,12 @@
     first, operands = pl.pallas_call(
         functools.partial(backward_kernel, False),
         out_shape=(block_shape, jax.ShapeDtypeStruct((dim, 2 * n_tokens), BF16)),
-        in_specs=[SMEM, SMEM, VMEM, VMEM, ANY, ANY, VMEM],
-        out_specs=(ANY, VMEM),
+        in_specs=[SMEM, SMEM, ANY, ANY, ANY, ANY, VMEM],
+        out_specs=(ANY, ANY),
         scratch_shapes=[
-            pltpu.VMEM((n_tokens, dim), F32), pltpu.VMEM((n_tokens, dim), F32),
+            pltpu.VMEM((2, n_tokens, dim), BF16),
+            pltpu.VMEM((n_tokens, dim), F32),
+            pltpu.VMEM((n_tokens, dim), F32),
         ] + streams,
         name="backward_first",
         **common,
@@ -529,7 +589,7 @@
         return pl.pallas_call(
             functools.partial(backward_kernel, True),
             out_shape=block_shape,
-            in_specs=[SMEM, ANY, ANY, VMEM],
+            in_specs=[SMEM, ANY, ANY, ANY],
             out_specs=ANY,
             scratch_shapes=streams,
             name="backward",

time: 83.1 us -> 82.5 us (level)
  transfers between devices with their start and end apart: 3 -> 3, of which waited for: 1 -> 1; matrix products, arithmetic and copies ran while one was open for 0% -> 0% of each run, Pallas kernels for 35% -> 34%
where the time goes in v14:
time: 82.5 us; the launch traced here: 81.9 us
  Pallas kernels  63.6 us (77%)
  starting transfers between devices  12.8 us (16%)
  waiting for transfers between devices  4.61 us (6%)
  between operations  0.89 us (1%)
    pallas_call x1, Pallas kernels, local(): pl.pallas_call(functools.partial(forward_kernel, n_code), out_shape=(jax....  30.4 us
    pallas_call x1, Pallas kernels, local(): pl.pallas_call(weigh_kernel, out_shape=(pltpu.HBM((tiles_in, n_tokens, wi...  12.8 us
    all_to_all x1, starting transfers between devices, local(): received = lax.all_to_all(sent, 'code', 0, 0, tiled=True)  8.34 us
    pallas_call x1, Pallas kernels, local(): pl.pallas_call(functools.partial(backward_kernel, False), out_shape=(bloc...  7.99 us
    pallas_call x1, Pallas kernels, backward(): pl.pallas_call(functools.partial(backward_kernel, True), out_shape=block_...  6.4 us
    all_to_all x1, waiting for transfers between devices, local(): received = lax.all_to_all(sent, 'code', 0, 0, tiled=True)  4.6 us
    all_to_all x1, starting transfers between devices, local(): gathered = lax.all_to_all(spread, 'code', 0, 0, tiled=True)  4.43 us
    pallas_call x1, Pallas kernels, local(): pl.pallas_call(functools.partial(add_kernel, n_dp), out_shape=jax.ShapeDt...  3.59 us
  transfers between devices with their start and end apart: 3, of which 1 were waited for; matrix products, arithmetic and copies ran while one was open for 0% of the time, Pallas kernels for 34%

profile of v14, /device:TPU:0, one launch (start us, length us, event | category | flops | bytes accessed | tf_op | source)
XLA Modules:
  0.0 81.9 jit_solution(7509304888738157086)
XLA Ops:
  0.6 30.4 %forward.1 = (bf16[16,32,640]{2,1,0:T(8,128)(2,1)}, f32[512,128]{1,0:T(8,128)}) custom-call(bf16[512,256]{1,0:T(8,128)(2,1)} %rest_1_.1, bf16[512,256]{1,0:T(8,128)(2,1)} %rest_2_.1, bf16[8192,256]{1,0:T(8,128)(2,1)} %codebook.3, bf16[512,8192]{1,0:T(8,128)(2,1)} %noise.3), custom_call_target="tpu_custom_call" | custom-call | flops 8589934592 | bytes 12582912 | tf_op jit(solution)/shard_map/forward/pallas_call | solution.py:477
  31.1 8.3 %all-to-all-start = ((bf16[16,32,640]{2,1,0:T(8,128)(2,1)}), bf16[16,32,640]{2,1,0:T(8,128)(2,1)S(1)}, u32[]{:S(2)}, u32[]{:S(2)}) async-start(bf16[16,32,640]{2,1,0:T(8,128)(2,1)} %get-tuple-element.15), calls=%async_computation | async-start | bytes 1310720 | tf_op jit(solution)/shard_map/all_to_all | solution.py:509
  39.4 12.8 %weigh.1 = (bf16[16,512,512]{2,1,0:T(8,128)(2,1)}, bf16[16,512,512]{2,1,0:T(8,128)(2,1)}) custom-call(bf16[512,256]{1,0:T(8,128)(2,1)} %rest_1_.1, bf16[512,256]{1,0:T(8,128)(2,1)} %rest_2_.1, bf16[8192,256]{1,0:T(8,128)(2,1)} %codebook.3, bf16[512,8192]{1,0:T(8,128)(2,1)} %noise.3, f32[512,128]{1,0:T(8,128)} %get-tuple-element.16.sides), custom_call_target="tpu_custom_call" | custom-call | flops 4294967296 | bytes 29360128 | tf_op jit(solution)/shard_map/weigh/pallas_call | solution.py:510
  52.2 4.6 %all-to-all-done.received.rest_5_ = bf16[16,32,640]{2,1,0:T(8,128)(2,1)S(1)} async-done(((bf16[16,32,640]{2,1,0:T(8,128)(2,1)}), bf16[16,32,640]{2,1,0:T(8,128)(2,1)S(1)}, u32[]{:S(2)}, u32[]{:S(2)}) %all-to-all-start) | async-done | bytes 655392 | tf_op jit(solution)/shard_map/all_to_all | solution.py:509
  56.8 0.0 copy-start
  56.8 1.4 %merge.1 = bf16[16,32,512]{2,1,0:T(8,128)(2,1)} custom-call(s32[1]{0:T(128)} %bitcast.me.rest_0_, bf16[16,32,640]{2,1,0:T(8,128)(2,1)S(1)} %all-to-all-done.received.rest_5_), custom_call_target="tpu_custom_call" | custom-call | tf_op jit(solution)/shard_map/merge/pallas_call | solution.py:535
  58.2 4.4 %all-to-all-start.1 = ((bf16[16,32,512]{2,1,0:T(8,128)(2,1)}), bf16[16,32,512]{2,1,0:T(8,128)(2,1)S(1)}, u32[]{:S(2)}, u32[]{:S(2)}) async-start(bf16[16,32,512]{2,1,0:T(8,128)(2,1)} %merge.1), calls=%async_computation.1 | async-start | bytes 1048576 | tf_op jit(solution)/shard_map/all_to_all | solution.py:544
  62.6 0.0 copy-done
  62.6 8.0 %backward_first.1 = (bf16[4096,256]{1,0:T(8,128)(2,1)}, bf16[256,1024]{1,0:T(8,128)(2,1)}) custom-call(s32[1]{0:T(128)} %bitcast.1.block, s32[1]{0:T(128)} %bitcast.me.rest_0_, bf16[512,256]{1,0:T(8,128)(2,1)} %rest_1_.1, bf16[512,256]{1,0:T(8,128)(2,1)} %rest_2_.1, bf16[16,512,512]{2,1,0:T(8,128)(2,1)} %get-tuple-element.22.rest_3_.rest_0_, ...), custom_call_target="tpu_custom_call" | custom-call | flops 1 | bytes 1 | tf_op jit(solution)/shard_map/backward_first/pallas_call | solution.py:572
  70.6 0.1 collective-permute-start
  70.7 6.4 %backward.1.refs_1_ = bf16[4096,256]{1,0:T(8,128)(2,1)} custom-call(s32[1]{0:T(128)} %bitcast.2.block, bf16[16,512,512]{2,1,0:T(8,128)(2,1)} %get-tuple-element.22.rest_3_.rest_0_, bf16[16,512,512]{2,1,0:T(8,128)(2,1)} %get-tuple-element.23.rest_4_.rest_1_, bf16[256,1024]{1,0:T(8,128)(2,1)} %get-tuple-element.26.rest_2_), custom_call_target="tpu_custom_call" | custom-call | flops 1 | bytes 1 | tf_op jit(solution)/shard_map/backward/pallas_call | solution.py:589
  77.1 0.0 all-to-all-done.1.gathered
  77.1 1.0 %unpack.1 = (f32[512,256]{1,0:T(8,128)}, f32[512,256]{1,0:T(8,128)}) custom-call(bf16[16,32,512]{2,1,0:T(8,128)(2,1)S(1)} %all-to-all-done.1.gathered), custom_call_target="tpu_custom_call" | custom-call | flops 214748364800 | bytes 419430400 | tf_op jit(solution)/shard_map/unpack/pallas_call | solution.py:545
  78.2 0.0 collective-permute-done.refs_0_
  78.2 3.6 %add.1 = f32[4096,256]{1,0:T(8,128)} custom-call(bf16[4096,256]{1,0:T(8,128)(2,1)} %collective-permute-done.refs_0_, bf16[4096,256]{1,0:T(8,128)(2,1)} %backward.1.refs_1_), custom_call_target="tpu_custom_call" | custom-call | bytes 8388608 | tf_op jit(solution)/shard_map/add/pallas_call | solution.py:603
Async XLA Ops:
  31.1 25.8 %all-to-all-start = ((bf16[16,32,640]{2,1,0:T(8,128)(2,1)}), bf16[16,32,640]{2,1,0:T(8,128)(2,1)S(1)}, u32[]{:S(2)}, u32[]{:S(2)}) async-start(bf16[16,32,640]{2,1,0:T(8,128)(2,1)} %get-tuple-element.15), calls=%async_computation | async-start | bytes 1310720 | tf_op jit(solution)/shard_map/all_to_all | solution.py:509
  56.8 5.8 %copy-start = (bf16[16,32,640]{2,1,0:T(8,128)(2,1)}, bf16[16,32,640]{2,1,0:T(8,128)(2,1)S(1)}, u32[]{:S(2)}) copy-start(bf16[16,32,640]{2,1,0:T(8,128)(2,1)S(1)} %all-to-all-done.received.rest_5_) | copy-start | bytes 1966084
  58.2 18.9 %all-to-all-start.1 = ((bf16[16,32,512]{2,1,0:T(8,128)(2,1)}), bf16[16,32,512]{2,1,0:T(8,128)(2,1)S(1)}, u32[]{:S(2)}, u32[]{:S(2)}) async-start(bf16[16,32,512]{2,1,0:T(8,128)(2,1)} %merge.1), calls=%async_computation.1 | async-start | bytes 1048576 | tf_op jit(solution)/shard_map/all_to_all | solution.py:544
  70.6 7.5 %collective-permute-start = (bf16[4096,256]{1,0:T(8,128)(2,1)}, bf16[4096,256]{1,0:T(8,128)(2,1)}, u32[]{:S(2)}, u32[]{:S(2)}) collective-permute-start(bf16[4096,256]{1,0:T(8,128)(2,1)} %get-tuple-element.25), channel_id=1, source_target_pairs={{0,16},{16,0},{1,17},{17,1},{2,18},{18,2},{3,19},{19,3},{4,20},{20... | collective-permute-start | bytes 6291464 | tf_op jit(solution)/shard_map/ppermute | solution.py:462

commit v15 on v14

--- a/solution.py
+++ b/solution.py
@@ -233,24 +233,25 @@
     return pltpu.roll(value, value.shape[1] - by, 1)
 
 
+def pair_sums(value):
+    both = value + roll_left(value, 1)
+    return both, roll_left(both, 2)
+
+
 def merged_stats(received):
     n_code = received.shape[0]
     lanes = stat_lanes(n_code)
     stats = [received[p, :, received.shape[2] - lanes :].astype(F32) for p in range(n_code)]
     top = functools.reduce(jnp.maximum, stats)
-    scales = [roll_left(jnp.exp(s - top), lanes // 2) for s in stats]
-    pairs = [s + roll_left(s, 1) for s in stats]
-    inners = [roll_left(s, 2) for s in pairs]
-    total = sum(a * s for a, s in zip(scales, pairs))
-    inner = sum(a * s for a, s in zip(scales, inners)) / total
-    means = [i / s for i, s in zip(inners, pairs)]
-    return [a / total for a in scales], means, inner
+    factors = [roll_left(jnp.exp(s - top), lanes // 2) for s in stats]
+    total, inner = pair_sums(sum(f * s for f, s in zip(factors, stats)))
+    return stats, factors, top, total, inner / total
 
 
 def merge_kernel(me, received, spread):
     n_code, rows, _ = received.shape
     dim = spread.shape[2] // 2
-    scales, means, inner = merged_stats(received)
+    stats, factors, _, total, inner = merged_stats(received)
     lane = lax.broadcasted_iota(jnp.int32, inner.shape, 1)
     mine = lane == 4 * me[0]
 
@@ -260,21 +261,24 @@
     quantized = jnp.zeros((rows, dim), F32)
     gradient = jnp.zeros((rows, dim), F32)
     for p in range(n_code):
-        scale = column(scales[p])
-        offset = column(scales[p] * (means[p] - inner))
+        own_total, own_inner = pair_sums(stats[p])
+        factor = column(factors[p])
+        offset = column(factors[p] * (own_inner / own_total - inner))
         mix = received[p, :, :dim].astype(F32)
-        quantized += scale * mix
-        gradient += scale * received[p, :, dim : 2 * dim].astype(F32) + offset * mix
-    quantized = quantized.astype(BF16)
-    gradient = (gradient / SOFTMAX_HEAT).astype(BF16)
+        quantized += factor * mix
+        gradient += factor * received[p, :, dim : 2 * dim].astype(F32) + offset * mix
+    scale = 1.0 / column(total)
+    quantized = (quantized * scale).astype(BF16)
+    gradient = (gradient * (scale / SOFTMAX_HEAT)).astype(BF16)
     for p in range(n_code):
         spread[p, :, :dim] = quantized
         spread[p, :, dim:] = gradient
 
 
 def weigh_kernel(
-    tokens, grad_out, codebook, noise, sides, codes, weighed,
-    book, noise_in, code_out, weighed_out, sharp, means, shifts, book_sem, noise_sem, out_sem,
+    tokens, grad_out, codebook, noise, sides, codes, weighed, turned,
+    book, noise_in, code_out, weighed_out, sharp, means, shifts, turned_out,
+    book_sem, noise_sem, out_sem, turned_sem,
 ):
     tiles, width, _ = book.shape
     wide = codes.shape[2]
@@ -312,6 +316,10 @@
     sharp[...] = tokens[...] * BF16(SHARPNESS)
     means[...] = jnp.broadcast_to(sides[:, :1], means.shape)
     shifts[...] = jnp.broadcast_to(sides[:, 64:65], shifts.shape)
+    turned_out[0] = grad_out[...].T
+    turned_out[1] = sharp[...].T
+    turned_copy = pltpu.make_async_copy(turned_out, turned, turned_sem)
+    turned_copy.start()
     ahead = products_of(steps[0])
     for k, (t, c) in enumerate(steps):
         score, gradient = ahead
@@ -328,14 +336,14 @@
     for k in range(len(steps)):
         for copy in send(k):
             copy.wait()
+    turned_copy.wait()
 
 
 def backward_kernel(prepared, block, *rest):
     if prepared:
         codes, weighed, given, out, *rest = rest
     else:
-        code_at, tokens, grad_out, codes, weighed, received, out, kept, *rest = rest
-        own, upper, lower, *rest = rest
+        code_at, turned, codes, weighed, received, out, kept, own, spread, *rest = rest
     both_in, result, operands, in_sem, out_sem, own_sem = rest
     tiles, width, dim = result.shape
     n_tokens = both_in.shape[1] // 2
@@ -358,10 +366,7 @@
     if prepared:
         own_copies = [pltpu.make_async_copy(given, operands, own_sem.at[0])]
     else:
-        own_copies = [
-            pltpu.make_async_copy(tokens, own.at[0], own_sem.at[0]),
-            pltpu.make_async_copy(grad_out, own.at[1], own_sem.at[1]),
-        ]
+        own_copies = [pltpu.make_async_copy(turned, own, own_sem.at[0])]
     for copy in own_copies:
         copy.start()
     for t in range(1, min(NEAR, tiles)):
@@ -371,23 +376,22 @@
         own_copies[0].wait()
     else:
         n_code, rows, _ = received.shape
-        scales, means, inner = merged_stats(received)
-        scale = jnp.zeros(inner.shape, F32)
-        mean = jnp.zeros(inner.shape, F32)
-        for p in range(n_code):
-            scale = jnp.where(code_at[0] == p, scales[p], scale)
-            mean = jnp.where(code_at[0] == p, means[p], mean)
-        offset = mean - inner
-        for copy in own_copies:
-            copy.wait()
+        _, _, top, total, inner = merged_stats(received)
+        lanes = top.shape[1]
+        stats = received[code_at[0], :, received.shape[2] - lanes :].astype(F32)
+        own_total, own_inner = pair_sums(stats)
+        scale = roll_left(jnp.exp(stats - top), lanes // 2) / total
+        offset = scale * (own_inner / own_total - inner)
+        lane = lax.broadcasted_iota(jnp.int32, (rows, 128), 1)
         for g in range(n_code):
-            part = slice(g * rows, (g + 1) * rows)
             at = slice(4 * g, 4 * g + 1)
-            token = scale[:, at] * (own[0, part].astype(F32) / SOFTMAX_HEAT)
-            upper[part] = scale[:, at] * own[1, part].astype(F32) + offset[:, at] * token
-            lower[part] = token
-        operands[:, :n_tokens] = upper[...].T.astype(BF16)
-        operands[:, n_tokens:] = lower[...].T.astype(BF16)
+            spread[g * rows : (g + 1) * rows] = jnp.where(lane < 64, scale[:, at], offset[:, at])
+        factors = spread[...].T
+        scale, offset = factors[:1], factors[64:65]
+        own_copies[0].wait()
+        grad, token = own[0].astype(F32), own[1].astype(F32)
+        operands[:, :n_tokens] = (scale * grad + offset * token).astype(BF16)
+        operands[:, n_tokens:] = (scale * token).astype(BF16)
         keep = pltpu.make_async_copy(operands, kept, own_sem.at[0])
         keep.start()
 
@@ -507,11 +511,12 @@
     )(tokens, grad_out, codebook, noise)
 
     received = lax.all_to_all(sent, "code", 0, 0, tiled=True)
-    codes, weighed = pl.pallas_call(
+    codes, weighed, turned = pl.pallas_call(
         weigh_kernel,
-        out_shape=(pltpu.HBM((tiles_in, n_tokens, wide), BF16),) * 2,
+        out_shape=(pltpu.HBM((tiles_in, n_tokens, wide), BF16),) * 2
+        + (jax.ShapeDtypeStruct((2, dim, n_tokens), BF16),),
         in_specs=[VMEM, VMEM, ANY, ANY, VMEM],
-        out_specs=(ANY, ANY),
+        out_specs=(ANY, ANY, ANY),
         scratch_shapes=[
             pltpu.VMEM((tiles, width, dim), BF16),
             pltpu.VMEM((tiles, n_tokens, width), BF16),
@@ -520,9 +525,11 @@
             pltpu.VMEM((n_tokens, dim), BF16),
             pltpu.VMEM((n_tokens, 128), F32),
             pltpu.VMEM((n_tokens, 128), F32),
+            pltpu.VMEM((2, dim, n_tokens), BF16),
             pltpu.SemaphoreType.DMA((tiles,)),
             pltpu.SemaphoreType.DMA((tiles,)),
             pltpu.SemaphoreType.DMA((2, tiles_in)),
+            pltpu.SemaphoreType.DMA,
         ],
         compiler_params=FULL,
         cost_estimate=pl.CostEstimate(
@@ -561,7 +568,7 @@
         pltpu.VMEM((dim, 2 * n_tokens), BF16),
         pltpu.SemaphoreType.DMA((2, block_tiles)),
         pltpu.SemaphoreType.DMA((block_tiles,)),
-        pltpu.SemaphoreType.DMA((2,)),
+        pltpu.SemaphoreType.DMA((1,)),
     ]
     block_shape = jax.ShapeDtypeStruct((block, dim), BF16)
     common = dict(
@@ -572,17 +579,16 @@
     first, operands = pl.pallas_call(
         functools.partial(backward_kernel, False),
         out_shape=(block_shape, jax.ShapeDtypeStruct((dim, 2 * n_tokens), BF16)),
-        in_specs=[SMEM, SMEM, ANY, ANY, ANY, ANY, VMEM],
+        in_specs=[SMEM, SMEM, ANY, ANY, ANY, VMEM],
         out_specs=(ANY, ANY),
         scratch_shapes=[
-            pltpu.VMEM((2, n_tokens, dim), BF16),
-            pltpu.VMEM((n_tokens, dim), F32),
-            pltpu.VMEM((n_tokens, dim), F32),
+            pltpu.VMEM((2, dim, n_tokens), BF16),
+            pltpu.VMEM((n_tokens, 128), F32),
         ] + streams,
         name="backward_first",
         **common,
     )(
-        (dp_at ^ (n_dp - 1))[None], code_at[None], tokens, grad_out, codes, weighed, received
+        (dp_at ^ (n_dp - 1))[None], code_at[None], turned, codes, weighed, received
     )
 
     def backward(at):

time: 82.5 us -> 83.7 us (1.015)
  Pallas kernels: 63.6 us -> 64.8 us
    pallas_call x1, Pallas kernels: 1.37 us -> 2.84 us  [local(): pl.pallas_call(merge_kernel, out_shape=jax.ShapeDtypeStruct((n_code, rows...]
  transfers between devices with their start and end apart: 3 -> 3, of which waited for: 1 -> 2; matrix products, arithmetic and copies ran while one was open for 0% -> 0% of each run, Pallas kernels for 34% -> 34%
where the time goes in v15:
time: 83.7 us; the launch traced here: 83.1 us
  Pallas kernels  64.8 us (77%)
  starting transfers between devices  12.8 us (15%)
  waiting for transfers between devices  4.57 us (5%)
  between operations  0.89 us (1%)
    pallas_call x1, Pallas kernels, local(): pl.pallas_call(functools.partial(forward_kernel, n_code), out_shape=(jax....  30.4 us
    pallas_call x1, Pallas kernels, local(): pl.pallas_call(weigh_kernel, out_shape=(pltpu.HBM((tiles_in, n_tokens, wi...  13 us
    all_to_all x1, starting transfers between devices, local(): received = lax.all_to_all(sent, 'code', 0, 0, tiled=True)  8.34 us
    pallas_call x1, Pallas kernels, local(): pl.pallas_call(functools.partial(backward_kernel, False), out_shape=(bloc...  7.57 us
    pallas_call x1, Pallas kernels, backward(): pl.pallas_call(functools.partial(backward_kernel, True), out_shape=block_...  6.39 us
    all_to_all x1, starting transfers between devices, local(): gathered = lax.all_to_all(spread, 'code', 0, 0, tiled=True)  4.43 us
    all_to_all x1, waiting for transfers between devices, local(): received = lax.all_to_all(sent, 'code', 0, 0, tiled=True)  4.41 us
    pallas_call x1, Pallas kernels, local(): pl.pallas_call(functools.partial(add_kernel, n_dp), out_shape=jax.ShapeDt...  3.59 us
  transfers between devices with their start and end apart: 3, of which 2 were waited for; matrix products, arithmetic and copies ran while one was open for 0% of the time, Pallas kernels for 34%

profile of v15, /device:TPU:0, one launch (start us, length us, event | category | flops | bytes accessed | tf_op | source)
XLA Modules:
  0.0 83.1 jit_solution(13152143781828832296)
XLA Ops:
  0.6 30.4 %forward.1 = (bf16[16,32,640]{2,1,0:T(8,128)(2,1)}, f32[512,128]{1,0:T(8,128)}) custom-call(bf16[512,256]{1,0:T(8,128)(2,1)} %tokens.3, bf16[512,256]{1,0:T(8,128)(2,1)} %grad_out.3, bf16[8192,256]{1,0:T(8,128)(2,1)} %codebook.3, bf16[512,8192]{1,0:T(8,128)(2,1)} %noise.3), custom_call_target="tpu_custom_call" | custom-call | flops 8589934592 | bytes 12582912 | tf_op jit(solution)/shard_map/forward/pallas_call | solution.py:481
  31.1 8.3 %all-to-all-start = ((bf16[16,32,640]{2,1,0:T(8,128)(2,1)}), bf16[16,32,640]{2,1,0:T(8,128)(2,1)S(1)}, u32[]{:S(2)}, u32[]{:S(2)}) async-start(bf16[16,32,640]{2,1,0:T(8,128)(2,1)} %get-tuple-element.16), calls=%async_computation | async-start | bytes 1310720 | tf_op jit(solution)/shard_map/all_to_all | solution.py:513
  39.4 13.0 %weigh.1 = (bf16[16,512,512]{2,1,0:T(8,128)(2,1)}, bf16[16,512,512]{2,1,0:T(8,128)(2,1)}, bf16[2,256,512]{2,1,0:T(8,128)(2,1)}) custom-call(bf16[512,256]{1,0:T(8,128)(2,1)} %tokens.3, bf16[512,256]{1,0:T(8,128)(2,1)} %grad_out.3, bf16[8192,256]{1,0:T(8,128)(2,1)} %codebook.3, bf16[512,8192]{1,0:T(8,128)(2,1)} %noise.3, f32[512,128]{1,0:T(8,128)} %get-tuple-element.17.sides), custom_call_target="tpu_custom_call" | custom-call | flops 4294967296 | bytes 29360128 | tf_op jit(solution)/shard_map/weigh/pallas_call | solution.py:514
  52.4 4.4 %all-to-all-done.received.rest_4_ = bf16[16,32,640]{2,1,0:T(8,128)(2,1)S(1)} async-done(((bf16[16,32,640]{2,1,0:T(8,128)(2,1)}), bf16[16,32,640]{2,1,0:T(8,128)(2,1)S(1)}, u32[]{:S(2)}, u32[]{:S(2)}) %all-to-all-start) | async-done | bytes 655392 | tf_op jit(solution)/shard_map/all_to_all | solution.py:513
  56.8 0.0 copy-start
  56.8 2.8 %merge.1 = bf16[16,32,512]{2,1,0:T(8,128)(2,1)} custom-call(s32[1]{0:T(128)} %bitcast.me.rest_0_, bf16[16,32,640]{2,1,0:T(8,128)(2,1)S(1)} %all-to-all-done.received.rest_4_), custom_call_target="tpu_custom_call" | custom-call | tf_op jit(solution)/shard_map/merge/pallas_call | solution.py:542
  59.7 4.4 %all-to-all-start.1 = ((bf16[16,32,512]{2,1,0:T(8,128)(2,1)}), bf16[16,32,512]{2,1,0:T(8,128)(2,1)S(1)}, u32[]{:S(2)}, u32[]{:S(2)}) async-start(bf16[16,32,512]{2,1,0:T(8,128)(2,1)} %merge.1), calls=%async_computation.1 | async-start | bytes 1048576 | tf_op jit(solution)/shard_map/all_to_all | solution.py:551
  64.1 0.0 copy-done
  64.1 7.6 %backward_first.1 = (bf16[4096,256]{1,0:T(8,128)(2,1)}, bf16[256,1024]{1,0:T(8,128)(2,1)}) custom-call(s32[1]{0:T(128)} %bitcast.1.block, s32[1]{0:T(128)} %bitcast.me.rest_0_, bf16[2,256,512]{2,1,0:T(8,128)(2,1)} %get-tuple-element.23.rest_1_, bf16[16,512,512]{2,1,0:T(8,128)(2,1)} %get-tuple-element.24.rest_2_.rest_0_, ...), custom_call_target="tpu_custom_call" | custom-call | flops 1 | bytes 1 | tf_op jit(solution)/shard_map/backward_first/pallas_call | solution.py:579
  71.7 0.1 collective-permute-start
  71.8 6.4 %backward.1.refs_1_ = bf16[4096,256]{1,0:T(8,128)(2,1)} custom-call(s32[1]{0:T(128)} %bitcast.2.block, bf16[16,512,512]{2,1,0:T(8,128)(2,1)} %get-tuple-element.24.rest_2_.rest_0_, bf16[16,512,512]{2,1,0:T(8,128)(2,1)} %get-tuple-element.25.rest_3_.rest_1_, bf16[256,1024]{1,0:T(8,128)(2,1)} %get-tuple-element.28.rest_2_), custom_call_target="tpu_custom_call" | custom-call | flops 1 | bytes 1 | tf_op jit(solution)/shard_map/backward/pallas_call | solution.py:595
  78.2 0.2 all-to-all-done.1.gathered
  78.3 1.0 %unpack.1 = (f32[512,256]{1,0:T(8,128)}, f32[512,256]{1,0:T(8,128)}) custom-call(bf16[16,32,512]{2,1,0:T(8,128)(2,1)S(1)} %all-to-all-done.1.gathered), custom_call_target="tpu_custom_call" | custom-call | flops 214748364800 | bytes 419430400 | tf_op jit(solution)/shard_map/unpack/pallas_call | solution.py:552
  79.4 0.0 collective-permute-done.refs_0_
  79.4 3.6 %add.1 = f32[4096,256]{1,0:T(8,128)} custom-call(bf16[4096,256]{1,0:T(8,128)(2,1)} %collective-permute-done.refs_0_, bf16[4096,256]{1,0:T(8,128)(2,1)} %backward.1.refs_1_), custom_call_target="tpu_custom_call" | custom-call | bytes 8388608 | tf_op jit(solution)/shard_map/add/pallas_call | solution.py:609
Async XLA Ops:
  31.1 25.8 %all-to-all-start = ((bf16[16,32,640]{2,1,0:T(8,128)(2,1)}), bf16[16,32,640]{2,1,0:T(8,128)(2,1)S(1)}, u32[]{:S(2)}, u32[]{:S(2)}) async-start(bf16[16,32,640]{2,1,0:T(8,128)(2,1)} %get-tuple-element.16), calls=%async_computation | async-start | bytes 1310720 | tf_op jit(solution)/shard_map/all_to_all | solution.py:513
  56.8 7.3 %copy-start = (bf16[16,32,640]{2,1,0:T(8,128)(2,1)}, bf16[16,32,640]{2,1,0:T(8,128)(2,1)S(1)}, u32[]{:S(2)}) copy-start(bf16[16,32,640]{2,1,0:T(8,128)(2,1)S(1)} %all-to-all-done.received.rest_4_) | copy-start | bytes 1966084
  59.7 18.7 %all-to-all-start.1 = ((bf16[16,32,512]{2,1,0:T(8,128)(2,1)}), bf16[16,32,512]{2,1,0:T(8,128)(2,1)S(1)}, u32[]{:S(2)}, u32[]{:S(2)}) async-start(bf16[16,32,512]{2,1,0:T(8,128)(2,1)} %merge.1), calls=%async_computation.1 | async-start | bytes 1048576 | tf_op jit(solution)/shard_map/all_to_all | solution.py:551
  71.7 7.7 %collective-permute-start = (bf16[4096,256]{1,0:T(8,128)(2,1)}, bf16[4096,256]{1,0:T(8,128)(2,1)}, u32[]{:S(2)}, u32[]{:S(2)}) collective-permute-start(bf16[4096,256]{1,0:T(8,128)(2,1)} %get-tuple-element.27), channel_id=1, source_target_pairs={{0,16},{16,0},{1,17},{17,1},{2,18},{18,2},{3,19},{19,3},{4,20},{20... | collective-permute-start | bytes 6291464 | tf_op jit(solution)/shard_map/ppermute | solution.py:466

commit v16 on v15

--- a/solution.py
+++ b/solution.py
@@ -16,6 +16,7 @@
 WIDE = 512
 AHEAD = 2
 NEAR = 3
+PACK = 16
 ROWS = 64
 LARGEST = 2.0**60
 VMEM = pl.BlockSpec(memory_space=pltpu.VMEM)
@@ -37,8 +38,8 @@
     return [value[:, j : j + 128] for j in range(0, value.shape[1], 128)]
 
 
-def stat_lanes(n_code):
-    return max(8 * n_code, 128)
+def stat_lanes(n_tokens):
+    return max(n_tokens // PACK * 4, 128)
 
 
 def high_low(value):
@@ -48,8 +49,8 @@
 
 def forward_kernel(
     n_code, tokens, grad_out, codebook, noise, sent, sides,
-    pair, book, noise_in, slot_a, slot_b, shifts, total, sums, sent_out, sides_out,
-    pair_sem, book_sem, noise_sem, first_sem, out_sem,
+    own, pair, book, noise_in, slot_a, slot_b, shifts, total, sums, sent_out, sides_out,
+    own_sem, book_sem, noise_sem, first_sem, out_sem,
 ):
     tiles, width, dim = book.shape
     n_tokens = tokens.shape[0]
@@ -71,16 +72,10 @@
         for copy in fetch(t):
             copy.wait()
 
-    pair_copies = []
-    for r in range(0, n_tokens, ROWS):
-        for half, source in enumerate((tokens, grad_out)):
-            pair_copies.append(
-                pltpu.make_async_copy(
-                    source.at[pl.ds(r, ROWS)],
-                    pair.at[pl.ds(2 * r + half * ROWS, ROWS)],
-                    pair_sem.at[len(pair_copies)],
-                )
-            )
+    own_copies = (
+        pltpu.make_async_copy(tokens, own.at[0], own_sem.at[0]),
+        pltpu.make_async_copy(grad_out, own.at[1], own_sem.at[1]),
+    )
     halves = []
     for h in range(2):
         at = pl.ds(h * (width // 2), width // 2)
@@ -88,10 +83,8 @@
             pltpu.make_async_copy(codebook.at[at], book.at[0, at], first_sem.at[h, 0]),
             pltpu.make_async_copy(noise.at[:, at], noise_in.at[0, :, at], first_sem.at[h, 1]),
         ))
-    halves[0][0].start()
-    for copy in pair_copies:
+    for copy in own_copies + halves[0]:
         copy.start()
-    halves[0][1].start()
     for copy in halves[1]:
         copy.start()
 
@@ -178,10 +171,11 @@
         fits = jnp.max(total[...]) < LARGEST
         return again + 1, jnp.logical_and(fresh, jnp.logical_not(fits))
 
-    for copy in pair_copies:
+    for copy in own_copies:
         copy.wait()
     for r in range(0, n_tokens, ROWS):
-        pair[2 * r : 2 * r + ROWS] = pair[2 * r : 2 * r + ROWS] * BF16(SHARPNESS)
+        pair[2 * r : 2 * r + ROWS] = own[0, r : r + ROWS] * BF16(SHARPNESS)
+        pair[2 * r + ROWS : 2 * r + 2 * ROWS] = own[1, r : r + ROWS]
     for copy in halves[0]:
         copy.wait()
     for t in range(1, min(AHEAD + 1, tiles)):
@@ -192,33 +186,30 @@
     mix = sums[:n_tokens]
     pulled = sums[n_tokens:]
     own_total = jnp.sum(total[...], axis=1, keepdims=True)
-    own_grad = jnp.concatenate(
-        [pair[2 * r + ROWS : 2 * r + 2 * ROWS] for r in range(0, n_tokens, ROWS)], axis=0
-    )
-    own_inner = jnp.sum(own_grad.astype(F32) * mix, axis=1, keepdims=True)
+    own_inner = jnp.sum(own[1].astype(F32) * mix, axis=1, keepdims=True)
     mean = own_inner / own_total
     side = lax.broadcasted_iota(jnp.int32, sides_out.shape, 1)
     sides_out[...] = jnp.where(side < 64, mean, shift)
     copies = [pltpu.make_async_copy(sides_out, sides, out_sem.at[0])]
     copies[0].start()
     rows = n_tokens // n_code
-    lanes = stat_lanes(n_code)
-    half = lanes // 2
-    lane = lax.broadcasted_iota(jnp.int32, (rows, lanes), 1)
-    stats = jnp.zeros((rows, lanes), F32)
-    parts = high_low(own_total) + high_low(own_inner)
-    for g in range(n_code):
-        at = slice(g * rows, (g + 1) * rows)
+    lanes = stat_lanes(n_tokens)
+    lane = lax.broadcasted_iota(jnp.int32, (PACK, lanes), 1)
+    stats = jnp.zeros((PACK, lanes), F32)
+    parts = (own_total,) + high_low(mean) + (shift,)
+    for q in range(n_tokens // PACK):
         for i, part in enumerate(parts):
-            stats = jnp.where(lane == 4 * g + i, part[at], stats)
-        stats = jnp.where((lane - half) // 4 == g, shift[at], stats)
-    stats = stats.astype(BF16)
+            stats = jnp.where(lane == 4 * q + i, part[q * PACK : (q + 1) * PACK], stats)
+    stats = [stats[:, j : j + 128].astype(BF16) for j in range(0, lanes, 128)]
     group = n_code // min(n_code, 4)
     for g in range(n_code):
         at = slice(g * rows, (g + 1) * rows)
-        sent_out[g, :, :dim] = mix[at].astype(BF16)
-        sent_out[g, :, dim : 2 * dim] = (pulled[at] - mean[at] * mix[at]).astype(BF16)
-        sent_out[g, :, 2 * dim :] = stats
+        data = lane_groups(mix[at]) + lane_groups(pulled[at] - mean[at] * mix[at])
+        for j, value in enumerate(data):
+            sent_out[g, j * rows : (j + 1) * rows] = value.astype(BF16)
+        for j, value in enumerate(stats):
+            first = len(data) * rows + j * PACK
+            sent_out[g, first : first + PACK] = value
         if (g + 1) % group == 0:
             part = pl.ds(g + 1 - group, group)
             copies.append(
@@ -233,46 +224,59 @@
     return pltpu.roll(value, value.shape[1] - by, 1)
 
 
-def pair_sums(value):
-    both = value + roll_left(value, 1)
-    return both, roll_left(both, 2)
-
-
-def merged_stats(received):
-    n_code = received.shape[0]
-    lanes = stat_lanes(n_code)
-    stats = [received[p, :, received.shape[2] - lanes :].astype(F32) for p in range(n_code)]
+def stats_of(received, p, n_tokens):
+    first = received.shape[1] - stat_lanes(n_tokens) // 128 * PACK
+    blocks = [received[p, r : r + PACK] for r in range(first, received.shape[1], PACK)]
+    return jnp.concatenate(blocks, axis=1).astype(F32)
+
+
+def factor_of(stats, top):
+    return roll_left(jnp.exp(stats - top), 3)
+
+
+def mean_of(stats):
+    return roll_left(stats, 1) + roll_left(stats, 2)
+
+
+def merged_stats(received, n_tokens):
+    stats = [stats_of(received, p, n_tokens) for p in range(received.shape[0])]
     top = functools.reduce(jnp.maximum, stats)
-    factors = [roll_left(jnp.exp(s - top), lanes // 2) for s in stats]
-    total, inner = pair_sums(sum(f * s for f, s in zip(factors, stats)))
-    return stats, factors, top, total, inner / total
+    factors = [factor_of(s, top) * s for s in stats]
+    means = [mean_of(s) for s in stats]
+    total = sum(factors)
+    inner = sum(f * m for f, m in zip(factors, means)) / total
+    scales = [factor_of(s, top) / total for s in stats]
+    return scales, means, top, total, inner
 
 
 def merge_kernel(me, received, spread):
-    n_code, rows, _ = received.shape
-    dim = spread.shape[2] // 2
-    stats, factors, _, total, inner = merged_stats(received)
+    n_code, rows, both = spread.shape
+    dim = both // 2
+    scales, means, _, _, inner = merged_stats(received, n_code * rows)
     lane = lax.broadcasted_iota(jnp.int32, inner.shape, 1)
-    mine = lane == 4 * me[0]
+    groups = rows // PACK
+    mine = [lane == 4 * (me[0] * groups + h) for h in range(groups)]
 
     def column(value):
-        return jnp.sum(jnp.where(mine, value, 0.0), axis=1, keepdims=True)
-
-    quantized = jnp.zeros((rows, dim), F32)
-    gradient = jnp.zeros((rows, dim), F32)
+        columns = [jnp.sum(jnp.where(m, value, 0.0), axis=1, keepdims=True) for m in mine]
+        return jnp.concatenate(columns, axis=0)
+
+    count = dim // 128
+    quantized = [jnp.zeros((rows, 128), F32)] * count
+    gradient = [jnp.zeros((rows, 128), F32)] * count
     for p in range(n_code):
-        own_total, own_inner = pair_sums(stats[p])
-        factor = column(factors[p])
-        offset = column(factors[p] * (own_inner / own_total - inner))
-        mix = received[p, :, :dim].astype(F32)
-        quantized += factor * mix
-        gradient += factor * received[p, :, dim : 2 * dim].astype(F32) + offset * mix
-    scale = 1.0 / column(total)
-    quantized = (quantized * scale).astype(BF16)
-    gradient = (gradient * (scale / SOFTMAX_HEAT)).astype(BF16)
-    for p in range(n_code):
-        spread[p, :, :dim] = quantized
-        spread[p, :, dim:] = gradient
+        scale = column(scales[p])
+        offset = column(scales[p] * (means[p] - inner))
+        for j in range(count):
+            mix = received[p, j * rows : (j + 1) * rows].astype(F32)
+            pulled = received[p, (count + j) * rows : (count + j + 1) * rows].astype(F32)
+            quantized[j] += scale * mix
+            gradient[j] += scale * pulled + offset * mix
+    for j in range(count):
+        results = (quantized[j].astype(BF16), (gradient[j] / SOFTMAX_HEAT).astype(BF16))
+        for p in range(n_code):
+            for i, result in enumerate(results):
+                spread[p, :, i * dim + j * 128 : i * dim + (j + 1) * 128] = result
 
 
 def weigh_kernel(
@@ -375,17 +379,16 @@
     if prepared:
         own_copies[0].wait()
     else:
-        n_code, rows, _ = received.shape
-        _, _, top, total, inner = merged_stats(received)
-        lanes = top.shape[1]
-        stats = received[code_at[0], :, received.shape[2] - lanes :].astype(F32)
-        own_total, own_inner = pair_sums(stats)
-        scale = roll_left(jnp.exp(stats - top), lanes // 2) / total
-        offset = scale * (own_inner / own_total - inner)
-        lane = lax.broadcasted_iota(jnp.int32, (rows, 128), 1)
-        for g in range(n_code):
-            at = slice(4 * g, 4 * g + 1)
-            spread[g * rows : (g + 1) * rows] = jnp.where(lane < 64, scale[:, at], offset[:, at])
+        _, _, top, total, inner = merged_stats(received, n_tokens)
+        stats = stats_of(received, code_at[0], n_tokens)
+        scale = factor_of(stats, top) / total
+        offset = scale * (mean_of(stats) - inner)
+        lane = lax.broadcasted_iota(jnp.int32, (PACK, 128), 1)
+        for q in range(n_tokens // PACK):
+            at = slice(4 * q, 4 * q + 1)
+            spread[q * PACK : (q + 1) * PACK] = jnp.where(
+                lane < 64, scale[:, at], offset[:, at]
+            )
         factors = spread[...].T
         scale, offset = factors[:1], factors[64:65]
         own_copies[0].wait()
@@ -475,18 +478,19 @@
     wide = min(WIDE, width)
     tiles_in = n_codes // wide
     tiles = n_codes // width
-    lanes = stat_lanes(n_code)
+    piece = rows * (2 * dim // 128) + stat_lanes(n_tokens) // 128 * PACK
     products = 2 * n_tokens * n_codes * dim
 
     sent, sides = pl.pallas_call(
         functools.partial(forward_kernel, n_code),
         out_shape=(
-            jax.ShapeDtypeStruct((n_code, rows, 2 * dim + lanes), BF16),
+            jax.ShapeDtypeStruct((n_code, piece, 128), BF16),
             jax.ShapeDtypeStruct((n_tokens, 128), F32),
         ),
         in_specs=[ANY, ANY, ANY, ANY],
         out_specs=(ANY, ANY),
         scratch_shapes=[
+            pltpu.VMEM((2, n_tokens, dim), BF16),
             pltpu.VMEM((2 * n_tokens, dim), BF16),
             pltpu.VMEM((tiles, width, dim), BF16),
             pltpu.VMEM((tiles, n_tokens, width), BF16),
@@ -495,9 +499,9 @@
             pltpu.VMEM((n_tokens, 128), F32),
             pltpu.VMEM((n_tokens, 128), F32),
             pltpu.VMEM((2 * n_tokens, dim), F32),
-            pltpu.VMEM((n_code, rows, 2 * dim + lanes), BF16),
+            pltpu.VMEM((n_code, piece, 128), BF16),
             pltpu.VMEM((n_tokens, 128), F32),
-            pltpu.SemaphoreType.DMA((2 * n_tokens // ROWS,)),
+            pltpu.SemaphoreType.DMA((2,)),
             pltpu.SemaphoreType.DMA((tiles,)),
             pltpu.SemaphoreType.DMA((tiles,)),
             pltpu.SemaphoreType.DMA((2, 2)),

time: 83.7 us -> 80.9 us (0.967)
  Pallas kernels: 64.8 us -> 63.5 us
  waiting for transfers between devices: 4.57 us -> 3.28 us
    pallas_call x1, Pallas kernels: 2.84 us -> 1.45 us  [local(): pl.pallas_call(merge_kernel, out_shape=jax.ShapeDtypeStruct((n_code, rows...]
    all_to_all x1, waiting for transfers between devices: 4.41 us -> 3.28 us  [local(): received = lax.all_to_all(sent, 'code', 0, 0, tiled=True)]
  transfers between devices with their start and end apart: 3 -> 3, of which waited for: 2 -> 1; matrix products, arithmetic and copies ran while one was open for 0% -> 0% of each run, Pallas kernels for 34% -> 35%
where the time goes in v16:
time: 80.9 us; the launch traced here: 80.3 us
  Pallas kernels  63.5 us (78%)
  starting transfers between devices  12.6 us (16%)
  waiting for transfers between devices  3.28 us (4%)
  between operations  0.89 us (1%)
    pallas_call x1, Pallas kernels, local(): pl.pallas_call(functools.partial(forward_kernel, n_code), out_shape=(jax....  30.3 us
    pallas_call x1, Pallas kernels, local(): pl.pallas_call(weigh_kernel, out_shape=(pltpu.HBM((tiles_in, n_tokens, wi...  13 us
    all_to_all x1, starting transfers between devices, local(): received = lax.all_to_all(sent, 'code', 0, 0, tiled=True)  8.32 us
    pallas_call x1, Pallas kernels, local(): pl.pallas_call(functools.partial(backward_kernel, False), out_shape=(bloc...  7.82 us
    pallas_call x1, Pallas kernels, backward(): pl.pallas_call(functools.partial(backward_kernel, True), out_shape=block_...  6.39 us
    all_to_all x1, starting transfers between devices, local(): gathered = lax.all_to_all(spread, 'code', 0, 0, tiled=True)  4.16 us
    pallas_call x1, Pallas kernels, local(): pl.pallas_call(functools.partial(add_kernel, n_dp), out_shape=jax.ShapeDt...  3.59 us
    all_to_all x1, waiting for transfers between devices, local(): received = lax.all_to_all(sent, 'code', 0, 0, tiled=True)  3.28 us
  transfers between devices with their start and end apart: 3, of which 1 were waited for; matrix products, arithmetic and copies ran while one was open for 0% of the time, Pallas kernels for 35%

profile of v16, /device:TPU:0, one launch (start us, length us, event | category | flops | bytes accessed | tf_op | source)
XLA Modules:
  0.0 80.3 jit_solution(3808380431125075723)
XLA Ops:
  0.6 30.3 %forward.1 = (bf16[16,144,128]{2,1,0:T(8,128)(2,1)}, f32[512,128]{1,0:T(8,128)}) custom-call(bf16[512,256]{1,0:T(8,128)(2,1)} %tokens.3, bf16[512,256]{1,0:T(8,128)(2,1)} %grad_out.3, bf16[8192,256]{1,0:T(8,128)(2,1)} %codebook.3, bf16[512,8192]{1,0:T(8,128)(2,1)} %noise.3), custom_call_target="tpu_custom_call" | custom-call | flops 8589934592 | bytes 12582912 | tf_op jit(solution)/shard_map/forward/pallas_call | solution.py:484
  30.9 8.3 %all-to-all-start = ((bf16[16,144,128]{2,1,0:T(8,128)(2,1)}), bf16[16,144,128]{2,1,0:T(8,128)(2,1)S(1)}, u32[]{:S(2)}, u32[]{:S(2)}) async-start(bf16[16,144,128]{2,1,0:T(8,128)(2,1)} %get-tuple-element.16), calls=%async_computation | async-start | bytes 1179648 | tf_op jit(solution)/shard_map/all_to_all | solution.py:517
  39.2 13.0 %weigh.1 = (bf16[16,512,512]{2,1,0:T(8,128)(2,1)}, bf16[16,512,512]{2,1,0:T(8,128)(2,1)}, bf16[2,256,512]{2,1,0:T(8,128)(2,1)}) custom-call(bf16[512,256]{1,0:T(8,128)(2,1)} %tokens.3, bf16[512,256]{1,0:T(8,128)(2,1)} %grad_out.3, bf16[8192,256]{1,0:T(8,128)(2,1)} %codebook.3, bf16[512,8192]{1,0:T(8,128)(2,1)} %noise.3, f32[512,128]{1,0:T(8,128)} %get-tuple-element.17.sides), custom_call_target="tpu_custom_call" | custom-call | flops 4294967296 | bytes 29360128 | tf_op jit(solution)/shard_map/weigh/pallas_call | solution.py:518
  52.2 3.3 %all-to-all-done.received.rest_4_ = bf16[16,144,128]{2,1,0:T(8,128)(2,1)S(1)} async-done(((bf16[16,144,128]{2,1,0:T(8,128)(2,1)}), bf16[16,144,128]{2,1,0:T(8,128)(2,1)S(1)}, u32[]{:S(2)}, u32[]{:S(2)}) %all-to-all-start) | async-done | bytes 589856 | tf_op jit(solution)/shard_map/all_to_all | solution.py:517
  55.5 0.0 copy-start
  55.5 1.4 %merge.1 = bf16[16,32,512]{2,1,0:T(8,128)(2,1)} custom-call(s32[1]{0:T(128)} %bitcast.me.rest_0_, bf16[16,144,128]{2,1,0:T(8,128)(2,1)S(1)} %all-to-all-done.received.rest_4_), custom_call_target="tpu_custom_call" | custom-call | tf_op jit(solution)/shard_map/merge/pallas_call | solution.py:546
  57.0 4.2 %all-to-all-start.1 = ((bf16[16,32,512]{2,1,0:T(8,128)(2,1)}), bf16[16,32,512]{2,1,0:T(8,128)(2,1)S(1)}, u32[]{:S(2)}, u32[]{:S(2)}) async-start(bf16[16,32,512]{2,1,0:T(8,128)(2,1)} %merge.1), calls=%async_computation.1 | async-start | bytes 1048576 | tf_op jit(solution)/shard_map/all_to_all | solution.py:555
  61.1 0.0 copy-done
  61.1 7.8 %backward_first.1 = (bf16[4096,256]{1,0:T(8,128)(2,1)}, bf16[256,1024]{1,0:T(8,128)(2,1)}) custom-call(s32[1]{0:T(128)} %bitcast.1.block, s32[1]{0:T(128)} %bitcast.me.rest_0_, bf16[2,256,512]{2,1,0:T(8,128)(2,1)} %get-tuple-element.23.rest_1_, bf16[16,512,512]{2,1,0:T(8,128)(2,1)} %get-tuple-element.24.rest_2_.rest_0_, ...), custom_call_target="tpu_custom_call" | custom-call | flops 1 | bytes 1 | tf_op jit(solution)/shard_map/backward_first/pallas_call | solution.py:583
  69.0 0.1 collective-permute-start
  69.1 6.4 %backward.1.refs_1_ = bf16[4096,256]{1,0:T(8,128)(2,1)} custom-call(s32[1]{0:T(128)} %bitcast.2.block, bf16[16,512,512]{2,1,0:T(8,128)(2,1)} %get-tuple-element.24.rest_2_.rest_0_, bf16[16,512,512]{2,1,0:T(8,128)(2,1)} %get-tuple-element.25.rest_3_.rest_1_, bf16[256,1024]{1,0:T(8,128)(2,1)} %get-tuple-element.28.rest_2_), custom_call_target="tpu_custom_call" | custom-call | flops 1 | bytes 1 | tf_op jit(solution)/shard_map/backward/pallas_call | solution.py:599
  75.5 0.0 all-to-all-done.1.gathered
  75.5 1.0 %unpack.1 = (f32[512,256]{1,0:T(8,128)}, f32[512,256]{1,0:T(8,128)}) custom-call(bf16[16,32,512]{2,1,0:T(8,128)(2,1)S(1)} %all-to-all-done.1.gathered), custom_call_target="tpu_custom_call" | custom-call | flops 214748364800 | bytes 419430400 | tf_op jit(solution)/shard_map/unpack/pallas_call | solution.py:556
  76.5 0.0 collective-permute-done.refs_0_
  76.5 3.6 %add.1 = f32[4096,256]{1,0:T(8,128)} custom-call(bf16[4096,256]{1,0:T(8,128)(2,1)} %collective-permute-done.refs_0_, bf16[4096,256]{1,0:T(8,128)(2,1)} %backward.1.refs_1_), custom_call_target="tpu_custom_call" | custom-call | bytes 8388608 | tf_op jit(solution)/shard_map/add/pallas_call | solution.py:613
Async XLA Ops:
  30.9 24.6 %all-to-all-start = ((bf16[16,144,128]{2,1,0:T(8,128)(2,1)}), bf16[16,144,128]{2,1,0:T(8,128)(2,1)S(1)}, u32[]{:S(2)}, u32[]{:S(2)}) async-start(bf16[16,144,128]{2,1,0:T(8,128)(2,1)} %get-tuple-element.16), calls=%async_computation | async-start | bytes 1179648 | tf_op jit(solution)/shard_map/all_to_all | solution.py:517
  55.5 5.6 %copy-start = (bf16[16,144,128]{2,1,0:T(8,128)(2,1)}, bf16[16,144,128]{2,1,0:T(8,128)(2,1)S(1)}, u32[]{:S(2)}) copy-start(bf16[16,144,128]{2,1,0:T(8,128)(2,1)S(1)} %all-to-all-done.received.rest_4_) | copy-start | bytes 1769476
  57.0 18.5 %all-to-all-start.1 = ((bf16[16,32,512]{2,1,0:T(8,128)(2,1)}), bf16[16,32,512]{2,1,0:T(8,128)(2,1)S(1)}, u32[]{:S(2)}, u32[]{:S(2)}) async-start(bf16[16,32,512]{2,1,0:T(8,128)(2,1)} %merge.1), calls=%async_computation.1 | async-start | bytes 1048576 | tf_op jit(solution)/shard_map/all_to_all | solution.py:555
  69.0 7.5 %collective-permute-start = (bf16[4096,256]{1,0:T(8,128)(2,1)}, bf16[4096,256]{1,0:T(8,128)(2,1)}, u32[]{:S(2)}, u32[]{:S(2)}) collective-permute-start(bf16[4096,256]{1,0:T(8,128)(2,1)} %get-tuple-element.27), channel_id=1, source_target_pairs={{0,16},{16,0},{1,17},{17,1},{2,18},{18,2},{3,19},{19,3},{4,20},{20... | collective-permute-start | bytes 6291464 | tf_op jit(solution)/shard_map/ppermute | solution.py:469

commit v17 on v16

--- a/solution.py
+++ b/solution.py
@@ -18,13 +18,12 @@
 NEAR = 3
 PACK = 16
 ROWS = 64
-LARGEST = 2.0**60
+LARGEST = 2.0**30
 VMEM = pl.BlockSpec(memory_space=pltpu.VMEM)
 SMEM = pl.BlockSpec(memory_space=pltpu.SMEM)
 ANY = pl.BlockSpec(memory_space=pl.ANY)
 FULL = pltpu.CompilerParams(vmem_limit_bytes=60 * MIB)
-MOST = pltpu.CompilerParams(vmem_limit_bytes=56 * MIB)
-PART = pltpu.CompilerParams(vmem_limit_bytes=58 * MIB)
+MOST = pltpu.CompilerParams(vmem_limit_bytes=54 * MIB)
 SOME = pltpu.CompilerParams(vmem_limit_bytes=24 * MIB)
 
 
@@ -138,7 +137,11 @@
 
         @pl.when(fresh)
         def _():
-            raise_shift(0, columns[:1])
+            for r in range(0, n_tokens, ROWS):
+                some = noise_in[0, r : r + ROWS, columns[0]] * BF16(SHARPNESS)
+                shifts[r : r + ROWS] = functools.reduce(
+                    jnp.maximum, lane_groups(some.astype(F32))
+                )
 
         @pl.when(jnp.logical_not(fresh))
         def _():
@@ -168,7 +171,9 @@
         lax.fori_loop(0, tiles // 2 - 1, soften_pair, 0)
         soften(tiles - 1, 1, fresh, lambda: accumulate(tiles - 2, 0))
         accumulate(tiles - 1, 1)
-        fits = jnp.max(total[...]) < LARGEST
+        row_total = jnp.sum(total[...], axis=1, keepdims=True)
+        total[...] = jnp.broadcast_to(row_total, total.shape)
+        fits = jnp.logical_and(jnp.max(total[...]) < LARGEST, jnp.min(total[...]) > 1 / LARGEST)
         return again + 1, jnp.logical_and(fresh, jnp.logical_not(fits))
 
     for copy in own_copies:
@@ -185,7 +190,7 @@
     shift = shifts[:, :1]
     mix = sums[:n_tokens]
     pulled = sums[n_tokens:]
-    own_total = jnp.sum(total[...], axis=1, keepdims=True)
+    own_total = total[:, :1]
     own_inner = jnp.sum(own[1].astype(F32) * mix, axis=1, keepdims=True)
     mean = own_inner / own_total
     side = lax.broadcasted_iota(jnp.int32, sides_out.shape, 1)
@@ -348,8 +353,10 @@
         codes, weighed, given, out, *rest = rest
     else:
         code_at, turned, codes, weighed, received, out, kept, own, spread, *rest = rest
-    both_in, result, operands, in_sem, out_sem, own_sem = rest
-    tiles, width, dim = result.shape
+    both_in, operands, in_sem, own_sem, *rest = rest
+    tiles, _, width = both_in.shape
+    if not prepared:
+        result, out_sem = rest
     n_tokens = both_in.shape[1] // 2
 
     def fetch(t):
@@ -420,17 +427,20 @@
         value = ahead
         if k + 1 < len(steps):
             ahead = product(steps[k + 1])
-        result[t, c] = value.astype(BF16).T
-        if c.stop == width:
-            send(t).start()
-    for t in range(tiles):
-        send(t).wait()
+        if prepared:
+            out[t * width + c.start : t * width + c.stop] = value.astype(BF16).T
+        else:
+            result[t, c] = value.astype(BF16).T
+            if c.stop == width:
+                send(t).start()
     if not prepared:
         keep.wait()
+        for t in range(tiles):
+            send(t).wait()
 
 
 def add_kernel(n_parts, *refs):
-    parts, out = refs[:n_parts], refs[n_parts]
+    parts, own, out = refs[: n_parts - 1], refs[n_parts - 1], refs[n_parts]
     held, result, in_sem, out_sem = refs[n_parts + 1 :]
     steps, rows, _ = result.shape
 
@@ -450,7 +460,8 @@
     for i in range(steps):
         for copy in fetch(i):
             copy.wait()
-        result[i] = sum(held[j, i].astype(F32) for j in range(n_parts))
+        mine = own[i * rows : (i + 1) * rows].astype(F32)
+        result[i] = sum((held[j, i].astype(F32) for j in range(len(parts))), mine)
         send(i).start()
     for i in range(steps):
         send(i).wait()
@@ -568,13 +579,10 @@
     block_tiles = block // wide
     streams = [
         pltpu.VMEM((block_tiles, 2 * n_tokens, wide), BF16),
-        pltpu.VMEM((block_tiles, wide, dim), BF16),
         pltpu.VMEM((dim, 2 * n_tokens), BF16),
         pltpu.SemaphoreType.DMA((2, block_tiles)),
-        pltpu.SemaphoreType.DMA((block_tiles,)),
         pltpu.SemaphoreType.DMA((1,)),
     ]
-    block_shape = jax.ShapeDtypeStruct((block, dim), BF16)
     common = dict(
         compiler_params=MOST,
         cost_estimate=pl.CostEstimate(flops=1, bytes_accessed=1, transcendentals=0),
@@ -582,13 +590,19 @@
     dp_at = lax.axis_index("dp")
     first, operands = pl.pallas_call(
         functools.partial(backward_kernel, False),
-        out_shape=(block_shape, jax.ShapeDtypeStruct((dim, 2 * n_tokens), BF16)),
+        out_shape=(
+            jax.ShapeDtypeStruct((block, dim), BF16),
+            jax.ShapeDtypeStruct((dim, 2 * n_tokens), BF16),
+        ),
         in_specs=[SMEM, SMEM, ANY, ANY, ANY, VMEM],
         out_specs=(ANY, ANY),
         scratch_shapes=[
             pltpu.VMEM((2, dim, n_tokens), BF16),
             pltpu.VMEM((n_tokens, 128), F32),
-        ] + streams,
+        ] + streams + [
+            pltpu.VMEM((block_tiles, wide, dim), BF16),
+            pltpu.SemaphoreType.DMA((block_tiles,)),
+        ],
         name="backward_first",
         **common,
     )(
@@ -598,9 +612,9 @@
     def backward(at):
         return pl.pallas_call(
             functools.partial(backward_kernel, True),
-            out_shape=block_shape,
+            out_shape=pltpu.VMEM((block, dim), BF16),
             in_specs=[SMEM, ANY, ANY, ANY],
-            out_specs=ANY,
+            out_specs=VMEM,
             scratch_shapes=streams,
             name="backward",
             **common,
@@ -613,15 +627,15 @@
     own_rows = pl.pallas_call(
         functools.partial(add_kernel, n_dp),
         out_shape=jax.ShapeDtypeStruct((block, dim), F32),
-        in_specs=[ANY] * n_dp,
+        in_specs=[ANY] * (n_dp - 1) + [VMEM],
         out_specs=ANY,
         scratch_shapes=[
-            pltpu.VMEM((n_dp, steps, block // steps, dim), BF16),
+            pltpu.VMEM((n_dp - 1, steps, block // steps, dim), BF16),
             pltpu.VMEM((steps, block // steps, dim), F32),
-            pltpu.SemaphoreType.DMA((n_dp, steps)),
+            pltpu.SemaphoreType.DMA((n_dp - 1, steps)),
             pltpu.SemaphoreType.DMA((steps,)),
         ],
-        compiler_params=PART,
+        compiler_params=SOME,
         cost_estimate=pl.CostEstimate(
             flops=0, bytes_accessed=(2 * n_dp + 4) * block * dim, transcendentals=0
         ),

time: 80.9 us -> 80.4 us (level)
  Pallas kernels: 63.5 us -> 62.4 us
  transfers between devices with their start and end apart: 3 -> 3, of which waited for: 1 -> 2; matrix products, arithmetic and copies ran while one was open for 0% -> 0% of each run, Pallas kernels for 35% -> 34%
where the time goes in v17:
time: 80.4 us; the launch traced here: 79.8 us
  Pallas kernels  62.4 us (78%)
  starting transfers between devices  12.6 us (16%)
  waiting for transfers between devices  4.04 us (5%)
  between operations  0.89 us (1%)
    pallas_call x1, Pallas kernels, local(): pl.pallas_call(functools.partial(forward_kernel, n_code), out_shape=(jax....  30.3 us
    pallas_call x1, Pallas kernels, local(): pl.pallas_call(weigh_kernel, out_shape=(pltpu.HBM((tiles_in, n_tokens, wi...  13 us
    all_to_all x1, starting transfers between devices, local(): received = lax.all_to_all(sent, 'code', 0, 0, tiled=True)  8.33 us
    pallas_call x1, Pallas kernels, local(): pl.pallas_call(functools.partial(backward_kernel, False), out_shape=(jax....  7.82 us
    pallas_call x1, Pallas kernels, backward(): pl.pallas_call(functools.partial(backward_kernel, True), out_shape=pltpu....  5.62 us
    all_to_all x1, starting transfers between devices, local(): gathered = lax.all_to_all(spread, 'code', 0, 0, tiled=True)  4.16 us
    all_to_all x1, waiting for transfers between devices, local(): received = lax.all_to_all(sent, 'code', 0, 0, tiled=True)  3.27 us
    pallas_call x1, Pallas kernels, local(): pl.pallas_call(functools.partial(add_kernel, n_dp), out_shape=jax.ShapeDt...  3.14 us
  transfers between devices with their start and end apart: 3, of which 2 were waited for; matrix products, arithmetic and copies ran while one was open for 0% of the time, Pallas kernels for 34%

profile of v17, /device:TPU:0, one launch (start us, length us, event | category | flops | bytes accessed | tf_op | source)
XLA Modules:
  0.0 79.8 jit_solution(12003232594707890833)
XLA Ops:
  0.6 30.3 %forward.1 = (bf16[16,144,128]{2,1,0:T(8,128)(2,1)}, f32[512,128]{1,0:T(8,128)}) custom-call(bf16[512,256]{1,0:T(8,128)(2,1)} %tokens.3, bf16[512,256]{1,0:T(8,128)(2,1)} %grad_out.3, bf16[8192,256]{1,0:T(8,128)(2,1)} %codebook.3, bf16[512,8192]{1,0:T(8,128)(2,1)} %noise.3), custom_call_target="tpu_custom_call" | custom-call | flops 8589934592 | bytes 12582912 | tf_op jit(solution)/shard_map/forward/pallas_call | solution.py:495
  30.9 8.3 %all-to-all-start = ((bf16[16,144,128]{2,1,0:T(8,128)(2,1)}), bf16[16,144,128]{2,1,0:T(8,128)(2,1)S(1)}, u32[]{:S(2)}, u32[]{:S(2)}) async-start(bf16[16,144,128]{2,1,0:T(8,128)(2,1)} %get-tuple-element.16), calls=%async_computation | async-start | bytes 1179648 | tf_op jit(solution)/shard_map/all_to_all | solution.py:528
  39.3 13.0 %weigh.1 = (bf16[16,512,512]{2,1,0:T(8,128)(2,1)}, bf16[16,512,512]{2,1,0:T(8,128)(2,1)}, bf16[2,256,512]{2,1,0:T(8,128)(2,1)}) custom-call(bf16[512,256]{1,0:T(8,128)(2,1)} %tokens.3, bf16[512,256]{1,0:T(8,128)(2,1)} %grad_out.3, bf16[8192,256]{1,0:T(8,128)(2,1)} %codebook.3, bf16[512,8192]{1,0:T(8,128)(2,1)} %noise.3, f32[512,128]{1,0:T(8,128)} %get-tuple-element.17.sides), custom_call_target="tpu_custom_call" | custom-call | flops 4294967296 | bytes 29360128 | tf_op jit(solution)/shard_map/weigh/pallas_call | solution.py:529
  52.3 3.3 %all-to-all-done.received.rest_4_ = bf16[16,144,128]{2,1,0:T(8,128)(2,1)S(1)} async-done(((bf16[16,144,128]{2,1,0:T(8,128)(2,1)}), bf16[16,144,128]{2,1,0:T(8,128)(2,1)S(1)}, u32[]{:S(2)}, u32[]{:S(2)}) %all-to-all-start) | async-done | bytes 589856 | tf_op jit(solution)/shard_map/all_to_all | solution.py:528
  55.5 0.0 copy-start
  55.5 1.4 %merge.1 = bf16[16,32,512]{2,1,0:T(8,128)(2,1)} custom-call(s32[1]{0:T(128)} %bitcast.me.rest_0_, bf16[16,144,128]{2,1,0:T(8,128)(2,1)S(1)} %all-to-all-done.received.rest_4_), custom_call_target="tpu_custom_call" | custom-call | tf_op jit(solution)/shard_map/merge/pallas_call | solution.py:557
  57.0 4.2 %all-to-all-start.1 = ((bf16[16,32,512]{2,1,0:T(8,128)(2,1)}), bf16[16,32,512]{2,1,0:T(8,128)(2,1)S(1)}, u32[]{:S(2)}, u32[]{:S(2)}) async-start(bf16[16,32,512]{2,1,0:T(8,128)(2,1)} %merge.1), calls=%async_computation.1 | async-start | bytes 1048576 | tf_op jit(solution)/shard_map/all_to_all | solution.py:566
  61.2 0.0 copy-done
  61.2 7.8 %backward_first.1 = (bf16[4096,256]{1,0:T(8,128)(2,1)}, bf16[256,1024]{1,0:T(8,128)(2,1)}) custom-call(s32[1]{0:T(128)} %bitcast.1.block, s32[1]{0:T(128)} %bitcast.me.rest_0_, bf16[2,256,512]{2,1,0:T(8,128)(2,1)} %get-tuple-element.23.rest_1_, bf16[16,512,512]{2,1,0:T(8,128)(2,1)} %get-tuple-element.24.rest_2_.rest_0_, ...), custom_call_target="tpu_custom_call" | custom-call | flops 1 | bytes 1 | tf_op jit(solution)/shard_map/backward_first/pallas_call | solution.py:591
  69.0 0.1 collective-permute-start
  69.1 5.6 %backward.1.refs_1_ = bf16[4096,256]{1,0:T(8,128)(2,1)S(1)} custom-call(s32[1]{0:T(128)} %bitcast.2.block, bf16[16,512,512]{2,1,0:T(8,128)(2,1)} %get-tuple-element.24.rest_2_.rest_0_, bf16[16,512,512]{2,1,0:T(8,128)(2,1)} %get-tuple-element.25.rest_3_.rest_1_, bf16[256,1024]{1,0:T(8,128)(2,1)} %get-tuple-element.28.rest_2_), custom_call_target="tpu_custom_call" | custom-call | flops 1 | bytes 1 | tf_op jit(solution)/shard_map/backward/pallas_call | solution.py:613
  74.7 0.8 all-to-all-done.1.gathered
  75.5 1.0 %unpack.1 = (f32[512,256]{1,0:T(8,128)}, f32[512,256]{1,0:T(8,128)}) custom-call(bf16[16,32,512]{2,1,0:T(8,128)(2,1)S(1)} %all-to-all-done.1.gathered), custom_call_target="tpu_custom_call" | custom-call | flops 214748364800 | bytes 419430400 | tf_op jit(solution)/shard_map/unpack/pallas_call | solution.py:567
  76.5 0.0 collective-permute-done.refs_0_
  76.5 3.1 %add.1 = f32[4096,256]{1,0:T(8,128)} custom-call(bf16[4096,256]{1,0:T(8,128)(2,1)} %collective-permute-done.refs_0_, bf16[4096,256]{1,0:T(8,128)(2,1)S(1)} %backward.1.refs_1_), custom_call_target="tpu_custom_call" | custom-call | bytes 8388608 | tf_op jit(solution)/shard_map/add/pallas_call | solution.py:627
Async XLA Ops:
  30.9 24.6 %all-to-all-start = ((bf16[16,144,128]{2,1,0:T(8,128)(2,1)}), bf16[16,144,128]{2,1,0:T(8,128)(2,1)S(1)}, u32[]{:S(2)}, u32[]{:S(2)}) async-start(bf16[16,144,128]{2,1,0:T(8,128)(2,1)} %get-tuple-element.16), calls=%async_computation | async-start | bytes 1179648 | tf_op jit(solution)/shard_map/all_to_all | solution.py:528
  55.5 5.6 %copy-start = (bf16[16,144,128]{2,1,0:T(8,128)(2,1)}, bf16[16,144,128]{2,1,0:T(8,128)(2,1)S(1)}, u32[]{:S(2)}) copy-start(bf16[16,144,128]{2,1,0:T(8,128)(2,1)S(1)} %all-to-all-done.received.rest_4_) | copy-start | bytes 1769476
  57.0 18.5 %all-to-all-start.1 = ((bf16[16,32,512]{2,1,0:T(8,128)(2,1)}), bf16[16,32,512]{2,1,0:T(8,128)(2,1)S(1)}, u32[]{:S(2)}, u32[]{:S(2)}) async-start(bf16[16,32,512]{2,1,0:T(8,128)(2,1)} %merge.1), calls=%async_computation.1 | async-start | bytes 1048576 | tf_op jit(solution)/shard_map/all_to_all | solution.py:566
  69.0 7.5 %collective-permute-start = (bf16[4096,256]{1,0:T(8,128)(2,1)}, bf16[4096,256]{1,0:T(8,128)(2,1)}, u32[]{:S(2)}, u32[]{:S(2)}) collective-permute-start(bf16[4096,256]{1,0:T(8,128)(2,1)} %get-tuple-element.27), channel_id=1, source_target_pairs={{0,16},{16,0},{1,17},{17,1},{2,18},{18,2},{3,19},{19,3},{4,20},{20... | collective-permute-start | bytes 6291464 | tf_op jit(solution)/shard_map/ppermute | solution.py:480

commit v18 on v17

--- a/solution.py
+++ b/solution.py
@@ -14,7 +14,6 @@
 MIB = 1 << 20
 CHUNK = 256
 WIDE = 512
-AHEAD = 2
 NEAR = 3
 PACK = 16
 ROWS = 64
@@ -100,16 +99,7 @@
                     jnp.maximum, lane_groups(logits(both, t, r, c)), shifts[at]
                 )
 
-    def soften(t, s, fresh, last=None):
-        if fresh is not None:
-            @pl.when(fresh)
-            def _():
-                arrive(t)
-
-                @pl.when(t + AHEAD < tiles)
-                def _():
-                    start(t + AHEAD)
-
+    def soften(t, s, last=None):
         slot = slots[s]
         ahead = dot(pair[...], book[t, columns[0]], 1, 1)
         for k, c in enumerate(columns):
@@ -161,15 +151,30 @@
             for copy in halves[1]:
                 copy.wait()
 
-        soften(0, 0, None)
+        soften(0, 0)
 
         def soften_pair(i, carry):
-            soften(2 * i + 1, 1, fresh, lambda: accumulate(2 * i, 0))
-            soften(2 * i + 2, 0, fresh, lambda: accumulate(2 * i + 1, 1))
+            @pl.when(fresh)
+            def _():
+                arrive(2 * i + 1)
+                arrive(2 * i + 2)
+                start(2 * i + 3)
+
+                @pl.when(2 * i + 4 < tiles)
+                def _():
+                    start(2 * i + 4)
+
+            soften(2 * i + 1, 1, lambda: accumulate(2 * i, 0))
+            soften(2 * i + 2, 0, lambda: accumulate(2 * i + 1, 1))
             return carry
 
         lax.fori_loop(0, tiles // 2 - 1, soften_pair, 0)
-        soften(tiles - 1, 1, fresh, lambda: accumulate(tiles - 2, 0))
+
+        @pl.when(fresh)
+        def _():
+            arrive(tiles - 1)
+
+        soften(tiles - 1, 1, lambda: accumulate(tiles - 2, 0))
         accumulate(tiles - 1, 1)
         row_total = jnp.sum(total[...], axis=1, keepdims=True)
         total[...] = jnp.broadcast_to(row_total, total.shape)
@@ -183,7 +188,7 @@
         pair[2 * r + ROWS : 2 * r + 2 * ROWS] = own[1, r : r + ROWS]
     for copy in halves[0]:
         copy.wait()
-    for t in range(1, min(AHEAD + 1, tiles)):
+    for t in range(1, min(3, tiles)):
         start(t)
     lax.while_loop(lambda state: state[1], attempt, (jnp.int32(0), jnp.bool_(True)))
 
@@ -439,10 +444,11 @@
             send(t).wait()
 
 
-def add_kernel(n_parts, *refs):
-    parts, own, out = refs[: n_parts - 1], refs[n_parts - 1], refs[n_parts]
-    held, result, in_sem, out_sem = refs[n_parts + 1 :]
-    steps, rows, _ = result.shape
+def finish_kernel(n_parts, gathered, *refs):
+    parts, own = refs[: n_parts - 1], refs[n_parts - 1]
+    quantized, gradient, out, held, result, both, in_sem, out_sem, both_sem = refs[n_parts:]
+    steps, rows, dim = result.shape
+    n_code, share, _ = gathered.shape
 
     def fetch(i):
         at = pl.ds(i * rows, rows)
@@ -457,23 +463,21 @@
     for i in range(steps):
         for copy in fetch(i):
             copy.start()
+    copies = []
+    for i, target in enumerate((quantized, gradient)):
+        for g in range(n_code):
+            at = slice(g * share, (g + 1) * share)
+            both[i, at] = gathered[g, :, i * dim : (i + 1) * dim].astype(F32)
+        copies.append(pltpu.make_async_copy(both.at[i], target, both_sem.at[i]))
+        copies[-1].start()
     for i in range(steps):
         for copy in fetch(i):
             copy.wait()
         mine = own[i * rows : (i + 1) * rows].astype(F32)
         result[i] = sum((held[j, i].astype(F32) for j in range(len(parts))), mine)
         send(i).start()
-    for i in range(steps):
-        send(i).wait()
-
-
-def unpack_kernel(gathered, quantized, gradient):
-    n_code, rows, both = gathered.shape
-    dim = both // 2
-    for g in range(n_code):
-        at = slice(g * rows, (g + 1) * rows)
-        quantized[at] = gathered[g, :, :dim].astype(F32)
-        gradient[at] = gathered[g, :, dim:].astype(F32)
+    for copy in copies + [send(i) for i in range(steps)]:
+        copy.wait()
 
 
 def swap(value, axis, size, mask):
@@ -564,18 +568,6 @@
     )(code_at[None], received)
     received, spread = lax.optimization_barrier((received, spread))
     gathered = lax.all_to_all(spread, "code", 0, 0, tiled=True)
-    quantized, token_gradient = pl.pallas_call(
-        unpack_kernel,
-        out_shape=(jax.ShapeDtypeStruct((n_tokens, dim), F32),) * 2,
-        in_specs=[VMEM],
-        out_specs=(VMEM, VMEM),
-        compiler_params=SOME,
-        cost_estimate=pl.CostEstimate(
-            flops=100 * products, bytes_accessed=400 * MIB, transcendentals=0
-        ),
-        name="unpack",
-    )(gathered)
-
     block_tiles = block // wide
     streams = [
         pltpu.VMEM((block_tiles, 2 * n_tokens, wide), BF16),
@@ -617,30 +609,39 @@
             out_specs=VMEM,
             scratch_shapes=streams,
             name="backward",
-            **common,
+            compiler_params=MOST,
+            cost_estimate=pl.CostEstimate(
+                flops=100 * products, bytes_accessed=400 * MIB, transcendentals=0
+            ),
         )(at[None], codes, weighed, operands)
 
     blocks = [swap(first, "dp", n_dp, n_dp - 1)]
     blocks += [swap(backward(dp_at ^ d), "dp", n_dp, d) for d in range(1, n_dp - 1)]
     blocks.append(backward(dp_at))
     steps = max(block // 512, 1)
-    own_rows = pl.pallas_call(
-        functools.partial(add_kernel, n_dp),
-        out_shape=jax.ShapeDtypeStruct((block, dim), F32),
-        in_specs=[ANY] * (n_dp - 1) + [VMEM],
-        out_specs=ANY,
+    quantized, token_gradient, own_rows = pl.pallas_call(
+        functools.partial(finish_kernel, n_dp),
+        out_shape=(
+            jax.ShapeDtypeStruct((n_tokens, dim), F32),
+            jax.ShapeDtypeStruct((n_tokens, dim), F32),
+            jax.ShapeDtypeStruct((block, dim), F32),
+        ),
+        in_specs=[VMEM] + [ANY] * (n_dp - 1) + [VMEM],
+        out_specs=(ANY, ANY, ANY),
         scratch_shapes=[
             pltpu.VMEM((n_dp - 1, steps, block // steps, dim), BF16),
             pltpu.VMEM((steps, block // steps, dim), F32),
+            pltpu.VMEM((2, n_tokens, dim), F32),
             pltpu.SemaphoreType.DMA((n_dp - 1, steps)),
             pltpu.SemaphoreType.DMA((steps,)),
+            pltpu.SemaphoreType.DMA((2,)),
         ],
         compiler_params=SOME,
         cost_estimate=pl.CostEstimate(
             flops=0, bytes_accessed=(2 * n_dp + 4) * block * dim, transcendentals=0
         ),
-        name="add",
-    )(*blocks)
+        name="finish",
+    )(gathered, *blocks)
     return quantized, token_gradient, own_rows[None]
 
 

time: 80.4 us -> 80.1 us (level)
    pallas_call x2 -> x1, Pallas kernels: 4.17 us -> 4.39 us  [local(): pl.pallas_call(functools.partial(finish_kernel, n_dp), out_shape=(jax.Sha...]
  transfers between devices with their start and end apart: 3 -> 3, of which waited for: 2 -> 2; matrix products, arithmetic and copies ran while one was open for 0% -> 0% of each run, Pallas kernels for 34% -> 33%
where the time goes in v18:
time: 80.1 us; the launch traced here: 79.5 us
  Pallas kernels  61.9 us (77%)
  starting transfers between devices  12.9 us (16%)
  waiting for transfers between devices  3.84 us (5%)
  between operations  0.88 us (1%)
    pallas_call x1, Pallas kernels, local(): pl.pallas_call(functools.partial(forward_kernel, n_code), out_shape=(jax....  29.6 us
    pallas_call x1, Pallas kernels, local(): pl.pallas_call(weigh_kernel, out_shape=(pltpu.HBM((tiles_in, n_tokens, wi...  13 us
    all_to_all x1, starting transfers between devices, local(): received = lax.all_to_all(sent, 'code', 0, 0, tiled=True)  8.33 us
    pallas_call x1, Pallas kernels, local(): pl.pallas_call(functools.partial(backward_kernel, False), out_shape=(jax....  7.82 us
    pallas_call x1, Pallas kernels, backward(): pl.pallas_call(functools.partial(backward_kernel, True), out_shape=pltpu....  5.62 us
    all_to_all x1, starting transfers between devices, local(): gathered = lax.all_to_all(spread, 'code', 0, 0, tiled=True)  4.46 us
    pallas_call x1, Pallas kernels, local(): pl.pallas_call(functools.partial(finish_kernel, n_dp), out_shape=(jax.Sha...  4.39 us
    all_to_all x1, waiting for transfers between devices, local(): received = lax.all_to_all(sent, 'code', 0, 0, tiled=True)  3.26 us
  transfers between devices with their start and end apart: 3, of which 2 were waited for; matrix products, arithmetic and copies ran while one was open for 0% of the time, Pallas kernels for 33%

profile of v18, /device:TPU:0, one launch (start us, length us, event | category | flops | bytes accessed | tf_op | source)
XLA Modules:
  0.0 79.5 jit_solution(10435561574032029757)
XLA Ops:
  0.6 29.6 %forward.1 = (bf16[16,144,128]{2,1,0:T(8,128)(2,1)}, f32[512,128]{1,0:T(8,128)}) custom-call(bf16[512,256]{1,0:T(8,128)(2,1)} %tokens.3, bf16[512,256]{1,0:T(8,128)(2,1)} %grad_out.3, bf16[8192,256]{1,0:T(8,128)(2,1)} %codebook.3, bf16[512,8192]{1,0:T(8,128)(2,1)} %noise.3), custom_call_target="tpu_custom_call" | custom-call | flops 8589934592 | bytes 12582912 | tf_op jit(solution)/shard_map/forward/pallas_call | solution.py:499
  30.2 8.3 %all-to-all-start = ((bf16[16,144,128]{2,1,0:T(8,128)(2,1)}), bf16[16,144,128]{2,1,0:T(8,128)(2,1)S(1)}, u32[]{:S(2)}, u32[]{:S(2)}) async-start(bf16[16,144,128]{2,1,0:T(8,128)(2,1)} %get-tuple-element.17), calls=%async_computation | async-start | bytes 1179648 | tf_op jit(solution)/shard_map/all_to_all | solution.py:532
  38.6 13.0 %weigh.1 = (bf16[16,512,512]{2,1,0:T(8,128)(2,1)}, bf16[16,512,512]{2,1,0:T(8,128)(2,1)}, bf16[2,256,512]{2,1,0:T(8,128)(2,1)}) custom-call(bf16[512,256]{1,0:T(8,128)(2,1)} %tokens.3, bf16[512,256]{1,0:T(8,128)(2,1)} %grad_out.3, bf16[8192,256]{1,0:T(8,128)(2,1)} %codebook.3, bf16[512,8192]{1,0:T(8,128)(2,1)} %noise.3, f32[512,128]{1,0:T(8,128)} %get-tuple-element.18.sides), custom_call_target="tpu_custom_call" | custom-call | flops 4294967296 | bytes 29360128 | tf_op jit(solution)/shard_map/weigh/pallas_call | solution.py:533
  51.6 3.3 %all-to-all-done.received.rest_4_ = bf16[16,144,128]{2,1,0:T(8,128)(2,1)S(1)} async-done(((bf16[16,144,128]{2,1,0:T(8,128)(2,1)}), bf16[16,144,128]{2,1,0:T(8,128)(2,1)S(1)}, u32[]{:S(2)}, u32[]{:S(2)}) %all-to-all-start) | async-done | bytes 589856 | tf_op jit(solution)/shard_map/all_to_all | solution.py:532
  54.8 0.0 copy-start
  54.8 1.4 %merge.1 = bf16[16,32,512]{2,1,0:T(8,128)(2,1)} custom-call(s32[1]{0:T(128)} %bitcast.me.rest_0_, bf16[16,144,128]{2,1,0:T(8,128)(2,1)S(1)} %all-to-all-done.received.rest_4_), custom_call_target="tpu_custom_call" | custom-call | tf_op jit(solution)/shard_map/merge/pallas_call | solution.py:561
  56.3 4.5 %all-to-all-start.1 = ((bf16[16,32,512]{2,1,0:T(8,128)(2,1)}), bf16[16,32,512]{2,1,0:T(8,128)(2,1)}, u32[]{:S(2)}, u32[]{:S(2)}) async-start(bf16[16,32,512]{2,1,0:T(8,128)(2,1)} %merge.1), calls=%async_computation.1 | async-start | bytes 1048576 | tf_op jit(solution)/shard_map/all_to_all | solution.py:570
  60.8 0.0 copy-done
  60.8 7.8 %backward_first.1 = (bf16[4096,256]{1,0:T(8,128)(2,1)}, bf16[256,1024]{1,0:T(8,128)(2,1)}) custom-call(s32[1]{0:T(128)} %bitcast.1.block, s32[1]{0:T(128)} %bitcast.me.rest_0_, bf16[2,256,512]{2,1,0:T(8,128)(2,1)} %get-tuple-element.22.rest_1_, bf16[16,512,512]{2,1,0:T(8,128)(2,1)} %get-tuple-element.23.rest_2_.rest_0_, ...), custom_call_target="tpu_custom_call" | custom-call | flops 1 | bytes 1 | tf_op jit(solution)/shard_map/backward_first/pallas_call | solution.py:583
  68.6 0.1 collective-permute-start
  68.7 5.6 %backward.1.refs_1_ = bf16[4096,256]{1,0:T(8,128)(2,1)S(1)} custom-call(s32[1]{0:T(128)} %bitcast.2.block, bf16[16,512,512]{2,1,0:T(8,128)(2,1)} %get-tuple-element.23.rest_2_.rest_0_, bf16[16,512,512]{2,1,0:T(8,128)(2,1)} %get-tuple-element.24.rest_3_.rest_1_, bf16[256,1024]{1,0:T(8,128)(2,1)} %get-tuple-element.27.rest_2_), custom_call_target="tpu_custom_call" | custom-call | flops 214748364800 | bytes 419430400 | tf_op jit(solution)/shard_map/backward/pallas_call | solution.py:605
  74.3 0.6 all-to-all-done.1.gathered
  74.9 0.0 collective-permute-done.refs_0_
  74.9 4.4 %finish.1 = (f32[512,256]{1,0:T(8,128)}, f32[512,256]{1,0:T(8,128)}, f32[4096,256]{1,0:T(8,128)}) custom-call(bf16[16,32,512]{2,1,0:T(8,128)(2,1)} %all-to-all-done.1.gathered, bf16[4096,256]{1,0:T(8,128)(2,1)} %collective-permute-done.refs_0_, bf16[4096,256]{1,0:T(8,128)(2,1)S(1)} %backward.1.refs_1_), custom_call_target="tpu_custom_call" | custom-call | bytes 8388608 | tf_op jit(solution)/shard_map/finish/pallas_call | solution.py:622
Async XLA Ops:
  30.2 24.6 %all-to-all-start = ((bf16[16,144,128]{2,1,0:T(8,128)(2,1)}), bf16[16,144,128]{2,1,0:T(8,128)(2,1)S(1)}, u32[]{:S(2)}, u32[]{:S(2)}) async-start(bf16[16,144,128]{2,1,0:T(8,128)(2,1)} %get-tuple-element.17), calls=%async_computation | async-start | bytes 1179648 | tf_op jit(solution)/shard_map/all_to_all | solution.py:532
  54.8 5.9 %copy-start = (bf16[16,144,128]{2,1,0:T(8,128)(2,1)}, bf16[16,144,128]{2,1,0:T(8,128)(2,1)S(1)}, u32[]{:S(2)}) copy-start(bf16[16,144,128]{2,1,0:T(8,128)(2,1)S(1)} %all-to-all-done.received.rest_4_) | copy-start | bytes 1769476
  56.3 18.6 %all-to-all-start.1 = ((bf16[16,32,512]{2,1,0:T(8,128)(2,1)}), bf16[16,32,512]{2,1,0:T(8,128)(2,1)}, u32[]{:S(2)}, u32[]{:S(2)}) async-start(bf16[16,32,512]{2,1,0:T(8,128)(2,1)} %merge.1), calls=%async_computation.1 | async-start | bytes 1048576 | tf_op jit(solution)/shard_map/all_to_all | solution.py:570
  68.6 6.3 %collective-permute-start = (bf16[4096,256]{1,0:T(8,128)(2,1)}, bf16[4096,256]{1,0:T(8,128)(2,1)}, u32[]{:S(2)}, u32[]{:S(2)}) collective-permute-start(bf16[4096,256]{1,0:T(8,128)(2,1)} %get-tuple-element.26), channel_id=1, source_target_pairs={{0,16},{16,0},{1,17},{17,1},{2,18},{18,2},{3,19},{19,3},{4,20},{20... | collective-permute-start | bytes 6291464 | tf_op jit(solution)/shard_map/ppermute | solution.py:484

commit v19 on v17

--- a/solution.py
+++ b/solution.py
@@ -254,10 +254,21 @@
     return scales, means, top, total, inner
 
 
-def merge_kernel(me, received, spread):
+def merge_kernel(me, received, spread, factors, columns):
     n_code, rows, both = spread.shape
     dim = both // 2
-    scales, means, _, _, inner = merged_stats(received, n_code * rows)
+    n_tokens = n_code * rows
+    scales, means, top, total, inner = merged_stats(received, n_tokens)
+    own = stats_of(received, me[0], n_tokens)
+    own_scale = factor_of(own, top) / total
+    own_offset = own_scale * (mean_of(own) - inner)
+    left = lax.broadcasted_iota(jnp.int32, (PACK, 128), 1) < 64
+    for q in range(n_tokens // PACK):
+        at = slice(4 * q, 4 * q + 1)
+        columns[q * PACK : (q + 1) * PACK] = jnp.where(left, own_scale[:, at], own_offset[:, at])
+    turned = columns[...].T
+    factors[:8] = turned[:8]
+    factors[8:] = turned[64:72]
     lane = lax.broadcasted_iota(jnp.int32, inner.shape, 1)
     groups = rows // PACK
     mine = [lane == 4 * (me[0] * groups + h) for h in range(groups)]
@@ -352,7 +363,7 @@
     if prepared:
         codes, weighed, given, out, *rest = rest
     else:
-        code_at, turned, codes, weighed, received, out, kept, own, spread, *rest = rest
+        turned, codes, weighed, factors, out, kept, own, *rest = rest
     both_in, operands, in_sem, own_sem, *rest = rest
     tiles, _, width = both_in.shape
     if not prepared:
@@ -386,18 +397,7 @@
     if prepared:
         own_copies[0].wait()
     else:
-        _, _, top, total, inner = merged_stats(received, n_tokens)
-        stats = stats_of(received, code_at[0], n_tokens)
-        scale = factor_of(stats, top) / total
-        offset = scale * (mean_of(stats) - inner)
-        lane = lax.broadcasted_iota(jnp.int32, (PACK, 128), 1)
-        for q in range(n_tokens // PACK):
-            at = slice(4 * q, 4 * q + 1)
-            spread[q * PACK : (q + 1) * PACK] = jnp.where(
-                lane < 64, scale[:, at], offset[:, at]
-            )
-        factors = spread[...].T
-        scale, offset = factors[:1], factors[64:65]
+        scale, offset = factors[:1], factors[8:9]
         own_copies[0].wait()
         grad, token = own[0].astype(F32), own[1].astype(F32)
         operands[:, :n_tokens] = (scale * grad + offset * token).astype(BF16)
@@ -554,28 +554,20 @@
     )(tokens, grad_out, codebook, noise, sides)
     received, weighed = lax.optimization_barrier((received, weighed))
     code_at = lax.axis_index("code")
-    spread = pl.pallas_call(
+    spread, factors = pl.pallas_call(
         merge_kernel,
-        out_shape=jax.ShapeDtypeStruct((n_code, rows, 2 * dim), BF16),
+        out_shape=(
+            jax.ShapeDtypeStruct((n_code, rows, 2 * dim), BF16),
+            jax.ShapeDtypeStruct((16, n_tokens), F32),
+        ),
         in_specs=[SMEM, VMEM],
-        out_specs=VMEM,
+        out_specs=(VMEM, VMEM),
+        scratch_shapes=[pltpu.VMEM((n_tokens, 128), F32)],
         compiler_params=SOME,
         name="merge",
     )(code_at[None], received)
-    received, spread = lax.optimization_barrier((received, spread))
+    spread, factors = lax.optimization_barrier((spread, factors))
     gathered = lax.all_to_all(spread, "code", 0, 0, tiled=True)
-    quantized, token_gradient = pl.pallas_call(
-        unpack_kernel,
-        out_shape=(jax.ShapeDtypeStruct((n_tokens, dim), F32),) * 2,
-        in_specs=[VMEM],
-        out_specs=(VMEM, VMEM),
-        compiler_params=SOME,
-        cost_estimate=pl.CostEstimate(
-            flops=100 * products, bytes_accessed=400 * MIB, transcendentals=0
-        ),
-        name="unpack",
-    )(gathered)
-
     block_tiles = block // wide
     streams = [
         pltpu.VMEM((block_tiles, 2 * n_tokens, wide), BF16),
@@ -594,20 +586,17 @@
             jax.ShapeDtypeStruct((block, dim), BF16),
             jax.ShapeDtypeStruct((dim, 2 * n_tokens), BF16),
         ),
-        in_specs=[SMEM, SMEM, ANY, ANY, ANY, VMEM],
+        in_specs=[SMEM, ANY, ANY, ANY, VMEM],
         out_specs=(ANY, ANY),
         scratch_shapes=[
             pltpu.VMEM((2, dim, n_tokens), BF16),
-            pltpu.VMEM((n_tokens, 128), F32),
         ] + streams + [
             pltpu.VMEM((block_tiles, wide, dim), BF16),
             pltpu.SemaphoreType.DMA((block_tiles,)),
         ],
         name="backward_first",
         **common,
-    )(
-        (dp_at ^ (n_dp - 1))[None], code_at[None], turned, codes, weighed, received
-    )
+    )((dp_at ^ (n_dp - 1))[None], turned, codes, weighed, factors)
 
     def backward(at):
         return pl.pallas_call(
@@ -617,7 +606,10 @@
             out_specs=VMEM,
             scratch_shapes=streams,
             name="backward",
-            **common,
+            compiler_params=MOST,
+            cost_estimate=pl.CostEstimate(
+                flops=100 * products, bytes_accessed=400 * MIB, transcendentals=0
+            ),
         )(at[None], codes, weighed, operands)
 
     blocks = [swap(first, "dp", n_dp, n_dp - 1)]
@@ -641,6 +633,18 @@
         ),
         name="add",
     )(*blocks)
+    gathered, own_rows = lax.optimization_barrier((gathered, own_rows))
+    quantized, token_gradient = pl.pallas_call(
+        unpack_kernel,
+        out_shape=(jax.ShapeDtypeStruct((n_tokens, dim), F32),) * 2,
+        in_specs=[VMEM],
+        out_specs=(VMEM, VMEM),
+        compiler_params=SOME,
+        cost_estimate=pl.CostEstimate(
+            flops=0, bytes_accessed=12 * n_tokens * dim, transcendentals=0
+        ),
+        name="unpack",
+    )(gathered)
     return quantized, token_gradient, own_rows[None]
 
 

time: 80.4 us -> 81.4 us (1.012)
    pallas_call x1, Pallas kernels: 1.03 us -> 2.08 us  [local(): pl.pallas_call(unpack_kernel, out_shape=(jax.ShapeDtypeStruct((n_tokens,...]
  transfers between devices with their start and end apart: 3 -> 3, of which waited for: 2 -> 1; matrix products, arithmetic and copies ran while one was open for 0% -> 0% of each run, Pallas kernels for 34% -> 36%
where the time goes in v19:
time: 81.4 us; the launch traced here: 80.7 us
  Pallas kernels  63.2 us (78%)
  starting transfers between devices  12.9 us (16%)
  waiting for transfers between devices  3.24 us (4%)
    pallas_call x1, Pallas kernels, local(): pl.pallas_call(functools.partial(forward_kernel, n_code), out_shape=(jax....  30.3 us
    pallas_call x1, Pallas kernels, local(): pl.pallas_call(weigh_kernel, out_shape=(pltpu.HBM((tiles_in, n_tokens, wi...  13 us
    all_to_all x1, starting transfers between devices, local(): received = lax.all_to_all(sent, 'code', 0, 0, tiled=True)  8.33 us
    pallas_call x1, Pallas kernels, local(): pl.pallas_call(functools.partial(backward_kernel, False), out_shape=(jax....  7.34 us
    pallas_call x1, Pallas kernels, backward(): pl.pallas_call(functools.partial(backward_kernel, True), out_shape=pltpu....  5.62 us
    all_to_all x1, starting transfers between devices, local(): gathered = lax.all_to_all(spread, 'code', 0, 0, tiled=True)  4.47 us
    all_to_all x1, waiting for transfers between devices, local(): received = lax.all_to_all(sent, 'code', 0, 0, tiled=True)  3.24 us
    pallas_call x1, Pallas kernels, local(): pl.pallas_call(functools.partial(add_kernel, n_dp), out_shape=jax.ShapeDt...  3.14 us
  transfers between devices with their start and end apart: 3, of which 1 were waited for; matrix products, arithmetic and copies ran while one was open for 0% of the time, Pallas kernels for 36%

profile of v19, /device:TPU:0, one launch (start us, length us, event | category | flops | bytes accessed | tf_op | source)
XLA Modules:
  0.0 80.7 jit_solution(11418031669835734995)
XLA Ops:
  0.6 30.3 %forward.1 = (bf16[16,144,128]{2,1,0:T(8,128)(2,1)}, f32[512,128]{1,0:T(8,128)}) custom-call(bf16[512,256]{1,0:T(8,128)(2,1)} %tokens.3, bf16[512,256]{1,0:T(8,128)(2,1)} %grad_out.3, bf16[8192,256]{1,0:T(8,128)(2,1)} %codebook.3, bf16[512,8192]{1,0:T(8,128)(2,1)} %noise.3), custom_call_target="tpu_custom_call" | custom-call | flops 8589934592 | bytes 12582912 | tf_op jit(solution)/shard_map/forward/pallas_call | solution.py:495
  30.9 8.3 %all-to-all-start = ((bf16[16,144,128]{2,1,0:T(8,128)(2,1)}), bf16[16,144,128]{2,1,0:T(8,128)(2,1)S(1)}, u32[]{:S(2)}, u32[]{:S(2)}) async-start(bf16[16,144,128]{2,1,0:T(8,128)(2,1)} %get-tuple-element.18), calls=%async_computation | async-start | bytes 1179648 | tf_op jit(solution)/shard_map/all_to_all | solution.py:528
  39.3 13.0 %weigh.1 = (bf16[16,512,512]{2,1,0:T(8,128)(2,1)}, bf16[16,512,512]{2,1,0:T(8,128)(2,1)}, bf16[2,256,512]{2,1,0:T(8,128)(2,1)}) custom-call(bf16[512,256]{1,0:T(8,128)(2,1)} %tokens.3, bf16[512,256]{1,0:T(8,128)(2,1)} %grad_out.3, bf16[8192,256]{1,0:T(8,128)(2,1)} %codebook.3, bf16[512,8192]{1,0:T(8,128)(2,1)} %noise.3, f32[512,128]{1,0:T(8,128)} %get-tuple-element.19.sides), custom_call_target="tpu_custom_call" | custom-call | flops 4294967296 | bytes 29360128 | tf_op jit(solution)/shard_map/weigh/pallas_call | solution.py:529
  52.3 3.2 %all-to-all-done.received = bf16[16,144,128]{2,1,0:T(8,128)(2,1)S(1)} async-done(((bf16[16,144,128]{2,1,0:T(8,128)(2,1)}), bf16[16,144,128]{2,1,0:T(8,128)(2,1)S(1)}, u32[]{:S(2)}, u32[]{:S(2)}) %all-to-all-start) | async-done | bytes 589856 | tf_op jit(solution)/shard_map/all_to_all | solution.py:528
  55.5 1.7 %merge.1 = (bf16[16,32,512]{2,1,0:T(8,128)(2,1)}, f32[16,512]{1,0:T(8,128)S(1)}) custom-call(s32[1]{0:T(128)} %bitcast.me, bf16[16,144,128]{2,1,0:T(8,128)(2,1)S(1)} %all-to-all-done.received), custom_call_target="tpu_custom_call" | custom-call | tf_op jit(solution)/shard_map/merge/pallas_call | solution.py:557
  57.3 0.0 copy-start
  57.3 0.6 copy-done
  57.9 4.5 %all-to-all-start.1 = ((bf16[16,32,512]{2,1,0:T(8,128)(2,1)}), bf16[16,32,512]{2,1,0:T(8,128)(2,1)}, u32[]{:S(2)}, u32[]{:S(2)}) async-start(bf16[16,32,512]{2,1,0:T(8,128)(2,1)} %get-tuple-element.22), calls=%async_computation.1 | async-start | bytes 1048576 | tf_op jit(solution)/shard_map/all_to_all | solution.py:570
  62.4 7.3 %backward_first.1 = (bf16[4096,256]{1,0:T(8,128)(2,1)}, bf16[256,1024]{1,0:T(8,128)(2,1)}) custom-call(s32[1]{0:T(128)} %bitcast.1.block, bf16[2,256,512]{2,1,0:T(8,128)(2,1)} %get-tuple-element.23.rest_0_, bf16[16,512,512]{2,1,0:T(8,128)(2,1)} %get-tuple-element.24.rest_1_.rest_0_, bf16[16,512,512]{2,1,0:T(8,128)(2,1)} %get-tuple-element.25.rest_2_.rest_1_, ...), custom_call_target="tpu_custom_call" | custom-call | flops 1 | bytes 1 | tf_op jit(solution)/shard_map/backward_first/pallas_call | solution.py:583
  69.7 0.1 collective-permute-start
  69.8 5.6 %backward.1.refs_1_ = bf16[4096,256]{1,0:T(8,128)(2,1)S(1)} custom-call(s32[1]{0:T(128)} %bitcast.2.block, bf16[16,512,512]{2,1,0:T(8,128)(2,1)} %get-tuple-element.24.rest_1_.rest_0_, bf16[16,512,512]{2,1,0:T(8,128)(2,1)} %get-tuple-element.25.rest_2_.rest_1_, bf16[256,1024]{1,0:T(8,128)(2,1)} %get-tuple-element.28.rest_2_), custom_call_target="tpu_custom_call" | custom-call | flops 214748364800 | bytes 419430400 | tf_op jit(solution)/shard_map/backward/pallas_call | solution.py:602
  75.4 0.0 collective-permute-done.refs_0_
  75.5 3.1 %add.1 = f32[4096,256]{1,0:T(8,128)} custom-call(bf16[4096,256]{1,0:T(8,128)(2,1)} %collective-permute-done.refs_0_, bf16[4096,256]{1,0:T(8,128)(2,1)S(1)} %backward.1.refs_1_), custom_call_target="tpu_custom_call" | custom-call | bytes 8388608 | tf_op jit(solution)/shard_map/add/pallas_call | solution.py:619
  78.6 0.0 all-to-all-done.1.gathered
  78.6 2.1 %unpack.1 = (f32[512,256]{1,0:T(8,128)}, f32[512,256]{1,0:T(8,128)}) custom-call(bf16[16,32,512]{2,1,0:T(8,128)(2,1)} %all-to-all-done.1.gathered), custom_call_target="tpu_custom_call" | custom-call | bytes 1572864 | tf_op jit(solution)/shard_map/unpack/pallas_call | solution.py:637
Async XLA Ops:
  30.9 24.6 %all-to-all-start = ((bf16[16,144,128]{2,1,0:T(8,128)(2,1)}), bf16[16,144,128]{2,1,0:T(8,128)(2,1)S(1)}, u32[]{:S(2)}, u32[]{:S(2)}) async-start(bf16[16,144,128]{2,1,0:T(8,128)(2,1)} %get-tuple-element.18), calls=%async_computation | async-start | bytes 1179648 | tf_op jit(solution)/shard_map/all_to_all | solution.py:528
  57.3 0.6 copy-start
  57.9 20.7 %all-to-all-start.1 = ((bf16[16,32,512]{2,1,0:T(8,128)(2,1)}), bf16[16,32,512]{2,1,0:T(8,128)(2,1)}, u32[]{:S(2)}, u32[]{:S(2)}) async-start(bf16[16,32,512]{2,1,0:T(8,128)(2,1)} %get-tuple-element.22), calls=%async_computation.1 | async-start | bytes 1048576 | tf_op jit(solution)/shard_map/all_to_all | solution.py:570
  69.7 5.7 %collective-permute-start = (bf16[4096,256]{1,0:T(8,128)(2,1)}, bf16[4096,256]{1,0:T(8,128)(2,1)}, u32[]{:S(2)}, u32[]{:S(2)}) collective-permute-start(bf16[4096,256]{1,0:T(8,128)(2,1)} %get-tuple-element.27), channel_id=1, source_target_pairs={{0,16},{16,0},{1,17},{17,1},{2,18},{18,2},{3,19},{19,3},{4,20},{20... | collective-permute-start | bytes 6291464 | tf_op jit(solution)/shard_map/ppermute | solution.py:480

commit v20 on v19

--- a/solution.py
+++ b/solution.py
@@ -254,7 +254,7 @@
     return scales, means, top, total, inner
 
 
-def merge_kernel(me, received, spread, factors, columns):
+def merge_kernel(me, received, spread, factors, columns, factors_out, factors_sem):
     n_code, rows, both = spread.shape
     dim = both // 2
     n_tokens = n_code * rows
@@ -267,8 +267,10 @@
         at = slice(4 * q, 4 * q + 1)
         columns[q * PACK : (q + 1) * PACK] = jnp.where(left, own_scale[:, at], own_offset[:, at])
     turned = columns[...].T
-    factors[:8] = turned[:8]
-    factors[8:] = turned[64:72]
+    factors_out[:8] = turned[:8]
+    factors_out[8:] = turned[64:72]
+    factors_copy = pltpu.make_async_copy(factors_out, factors, factors_sem)
+    factors_copy.start()
     lane = lax.broadcasted_iota(jnp.int32, inner.shape, 1)
     groups = rows // PACK
     mine = [lane == 4 * (me[0] * groups + h) for h in range(groups)]
@@ -293,6 +295,7 @@
         for p in range(n_code):
             for i, result in enumerate(results):
                 spread[p, :, i * dim + j * 128 : i * dim + (j + 1) * 128] = result
+    factors_copy.wait()
 
 
 def weigh_kernel(
@@ -363,7 +366,7 @@
     if prepared:
         codes, weighed, given, out, *rest = rest
     else:
-        turned, codes, weighed, factors, out, kept, own, *rest = rest
+        turned, codes, weighed, given, out, kept, own, factors, *rest = rest
     both_in, operands, in_sem, own_sem, *rest = rest
     tiles, _, width = both_in.shape
     if not prepared:
@@ -388,7 +391,10 @@
     if prepared:
         own_copies = [pltpu.make_async_copy(given, operands, own_sem.at[0])]
     else:
-        own_copies = [pltpu.make_async_copy(turned, own, own_sem.at[0])]
+        own_copies = [
+            pltpu.make_async_copy(turned, own, own_sem.at[0]),
+            pltpu.make_async_copy(given, factors, own_sem.at[1]),
+        ]
     for copy in own_copies:
         copy.start()
     for t in range(1, min(NEAR, tiles)):
@@ -397,8 +403,9 @@
     if prepared:
         own_copies[0].wait()
     else:
+        for copy in own_copies:
+            copy.wait()
         scale, offset = factors[:1], factors[8:9]
-        own_copies[0].wait()
         grad, token = own[0].astype(F32), own[1].astype(F32)
         operands[:, :n_tokens] = (scale * grad + offset * token).astype(BF16)
         operands[:, n_tokens:] = (scale * token).astype(BF16)
@@ -467,7 +474,7 @@
         send(i).wait()
 
 
-def unpack_kernel(gathered, quantized, gradient):
+def unpack_kernel(gathered, _, quantized, gradient):
     n_code, rows, both = gathered.shape
     dim = both // 2
     for g in range(n_code):
@@ -558,11 +565,15 @@
         merge_kernel,
         out_shape=(
             jax.ShapeDtypeStruct((n_code, rows, 2 * dim), BF16),
-            jax.ShapeDtypeStruct((16, n_tokens), F32),
+            pltpu.HBM((16, n_tokens), F32),
         ),
         in_specs=[SMEM, VMEM],
-        out_specs=(VMEM, VMEM),
-        scratch_shapes=[pltpu.VMEM((n_tokens, 128), F32)],
+        out_specs=(VMEM, ANY),
+        scratch_shapes=[
+            pltpu.VMEM((n_tokens, 128), F32),
+            pltpu.VMEM((16, n_tokens), F32),
+            pltpu.SemaphoreType.DMA,
+        ],
         compiler_params=SOME,
         name="merge",
     )(code_at[None], received)
@@ -573,7 +584,7 @@
         pltpu.VMEM((block_tiles, 2 * n_tokens, wide), BF16),
         pltpu.VMEM((dim, 2 * n_tokens), BF16),
         pltpu.SemaphoreType.DMA((2, block_tiles)),
-        pltpu.SemaphoreType.DMA((1,)),
+        pltpu.SemaphoreType.DMA((2,)),
     ]
     common = dict(
         compiler_params=MOST,
@@ -586,10 +597,11 @@
             jax.ShapeDtypeStruct((block, dim), BF16),
             jax.ShapeDtypeStruct((dim, 2 * n_tokens), BF16),
         ),
-        in_specs=[SMEM, ANY, ANY, ANY, VMEM],
+        in_specs=[SMEM, ANY, ANY, ANY, ANY],
         out_specs=(ANY, ANY),
         scratch_shapes=[
             pltpu.VMEM((2, dim, n_tokens), BF16),
+            pltpu.VMEM((16, n_tokens), F32),
         ] + streams + [
             pltpu.VMEM((block_tiles, wide, dim), BF16),
             pltpu.SemaphoreType.DMA((block_tiles,)),
@@ -633,18 +645,17 @@
         ),
         name="add",
     )(*blocks)
-    gathered, own_rows = lax.optimization_barrier((gathered, own_rows))
     quantized, token_gradient = pl.pallas_call(
         unpack_kernel,
         out_shape=(jax.ShapeDtypeStruct((n_tokens, dim), F32),) * 2,
-        in_specs=[VMEM],
+        in_specs=[VMEM, ANY],
         out_specs=(VMEM, VMEM),
         compiler_params=SOME,
         cost_estimate=pl.CostEstimate(
             flops=0, bytes_accessed=12 * n_tokens * dim, transcendentals=0
         ),
         name="unpack",
-    )(gathered)
+    )(gathered, own_rows)
     return quantized, token_gradient, own_rows[None]
 
 

time: 81.4 us -> 82.3 us (1.011)
  local copies, waits for them, and re-layouts: 0.62 us -> 2.18 us
    unnamed x2, local copies, waits for them, and re-layouts: 0.62 us -> 2.18 us
    pallas_call x1, Pallas kernels: 7.34 us -> 6.51 us  [local(): pl.pallas_call(functools.partial(backward_kernel, False), out_shape=(jax....]
  transfers between devices with their start and end apart: 3 -> 3, of which waited for: 1 -> 1; matrix products, arithmetic and copies ran while one was open for 0% -> 0% of each run, Pallas kernels for 36% -> 35%
where the time goes in v20:
time: 82.3 us; the launch traced here: 81.7 us
  Pallas kernels  62.6 us (76%)
  starting transfers between devices  12.9 us (16%)
  waiting for transfers between devices  3.24 us (4%)
  local copies, waits for them, and re-layouts  2.18 us (3%)
    pallas_call x1, Pallas kernels, local(): pl.pallas_call(functools.partial(forward_kernel, n_code), out_shape=(jax....  30.3 us
    pallas_call x1, Pallas kernels, local(): pl.pallas_call(weigh_kernel, out_shape=(pltpu.HBM((tiles_in, n_tokens, wi...  13 us
    all_to_all x1, starting transfers between devices, local(): received = lax.all_to_all(sent, 'code', 0, 0, tiled=True)  8.33 us
    pallas_call x1, Pallas kernels, local(): pl.pallas_call(functools.partial(backward_kernel, False), out_shape=(jax....  6.51 us
    pallas_call x1, Pallas kernels, backward(): pl.pallas_call(functools.partial(backward_kernel, True), out_shape=pltpu....  5.63 us
    all_to_all x1, starting transfers between devices, local(): gathered = lax.all_to_all(spread, 'code', 0, 0, tiled=True)  4.48 us
    all_to_all x1, waiting for transfers between devices, local(): received = lax.all_to_all(sent, 'code', 0, 0, tiled=True)  3.24 us
    pallas_call x1, Pallas kernels, local(): pl.pallas_call(functools.partial(add_kernel, n_dp), out_shape=jax.ShapeDt...  3.14 us
  transfers between devices with their start and end apart: 3, of which 1 were waited for; matrix products, arithmetic and copies ran while one was open for 0% of the time, Pallas kernels for 35%

profile of v20, /device:TPU:0, one launch (start us, length us, event | category | flops | bytes accessed | tf_op | source)
XLA Modules:
  0.0 81.7 jit_solution(10159353076426628049)
XLA Ops:
  0.6 30.3 %forward.1 = (bf16[16,144,128]{2,1,0:T(8,128)(2,1)}, f32[512,128]{1,0:T(8,128)}) custom-call(bf16[512,256]{1,0:T(8,128)(2,1)} %tokens.3, bf16[512,256]{1,0:T(8,128)(2,1)} %grad_out.3, bf16[8192,256]{1,0:T(8,128)(2,1)} %codebook.3, bf16[512,8192]{1,0:T(8,128)(2,1)} %noise.3), custom_call_target="tpu_custom_call" | custom-call | flops 8589934592 | bytes 12582912 | tf_op jit(solution)/shard_map/forward/pallas_call | solution.py:502
  30.9 8.3 %all-to-all-start = ((bf16[16,144,128]{2,1,0:T(8,128)(2,1)}), bf16[16,144,128]{2,1,0:T(8,128)(2,1)S(1)}, u32[]{:S(2)}, u32[]{:S(2)}) async-start(bf16[16,144,128]{2,1,0:T(8,128)(2,1)} %get-tuple-element.16), calls=%async_computation | async-start | bytes 1179648 | tf_op jit(solution)/shard_map/all_to_all | solution.py:535
  39.3 13.0 %weigh.1 = (bf16[16,512,512]{2,1,0:T(8,128)(2,1)}, bf16[16,512,512]{2,1,0:T(8,128)(2,1)}, bf16[2,256,512]{2,1,0:T(8,128)(2,1)}) custom-call(bf16[512,256]{1,0:T(8,128)(2,1)} %tokens.3, bf16[512,256]{1,0:T(8,128)(2,1)} %grad_out.3, bf16[8192,256]{1,0:T(8,128)(2,1)} %codebook.3, bf16[512,8192]{1,0:T(8,128)(2,1)} %noise.3, f32[512,128]{1,0:T(8,128)} %get-tuple-element.17.sides), custom_call_target="tpu_custom_call" | custom-call | flops 4294967296 | bytes 29360128 | tf_op jit(solution)/shard_map/weigh/pallas_call | solution.py:536
  52.3 3.2 %all-to-all-done.received = bf16[16,144,128]{2,1,0:T(8,128)(2,1)S(1)} async-done(((bf16[16,144,128]{2,1,0:T(8,128)(2,1)}), bf16[16,144,128]{2,1,0:T(8,128)(2,1)S(1)}, u32[]{:S(2)}, u32[]{:S(2)}) %all-to-all-start) | async-done | bytes 589856 | tf_op jit(solution)/shard_map/all_to_all | solution.py:535
  55.5 1.9 %merge.1 = (bf16[16,32,512]{2,1,0:T(8,128)(2,1)}, f32[16,512]{1,0:T(8,128)}) custom-call(s32[1]{0:T(128)} %bitcast.me, bf16[16,144,128]{2,1,0:T(8,128)(2,1)S(1)} %all-to-all-done.received), custom_call_target="tpu_custom_call" | custom-call | tf_op jit(solution)/shard_map/merge/pallas_call | solution.py:564
  57.5 4.5 %all-to-all-start.1 = ((bf16[16,32,512]{2,1,0:T(8,128)(2,1)}), bf16[16,32,512]{2,1,0:T(8,128)(2,1)}, u32[]{:S(2)}, u32[]{:S(2)}) async-start(bf16[16,32,512]{2,1,0:T(8,128)(2,1)} %get-tuple-element.20), calls=%async_computation.1 | async-start | bytes 1048576 | tf_op jit(solution)/shard_map/all_to_all | solution.py:581
  62.0 6.5 %backward_first.1 = (bf16[4096,256]{1,0:T(8,128)(2,1)}, bf16[256,1024]{1,0:T(8,128)(2,1)}) custom-call(s32[1]{0:T(128)} %bitcast.1.block, bf16[2,256,512]{2,1,0:T(8,128)(2,1)} %get-tuple-element.21.rest_0_, bf16[16,512,512]{2,1,0:T(8,128)(2,1)} %get-tuple-element.22.rest_1_.rest_0_, bf16[16,512,512]{2,1,0:T(8,128)(2,1)} %get-tuple-element.23.rest_2_.rest_1_, ...), custom_call_target="tpu_custom_call" | custom-call | flops 1 | bytes 1 | tf_op jit(solution)/shard_map/backward_first/pallas_call | solution.py:594
  68.5 0.1 collective-permute-start
  68.6 5.6 %backward.1.refs_1_ = bf16[4096,256]{1,0:T(8,128)(2,1)S(1)} custom-call(s32[1]{0:T(128)} %bitcast.2.block, bf16[16,512,512]{2,1,0:T(8,128)(2,1)} %get-tuple-element.22.rest_1_.rest_0_, bf16[16,512,512]{2,1,0:T(8,128)(2,1)} %get-tuple-element.23.rest_2_.rest_1_, bf16[256,1024]{1,0:T(8,128)(2,1)} %get-tuple-element.26.rest_2_), custom_call_target="tpu_custom_call" | custom-call | flops 214748364800 | bytes 419430400 | tf_op jit(solution)/shard_map/backward/pallas_call | solution.py:614
  74.2 0.0 collective-permute-done.refs_0_
  74.2 3.1 %add.1._ = f32[4096,256]{1,0:T(8,128)} custom-call(bf16[4096,256]{1,0:T(8,128)(2,1)} %collective-permute-done.refs_0_, bf16[4096,256]{1,0:T(8,128)(2,1)S(1)} %backward.1.refs_1_), custom_call_target="tpu_custom_call" | custom-call | bytes 8388608 | tf_op jit(solution)/shard_map/add/pallas_call | solution.py:631
  77.4 0.0 all-to-all-done.1.gathered
  77.4 0.0 copy-start
  77.4 2.2 %copy-done = f32[4096,256]{1,0:T(8,128)S(1)} copy-done((f32[4096,256]{1,0:T(8,128)S(1)}, f32[4096,256]{1,0:T(8,128)}, u32[]{:S(2)}) %copy-start) | copy-done | bytes 4194328
  79.6 2.1 %unpack.1 = (f32[512,256]{1,0:T(8,128)}, f32[512,256]{1,0:T(8,128)}) custom-call(bf16[16,32,512]{2,1,0:T(8,128)(2,1)} %all-to-all-done.1.gathered, f32[4096,256]{1,0:T(8,128)S(1)} %copy-done), custom_call_target="tpu_custom_call" | custom-call | bytes 1572864 | tf_op jit(solution)/shard_map/unpack/pallas_call | solution.py:648
Async XLA Ops:
  30.9 24.6 %all-to-all-start = ((bf16[16,144,128]{2,1,0:T(8,128)(2,1)}), bf16[16,144,128]{2,1,0:T(8,128)(2,1)S(1)}, u32[]{:S(2)}, u32[]{:S(2)}) async-start(bf16[16,144,128]{2,1,0:T(8,128)(2,1)} %get-tuple-element.16), calls=%async_computation | async-start | bytes 1179648 | tf_op jit(solution)/shard_map/all_to_all | solution.py:535
  57.5 19.9 %all-to-all-start.1 = ((bf16[16,32,512]{2,1,0:T(8,128)(2,1)}), bf16[16,32,512]{2,1,0:T(8,128)(2,1)}, u32[]{:S(2)}, u32[]{:S(2)}) async-start(bf16[16,32,512]{2,1,0:T(8,128)(2,1)} %get-tuple-element.20), calls=%async_computation.1 | async-start | bytes 1048576 | tf_op jit(solution)/shard_map/all_to_all | solution.py:581
  68.5 5.7 %collective-permute-start = (bf16[4096,256]{1,0:T(8,128)(2,1)}, bf16[4096,256]{1,0:T(8,128)(2,1)}, u32[]{:S(2)}, u32[]{:S(2)}) collective-permute-start(bf16[4096,256]{1,0:T(8,128)(2,1)} %get-tuple-element.25), channel_id=1, source_target_pairs={{0,16},{16,0},{1,17},{17,1},{2,18},{18,2},{3,19},{19,3},{4,20},{20... | collective-permute-start | bytes 6291464 | tf_op jit(solution)/shard_map/ppermute | solution.py:487
  77.4 2.2 %copy-start = (f32[4096,256]{1,0:T(8,128)S(1)}, f32[4096,256]{1,0:T(8,128)}, u32[]{:S(2)}) copy-start(f32[4096,256]{1,0:T(8,128)} %add.1._) | copy-start | bytes 12582916

commit v21 on v20

--- a/solution.py
+++ b/solution.py
@@ -447,8 +447,9 @@
 
 
 def add_kernel(n_parts, *refs):
-    parts, own, out = refs[: n_parts - 1], refs[n_parts - 1], refs[n_parts]
-    held, result, in_sem, out_sem = refs[n_parts + 1 :]
+    parts, own, out, mark = refs[: n_parts - 1], refs[n_parts - 1], refs[n_parts], refs[n_parts + 1]
+    held, result, in_sem, out_sem = refs[n_parts + 2 :]
+    mark[...] = jnp.zeros(mark.shape, F32)
     steps, rows, _ = result.shape
 
     def fetch(i):
@@ -474,13 +475,36 @@
         send(i).wait()
 
 
-def unpack_kernel(gathered, _, quantized, gradient):
-    n_code, rows, both = gathered.shape
-    dim = both // 2
-    for g in range(n_code):
-        at = slice(g * rows, (g + 1) * rows)
-        quantized[at] = gathered[g, :, :dim].astype(F32)
-        gradient[at] = gathered[g, :, dim:].astype(F32)
+def unpack_kernel(gathered, _, quantized, gradient, held, both, in_sem, out_sem):
+    n_code, rows, width = gathered.shape
+    dim = width // 2
+    steps = min(n_code, 4)
+    group = n_code // steps
+
+    def fetch(i):
+        at = pl.ds(i * group, group)
+        return pltpu.make_async_copy(gathered.at[at], held.at[at], in_sem.at[i])
+
+    def send(i):
+        at = pl.ds(i * group * rows, group * rows)
+        return [
+            pltpu.make_async_copy(both.at[k, at], target.at[at], out_sem.at[k, i])
+            for k, target in enumerate((quantized, gradient))
+        ]
+
+    for i in range(steps):
+        fetch(i).start()
+    for i in range(steps):
+        fetch(i).wait()
+        for g in range(i * group, (i + 1) * group):
+            at = slice(g * rows, (g + 1) * rows)
+            both[0, at] = held[g, :, :dim].astype(F32)
+            both[1, at] = held[g, :, dim:].astype(F32)
+        for copy in send(i):
+            copy.start()
+    for i in range(steps):
+        for copy in send(i):
+            copy.wait()
 
 
 def swap(value, axis, size, mask):
@@ -628,11 +652,14 @@
     blocks += [swap(backward(dp_at ^ d), "dp", n_dp, d) for d in range(1, n_dp - 1)]
     blocks.append(backward(dp_at))
     steps = max(block // 512, 1)
-    own_rows = pl.pallas_call(
+    own_rows, mark = pl.pallas_call(
         functools.partial(add_kernel, n_dp),
-        out_shape=jax.ShapeDtypeStruct((block, dim), F32),
+        out_shape=(
+            jax.ShapeDtypeStruct((block, dim), F32),
+            jax.ShapeDtypeStruct((8, 128), F32),
+        ),
         in_specs=[ANY] * (n_dp - 1) + [VMEM],
-        out_specs=ANY,
+        out_specs=(ANY, VMEM),
         scratch_shapes=[
             pltpu.VMEM((n_dp - 1, steps, block // steps, dim), BF16),
             pltpu.VMEM((steps, block // steps, dim), F32),
@@ -648,14 +675,20 @@
     quantized, token_gradient = pl.pallas_call(
         unpack_kernel,
         out_shape=(jax.ShapeDtypeStruct((n_tokens, dim), F32),) * 2,
-        in_specs=[VMEM, ANY],
-        out_specs=(VMEM, VMEM),
+        in_specs=[ANY, VMEM],
+        out_specs=(ANY, ANY),
+        scratch_shapes=[
+            pltpu.VMEM((n_code, rows, 2 * dim), BF16),
+            pltpu.VMEM((2, n_tokens, dim), F32),
+            pltpu.SemaphoreType.DMA((min(n_code, 4),)),
+            pltpu.SemaphoreType.DMA((2, min(n_code, 4))),
+        ],
         compiler_params=SOME,
         cost_estimate=pl.CostEstimate(
             flops=0, bytes_accessed=12 * n_tokens * dim, transcendentals=0
         ),
         name="unpack",
-    )(gathered, own_rows)
+    )(gathered, mark)
     return quantized, token_gradient, own_rows[None]
 
 

time: 82.3 us -> 80.1 us (0.973)
  local copies, waits for them, and re-layouts: 2.18 us -> 0 us
    unnamed x2 -> x0, local copies, waits for them, and re-layouts: 2.18 us -> none
  transfers between devices with their start and end apart: 3 -> 3, of which waited for: 1 -> 1; matrix products, arithmetic and copies ran while one was open for 0% -> 0% of each run, Pallas kernels for 35% -> 36%
where the time goes in v21:
time: 80.1 us; the launch traced here: 79.6 us
  Pallas kernels  62.5 us (78%)
  starting transfers between devices  12.9 us (16%)
  waiting for transfers between devices  3.24 us (4%)
  between operations  0.9 us (1%)
    pallas_call x1, Pallas kernels, local(): pl.pallas_call(functools.partial(forward_kernel, n_code), out_shape=(jax....  30.3 us
    pallas_call x1, Pallas kernels, local(): pl.pallas_call(weigh_kernel, out_shape=(pltpu.HBM((tiles_in, n_tokens, wi...  13 us
    all_to_all x1, starting transfers between devices, local(): received = lax.all_to_all(sent, 'code', 0, 0, tiled=True)  8.33 us
    pallas_call x1, Pallas kernels, local(): pl.pallas_call(functools.partial(backward_kernel, False), out_shape=(jax....  6.51 us
    pallas_call x1, Pallas kernels, backward(): pl.pallas_call(functools.partial(backward_kernel, True), out_shape=pltpu....  5.63 us
    all_to_all x1, starting transfers between devices, local(): gathered = lax.all_to_all(spread, 'code', 0, 0, tiled=True)  4.48 us
    all_to_all x1, waiting for transfers between devices, local(): received = lax.all_to_all(sent, 'code', 0, 0, tiled=True)  3.24 us
    pallas_call x1, Pallas kernels, local(): pl.pallas_call(functools.partial(add_kernel, n_dp), out_shape=(jax.ShapeD...  3.14 us
  transfers between devices with their start and end apart: 3, of which 1 were waited for; matrix products, arithmetic and copies ran while one was open for 0% of the time, Pallas kernels for 36%

profile of v21, /device:TPU:0, one launch (start us, length us, event | category | flops | bytes accessed | tf_op | source)
XLA Modules:
  0.0 79.6 jit_solution(14573865915603735582)
XLA Ops:
  0.6 30.3 %forward.1 = (bf16[16,144,128]{2,1,0:T(8,128)(2,1)}, f32[512,128]{1,0:T(8,128)}) custom-call(bf16[512,256]{1,0:T(8,128)(2,1)} %tokens.3, bf16[512,256]{1,0:T(8,128)(2,1)} %grad_out.3, bf16[8192,256]{1,0:T(8,128)(2,1)} %codebook.3, bf16[512,8192]{1,0:T(8,128)(2,1)} %noise.3), custom_call_target="tpu_custom_call" | custom-call | flops 8589934592 | bytes 12582912 | tf_op jit(solution)/shard_map/forward/pallas_call | solution.py:526
  30.9 8.3 %all-to-all-start = ((bf16[16,144,128]{2,1,0:T(8,128)(2,1)}), bf16[16,144,128]{2,1,0:T(8,128)(2,1)S(1)}, u32[]{:S(2)}, u32[]{:S(2)}) async-start(bf16[16,144,128]{2,1,0:T(8,128)(2,1)} %get-tuple-element.18), calls=%async_computation | async-start | bytes 1179648 | tf_op jit(solution)/shard_map/all_to_all | solution.py:559
  39.3 13.0 %weigh.1 = (bf16[16,512,512]{2,1,0:T(8,128)(2,1)}, bf16[16,512,512]{2,1,0:T(8,128)(2,1)}, bf16[2,256,512]{2,1,0:T(8,128)(2,1)}) custom-call(bf16[512,256]{1,0:T(8,128)(2,1)} %tokens.3, bf16[512,256]{1,0:T(8,128)(2,1)} %grad_out.3, bf16[8192,256]{1,0:T(8,128)(2,1)} %codebook.3, bf16[512,8192]{1,0:T(8,128)(2,1)} %noise.3, f32[512,128]{1,0:T(8,128)} %get-tuple-element.19.sides), custom_call_target="tpu_custom_call" | custom-call | flops 4294967296 | bytes 29360128 | tf_op jit(solution)/shard_map/weigh/pallas_call | solution.py:560
  52.3 3.2 %all-to-all-done.received = bf16[16,144,128]{2,1,0:T(8,128)(2,1)S(1)} async-done(((bf16[16,144,128]{2,1,0:T(8,128)(2,1)}), bf16[16,144,128]{2,1,0:T(8,128)(2,1)S(1)}, u32[]{:S(2)}, u32[]{:S(2)}) %all-to-all-start) | async-done | bytes 589856 | tf_op jit(solution)/shard_map/all_to_all | solution.py:559
  55.5 1.9 %merge.1 = (bf16[16,32,512]{2,1,0:T(8,128)(2,1)}, f32[16,512]{1,0:T(8,128)}) custom-call(s32[1]{0:T(128)} %bitcast.me, bf16[16,144,128]{2,1,0:T(8,128)(2,1)S(1)} %all-to-all-done.received), custom_call_target="tpu_custom_call" | custom-call | tf_op jit(solution)/shard_map/merge/pallas_call | solution.py:588
  57.5 4.5 %all-to-all-start.1 = ((bf16[16,32,512]{2,1,0:T(8,128)(2,1)}), bf16[16,32,512]{2,1,0:T(8,128)(2,1)}, u32[]{:S(2)}, u32[]{:S(2)}) async-start(bf16[16,32,512]{2,1,0:T(8,128)(2,1)} %get-tuple-element.22), calls=%async_computation.1 | async-start | bytes 1048576 | tf_op jit(solution)/shard_map/all_to_all | solution.py:605
  62.0 6.5 %backward_first.1 = (bf16[4096,256]{1,0:T(8,128)(2,1)}, bf16[256,1024]{1,0:T(8,128)(2,1)}) custom-call(s32[1]{0:T(128)} %bitcast.1.block, bf16[2,256,512]{2,1,0:T(8,128)(2,1)} %get-tuple-element.23.rest_0_, bf16[16,512,512]{2,1,0:T(8,128)(2,1)} %get-tuple-element.24.rest_1_.rest_0_, bf16[16,512,512]{2,1,0:T(8,128)(2,1)} %get-tuple-element.25.rest_2_.rest_1_, ...), custom_call_target="tpu_custom_call" | custom-call | flops 1 | bytes 1 | tf_op jit(solution)/shard_map/backward_first/pallas_call | solution.py:618
  68.5 0.1 collective-permute-start
  68.6 5.6 %backward.1.refs_1_ = bf16[4096,256]{1,0:T(8,128)(2,1)S(1)} custom-call(s32[1]{0:T(128)} %bitcast.2.block, bf16[16,512,512]{2,1,0:T(8,128)(2,1)} %get-tuple-element.24.rest_1_.rest_0_, bf16[16,512,512]{2,1,0:T(8,128)(2,1)} %get-tuple-element.25.rest_2_.rest_1_, bf16[256,1024]{1,0:T(8,128)(2,1)} %get-tuple-element.28.rest_2_), custom_call_target="tpu_custom_call" | custom-call | flops 214748364800 | bytes 419430400 | tf_op jit(solution)/shard_map/backward/pallas_call | solution.py:638
  74.2 0.0 collective-permute-done.refs_0_
  74.2 3.1 %add.1 = (f32[4096,256]{1,0:T(8,128)}, f32[8,128]{1,0:T(8,128)S(1)}) custom-call(bf16[4096,256]{1,0:T(8,128)(2,1)} %collective-permute-done.refs_0_, bf16[4096,256]{1,0:T(8,128)(2,1)S(1)} %backward.1.refs_1_), custom_call_target="tpu_custom_call" | custom-call | bytes 8388608 | tf_op jit(solution)/shard_map/add/pallas_call | solution.py:655
  77.4 0.0 all-to-all-done.1.gathered
  77.4 2.0 %unpack.1 = (f32[512,256]{1,0:T(8,128)}, f32[512,256]{1,0:T(8,128)}) custom-call(bf16[16,32,512]{2,1,0:T(8,128)(2,1)} %all-to-all-done.1.gathered, f32[8,128]{1,0:T(8,128)S(1)} %get-tuple-element.29._), custom_call_target="tpu_custom_call" | custom-call | bytes 1572864 | tf_op jit(solution)/shard_map/unpack/pallas_call | solution.py:675
Async XLA Ops:
  30.9 24.6 %all-to-all-start = ((bf16[16,144,128]{2,1,0:T(8,128)(2,1)}), bf16[16,144,128]{2,1,0:T(8,128)(2,1)S(1)}, u32[]{:S(2)}, u32[]{:S(2)}) async-start(bf16[16,144,128]{2,1,0:T(8,128)(2,1)} %get-tuple-element.18), calls=%async_computation | async-start | bytes 1179648 | tf_op jit(solution)/shard_map/all_to_all | solution.py:559
  57.5 19.9 %all-to-all-start.1 = ((bf16[16,32,512]{2,1,0:T(8,128)(2,1)}), bf16[16,32,512]{2,1,0:T(8,128)(2,1)}, u32[]{:S(2)}, u32[]{:S(2)}) async-start(bf16[16,32,512]{2,1,0:T(8,128)(2,1)} %get-tuple-element.22), calls=%async_computation.1 | async-start | bytes 1048576 | tf_op jit(solution)/shard_map/all_to_all | solution.py:605
  68.5 5.7 %collective-permute-start = (bf16[4096,256]{1,0:T(8,128)(2,1)}, bf16[4096,256]{1,0:T(8,128)(2,1)}, u32[]{:S(2)}, u32[]{:S(2)}) collective-permute-start(bf16[4096,256]{1,0:T(8,128)(2,1)} %get-tuple-element.27), channel_id=1, source_target_pairs={{0,16},{16,0},{1,17},{17,1},{2,18},{18,2},{3,19},{19,3},{4,20},{20... | collective-permute-start | bytes 6291464 | tf_op jit(solution)/shard_map/ppermute | solution.py:511

commit v22 on v21

--- a/solution.py
+++ b/solution.py
@@ -23,8 +23,8 @@
 SMEM = pl.BlockSpec(memory_space=pltpu.SMEM)
 ANY = pl.BlockSpec(memory_space=pl.ANY)
 FULL = pltpu.CompilerParams(vmem_limit_bytes=60 * MIB)
-MOST = pltpu.CompilerParams(vmem_limit_bytes=54 * MIB)
-SOME = pltpu.CompilerParams(vmem_limit_bytes=24 * MIB)
+MOST = pltpu.CompilerParams(vmem_limit_bytes=52 * MIB)
+SOME = pltpu.CompilerParams(vmem_limit_bytes=16 * MIB)
 
 
 def dot(left, right, left_dim=1, right_dim=0):
@@ -475,15 +475,11 @@
         send(i).wait()
 
 
-def unpack_kernel(gathered, _, quantized, gradient, held, both, in_sem, out_sem):
+def unpack_kernel(gathered, _, quantized, gradient, both, out_sem):
     n_code, rows, width = gathered.shape
     dim = width // 2
     steps = min(n_code, 4)
     group = n_code // steps
-
-    def fetch(i):
-        at = pl.ds(i * group, group)
-        return pltpu.make_async_copy(gathered.at[at], held.at[at], in_sem.at[i])
 
     def send(i):
         at = pl.ds(i * group * rows, group * rows)
@@ -493,13 +489,10 @@
         ]
 
     for i in range(steps):
-        fetch(i).start()
-    for i in range(steps):
-        fetch(i).wait()
         for g in range(i * group, (i + 1) * group):
             at = slice(g * rows, (g + 1) * rows)
-            both[0, at] = held[g, :, :dim].astype(F32)
-            both[1, at] = held[g, :, dim:].astype(F32)
+            both[0, at] = gathered[g, :, :dim].astype(F32)
+            both[1, at] = gathered[g, :, dim:].astype(F32)
         for copy in send(i):
             copy.start()
     for i in range(steps):
@@ -675,12 +668,10 @@
     quantized, token_gradient = pl.pallas_call(
         unpack_kernel,
         out_shape=(jax.ShapeDtypeStruct((n_tokens, dim), F32),) * 2,
-        in_specs=[ANY, VMEM],
+        in_specs=[VMEM, VMEM],
         out_specs=(ANY, ANY),
         scratch_shapes=[
-            pltpu.VMEM((n_code, rows, 2 * dim), BF16),
             pltpu.VMEM((2, n_tokens, dim), F32),
-            pltpu.SemaphoreType.DMA((min(n_code, 4),)),
             pltpu.SemaphoreType.DMA((2, min(n_code, 4))),
         ],
         compiler_params=SOME,

time: 80.1 us -> 82.2 us (1.026)
  local copies, waits for them, and re-layouts: 0 us -> 2.58 us
    unnamed x0 -> x6, local copies, waits for them, and re-layouts: none -> 2.58 us
  transfers between devices with their start and end apart: 3 -> 3, of which waited for: 1 -> 1; matrix products, arithmetic and copies ran while one was open for 0% -> 0% of each run, Pallas kernels for 36% -> 34%
where the time goes in v22:
time: 82.2 us; the launch traced here: 81.4 us
  Pallas kernels  61.9 us (75%)
  starting transfers between devices  12.8 us (16%)
  waiting for transfers between devices  3.27 us (4%)
  local copies, waits for them, and re-layouts  2.58 us (3%)
  between operations  0.92 us (1%)
    pallas_call x1, Pallas kernels, local(): pl.pallas_call(functools.partial(forward_kernel, n_code), out_shape=(jax....  30.3 us
    pallas_call x1, Pallas kernels, local(): pl.pallas_call(weigh_kernel, out_shape=(pltpu.HBM((tiles_in, n_tokens, wi...  13 us
    all_to_all x1, starting transfers between devices, local(): received = lax.all_to_all(sent, 'code', 0, 0, tiled=True)  8.33 us
    pallas_call x1, Pallas kernels, local(): pl.pallas_call(functools.partial(backward_kernel, False), out_shape=(jax....  5.8 us
    pallas_call x1, Pallas kernels, backward(): pl.pallas_call(functools.partial(backward_kernel, True), out_shape=pltpu....  5.62 us
    all_to_all x1, starting transfers between devices, local(): gathered = lax.all_to_all(spread, 'code', 0, 0, tiled=True)  4.47 us
    all_to_all x1, waiting for transfers between devices, local(): received = lax.all_to_all(sent, 'code', 0, 0, tiled=True)  3.26 us
    pallas_call x1, Pallas kernels, local(): pl.pallas_call(functools.partial(add_kernel, n_dp), out_shape=(jax.ShapeD...  3.14 us
  transfers between devices with their start and end apart: 3, of which 1 were waited for; matrix products, arithmetic and copies ran while one was open for 0% of the time, Pallas kernels for 34%

profile of v22, /device:TPU:0, one launch (start us, length us, event | category | flops | bytes accessed | tf_op | source)
XLA Modules:
  0.0 81.4 jit_solution(8700039304953198158)
XLA Ops:
  0.6 30.3 %forward.1 = (bf16[16,144,128]{2,1,0:T(8,128)(2,1)}, f32[512,128]{1,0:T(8,128)}) custom-call(bf16[512,256]{1,0:T(8,128)(2,1)} %tokens.3, bf16[512,256]{1,0:T(8,128)(2,1)} %grad_out.3, bf16[8192,256]{1,0:T(8,128)(2,1)} %codebook.3, bf16[512,8192]{1,0:T(8,128)(2,1)} %noise.3), custom_call_target="tpu_custom_call" | custom-call | flops 8589934592 | bytes 12582912 | tf_op jit(solution)/shard_map/forward/pallas_call | solution.py:519
  30.9 8.3 %all-to-all-start = ((bf16[16,144,128]{2,1,0:T(8,128)(2,1)}), bf16[16,144,128]{2,1,0:T(8,128)(2,1)S(1)}, u32[]{:S(2)}, u32[]{:S(2)}) async-start(bf16[16,144,128]{2,1,0:T(8,128)(2,1)} %get-tuple-element.18), calls=%async_computation | async-start | bytes 1179648 | tf_op jit(solution)/shard_map/all_to_all | solution.py:552
  39.3 13.0 %weigh.1 = (bf16[16,512,512]{2,1,0:T(8,128)(2,1)}, bf16[16,512,512]{2,1,0:T(8,128)(2,1)}, bf16[2,256,512]{2,1,0:T(8,128)(2,1)}) custom-call(bf16[512,256]{1,0:T(8,128)(2,1)} %tokens.3, bf16[512,256]{1,0:T(8,128)(2,1)} %grad_out.3, bf16[8192,256]{1,0:T(8,128)(2,1)} %codebook.3, bf16[512,8192]{1,0:T(8,128)(2,1)} %noise.3, f32[512,128]{1,0:T(8,128)} %get-tuple-element.19.sides), custom_call_target="tpu_custom_call" | custom-call | flops 4294967296 | bytes 29360128 | tf_op jit(solution)/shard_map/weigh/pallas_call | solution.py:553
  52.3 3.3 %all-to-all-done.received = bf16[16,144,128]{2,1,0:T(8,128)(2,1)S(1)} async-done(((bf16[16,144,128]{2,1,0:T(8,128)(2,1)}), bf16[16,144,128]{2,1,0:T(8,128)(2,1)S(1)}, u32[]{:S(2)}, u32[]{:S(2)}) %all-to-all-start) | async-done | bytes 589856 | tf_op jit(solution)/shard_map/all_to_all | solution.py:552
  55.5 1.9 %merge.1 = (bf16[16,32,512]{2,1,0:T(8,128)(2,1)}, f32[16,512]{1,0:T(8,128)}) custom-call(s32[1]{0:T(128)} %bitcast.me, bf16[16,144,128]{2,1,0:T(8,128)(2,1)S(1)} %all-to-all-done.received), custom_call_target="tpu_custom_call" | custom-call | tf_op jit(solution)/shard_map/merge/pallas_call | solution.py:581
  57.5 4.5 %all-to-all-start.1 = ((bf16[16,32,512]{2,1,0:T(8,128)(2,1)}), bf16[16,32,512]{2,1,0:T(8,128)(2,1)}, u32[]{:S(2)}, u32[]{:S(2)}) async-start(bf16[16,32,512]{2,1,0:T(8,128)(2,1)} %get-tuple-element.22), calls=%async_computation.1 | async-start | bytes 1048576 | tf_op jit(solution)/shard_map/all_to_all | solution.py:598
  62.0 0.0 copy-start
  62.0 1.0 %copy-done = bf16[2,256,512]{2,1,0:T(8,128)(2,1)S(1)} copy-done((bf16[2,256,512]{2,1,0:T(8,128)(2,1)S(1)}, bf16[2,256,512]{2,1,0:T(8,128)(2,1)}, u32[]{:S(2)}) %copy-start) | copy-done | bytes 524312
  63.0 0.0 copy-start.1
  63.0 0.8 copy-done.1
  63.8 5.8 %backward_first.1 = (bf16[4096,256]{1,0:T(8,128)(2,1)}, bf16[256,1024]{1,0:T(8,128)(2,1)S(1)}) custom-call(s32[1]{0:T(128)} %bitcast.1.block, bf16[2,256,512]{2,1,0:T(8,128)(2,1)S(1)} %copy-done, bf16[16,512,512]{2,1,0:T(8,128)(2,1)} %get-tuple-element.24.rest_1_.rest_0_, bf16[16,512,512]{2,1,0:T(8,128)(2,1)} %get-tuple-element.25.rest_2_.rest_1_, ...), custom_call_target="tpu_custom_call" | custom-call | flops 1 | bytes 1 | tf_op jit(solution)/shard_map/backward_first/pallas_call | solution.py:611
  69.6 0.0 copy-start.2
  69.6 0.8 copy-done.2
  70.4 0.0 collective-permute-start
  70.4 5.6 %backward.1.refs_1_ = bf16[4096,256]{1,0:T(8,128)(2,1)S(1)} custom-call(s32[1]{0:T(128)} %bitcast.2.block, bf16[16,512,512]{2,1,0:T(8,128)(2,1)} %get-tuple-element.24.rest_1_.rest_0_, bf16[16,512,512]{2,1,0:T(8,128)(2,1)} %get-tuple-element.25.rest_2_.rest_1_, bf16[256,1024]{1,0:T(8,128)(2,1)} %copy-done.2), custom_call_target="tpu_custom_call" | custom-call | flops 214748364800 | bytes 419430400 | tf_op jit(solution)/shard_map/backward/pallas_call | solution.py:631
  76.0 0.0 collective-permute-done.refs_0_
  76.0 3.1 %add.1 = (f32[4096,256]{1,0:T(8,128)}, f32[8,128]{1,0:T(8,128)S(1)}) custom-call(bf16[4096,256]{1,0:T(8,128)(2,1)} %collective-permute-done.refs_0_, bf16[4096,256]{1,0:T(8,128)(2,1)S(1)} %backward.1.refs_1_), custom_call_target="tpu_custom_call" | custom-call | bytes 8388608 | tf_op jit(solution)/shard_map/add/pallas_call | solution.py:648
  79.2 0.0 all-to-all-done.1.gathered
  79.2 2.1 %unpack.1 = (f32[512,256]{1,0:T(8,128)}, f32[512,256]{1,0:T(8,128)}) custom-call(bf16[16,32,512]{2,1,0:T(8,128)(2,1)} %all-to-all-done.1.gathered, f32[8,128]{1,0:T(8,128)S(1)} %get-tuple-element.29._), custom_call_target="tpu_custom_call" | custom-call | bytes 1572864 | tf_op jit(solution)/shard_map/unpack/pallas_call | solution.py:668
Async XLA Ops:
  30.9 24.6 %all-to-all-start = ((bf16[16,144,128]{2,1,0:T(8,128)(2,1)}), bf16[16,144,128]{2,1,0:T(8,128)(2,1)S(1)}, u32[]{:S(2)}, u32[]{:S(2)}) async-start(bf16[16,144,128]{2,1,0:T(8,128)(2,1)} %get-tuple-element.18), calls=%async_computation | async-start | bytes 1179648 | tf_op jit(solution)/shard_map/all_to_all | solution.py:552
  57.5 21.7 %all-to-all-start.1 = ((bf16[16,32,512]{2,1,0:T(8,128)(2,1)}), bf16[16,32,512]{2,1,0:T(8,128)(2,1)}, u32[]{:S(2)}, u32[]{:S(2)}) async-start(bf16[16,32,512]{2,1,0:T(8,128)(2,1)} %get-tuple-element.22), calls=%async_computation.1 | async-start | bytes 1048576 | tf_op jit(solution)/shard_map/all_to_all | solution.py:598
  62.0 1.0 %copy-start = (bf16[2,256,512]{2,1,0:T(8,128)(2,1)S(1)}, bf16[2,256,512]{2,1,0:T(8,128)(2,1)}, u32[]{:S(2)}) copy-start(bf16[2,256,512]{2,1,0:T(8,128)(2,1)} %get-tuple-element.23.rest_0_) | copy-start | bytes 1572868
  63.0 0.8 copy-start.1
  69.6 0.8 copy-start.2
  70.4 5.6 %collective-permute-start = (bf16[4096,256]{1,0:T(8,128)(2,1)}, bf16[4096,256]{1,0:T(8,128)(2,1)}, u32[]{:S(2)}, u32[]{:S(2)}) collective-permute-start(bf16[4096,256]{1,0:T(8,128)(2,1)} %get-tuple-element.27), channel_id=1, source_target_pairs={{0,16},{16,0},{1,17},{17,1},{2,18},{18,2},{3,19},{19,3},{4,20},{20... | collective-permute-start | bytes 6291464 | tf_op jit(solution)/shard_map/ppermute | solution.py:504
